TPU v7x, 32 devices: a whole 2x2x4 slice. The times are simulated.
32 devices in a mesh: gz: 4 (over x, core), gx: 8 (over z, y).
Axes of the slice: x: 2, y: 2, z: 4, core: 2. Of those that a mesh axis runs over, the one named last changes fastest.
Arguments:
- clean_field: float32 [3, 8, 4, 512], P(None, 'gx', None, 'gz'), may hold values from -64 to 64
- noise_field: float32 [3, 8, 4, 512], P(None, 'gx', None, 'gz'), may hold values from -6 to 6
- timestep: int32 [1], replicated, may hold values from 0 to 499
- dilations: int32 [2], replicated, may hold values from 1 to 256, as said below
- w_in: float32 [3, 128], replicated, may hold values from -3.5 to 3.5
- w_time: float32 [128, 128], replicated, may hold values from -0.5 to 0.5
- w_z: bfloat16 [2, 3, 128, 128], replicated, may hold values from -0.15625 to 0.15625
- w_xy: bfloat16 [2, 8, 128, 128], replicated, may hold values from -0.15625 to 0.15625
- w_point: bfloat16 [2, 128, 128], replicated, may hold values from -0.5 to 0.5
- biases: float32 [2, 128], replicated, may hold values from -3 to 3
- norm_gains: float32 [3, 128], replicated, may hold values from 0.25 to 1.75
- w_out: bfloat16 [3, 128], replicated, may hold values from -0.5 to 0.5
Outputs:
- prediction: float32 [3, 8, 4, 512], P(None, 'gx', None, 'gz')
- field_grad: float32 [3, 8, 4, 512], P(None, 'gx', None, 'gz')
- grad_w_in: float32 [3, 128], replicated
- grad_w_time: float32 [128, 128], replicated
- grad_w_z: float32 [2, 3, 128, 128], replicated
- grad_w_xy: float32 [2, 8, 128, 128], replicated
- grad_w_point: float32 [2, 128, 128], replicated
- grad_biases: float32 [2, 128], replicated
- grad_norm_gains: float32 [3, 128], replicated
- grad_w_out: float32 [3, 128], replicated
Inputs may be any that keep to these rules, and one draw needn't show every extreme that they name: `dilations`: every layer's dilation is a power of two no larger than 256; one layer's dilation equals 256 and every other layer's is at most 128.
All inputs are finite; a program needn't handle non-finite values.
Results may differ from a plain program's by a relative error of at most 0.0043.
Values may be sent and summed in bfloat16 or wider, within the bound.
No kernel may reach another device: no remote copies, remote signals or barrier semaphores. Data moves between devices by JAX's collectives and lax.ppermute only.
A program may use at most 64 MiB of HBM per device.

v0:
```python
import math

import jax
import jax.numpy as jnp
from jax import lax
from jax.sharding import PartitionSpec as P

STEPS = 1000


eps_norm = 1e-05
highest = lax.Precision.HIGHEST
plane_offsets = ((-1, -1), (-1, 0), (-1, 1), (0, -1), (0, 1), (1, -1), (1, 0), (1, 1))


def padded_2(cells, sides, width):
    for axis, dim in sides:
        count = lax.axis_size(axis)
        head = lax.slice_in_dim(cells, 0, width, axis=dim)
        tail = lax.slice_in_dim(cells, cells.shape[dim] - width, cells.shape[dim], axis=dim)
        cells = jnp.concatenate(
            [
                lax.ppermute(tail, axis, [(i, (i + 1) % count) for i in range(count)]),
                cells,
                lax.ppermute(head, axis, [((i + 1) % count, i) for i in range(count)]),
            ],
            axis=dim,
        )
    return cells


def passed_along(value, axis, steps):
    count = lax.axis_size(axis)
    pairs = [(source, (source + steps) % count) for source in range(count)]
    return lax.ppermute(value, axis, pairs)


def time_terms(timestep, w_time):
    moment = timestep[0].astype(jnp.float32)
    half_width = w_time.shape[0] // 2
    alpha_bar = jnp.cos(0.5 * math.pi * (moment + 0.5) / STEPS) ** 2
    ladder = jnp.exp(-math.log(10000.0) * jnp.arange(half_width, dtype=jnp.float32) / half_width)
    angles = moment * ladder
    features = jnp.concatenate([jnp.sin(angles), jnp.cos(angles)])
    time_raw = jnp.dot(features, w_time, precision=highest)
    return (alpha_bar, features, time_raw, jax.nn.silu(time_raw))


def contract_cells(left, right):
    return lax.dot_general(
        left, right, (((0, 1, 2), (0, 1, 2)), ((), ())), preferred_element_type=jnp.float32
    )


def plane_tap(padded, shift_x, shift_y, rows_x, rows_y):
    return padded[1 + shift_x : 1 + shift_x + rows_x, 1 + shift_y : 1 + shift_y + rows_y]


def plane_pad(source):
    rimmed = padded_2(source, (("gx", 0),), 1)
    return jnp.pad(rimmed, ((0, 0), (1, 1), (0, 0), (0, 0)))


def slab_windows(source, dilation):
    slab_depth = source.shape[2]
    above = passed_along(source, "gz", -1)
    above_far = passed_along(source, "gz", -2)
    below = passed_along(source, "gz", 1)
    below_far = passed_along(source, "gz", 2)
    ahead_rows = jnp.concatenate([source, above, above_far], axis=2)
    behind_rows = jnp.concatenate([below_far, below, source], axis=2)
    upper = lax.dynamic_slice_in_dim(ahead_rows, dilation, slab_depth, 2)
    lower = lax.dynamic_slice_in_dim(behind_rows, 2 * slab_depth - dilation, slab_depth, 2)
    return (lower, upper)


def normalize(hidden, gains, cell_count):
    average = lax.psum(jnp.sum(hidden, axis=(0, 1, 2)), ("gz", "gx")) / cell_count
    centered = hidden - average
    spread = lax.psum(jnp.sum(centered * centered, axis=(0, 1, 2)), ("gz", "gx")) / cell_count
    inverse_std = lax.rsqrt(spread + eps_norm)
    whitened = (hidden - average) * inverse_std
    return ((whitened * gains).astype(jnp.bfloat16), whitened, inverse_std)


def norm_back(d_normed, whitened, inverse_std, gains, cell_count):
    scaled = d_normed * gains
    sum_grad, sum_cross = lax.psum(
        (jnp.sum(scaled, axis=(0, 1, 2)), jnp.sum(scaled * whitened, axis=(0, 1, 2))), ("gz", "gx")
    )
    d_hidden = inverse_std * (scaled - sum_grad / cell_count - whitened * (sum_cross / cell_count))
    return (d_hidden, jnp.sum(d_normed * whitened, axis=(0, 1, 2)))


def conv_forward(normed, dilation, weights_z, weights_xy):
    rows_x, rows_y = (normed.shape[0], normed.shape[1])
    lower, upper = slab_windows(normed, dilation)
    padded = plane_pad(normed)
    summed = jnp.dot(lower, weights_z[0], preferred_element_type=jnp.float32)
    summed = summed + jnp.dot(normed, weights_z[1], preferred_element_type=jnp.float32)
    summed = summed + jnp.dot(upper, weights_z[2], preferred_element_type=jnp.float32)
    for tap_number, (shift_x, shift_y) in enumerate(plane_offsets):
        summed = summed + jnp.dot(
            plane_tap(padded, shift_x, shift_y, rows_x, rows_y),
            weights_xy[tap_number],
            preferred_element_type=jnp.float32,
        )
    return summed


def conv_backward(pre_cot, normed, dilation, weights_z, weights_xy):
    rows_x, rows_y = (normed.shape[0], normed.shape[1])
    lower_cot, upper_cot = slab_windows(pre_cot, dilation)
    padded_cot = plane_pad(pre_cot)
    d_normed = jnp.dot(upper_cot, weights_z[0].T, preferred_element_type=jnp.float32)
    d_normed = d_normed + jnp.dot(pre_cot, weights_z[1].T, preferred_element_type=jnp.float32)
    d_normed = d_normed + jnp.dot(lower_cot, weights_z[2].T, preferred_element_type=jnp.float32)
    xy_terms = []
    for tap_number, (shift_x, shift_y) in enumerate(plane_offsets):
        shifted = plane_tap(padded_cot, -shift_x, -shift_y, rows_x, rows_y)
        d_normed = d_normed + jnp.dot(
            shifted, weights_xy[tap_number].T, preferred_element_type=jnp.float32
        )
        xy_terms.append(contract_cells(normed, shifted))
    z_terms = jnp.stack(
        [
            contract_cells(normed, upper_cot),
            contract_cells(normed, pre_cot),
            contract_cells(normed, lower_cot),
        ]
    )
    return (d_normed, z_terms, jnp.stack(xy_terms))


def per_device(
    clean_field,
    noise_field,
    timestep,
    dilations,
    w_in,
    w_time,
    w_z,
    w_xy,
    w_point,
    biases,
    norm_gains,
    w_out,
):
    layer_total = w_z.shape[0]
    rows_x, rows_y, slab_depth = (clean_field.shape[1], clean_field.shape[2], clean_field.shape[3])
    plane_cells = rows_x * lax.axis_size("gx") * slab_depth * lax.axis_size("gz")
    cell_count = float(plane_cells * rows_y)
    inv_area = 1.0 / plane_cells
    alpha_bar, features, time_raw, time_code = time_terms(timestep, w_time)
    noisy = jnp.sqrt(alpha_bar) * clean_field + jnp.sqrt(1.0 - alpha_bar) * noise_field
    stream = jnp.einsum("kxyz,kc->xyzc", noisy, w_in, precision=highest)
    saved = []
    for which_layer in range(layer_total):
        normed, whitened, inverse_std = normalize(stream, norm_gains[which_layer], cell_count)
        pre_act = conv_forward(normed, dilations[which_layer], w_z[which_layer], w_xy[which_layer])
        pre_act = pre_act + biases[which_layer] + time_code
        activated = jax.nn.gelu(pre_act).astype(jnp.bfloat16)
        saved.append((normed, whitened, inverse_std, pre_act, activated))
        stream = stream + jnp.dot(
            activated, w_point[which_layer], preferred_element_type=jnp.float32
        )
    out_normed, out_white, out_inverse = normalize(stream, norm_gains[layer_total], cell_count)
    prediction = jnp.einsum("xyzc,kc->kxyz", out_normed, w_out, preferred_element_type=jnp.float32)
    misfit = prediction - noise_field
    d_out = jnp.einsum("kxyz,kc->xyzc", misfit, w_out.astype(jnp.float32), precision=highest)
    out_raw = jnp.einsum(
        "kxyz,xyzc->kc", misfit, out_normed, precision=highest, preferred_element_type=jnp.float32
    )
    d_stream, out_gain_raw = norm_back(
        d_out, out_white, out_inverse, norm_gains[layer_total], cell_count
    )
    z_list, xy_list, point_list, bias_list, gain_list = ([], [], [], [], [])
    for which_layer in reversed(range(layer_total)):
        normed, whitened, inverse_std, pre_act, activated = saved[which_layer]
        stream_cot = d_stream.astype(jnp.bfloat16)
        point_raw = contract_cells(activated, stream_cot)
        d_act = jnp.dot(stream_cot, w_point[which_layer].T, preferred_element_type=jnp.float32)
        gelu_back = jax.vjp(jax.nn.gelu, pre_act)[1]
        pre_cot = gelu_back(d_act)[0].astype(jnp.bfloat16)
        bias_raw = jnp.sum(pre_cot, axis=(0, 1, 2), dtype=jnp.float32)
        d_normed, z_raw, xy_raw = conv_backward(
            pre_cot, normed, dilations[which_layer], w_z[which_layer], w_xy[which_layer]
        )
        d_back, gain_raw = norm_back(
            d_normed, whitened, inverse_std, norm_gains[which_layer], cell_count
        )
        d_stream = d_stream + d_back
        z_list.insert(0, z_raw)
        xy_list.insert(0, xy_raw)
        point_list.insert(0, point_raw)
        bias_list.insert(0, bias_raw)
        gain_list.insert(0, gain_raw)
    field_grad = jnp.einsum("xyzc,kc->kxyz", d_stream, w_in, precision=highest)
    in_raw = jnp.einsum("kxyz,xyzc->kc", noisy, d_stream, precision=highest)
    z_all, xy_all, point_all, bias_all, gain_all, in_raw, out_raw = lax.psum(
        (
            jnp.stack(z_list),
            jnp.stack(xy_list),
            jnp.stack(point_list),
            jnp.stack(bias_list),
            jnp.stack(gain_list + [out_gain_raw]),
            in_raw,
            out_raw,
        ),
        ("gz", "gx"),
    )
    time_back = jax.vjp(jax.nn.silu, time_raw)[1](jnp.sum(bias_all, axis=0))[0]
    grad_w_time = inv_area * jnp.outer(features, time_back)
    return (
        prediction,
        field_grad,
        inv_area * in_raw,
        grad_w_time,
        inv_area * z_all,
        inv_area * xy_all,
        inv_area * point_all,
        inv_area * bias_all,
        inv_area * gain_all,
        inv_area * out_raw,
    )


def solution(mesh):
    return jax.shard_map(
        per_device,
        mesh=mesh,
        in_specs=(
            P(None, "gx", None, "gz"),
            P(None, "gx", None, "gz"),
            P(),
            P(),
            P(),
            P(),
            P(),
            P(),
            P(),
            P(),
            P(),
            P(),
        ),
        out_specs=(
            P(None, "gx", None, "gz"),
            P(None, "gx", None, "gz"),
            P(),
            P(),
            P(),
            P(),
            P(),
            P(),
            P(),
            P(),
        ),
        check_vma=False,
    )
```

profile of v0, /device:TPU:0, one launch (start us, length us, event | category | flops | bytes accessed | tf_op | source)
XLA Modules:
  0.0 635.6 jit_solution(4113949629756468828)
XLA Ops:
  8.1 0.8 slice_bitcast_fusion.60
  8.9 0.7 add_bitcast_fusion
  9.7 1.3 fusion.220
  10.9 42.0 %psum.133 = f32[128]{0:T(128)S(1)} all-reduce(f32[128]{0:T(128)S(1)} %get-tuple-element.57), channel_id=1, replica_groups=mesh['gz'=4,'gx'=8] {'gz','gx'}, use_global_device_ids=true, to_apply=%region_1.2 | all-reduce | flops 128 | bytes 1024 | tf_op jit(solution)/shard_map/psum | solution.py:78
  53.1 40.1 %psum.134 = f32[128]{0:T(128)S(1)} all-reduce(f32[128]{0:T(128)S(1)} %multiply_reduce_fusion.8), channel_id=1, replica_groups=mesh['gz'=4,'gx'=8] {'gz','gx'}, use_global_device_ids=true, to_apply=%region_3.4 | all-reduce | flops 128 | bytes 1024 | tf_op jit(solution)/shard_map/psum | solution.py:80
  93.3 4.0 collective-permute-start.4
  97.7 1.5 collective-permute-start
  99.3 1.3 fusion.219
  107.3 0.8 fusion.218
  111.4 39.1 %psum.135 = f32[128]{0:T(128)S(1)} all-reduce(f32[128]{0:T(128)S(1)} %get-tuple-element.60), channel_id=1, replica_groups=mesh['gz'=4,'gx'=8] {'gz','gx'}, use_global_device_ids=true, to_apply=%region_5.6 | all-reduce | flops 128 | bytes 1024 | tf_op jit(solution)/shard_map/psum | solution.py:78
  150.6 41.6 %psum.136 = f32[128]{0:T(128)S(1)} all-reduce(f32[128]{0:T(128)S(1)} %multiply_reduce_fusion.7), channel_id=1, replica_groups=mesh['gz'=4,'gx'=8] {'gz','gx'}, use_global_device_ids=true, to_apply=%region_7.8 | all-reduce | flops 128 | bytes 1024 | tf_op jit(solution)/shard_map/psum | solution.py:80
  192.3 4.0 collective-permute-start.9
  197.4 1.4 collective-permute-done.9
  198.9 5.1 collective-permute-done.8
  206.7 39.8 %psum.137 = f32[128]{0:T(128)S(1)} all-reduce(f32[128]{0:T(128)S(1)} %get-tuple-element.62), channel_id=1, replica_groups=mesh['gz'=4,'gx'=8] {'gz','gx'}, use_global_device_ids=true, to_apply=%region_9.10 | all-reduce | flops 128 | bytes 1024 | tf_op jit(solution)/shard_map/psum | solution.py:78
  246.6 40.3 %psum.138 = f32[128]{0:T(128)S(1)} all-reduce(f32[128]{0:T(128)S(1)} %multiply_reduce_fusion.6), channel_id=1, replica_groups=mesh['gz'=4,'gx'=8] {'gz','gx'}, use_global_device_ids=true, to_apply=%region_11.12 | all-reduce | flops 128 | bytes 1024 | tf_op jit(solution)/shard_map/psum | solution.py:80
  287.1 0.9 multiply_reduce_fusion
  288.1 39.6 %all-reduce.7 = (f32[128]{0:T(128)S(1)}, f32[128]{0:T(128)S(1)}) all-reduce(f32[128]{0:T(128)S(1)} %get-tuple-element.25, f32[128]{0:T(128)S(1)} %get-tuple-element.26), channel_id=1, replica_groups=mesh['gz'=4,'gx'=8] {'gz','gx'}, use_global_device_ids=true, to_apply=%region_15.16 | all-reduce | flops 256 | bytes 2048 | tf_op jit(solution)/shard_map/psum | solution.py:88
  327.8 0.9 convolution_bitcast_fusion
  328.7 0.9 convert_reduce_fusion
  329.6 4.0 collective-permute-start.14
  333.7 0.9 convolution_bitcast_fusion.19
  334.6 0.6 copy.49
  335.5 1.4 collective-permute-start.10
  337.0 0.8 convolution_bitcast_fusion.26
  337.8 3.4 collective-permute-done.13
  342.1 0.9 convolution_bitcast_fusion.18
  343.0 0.9 convolution_bitcast_fusion.20
  345.3 0.8 multiply_reduce_fusion.1
  346.1 40.9 %all-reduce.6 = (f32[128]{0:T(128)S(1)}, f32[128]{0:T(128)S(1)}) all-reduce(f32[128]{0:T(128)S(1)} %get-tuple-element.23, f32[128]{0:T(128)S(1)} %get-tuple-element.27), channel_id=1, replica_groups=mesh['gz'=4,'gx'=8] {'gz','gx'}, use_global_device_ids=true, to_apply=%region_19.20 | all-reduce | flops 256 | bytes 2048 | tf_op jit(solution)/shard_map/psum | solution.py:88
  387.0 0.7 multiply_add_fusion.1
  388.5 4.0 collective-permute-start.19
  393.0 1.4 collective-permute-start.15
  396.5 0.7 pad_maximum_fusion.2
  397.2 3.0 collective-permute-done.18
  401.1 0.9 convolution_bitcast_fusion.21
  402.0 0.9 convolution_bitcast_fusion.23
  404.6 38.9 %all-reduce.5 = (f32[128]{0:T(128)S(1)}, f32[128]{0:T(128)S(1)}) all-reduce(f32[128]{0:T(128)S(1)} %get-tuple-element.21, f32[128]{0:T(128)S(1)} %get-tuple-element.28), channel_id=1, replica_groups=mesh['gz'=4,'gx'=8] {'gz','gx'}, use_global_device_ids=true, to_apply=%region_23.24 | all-reduce | flops 256 | bytes 2048 | tf_op jit(solution)/shard_map/psum | solution.py:88
  444.4 0.6 copy.50
  445.1 40.5 %all-reduce.4 = (f32[3,128]{1,0:T(4,128)S(1)}, f32[2,128]{1,0:T(2,128)S(1)}, f32[3,128]{1,0:T(4,128)S(1)}, f32[3,128]{1,0:T(4,128)S(1)}) all-reduce(f32[3,128]{1,0:T(4,128)S(1)} %convolution_bitcast_fusion.27, f32[2,128]{1,0:T(2,128)S(1)} %pad_maximum_fusion.4, ...), channel_id=1, replica_groups=mesh['gz'=4,'gx'=8] {'gz','gx'}, use_global_device_ids=true, to_apply=%region_24.25 | all-reduce | flops 1408 | bytes 11264 | tf_op jit(solution)/shard_map/psum | solution.py:200
  488.4 0.8 pad_maximum_fusion.1
  489.2 1.0 pad_maximum_fusion
  490.3 0.6 copy-done.28
  492.1 0.7 multiply_multiply_fusion.4
  492.8 131.5 %all-reduce.11.cloned.1.call-done = (f32[2,3,128,128]{3,2,1,0:T(8,128)}, f32[2,8,128,128]{3,2,1,0:T(8,128)}, f32[2,128,128]{2,1,0:T(8,128)}) async-done(((f32[2,3,128,128]{3,2,1,0:T(8,128)}, f32[2,8,128,128]{3,2,1,0:T(8,128)}, f32[2,128,128]{2,1,0:T(8,128)}), (f32[2,3,128,128]{3,2,1,0:T(8,128)}, f32[2,8,128,128]{3,2,1,0:T(8,128)}, f32[2,128,128]{2,1,0:T(8,128)})) %all-reduce.11.cloned.1.call-update) | async-done | bytes 1572880 | tf_op jit(solution)/shard_map/psum | solution.py:200
  624.3 1.9 broadcast_multiply_fusion.1
  626.2 1.6 broadcast_multiply_fusion.2
  627.7 1.1 broadcast_multiply_fusion
  (202 shorter events, 21.6 us)
Async XLA Ops:
  7.2 100.1 %copy-start = (f32[128,128]{1,0:T(8,128)S(1)}, f32[128,128]{1,0:T(8,128)}, u32[]{:S(2)}) copy-start(f32[128,128]{1,0:T(8,128)} %param.17) | copy-start | bytes 196612
  7.2 100.8 %copy-start.31 = (f32[2,128]{1,0:T(2,128)S(1)}, f32[2,128]{1,0:T(2,128)}, u32[]{:S(2)}) copy-start(f32[2,128]{1,0:T(2,128)} %param.21) | copy-start | bytes 3076
  7.2 100.9 %copy-start.3 = (bf16[2,3,128,128]{3,2,1,0:T(8,128)(2,1)S(1)}, bf16[2,3,128,128]{3,2,1,0:T(8,128)(2,1)}, u32[]{:S(2)}) copy-start(bf16[2,3,128,128]{3,2,1,0:T(8,128)(2,1)} %param.18) | copy-start | bytes 589828
  7.2 617.1 %all-reduce.11.cloned.1.call-start = ((), (), s32[]{:S(2)}) async-start(), calls=%async_computation | async-start | bytes 3145728 | tf_op jit(solution)/shard_map/psum | solution.py:200
  8.9 99.5 %copy-start.14 = (f32[128]{0:T(128)}, f32[128]{0:T(128)S(1)}, u32[]{:S(2)}) copy-start(f32[128]{0:T(128)S(1)} %get-tuple-element.49) | copy-start | bytes 1540
  8.9 188.4 %copy-start.16 = (f32[128]{0:T(128)}, f32[128]{0:T(128)S(1)}, u32[]{:S(2)}) copy-start(f32[128]{0:T(128)S(1)} %get-tuple-element.50) | copy-start | bytes 1540
  93.2 15.4 %copy-start.19 = (f32[128]{0:T(128)}, f32[128]{0:T(128)S(1)}, u32[]{:S(2)}) copy-start(f32[128]{0:T(128)S(1)} %add_rsqrt_fusion.2) | copy-start | bytes 1540
  93.3 15.4 %collective-permute-start.4 = (bf16[1,4,128,128]{3,2,1,0:T(8,128)(2,1)S(1)}, bf16[1,4,128,128]{3,2,1,0:T(8,128)(2,1)S(1)}, u32[]{:S(2)}, u32[]{:S(2)}) collective-permute-start(bf16[1,4,128,128]{3,2,1,0:T(8,128)(2,1)S(1)} %fusion.263), channel_id=1, source_target_pairs={{1,0},{2,1},{3,2},{4,3},{5,4},{6,5},{7,6},{0,7},{9,8},{10,9},{11,1... | collective-permute-start | bytes 393224 | tf_op jit(solution)/shard_map/ppermute | solution.py:25
  97.2 11.4 %collective-permute-start.3 = (bf16[1,4,128,128]{3,2,1,0:T(8,128)(2,1)S(1)}, bf16[1,4,128,128]{3,2,1,0:T(8,128)(2,1)S(1)}, u32[]{:S(2)}, u32[]{:S(2)}) collective-permute-start(bf16[1,4,128,128]{3,2,1,0:T(8,128)(2,1)S(1)} %fusion.263), channel_id=1, source_target_pairs={{0,1},{1,2},{2,3},{3,4},{4,5},{5,6},{6,7},{7,0},{8,9},{9,10},{10,1... | collective-permute-start | bytes 393224 | tf_op jit(solution)/shard_map/ppermute | solution.py:23
  97.2 12.2 %collective-permute-start.2 = (bf16[1,4,128,128]{3,2,1,0:T(8,128)(2,1)S(1)}, bf16[1,4,128,128]{3,2,1,0:T(8,128)(2,1)S(1)}, u32[]{:S(2)}, u32[]{:S(2)}) collective-permute-start(bf16[1,4,128,128]{3,2,1,0:T(8,128)(2,1)S(1)} %fusion.263), channel_id=1, source_target_pairs={{0,24},{8,0},{16,8},{24,16},{1,25},{9,1},{17,9},{25,17},{2,26},{10... | collective-permute-start | bytes 393224 | tf_op jit(solution)/shard_map/ppermute | solution.py:35
  97.2 10.8 %collective-permute-start.1 = (bf16[1,4,128,128]{3,2,1,0:T(8,128)(2,1)S(1)}, bf16[1,4,128,128]{3,2,1,0:T(8,128)(2,1)S(1)}, u32[]{:S(2)}, u32[]{:S(2)}) collective-permute-start(bf16[1,4,128,128]{3,2,1,0:T(8,128)(2,1)S(1)} %fusion.263), channel_id=1, source_target_pairs={{0,8},{8,16},{16,24},{24,0},{1,9},{9,17},{17,25},{25,1},{2,10},{10... | collective-permute-start | bytes 393224 | tf_op jit(solution)/shard_map/ppermute | solution.py:35
  97.7 10.3 %collective-permute-start = (bf16[1,4,128,128]{3,2,1,0:T(8,128)(2,1)S(1)}, bf16[1,4,128,128]{3,2,1,0:T(8,128)(2,1)S(1)}, u32[]{:S(2)}, u32[]{:S(2)}) collective-permute-start(bf16[1,4,128,128]{3,2,1,0:T(8,128)(2,1)S(1)} %fusion.263), channel_id=1, source_target_pairs={{0,16},{8,24},{16,0},{24,8},{1,17},{9,25},{17,1},{25,9},{2,18},{10... | collective-permute-start | bytes 393224 | tf_op jit(solution)/shard_map/ppermute | solution.py:35
  105.9 2.8 copy-start.25
  108.0 1.0 copy-start.1
  110.3 0.8 copy-start.11
  192.3 13.5 %copy-start.21 = (f32[128]{0:T(128)}, f32[128]{0:T(128)S(1)}, u32[]{:S(2)}) copy-start(f32[128]{0:T(128)S(1)} %add_rsqrt_fusion.1) | copy-start | bytes 1540
  192.3 6.6 %collective-permute-start.9 = (bf16[1,4,128,128]{3,2,1,0:T(8,128)(2,1)S(1)}, bf16[1,4,128,128]{3,2,1,0:T(8,128)(2,1)S(1)}, u32[]{:S(2)}, u32[]{:S(2)}) collective-permute-start(bf16[1,4,128,128]{3,2,1,0:T(8,128)(2,1)S(1)} %fusion.262), channel_id=1, source_target_pairs={{1,0},{2,1},{3,2},{4,3},{5,4},{6,5},{7,6},{0,7},{9,8},{10,9},{11,1... | collective-permute-start | bytes 393224 | tf_op jit(solution)/shard_map/ppermute | solution.py:25
  196.3 7.7 %collective-permute-start.8 = (bf16[1,4,128,128]{3,2,1,0:T(8,128)(2,1)S(1)}, bf16[1,4,128,128]{3,2,1,0:T(8,128)(2,1)S(1)}, u32[]{:S(2)}, u32[]{:S(2)}) collective-permute-start(bf16[1,4,128,128]{3,2,1,0:T(8,128)(2,1)S(1)} %fusion.262), channel_id=1, source_target_pairs={{0,1},{1,2},{2,3},{3,4},{4,5},{5,6},{6,7},{7,0},{8,9},{9,10},{10,1... | collective-permute-start | bytes 393224 | tf_op jit(solution)/shard_map/ppermute | solution.py:23
  196.3 8.7 %collective-permute-start.7 = (bf16[1,4,128,128]{3,2,1,0:T(8,128)(2,1)S(1)}, bf16[1,4,128,128]{3,2,1,0:T(8,128)(2,1)S(1)}, u32[]{:S(2)}, u32[]{:S(2)}) collective-permute-start(bf16[1,4,128,128]{3,2,1,0:T(8,128)(2,1)S(1)} %fusion.262), channel_id=1, source_target_pairs={{0,24},{8,0},{16,8},{24,16},{1,25},{9,1},{17,9},{25,17},{2,26},{10... | collective-permute-start | bytes 393224 | tf_op jit(solution)/shard_map/ppermute | solution.py:35
  196.3 7.9 %collective-permute-start.6 = (bf16[1,4,128,128]{3,2,1,0:T(8,128)(2,1)S(1)}, bf16[1,4,128,128]{3,2,1,0:T(8,128)(2,1)S(1)}, u32[]{:S(2)}, u32[]{:S(2)}) collective-permute-start(bf16[1,4,128,128]{3,2,1,0:T(8,128)(2,1)S(1)} %fusion.262), channel_id=1, source_target_pairs={{0,8},{8,16},{16,24},{24,0},{1,9},{9,17},{17,25},{25,1},{2,10},{10... | collective-permute-start | bytes 393224 | tf_op jit(solution)/shard_map/ppermute | solution.py:35
  196.9 7.4 %collective-permute-start.5 = (bf16[1,4,128,128]{3,2,1,0:T(8,128)(2,1)S(1)}, bf16[1,4,128,128]{3,2,1,0:T(8,128)(2,1)S(1)}, u32[]{:S(2)}, u32[]{:S(2)}) collective-permute-start(bf16[1,4,128,128]{3,2,1,0:T(8,128)(2,1)S(1)} %fusion.262), channel_id=1, source_target_pairs={{0,16},{8,24},{16,0},{24,8},{1,17},{9,25},{17,1},{25,9},{2,18},{10... | collective-permute-start | bytes 393224 | tf_op jit(solution)/shard_map/ppermute | solution.py:35
  206.3 80.7 %copy-start.24 = (bf16[3,128]{1,0:T(4,128)(2,1)S(1)}, bf16[3,128]{1,0:T(4,128)(2,1)}, u32[]{:S(2)}) copy-start(bf16[3,128]{1,0:T(4,128)(2,1)} %param.23) | copy-start | bytes 2308
  206.3 80.8 %copy-start.10 = (f32[3,1,4,128]{3,2,1,0:T(4,128)S(1)}, f32[3,1,4,128]{3,2,1,0:T(4,128)}, u32[]{:S(2)}) copy-start(f32[3,1,4,128]{3,2,1,0:T(4,128)} %param.13) | copy-start | bytes 18436
  329.6 8.2 %collective-permute-start.14 = (bf16[1,4,128,128]{3,2,1,0:T(8,128)(2,1)S(1)}, bf16[1,4,128,128]{3,2,1,0:T(8,128)(2,1)S(1)}, u32[]{:S(2)}, u32[]{:S(2)}) collective-permute-start(bf16[1,4,128,128]{3,2,1,0:T(8,128)(2,1)S(1)} %bitcast.540), channel_id=1, source_target_pairs={{1,0},{2,1},{3,2},{4,3},{5,4},{6,5},{7,6},{0,7},{9,8},{10,9},{11,1... | collective-permute-start | bytes 393224 | tf_op jit(solution)/shard_map/ppermute | solution.py:25
  333.6 7.7 %collective-permute-start.13 = (bf16[1,4,128,128]{3,2,1,0:T(8,128)(2,1)S(1)}, bf16[1,4,128,128]{3,2,1,0:T(8,128)(2,1)S(1)}, u32[]{:S(2)}, u32[]{:S(2)}) collective-permute-start(bf16[1,4,128,128]{3,2,1,0:T(8,128)(2,1)S(1)} %bitcast.541), channel_id=1, source_target_pairs={{0,1},{1,2},{2,3},{3,4},{4,5},{5,6},{6,7},{7,0},{8,9},{9,10},{10,1... | collective-permute-start | bytes 393224 | tf_op jit(solution)/shard_map/ppermute | solution.py:23
  335.2 6.5 %collective-permute-start.12 = (bf16[1,4,128,128]{3,2,1,0:T(8,128)(2,1)S(1)}, bf16[1,4,128,128]{3,2,1,0:T(8,128)(2,1)S(1)}, u32[]{:S(2)}, u32[]{:S(2)}) collective-permute-start(bf16[1,4,128,128]{3,2,1,0:T(8,128)(2,1)S(1)} %bitcast.542), channel_id=1, source_target_pairs={{0,8},{8,16},{16,24},{24,0},{1,9},{9,17},{17,25},{25,1},{2,10},{10... | collective-permute-start | bytes 393224 | tf_op jit(solution)/shard_map/ppermute | solution.py:35
  335.2 6.5 %collective-permute-start.11 = (bf16[1,4,128,128]{3,2,1,0:T(8,128)(2,1)S(1)}, bf16[1,4,128,128]{3,2,1,0:T(8,128)(2,1)S(1)}, u32[]{:S(2)}, u32[]{:S(2)}) collective-permute-start(bf16[1,4,128,128]{3,2,1,0:T(8,128)(2,1)S(1)} %bitcast.543), channel_id=1, source_target_pairs={{0,16},{8,24},{16,0},{24,8},{1,17},{9,25},{17,1},{25,9},{2,18},{10... | collective-permute-start | bytes 393224 | tf_op jit(solution)/shard_map/ppermute | solution.py:35
  335.5 6.1 collective-permute-start.10
  346.1 41.9 %copy-start.12 = (bf16[2,128,128]{2,1,0:T(8,128)(2,1)S(1)}, bf16[2,128,128]{2,1,0:T(8,128)(2,1)}, u32[]{:S(2)}) copy-start(bf16[2,128,128]{2,1,0:T(8,128)(2,1)} %param.20) | copy-start | bytes 196612
  388.0 6.4 %copy-start.4 = (bf16[2,3,128,128]{3,2,1,0:T(8,128)(2,1)S(1)}, bf16[2,3,128,128]{3,2,1,0:T(8,128)(2,1)}, u32[]{:S(2)}) copy-start(bf16[2,3,128,128]{3,2,1,0:T(8,128)(2,1)} %param.18) | copy-start | bytes 589828
  388.5 8.7 %collective-permute-start.19 = (bf16[1,4,128,128]{3,2,1,0:T(8,128)(2,1)S(1)}, bf16[1,4,128,128]{3,2,1,0:T(8,128)(2,1)S(1)}, u32[]{:S(2)}, u32[]{:S(2)}) collective-permute-start(bf16[1,4,128,128]{3,2,1,0:T(8,128)(2,1)S(1)} %bitcast.533), channel_id=1, source_target_pairs={{1,0},{2,1},{3,2},{4,3},{5,4},{6,5},{7,6},{0,7},{9,8},{10,9},{11,1... | collective-permute-start | bytes 393224 | tf_op jit(solution)/shard_map/ppermute | solution.py:25
  392.6 7.7 %collective-permute-start.18 = (bf16[1,4,128,128]{3,2,1,0:T(8,128)(2,1)S(1)}, bf16[1,4,128,128]{3,2,1,0:T(8,128)(2,1)S(1)}, u32[]{:S(2)}, u32[]{:S(2)}) collective-permute-start(bf16[1,4,128,128]{3,2,1,0:T(8,128)(2,1)S(1)} %bitcast.534), channel_id=1, source_target_pairs={{0,1},{1,2},{2,3},{3,4},{4,5},{5,6},{6,7},{7,0},{8,9},{9,10},{10,1... | collective-permute-start | bytes 393224 | tf_op jit(solution)/shard_map/ppermute | solution.py:23
  392.6 8.1 %collective-permute-start.17 = (bf16[1,4,128,128]{3,2,1,0:T(8,128)(2,1)S(1)}, bf16[1,4,128,128]{3,2,1,0:T(8,128)(2,1)S(1)}, u32[]{:S(2)}, u32[]{:S(2)}) collective-permute-start(bf16[1,4,128,128]{3,2,1,0:T(8,128)(2,1)S(1)} %bitcast.535), channel_id=1, source_target_pairs={{0,8},{8,16},{16,24},{24,0},{1,9},{9,17},{17,25},{25,1},{2,10},{10... | collective-permute-start | bytes 393224 | tf_op jit(solution)/shard_map/ppermute | solution.py:35
  392.6 8.1 %collective-permute-start.16 = (bf16[1,4,128,128]{3,2,1,0:T(8,128)(2,1)S(1)}, bf16[1,4,128,128]{3,2,1,0:T(8,128)(2,1)S(1)}, u32[]{:S(2)}, u32[]{:S(2)}) collective-permute-start(bf16[1,4,128,128]{3,2,1,0:T(8,128)(2,1)S(1)} %bitcast.536), channel_id=1, source_target_pairs={{0,16},{8,24},{16,0},{24,8},{1,17},{9,25},{17,1},{25,9},{2,18},{10... | collective-permute-start | bytes 393224 | tf_op jit(solution)/shard_map/ppermute | solution.py:35
  393.0 7.7 %collective-permute-start.15 = (bf16[1,4,128,128]{3,2,1,0:T(8,128)(2,1)S(1)}, bf16[1,4,128,128]{3,2,1,0:T(8,128)(2,1)S(1)}, u32[]{:S(2)}, u32[]{:S(2)}) collective-permute-start(bf16[1,4,128,128]{3,2,1,0:T(8,128)(2,1)S(1)} %bitcast.537), channel_id=1, source_target_pairs={{0,24},{8,0},{16,8},{24,16},{1,25},{9,1},{17,9},{25,17},{2,26},{10... | collective-permute-start | bytes 393224 | tf_op jit(solution)/shard_map/ppermute | solution.py:35
  395.0 1.5 copy-start.13
  395.0 2.1 copy-start.32
  395.1 2.1 copy-start.5
  395.1 2.1 copy-start.6
  395.1 2.1 copy-start.7
  404.3 39.5 %copy-start.18 = (f32[3,128]{1,0:T(4,128)S(1)}, f32[3,128]{1,0:T(4,128)}, u32[]{:S(2)}) copy-start(f32[3,128]{1,0:T(4,128)} %param.16) | copy-start | bytes 4612
  404.6 40.5 %copy-start.27 = (f32[128]{0:T(128)S(1)}, f32[128]{0:T(128)}, u32[]{:S(2)}) copy-start(f32[128]{0:T(128)} %get-tuple-element.22) | copy-start | bytes 1540
  404.6 40.5 %copy-start.30 = (f32[128]{0:T(128)S(1)}, f32[128]{0:T(128)}, u32[]{:S(2)}) copy-start(f32[128]{0:T(128)} %get-tuple-element.24) | copy-start | bytes 1540
  404.6 40.5 %copy-start.23 = (f32[3,128]{1,0:T(4,128)S(1)}, f32[3,128]{1,0:T(4,128)}, u32[]{:S(2)}) copy-start(f32[3,128]{1,0:T(4,128)} %convolution_bitcast_fusion.26) | copy-start | bytes 4612
  487.0 1.4 copy-start.8
  487.0 1.4 copy-start.9
  490.3 1.9 copy-start.26
  624.3 3.4 copy-start.2
  (6 other events, 3.9 us)
Sparse Core Ops, SparseCore 0:
  490.4 133.8 all-reduce.10
where the time goes:
time: 638 us; the launch traced here: 636 us
  blocking collectives  403 us (63%)
  waiting for transfers between devices  145 us (23%)
  matrix products  24.7 us (4%)
  starting transfers between devices  22.7 us (4%)
  between operations  22.4 us (4%)
  other arithmetic  13.3 us (2%)
    psum x1, waiting for transfers between devices, per_device(): lax.psum((jnp.stack(z_list), jnp.stack(xy_list), jnp.stack(point_list), j...  131 us
    psum x3, blocking collectives, normalize(): lax.psum(jnp.sum(centered * centered, axis=(0, 1, 2)), ('gz', 'gx'))  122 us
    psum x3, blocking collectives, normalize(): lax.psum(jnp.sum(hidden, axis=(0, 1, 2)), ('gz', 'gx')) / cell_count  121 us
    psum x3, blocking collectives, norm_back(): lax.psum((jnp.sum(scaled, axis=(0, 1, 2)), jnp.sum(scaled * whitened, axi...  119 us
    psum x1, blocking collectives, per_device(): lax.psum((jnp.stack(z_list), jnp.stack(xy_list), jnp.stack(point_list), j...  40.5 us
    ppermute x4, starting transfers between devices, padded_2(): lax.ppermute(head, axis, [((i + 1) % count, i) for i in range(count)])  16 us
  transfers between devices with their start and end apart: 21, of which 5 were waited for; matrix products, arithmetic and copies ran while one was open for 2% of the time, Pallas kernels for 0%

commit v1 on v0

--- a/solution.py
+++ b/solution.py
@@ -1,16 +1,791 @@
+import functools
 import math
 
 import jax
 import jax.numpy as jnp
 from jax import lax
+from jax.experimental import pallas as pl
+from jax.experimental.pallas import tpu as pltpu
 from jax.sharding import PartitionSpec as P
 
 STEPS = 1000
-
+REACH = 256
+RIM = 4
 
 eps_norm = 1e-05
 highest = lax.Precision.HIGHEST
+bf16 = jnp.bfloat16
+f32 = jnp.float32
 plane_offsets = ((-1, -1), (-1, 0), (-1, 1), (0, -1), (0, 1), (1, -1), (1, 0), (1, 1))
+
+
+def time_terms(timestep, w_time):
+    moment = timestep[0].astype(jnp.float32)
+    half_width = w_time.shape[0] // 2
+    alpha_bar = jnp.cos(0.5 * math.pi * (moment + 0.5) / STEPS) ** 2
+    ladder = jnp.exp(-math.log(10000.0) * jnp.arange(half_width, dtype=jnp.float32) / half_width)
+    angles = moment * ladder
+    features = jnp.concatenate([jnp.sin(angles), jnp.cos(angles)])
+    time_raw = jnp.dot(features, w_time, precision=highest)
+    return (alpha_bar, features, time_raw, jax.nn.silu(time_raw))
+
+
+def mm(left, right):
+    return lax.dot_general(left, right, (((1,), (0,)), ((), ())), preferred_element_type=f32)
+
+
+def mm_nt(left, right):
+    return lax.dot_general(left, right, (((1,), (1,)), ((), ())), preferred_element_type=f32)
+
+
+def mm_tn(left, right):
+    return lax.dot_general(left, right, (((0,), (0,)), ((), ())), preferred_element_type=f32)
+
+
+def halves(value):
+    high = value.astype(bf16)
+    return high, (value - high.astype(f32)).astype(bf16)
+
+
+def wide(vector):
+    return jnp.concatenate([vector] * 4, axis=1)
+
+
+def folded(vector):
+    channels = vector.shape[1] // 4
+    return sum(vector[:, y * channels : (y + 1) * channels] for y in range(4))
+
+
+def own_rows(sc, shape, span):
+    row = lax.broadcasted_iota(jnp.int32, shape, 0)
+    in_span = lax.rem(row, span)
+    near = (in_span >= RIM) & (in_span < span - RIM)
+    wide_step = (sc[1] >= sc[6]).astype(jnp.int32)
+    far = row < sc[2]
+    flag = jnp.where(wide_step == 1, far.astype(jnp.int32), near.astype(jnp.int32))
+    return flag == 1
+
+
+def z_of_rows(sc, shape, span, cells_z):
+    row = lax.broadcasted_iota(jnp.int32, shape, 0)
+    members, reach_own = sc[6], span - 2 * RIM
+    residues = jnp.minimum(sc[1], members)
+    member = sc[0]
+    step_far = row * members + member
+    part = member // residues
+    start = lax.rem(member, residues)
+    period = row // span
+    inside = row - period * span - RIM + part * reach_own
+    step_near = start + residues * inside + period * REACH
+    wide_step = (sc[1] >= members).astype(jnp.int32)
+    z = jnp.where(wide_step == 1, step_far, step_near)
+    return lax.rem(z + 2 * cells_z, cells_z)
+
+
+def pick_z(sc, rows, span, cells_z):
+    z = z_of_rows(sc, (rows, cells_z), span, cells_z)
+    return (z == lax.broadcasted_iota(jnp.int32, (rows, cells_z), 1)).astype(f32).astype(bf16)
+
+
+def shifts(rows, length, step):
+    row = lax.broadcasted_iota(jnp.int32, (rows, rows), 0)
+    col = lax.broadcasted_iota(jnp.int32, (rows, rows), 1)
+    down = row - step
+    down = jnp.where(down < 0, down + length, down)
+    up = row + step
+    up = jnp.where(up >= length, up - length, up)
+    return jnp.concatenate(
+        [(down == col).astype(f32).astype(bf16), (up == col).astype(f32).astype(bf16)], axis=0
+    )
+
+
+def build_taps(w, taps, taps_z):
+    channels = w.shape[-1]
+    zero = jnp.zeros((channels, channels), bf16)
+    for q in range(2):
+        for i in range(3):
+            for y_in in range(4):
+                for side in range(2):
+                    j = y_in - (2 * q + side)
+                    block = w[i * 3 + j + 1] if abs(j) <= 1 else zero
+                    taps[
+                        q,
+                        i,
+                        y_in * channels : (y_in + 1) * channels,
+                        side * channels : (side + 1) * channels,
+                    ] = block
+    for m in range(2):
+        build_pair(w[9 + m], taps_z, m)
+
+
+def build_pair(block, target, m):
+    channels = block.shape[-1]
+    zero = jnp.zeros((channels, channels), bf16)
+    target[m, :channels, :channels] = block
+    target[m, channels:, channels:] = block
+    target[m, :channels, channels:] = zero
+    target[m, channels:, :channels] = zero
+
+
+def fill_rims(padded, planes):
+    padded[0] = padded[planes]
+    padded[planes + 1] = padded[1]
+
+
+def fill_shifted(padded, shifted, both, planes):
+    rows = padded.shape[1]
+
+    def body(x, carry):
+        moved = mm(both, padded[x + 1]).astype(bf16)
+        shifted[0, x] = moved[:rows]
+        shifted[1, x] = moved[rows:]
+        return carry
+
+    lax.fori_loop(0, planes, body, 0)
+
+
+def conv_half(padded, shifted, taps, taps_z, x0, count, q):
+    rows, lanes = padded.shape[1:]
+    half = lanes // 2
+    total = None
+    for i in range(3):
+        part = mm(padded[pl.ds(x0 + i, count)].reshape(count * rows, lanes), taps[q, i])
+        total = part if total is None else total + part
+    for m in range(2):
+        source = shifted[m, pl.ds(x0, count), :, q * half : (q + 1) * half]
+        total = total + mm(source.reshape(count * rows, half), taps_z[m])
+    return total
+
+
+def gelu_pair(value):
+    scale = math.sqrt(2.0 / math.pi)
+    square = value * value
+    bent = jnp.tanh(scale * value * (1.0 + 0.044715 * square))
+    half = 0.5 + 0.5 * bent
+    slope = half + 0.5 * value * (1.0 - bent * bent) * (
+        scale * (1.0 + 3.0 * 0.044715 * square)
+    )
+    return value * half, slope
+
+
+def merged_stats(parts, per_member):
+    found = []
+    for part in parts:
+        for at in range(0, part.shape[0], 8):
+            found.append((part[at : at + 1], part[at + 1 : at + 2]))
+    total = sum(one[0] for one in found)
+    mean = total / (per_member * len(found))
+    spread = sum(one[1] for one in found)
+    for one in found:
+        gap = one[0] / per_member - mean
+        spread = spread + per_member * gap * gap
+    return mean, lax.rsqrt(spread / (per_member * len(found)) + eps_norm)
+
+
+def merged_sums(parts):
+    found = []
+    for part in parts:
+        for at in range(0, part.shape[0], 8):
+            found.append(part[at : at + 8])
+    return sum(found)
+
+
+def put_rows(ref, *vectors):
+    rows = list(vectors)
+    rows += [jnp.zeros((1, ref.shape[1]), f32)] * (ref.shape[0] - len(rows))
+    ref[...] = jnp.concatenate(rows, axis=0)
+
+
+def layer_forward(sc, which, padded, shifted, taps, taps_z, pair, w, wp, shift_bias, old, stream,
+                  act, slope, stats, acc, span, per_member):
+    planes, rows, lanes = stream.shape
+    half = lanes // 2
+    count = 2
+    build_taps(w, taps, taps_z)
+    build_pair(wp[...], pair, 0)
+    fill_rims(padded, planes)
+    fill_shifted(padded, shifted, shifts(rows, sc[2], sc[3 + which]), planes)
+    acc[...] = jnp.zeros_like(acc)
+    bias = wide(shift_bias)[:, :half]
+
+    def body(step, carry):
+        x0 = step * count
+        for q in range(2):
+            side = slice(q * half, (q + 1) * half)
+            pre = conv_half(padded, shifted, taps, taps_z, x0, count, q) + bias
+            value, grad = gelu_pair(pre)
+            value = value.astype(bf16)
+            act[pl.ds(x0, count), :, side] = value.reshape(count, rows, half)
+            slope[pl.ds(x0, count), :, side] = grad.astype(bf16).reshape(count, rows, half)
+            branch = mm(value, pair[0]).reshape(count, rows, half)
+            new = old[pl.ds(x0, count), :, side] + branch
+            stream[pl.ds(x0, count), :, side] = new
+            acc[:, side] += jnp.sum(new, axis=0)
+        return carry
+
+    lax.fori_loop(0, planes // count, body, 0)
+    mask = own_rows(sc, (rows, lanes), span)
+    total = folded(jnp.sum(jnp.where(mask, acc[...], 0.0), axis=0, keepdims=True))
+    mean = wide(total / per_member)
+    spread = jnp.zeros((rows, lanes), f32)
+    for x in range(planes):
+        gap = stream[x] - mean
+        spread = spread + gap * gap
+    spread = folded(jnp.sum(jnp.where(mask, spread, 0.0), axis=0, keepdims=True))
+    put_rows(stats, total, spread)
+
+
+def kernel_first(span, cells_z, per_member, sc, fields, lift_hi, lift_lo, w_in, gain, shift_bias, w, wp,
+                 stream, normed, act, slope, gathered, stats, consts,
+                 padded, shifted, taps, taps_z, pair, acc, old, staged):
+    planes, rows, lanes = stream.shape
+    channels = lanes // 4
+    slabs = cells_z // fields.shape[2]
+    cell_count = float(planes * 4 * cells_z)
+    comps = [fields[:, 4 * k : 4 * k + 4, :] for k in range(3)]
+
+    def all_sum(value):
+        value = jnp.sum(jnp.sum(value, axis=0), axis=0, keepdims=True)
+        return jnp.sum(value, axis=1, keepdims=True)
+
+    means = [all_sum(comp) / cell_count for comp in comps]
+    gaps = [comp - mean[None] for comp, mean in zip(comps, means)]
+    covs = {}
+    for j in range(3):
+        for k in range(j, 3):
+            covs[j, k] = all_sum(gaps[j] * gaps[k]) / cell_count
+    rows_in = [w_in[k : k + 1, :] for k in range(3)]
+    mean_c = sum(means[k] * rows_in[k] for k in range(3))
+    var_c = jnp.zeros((1, channels), f32)
+    for (j, k), cov in covs.items():
+        var_c = var_c + (1.0 if j == k else 2.0) * cov * (rows_in[j] * rows_in[k])
+    inv_c = lax.rsqrt(jnp.maximum(var_c, 0.0) + eps_norm)
+    flat = [jnp.broadcast_to(value, (1, channels)) for value in means + list(covs.values())]
+    put_rows(consts, mean_c, inv_c, *flat)
+    pick = pick_z(sc, rows, span, cells_z)
+    depth = fields.shape[2]
+    got = [jnp.zeros((rows, planes * 32), f32) for _ in range(2)]
+    staged[:, 24:, :] = jnp.zeros((planes, 8, depth), f32)
+    for s in range(slabs):
+        staged[:, :24, :] = fields[s * planes : (s + 1) * planes]
+        both = halves(staged[...].reshape(planes * 32, depth))
+        for at in range(2):
+            got[at] = got[at] + mm_nt(pick[:, s * depth : (s + 1) * depth], both[at])
+    high, low = got[0].astype(bf16), got[1].astype(bf16)
+    gathered[:, : planes * 32] = high
+    gathered[:, planes * 32 :] = low
+    scale = wide(inv_c * gain[...])
+    mean_w = wide(mean_c)
+    for x in range(planes):
+        at = slice((planes - 1 - x) * 32, (planes - 1 - x) * 32 + planes * 32)
+        value = mm(high, lift_hi[at]) + mm(low, lift_hi[at]) + mm(high, lift_lo[at])
+        old[x] = value
+        unit = ((value - mean_w) * scale).astype(bf16)
+        padded[x + 1] = unit
+        normed[x] = unit
+    layer_forward(sc, 0, padded, shifted, taps, taps_z, pair, w, wp, shift_bias[...], old, stream, act,
+                  slope, stats, acc, span, per_member)
+
+
+def kernel_second(span, per_member, sc, *refs):
+    parts, refs = refs[:3], refs[3:]
+    (old, gain, shift_bias, w, wp, stream, normed, act, slope, stats, consts,
+     padded, shifted, taps, taps_z, pair, acc) = refs
+    planes = stream.shape[0]
+    mean, inverse = merged_stats(parts, per_member)
+    put_rows(consts, mean, inverse)
+    mean_w, scale = wide(mean), wide(inverse * gain[...])
+    for x in range(planes):
+        unit = ((old[x] - mean_w) * scale).astype(bf16)
+        padded[x + 1] = unit
+        normed[x] = unit
+    layer_forward(sc, 1, padded, shifted, taps, taps_z, pair, w, wp, shift_bias[...], old, stream, act,
+                  slope, stats, acc, span, per_member)
+
+
+def kernel_out(span, per_member, sc, *refs):
+    parts, refs = refs[:3], refs[3:]
+    stream, gain, gathered, lift_out, prediction, misfit, sums, w_out_raw, consts, acc = refs
+    planes, rows, lanes = stream.shape
+    half = planes * 32
+    mean, inverse = merged_stats(parts, per_member)
+    put_rows(consts, mean, inverse)
+    mean_w, inv_w, gain_w = wide(mean), wide(inverse), wide(gain[...])
+    total = jnp.zeros((rows, half), f32)
+
+    def place(x):
+        return slice((planes - 1 - x) * 32, (planes - 1 - x) * 32 + half)
+
+    for x in range(planes):
+        unit = ((stream[x] - mean_w) * (inv_w * gain_w)).astype(bf16)
+        total = total + mm_nt(unit, lift_out[place(x)])
+    slot = lax.rem(lax.broadcasted_iota(jnp.int32, (rows, half), 1), 32)
+    noise = gathered[:, :half].astype(f32) + gathered[:, half:].astype(f32)
+    gap = jnp.where((slot >= 12) & (slot < 24), total - noise, 0.0)
+    prediction[...] = total
+    high, low = halves(gap)
+    misfit[:, :half] = high
+    misfit[:, half:] = low
+    mask = own_rows(sc, (rows, half), span)
+    high_own = jnp.where(mask, gap, 0.0).astype(bf16)
+    low_own = jnp.where(mask, low.astype(f32), 0.0).astype(bf16)
+    plain = jnp.zeros((rows, lanes), f32)
+    cross = jnp.zeros((rows, lanes), f32)
+    raw = jnp.zeros((32, lanes), f32)
+    for x in range(planes):
+        white = (stream[x] - mean_w) * inv_w
+        unit = (white * gain_w).astype(bf16)
+        d_out = mm(high, lift_out[place(x)]) + mm(low, lift_out[place(x)])
+        plain = plain + d_out
+        cross = cross + d_out * white
+        got = mm_tn(high_own, unit) + mm_tn(low_own, unit)
+        raw = raw + got[x * 32 : x * 32 + 32]
+    mask = own_rows(sc, (rows, lanes), span)
+    s_plain = folded(jnp.sum(jnp.where(mask, plain, 0.0), axis=0, keepdims=True))
+    s_cross = folded(jnp.sum(jnp.where(mask, cross, 0.0), axis=0, keepdims=True))
+    put_rows(sums, s_plain, s_cross)
+    put_rows(w_out_raw, *by_component(raw, 3))
+
+
+def by_component(raw, first):
+    channels = raw.shape[1] // 4
+    found = []
+    for k in range(first, first + 3):
+        found.append(
+            sum(raw[k * 4 + y : k * 4 + y + 1, y * channels : (y + 1) * channels] for y in range(4))
+        )
+    return found
+
+
+def branch_backward(sc, planes, d_stream_of, pair, act, slope, normed, padded, scot, span, bias_acc):
+    rows, lanes = padded.shape[1:]
+    half = lanes // 2
+
+    def body(x, carry):
+        cot = d_stream_of(x).astype(bf16)
+        scot[x] = cot
+        for q in range(2):
+            side = slice(q * half, (q + 1) * half)
+            d_act = mm(cot[:, side], pair[0])
+            pre = (d_act * slope[x, :, side].astype(f32)).astype(bf16)
+            padded[x + 1, :, side] = pre
+            bias_acc[:, side] += pre.astype(f32)
+        return carry
+
+    lax.fori_loop(0, planes, body, 0)
+
+
+def weight_grads(sc, which, planes, padded, scot, normed, act, grads, picked, wide_left, own_pre, span, share):
+    rows, lanes = padded.shape[1:]
+    channels = lanes // 4
+    wide_share = 4 * share
+    row = lax.broadcasted_iota(jnp.int32, (lanes, wide_share), 0)
+    col = lax.broadcasted_iota(jnp.int32, (lanes, wide_share), 1)
+    hit = (row // channels == col // share) & (
+        lax.rem(row, channels) == lax.rem(col, share) + sc[5] * share
+    )
+    choose = hit.astype(f32).astype(bf16)
+    both = shifts(rows, sc[2], sc[3 + which])
+    mask = own_rows(sc, (rows, lanes), span)
+
+    def gather(x, carry):
+        picked[x] = mm(normed[x], choose).astype(bf16)
+        return carry
+
+    lax.fori_loop(0, planes, gather, 0)
+    raw = jnp.zeros((5 * wide_share, lanes), f32)
+    raw_point = jnp.zeros((wide_share, lanes), f32)
+    for x in range(planes):
+        here = picked[x]
+        moved = mm(both, here).astype(bf16)
+        left = jnp.concatenate(
+            [picked[(x - 1) % planes], here, picked[(x + 1) % planes], moved[:rows], moved[rows:]],
+            axis=1,
+        )
+        wide_left[x] = left
+        own_pre[x] = jnp.where(mask, padded[x + 1].astype(f32), 0.0).astype(bf16)
+    raw = mm_tn(
+        wide_left[...].reshape(planes * rows, 5 * wide_share), own_pre[...].reshape(planes * rows, lanes)
+    )
+
+    def gather_act(x, carry):
+        picked[x] = mm(act[x], choose).astype(bf16)
+        own_pre[x] = jnp.where(mask, scot[x].astype(f32), 0.0).astype(bf16)
+        return carry
+
+    lax.fori_loop(0, planes, gather_act, 0)
+    raw_point = mm_tn(
+        picked[...].reshape(planes * rows, wide_share), own_pre[...].reshape(planes * rows, lanes)
+    )
+
+    def block(source, part, y_in, y_out):
+        at = part * wide_share + y_in * share
+        return source[at : at + share, y_out * channels : (y_out + 1) * channels]
+
+    for i in range(3):
+        for j in range(-1, 2):
+            grads[i * 3 + j + 1] = sum(
+                block(raw, i, y + j, y) for y in range(4) if 0 <= y + j < 4
+            )
+    for m in range(2):
+        grads[9 + m] = sum(block(raw, 3 + m, y, y) for y in range(4))
+    grads[11] = sum(block(raw_point, 0, y, y) for y in range(4))
+
+
+def conv_backward(sc, which, planes, padded, shifted, taps, taps_z, w, emit):
+    rows, lanes = padded.shape[1:]
+    half = lanes // 2
+    build_taps(w, taps, taps_z)
+    fill_rims(padded, planes)
+    fill_shifted(padded, shifted, shifts(rows, sc[2], sc[3 + which]), planes)
+    count = 2
+
+    def body(step, carry):
+        x0 = step * count
+        for q in range(2):
+            emit(x0, count, q, conv_half(padded, shifted, taps, taps_z, x0, count, q))
+        return carry
+
+    lax.fori_loop(0, planes // count, body, 0)
+
+
+def masked_total(sc, value, span):
+    mask = own_rows(sc, value.shape, span)
+    return folded(jnp.sum(jnp.where(mask, value, 0.0), axis=0, keepdims=True))
+
+
+def kernel_back_second(span, share, cell_count, sc, *refs):
+    parts, refs = refs[:3], refs[3:]
+    (stream, out_consts, gain_out, gain, misfit, lift_out, act, slope, normed, w, wp,
+     d_stream, d_normed, sums, grads,
+     padded, shifted, taps, taps_z, pair, acc, acc2, scot, picked, wide_left, own_pre) = refs
+    planes, rows, lanes = stream.shape
+    half = lanes // 2
+    sums_out = merged_sums(parts)
+    gain_w = wide(gain_out[...])
+    mean_w, inv_w = wide(out_consts[0:1]), wide(out_consts[1:2])
+    m_plain = gain_w * wide(sums_out[0:1]) / cell_count
+    m_cross = gain_w * wide(sums_out[1:2]) / cell_count
+    high, low = misfit[:, : planes * 32], misfit[:, planes * 32 :]
+    build_pair(wp[...], pair, 0)
+    acc[...] = jnp.zeros_like(acc)
+
+    def d_stream_of(x):
+        at = pl.ds(pl.multiple_of((planes - 1 - x) * 32, 32), planes * 32)
+        d_out = mm(high, lift_out[at]) + mm(low, lift_out[at])
+        white = (stream[x] - mean_w) * inv_w
+        value = inv_w * (gain_w * d_out - m_plain - white * m_cross)
+        d_stream[x] = value
+        return value
+
+    branch_backward(sc, planes, d_stream_of, pair, act, slope, normed, padded, scot, span, acc)
+    s_bias = masked_total(sc, acc[...], span)
+    acc[...] = jnp.zeros_like(acc)
+    acc2[...] = jnp.zeros_like(acc2)
+
+    def emit(x0, count, q, value):
+        side = slice(q * half, (q + 1) * half)
+        value = value.reshape(count, rows, half)
+        d_normed[pl.ds(x0, count), :, side] = value
+        acc[:, side] += jnp.sum(value, axis=0)
+        acc2[:, side] += jnp.sum(value * normed[pl.ds(x0, count), :, side].astype(f32), axis=0)
+
+    conv_backward(sc, 1, planes, padded, shifted, taps, taps_z, w, emit)
+    s_plain = masked_total(sc, acc[...], span)
+    s_cross = masked_total(sc, acc2[...], span) / gain[...]
+    put_rows(sums, s_plain, s_cross, s_bias)
+    weight_grads(sc, 1, planes, padded, scot, normed, act, grads, picked, wide_left, own_pre, span, share)
+
+
+def kernel_back_first(span, share, cell_count, sc, *refs):
+    parts, refs = refs[:3], refs[3:]
+    (consts, d_next, d_normed, normed_next, gain_next, act, slope, normed, wp,
+     d_stream, pre_cot, sums, grads,
+     padded, pair, acc, scot, picked, wide_left, own_pre) = refs
+    planes, rows, lanes = d_next.shape
+    sums_in = merged_sums(parts)
+    gain_w = wide(gain_next[...])
+    inv_w = wide(consts[1:2])
+    m_plain = gain_w * wide(sums_in[0:1]) / cell_count
+    m_cross = wide(sums_in[1:2]) / cell_count
+    build_pair(wp[...], pair, 0)
+    acc[...] = jnp.zeros_like(acc)
+
+    def d_stream_of(x):
+        back = gain_w * d_normed[x] - m_plain - normed_next[x].astype(f32) * m_cross
+        value = d_next[x] + inv_w * back
+        d_stream[x] = value
+        return value
+
+    branch_backward(sc, planes, d_stream_of, pair, act, slope, normed, padded, scot, span, acc)
+    put_rows(sums, masked_total(sc, acc[...], span))
+
+    def hand_on(x, carry):
+        pre_cot[x] = padded[x + 1]
+        return carry
+
+    lax.fori_loop(0, planes, hand_on, 0)
+    weight_grads(sc, 0, planes, padded, scot, normed, act, grads, picked, wide_left, own_pre, span, share)
+
+
+def kernel_last(span, cells_z, sc, pre_cot, d_stream, normed, gain, consts, gathered, lift_hi, lift_lo, w,
+                prediction, slab, sums, in_raw,
+                padded, shifted, taps, taps_z, acc, acc2, field, raw, turned):
+    planes, rows, lanes = d_stream.shape
+    half = lanes // 2
+    wide_in = planes * 32
+
+    def take(x, carry):
+        padded[x + 1] = pre_cot[x]
+        return carry
+
+    lax.fori_loop(0, planes, take, 0)
+    acc[...] = jnp.zeros_like(acc)
+    acc2[...] = jnp.zeros_like(acc2)
+    slot = lax.rem(lax.broadcasted_iota(jnp.int32, (rows, wide_in), 1), 32)
+    field[...] = jnp.where((slot >= 12) & (slot < 24), prediction[...], 0.0)
+    raw[...] = jnp.zeros_like(raw)
+    mask = own_rows(sc, (rows, wide_in), span)
+    keep = lambda value: jnp.where(mask, value.astype(f32), 0.0).astype(bf16)
+    high_own = keep(gathered[:, :wide_in])
+    low_own = keep(gathered[:, wide_in:])
+    scale = wide(consts[1:2] * gain[...])
+
+    def emit(x0, count, q, value):
+        side = slice(q * half, (q + 1) * half)
+        value = value.reshape(count, rows, half)
+        acc[:, side] += jnp.sum(value, axis=0)
+        acc2[:, side] += jnp.sum(value * normed[pl.ds(x0, count), :, side].astype(f32), axis=0)
+        full = d_stream[pl.ds(x0, count), :, side] + value * scale[:, side]
+        for t in range(count):
+            high, low = halves(full[t])
+            at = pl.ds(pl.multiple_of((planes - 1 - x0 - t) * 32, 32), wide_in)
+            l_hi, l_lo = lift_hi[at, side], lift_lo[at, side]
+            field[...] += mm_nt(high, l_hi) + mm_nt(low, l_hi) + mm_nt(high, l_lo)
+            got = mm_tn(high_own, high) + mm_tn(high_own, low) + mm_tn(low_own, high)
+            turned[:, :half] = got
+            raw[:, side] += turned[pl.ds(pl.multiple_of((x0 + t) * 32, 32), 32), :half]
+
+    conv_backward(sc, 0, planes, padded, shifted, taps, taps_z, w, emit)
+    s_plain = masked_total(sc, acc[...], span)
+    s_cross = masked_total(sc, acc2[...], span) / gain[...]
+    put_rows(sums, s_plain, s_cross)
+    put_rows(in_raw, *by_component(raw[...], 0))
+    pick = pick_z(sc, rows, span, cells_z)
+    pick = jnp.where(own_rows(sc, pick.shape, span), pick.astype(f32), 0.0).astype(bf16)
+    high, low = halves(field[...])
+    turned[...] = mm_tn(high, pick) + mm_tn(low, pick)
+    slab[...] = turned[pl.ds(pl.multiple_of(sc[7] * 32, 32), 32)]
+
+
+def call(kernel, outs, scratch, scalars, *args):
+    spec = pl.BlockSpec(memory_space=pltpu.VMEM)
+    return pl.pallas_call(
+        kernel,
+        out_shape=[jax.ShapeDtypeStruct(shape, dtype) for shape, dtype in outs],
+        in_specs=[pl.BlockSpec(memory_space=pltpu.SMEM)] + [spec] * len(args),
+        out_specs=[spec] * len(outs),
+        scratch_shapes=[pltpu.VMEM(shape, dtype) for shape, dtype in scratch],
+        compiler_params=pltpu.CompilerParams(vmem_limit_bytes=56 * 2**20),
+    )(scalars, *args)
+
+
+def swapped(value, axis, bit):
+    count = lax.axis_size(axis)
+    return lax.ppermute(value, axis, [(i, i ^ bit) for i in range(count)])
+
+
+def group_parts(value):
+    beside = swapped(value, "gz", 1)
+    pair = jnp.concatenate([value, beside], axis=0)
+    return (value, beside, swapped(pair, "gz", 2))
+
+
+def group_sum(value):
+    value = value + swapped(value, "gz", 1)
+    return value + swapped(value, "gz", 2)
+
+
+def shared_grads(grads):
+    members = lax.axis_size("gz")
+    taps, share, channels = grads.shape
+    pieces = grads.reshape(members, (taps // members) * share, channels)
+    mine = jnp.sum(lax.all_to_all(pieces, "gz", 0, 0), axis=0).astype(bf16)
+    total = members * lax.axis_size("gx")
+    every = lax.all_to_all(
+        jnp.broadcast_to(mine[None], (total,) + mine.shape), ("gz", "gx"), 0, 0
+    )
+    every = every.reshape(members, total // members, taps // members, share, channels)
+    return every.transpose(0, 2, 1, 3, 4).reshape(taps, channels, channels)
+
+
+def per_device_grouped(clean_field, noise_field, timestep, dilations, w_in, w_time, w_z, w_xy, w_point,
+                       biases, norm_gains, w_out):
+    members, groups = lax.axis_size("gz"), lax.axis_size("gx")
+    depth = clean_field.shape[3]
+    planes, cells_z = groups, depth * members
+    channels = w_in.shape[1]
+    lanes = 4 * channels
+    periods = cells_z // REACH
+    span = REACH // members + 2 * RIM
+    rows = periods * span
+    share = channels // groups
+    per_member = float(planes * 4 * depth)
+    cell_count = per_member * members
+    inv_area = 4.0 / cell_count
+
+    alpha_bar, features, time_raw, time_code = time_terms(timestep, w_time)
+    noisy = jnp.sqrt(alpha_bar) * clean_field + jnp.sqrt(1.0 - alpha_bar) * noise_field
+    block = jnp.concatenate([noisy, noise_field], axis=0).reshape(24, depth)
+    total = members * groups
+    fields = lax.all_to_all(
+        jnp.broadcast_to(block[None], (total, 24, depth)), ("gz", "gx"), 0, 0
+    )
+
+    small = jnp.min(dilations)
+    coarse = small >= members
+    length = jnp.where(coarse, depth, rows)
+    step_small = jnp.where(coarse, small // members, 1)
+    step_far = jnp.where(coarse, REACH // members, span)
+    steps = jnp.where(dilations == REACH, step_far, step_small)
+    scalars = jnp.stack(
+        [
+            lax.axis_index("gz"),
+            small,
+            length,
+            steps[0],
+            steps[1],
+            lax.axis_index("gx"),
+            jnp.int32(members),
+            lax.axis_index("gx"),
+        ]
+    ).astype(jnp.int32)
+
+    eye = jnp.eye(4, dtype=f32)
+
+    def lifted(weights, first):
+        spread = (eye[None, :, :, None] * weights[:, None, None, :]).reshape(12, lanes)
+        spread = jnp.pad(spread, ((first * 4, 20 - first * 4), (0, 0)))
+        return jnp.pad(spread, (((planes - 1) * 32, (planes - 1) * 32), (0, 0)))
+
+    in_hi = lax.reduce_precision(w_in, 8, 7)
+    lift_hi, lift_lo = (lifted(part, 0).astype(bf16) for part in (in_hi, w_in - in_hi))
+    lift_out = lifted(w_out.astype(f32), 3).astype(bf16)
+    taps_f = jnp.concatenate([w_xy[:, :4], w_z[:, 1:2], w_xy[:, 4:], w_z[:, 0:1], w_z[:, 2:3]], axis=1)
+    turned = taps_f.swapaxes(-1, -2)
+    taps_b = jnp.concatenate([turned[:, 8::-1], turned[:, 10:11], turned[:, 9:10]], axis=1)
+    point_t = w_point.swapaxes(-1, -2)
+    shift_bias = biases + time_code
+    gains = [norm_gains[l : l + 1] for l in range(3)]
+
+    big = (planes, rows, lanes)
+    vec = ((8, channels), f32)
+    conv_scratch = [
+        ((planes + 2, rows, lanes), bf16),
+        ((2,) + big, bf16),
+        ((2, 3, lanes, lanes // 2), bf16),
+        ((2, lanes // 2, lanes // 2), bf16),
+    ]
+    pair = ((1, lanes // 2, lanes // 2), bf16)
+    flat = ((rows, lanes), f32)
+    wide_share = 4 * share
+    grad_scratch = [
+        (big, bf16),
+        ((planes, rows, wide_share), bf16),
+        ((planes, rows, 5 * wide_share), bf16),
+        (big, bf16),
+    ]
+
+    stream1, normed0, act0, slope0, gathered, stats1, consts0 = call(
+        functools.partial(kernel_first, span, cells_z, per_member),
+        [(big, f32), (big, bf16), (big, bf16), (big, bf16), ((rows, 2 * planes * 32), bf16), vec,
+         ((16, channels), f32)],
+        conv_scratch + [pair, flat, (big, f32), ((planes, 32, depth), f32)],
+        scalars, fields, lift_hi, lift_lo, w_in, gains[0], shift_bias[0:1], taps_f[0], w_point[0],
+    )
+    stream2, normed1, act1, slope1, stats2, consts1 = call(
+        functools.partial(kernel_second, span, per_member),
+        [(big, f32), (big, bf16), (big, bf16), (big, bf16), vec, vec],
+        conv_scratch + [pair, flat],
+        scalars, *group_parts(stats1), stream1, gains[1], shift_bias[1:2], taps_f[1], w_point[1],
+    )
+    prediction, misfit, sums2, out_raw, consts2 = call(
+        functools.partial(kernel_out, span, per_member),
+        [((rows, planes * 32), f32), ((rows, 2 * planes * 32), bf16), vec, vec, vec],
+        [flat],
+        scalars, *group_parts(stats2), stream2, gains[2], gathered, lift_out,
+    )
+    parts2 = group_parts(sums2)
+    d_stream2, d_normed1, sums1, grads1 = call(
+        functools.partial(kernel_back_second, span, share, cell_count),
+        [(big, f32), (big, f32), vec, ((12, share, channels), f32)],
+        conv_scratch + [pair, flat, flat] + grad_scratch,
+        scalars, *parts2, stream2, consts2, gains[2], gains[1], misfit, lift_out, act1, slope1, normed1,
+        taps_b[1], point_t[1],
+    )
+    parts1 = group_parts(sums1)
+    d_stream1, pre_cot0, sums_b0, grads0 = call(
+        functools.partial(kernel_back_first, span, share, cell_count),
+        [(big, f32), (big, bf16), vec, ((12, share, channels), f32)],
+        [conv_scratch[0], pair, flat] + grad_scratch,
+        scalars, *parts1, consts1, d_stream2, d_normed1, normed1, gains[1], act0, slope0, normed0,
+        point_t[0],
+    )
+    slab, sums0, in_part = call(
+        functools.partial(kernel_last, span, cells_z),
+        [((32, cells_z), f32), vec, vec],
+        conv_scratch + [flat, flat, ((rows, planes * 32), f32), ((32, lanes), f32),
+                        ((planes * 32, cells_z), f32)],
+        scalars, pre_cot0, d_stream1, normed0, gains[0], consts0, gathered, lift_hi, lift_lo, taps_b[0],
+        prediction,
+    )
+    all1 = shared_grads(grads1)
+    all0 = shared_grads(grads0)
+
+    tails = group_sum(jnp.concatenate([sums0, in_part, sums_b0, out_raw], axis=0))
+    s_plain, s_cross, in_sum = tails[0], tails[1], tails[8:11]
+    bias0, out_sum = tails[16], tails[24:27]
+    s1 = sum(part[at : at + 8] for part in parts1 for at in range(0, part.shape[0], 8))
+    s2 = sum(part[at : at + 8] for part in parts2 for at in range(0, part.shape[0], 8))
+    inverse = consts0[1]
+    m_plain = norm_gains[0] * s_plain / cell_count
+    m_cross = norm_gains[0] * s_cross / cell_count
+    mean_k = consts0[2:5, 0]
+    c00, c01, c02, c11, c12, c22 = (consts0[5 + at, 0] for at in range(6))
+    cov = jnp.stack([jnp.stack([c00, c01, c02]), jnp.stack([c01, c11, c12]), jnp.stack([c02, c12, c22])])
+    offset = jnp.sum(w_in * (inverse * m_plain), axis=1)
+    mix = jnp.sum(w_in[:, None, :] * (inverse * inverse * m_cross) * w_in[None, :, :], axis=2)
+    pieces = slab.reshape(32, members, depth)[:24].transpose(1, 0, 2)
+    landed = jnp.sum(lax.all_to_all(pieces, "gz", 0, 0), axis=0)
+    landed = landed.reshape(6, 1, 4, depth)
+    centered = noisy - mean_k[:, None, None, None]
+    field_grad = landed[:3] - offset[:, None, None, None] - sum(
+        mix[:, j, None, None, None] * centered[j][None] for j in range(3)
+    )
+    prediction_out = landed[3:]
+    cross_in = jnp.sum(cov[:, :, None] * w_in[None, :, :], axis=1)
+    in_raw = in_sum - cell_count * (
+        mean_k[:, None] * (inverse * m_plain) + (inverse * inverse * m_cross) * cross_in
+    )
+    bias_all = jnp.stack([bias0, s1[2]])
+    gain_all = jnp.stack([s_cross, s1[1], s2[1]])
+    weights = jnp.stack([all0, all1]).astype(f32) * inv_area
+    z_all = jnp.stack([weights[:, 9], weights[:, 4], weights[:, 10]], axis=1)
+    xy_all = jnp.concatenate([weights[:, :4], weights[:, 5:9]], axis=1)
+    time_back = jax.vjp(jax.nn.silu, time_raw)[1](jnp.sum(bias_all, axis=0))[0]
+    grad_w_time = inv_area * jnp.outer(features, time_back)
+    return (
+        prediction_out,
+        field_grad,
+        inv_area * in_raw,
+        grad_w_time,
+        z_all,
+        xy_all,
+        weights[:, 11],
+        inv_area * bias_all,
+        inv_area * gain_all,
+        inv_area * out_sum,
+    )
 
 
 def padded_2(cells, sides, width):
@@ -35,17 +810,6 @@
     return lax.ppermute(value, axis, pairs)
 
 
-def time_terms(timestep, w_time):
-    moment = timestep[0].astype(jnp.float32)
-    half_width = w_time.shape[0] // 2
-    alpha_bar = jnp.cos(0.5 * math.pi * (moment + 0.5) / STEPS) ** 2
-    ladder = jnp.exp(-math.log(10000.0) * jnp.arange(half_width, dtype=jnp.float32) / half_width)
-    angles = moment * ladder
-    features = jnp.concatenate([jnp.sin(angles), jnp.cos(angles)])
-    time_raw = jnp.dot(features, w_time, precision=highest)
-    return (alpha_bar, features, time_raw, jax.nn.silu(time_raw))
-
-
 def contract_cells(left, right):
     return lax.dot_general(
         left, right, (((0, 1, 2), (0, 1, 2)), ((), ())), preferred_element_type=jnp.float32
@@ -108,7 +872,7 @@
     return summed
 
 
-def conv_backward(pre_cot, normed, dilation, weights_z, weights_xy):
+def conv_backward_split(pre_cot, normed, dilation, weights_z, weights_xy):
     rows_x, rows_y = (normed.shape[0], normed.shape[1])
     lower_cot, upper_cot = slab_windows(pre_cot, dilation)
     padded_cot = plane_pad(pre_cot)
@@ -132,7 +896,7 @@
     return (d_normed, z_terms, jnp.stack(xy_terms))
 
 
-def per_device(
+def per_device_split(
     clean_field,
     noise_field,
     timestep,
@@ -183,7 +947,7 @@
         gelu_back = jax.vjp(jax.nn.gelu, pre_act)[1]
         pre_cot = gelu_back(d_act)[0].astype(jnp.bfloat16)
         bias_raw = jnp.sum(pre_cot, axis=(0, 1, 2), dtype=jnp.float32)
-        d_normed, z_raw, xy_raw = conv_backward(
+        d_normed, z_raw, xy_raw = conv_backward_split(
             pre_cot, normed, dilations[which_layer], w_z[which_layer], w_xy[which_layer]
         )
         d_back, gain_raw = norm_back(
@@ -225,6 +989,13 @@
     )
 
 
+def per_device(*args):
+    members, groups = lax.axis_size("gz"), lax.axis_size("gx")
+    _, rows_x, rows_y, depth = args[0].shape
+    small = rows_x == 1 and rows_y == 4 and members == 4 and groups == 8 and depth * members == 2 * REACH
+    return per_device_grouped(*args) if small else per_device_split(*args)
+
+
 def solution(mesh):
     return jax.shard_map(
         per_device,

time: 638 us -> 199 us (0.31)
  blocking collectives: 403 us -> 0 us
  waiting for transfers between devices: 145 us -> 38.5 us
  Pallas kernels: 0 us -> 79.3 us
  matrix products: 24.7 us -> 0.16 us
  local copies, waits for them, and re-layouts: 4.9 us -> 22.3 us
  between operations: 22.4 us -> 5.37 us
  starting transfers between devices: 22.7 us -> 33.7 us
    psum x10 -> x0, blocking collectives: 403 us -> none  [the longest x3 122 us: normalize(): lax.psum(jnp.sum(centered * centered, axis=(0, 1, 2)), ('gz', 'gx'))]
    psum x1 -> x0, waiting for transfers between devices: 131 us -> none  [per_device(): lax.psum((jnp.stack(z_list), jnp.stack(xy_list), jnp.stack(point_list), j...]
    pallas_call x0 -> x6, Pallas kernels: none -> 79.3 us  [call(): pl.pallas_call(kernel, out_shape=[jax.ShapeDtypeStruct(shape, dtype) for...]
    all_to_all x0 -> x6, waiting for transfers between devices: none -> 30.6 us  [the longest x2 22.9 us: shared_grads(): lax.all_to_all(jnp.broadcast_to(mine[None], (total,) + mine.shape), ('gz'...]
    all_to_all x0 -> x6, starting transfers between devices: none -> 24.4 us  [the longest x1 7.3 us: per_device_grouped(): lax.all_to_all(jnp.broadcast_to(block[None], (total, 24, depth)), ('gz',...]
    dot_general x78 -> x0, matrix products: 24 us -> none  [the longest x24 9.32 us: contract_cells(): lax.dot_general(left, right, (((0, 1, 2), (0, 1, 2)), ((), ())), preferre...]
    ppermute x20 -> x10, starting transfers between devices: 22.7 us -> 9.31 us  [swapped(): return lax.ppermute(value, axis, [(i, i ^ bit) for i in range(count)])]
    ppermute x20 -> x10, waiting for transfers between devices: 13 us -> 7.92 us  [swapped(): return lax.ppermute(value, axis, [(i, i ^ bit) for i in range(count)])]
  transfers between devices with their start and end apart: 21 -> 16, of which waited for: 5 -> 11; matrix products, arithmetic and copies ran while one was open for 2% -> 14% of each run, Pallas kernels for 0% -> 0%
where the time goes in v1:
time: 199 us; the launch traced here: 198 us
  Pallas kernels  79.3 us (40%)
  waiting for transfers between devices  38.5 us (19%)
  starting transfers between devices  33.7 us (17%)
  local copies, waits for them, and re-layouts  22.3 us (11%)
  other arithmetic  18.7 us (9%)
  between operations  5.37 us (3%)
    pallas_call x6, Pallas kernels, call(): pl.pallas_call(kernel, out_shape=[jax.ShapeDtypeStruct(shape, dtype) for...  79.3 us
    all_to_all x2, waiting for transfers between devices, shared_grads(): lax.all_to_all(jnp.broadcast_to(mine[None], (total,) + mine.shape), ('gz'...  22.9 us
    ppermute x10, starting transfers between devices, swapped(): return lax.ppermute(value, axis, [(i, i ^ bit) for i in range(count)])  9.31 us
    ppermute x10, waiting for transfers between devices, swapped(): return lax.ppermute(value, axis, [(i, i ^ bit) for i in range(count)])  7.92 us
    all_to_all x2, waiting for transfers between devices, shared_grads(): mine = jnp.sum(lax.all_to_all(pieces, 'gz', 0, 0), axis=0).astype(bf16)  7.69 us
    all_to_all x1, starting transfers between devices, per_device_grouped(): lax.all_to_all(jnp.broadcast_to(block[None], (total, 24, depth)), ('gz',...  7.3 us
    all_to_all x2, starting transfers between devices, shared_grads(): lax.all_to_all(jnp.broadcast_to(mine[None], (total,) + mine.shape), ('gz'...  7.22 us
    all_to_all x2, starting transfers between devices, shared_grads(): mine = jnp.sum(lax.all_to_all(pieces, 'gz', 0, 0), axis=0).astype(bf16)  6.62 us
  transfers between devices with their start and end apart: 16, of which 11 were waited for; matrix products, arithmetic and copies ran while one was open for 14% of the time, Pallas kernels for 0%

profile of v1, /device:TPU:0, one launch (start us, length us, event | category | flops | bytes accessed | tf_op | source)
XLA Modules:
  0.0 198.1 jit_solution(3769256064645462524)
XLA Ops:
  1.5 0.7 multiply_add_fusion
  3.0 0.8 broadcast_in_dim.19
  3.7 7.3 %all-to-all-start = ((f32[32,24,128]{2,1,0:T(8,128)}), f32[32,24,128]{2,1,0:T(8,128)S(1)}, u32[]{:S(2)}, u32[]{:S(2)}) async-start(f32[32,24,128]{2,1,0:T(8,128)} %broadcast_in_dim.19), calls=%async_computation | async-start | bytes 786432 | tf_op jit(solution)/shard_map/all_to_all | solution.py:641
  11.0 1.3 reduce_min.9
  18.6 0.8 pad.72.lift_hi
  19.5 0.8 pad.73.lift_lo
  20.3 0.9 copy.79.w
  21.2 0.9 copy.80.refs_6_
  22.1 0.8 pad.74.refs_6_.refs_8_
  23.1 1.3 stack.53.sc
  25.7 0.9 slice_bitcast_fusion
  26.6 0.7 copy-done.1
  27.4 14.4 %shard_map.195 = (f32[8,144,512]{2,1,0:T(8,128)}, bf16[8,144,512]{2,1,0:T(8,128)(2,1)}, bf16[8,144,512]{2,1,0:T(8,128)(2,1)}, bf16[8,144,512]{2,1,0:T(8,128)(2,1...) custom-call(s32[8]{0:T(128)} %stack.53.sc, f32[32,24,128]{2,1,0:T(8,128)} %copy-done.1, ...), custom_call_target="tpu_custom_call" | custom-call | tf_op jit(solution)/shard_map/pallas_call | solution.py:583
  42.0 0.8 slice_reduce_fusion.2
  43.8 1.8 collective-permute-start.1
  45.6 1.9 collective-permute-done.1.refs_2_
  48.1 13.7 %shard_map.196 = (f32[8,144,512]{2,1,0:T(8,128)}, bf16[8,144,512]{2,1,0:T(8,128)(2,1)}, bf16[8,144,512]{2,1,0:T(8,128)(2,1)}, bf16[8,144,512]{2,1,0:T(8,128)(2,1)}, f32[8,128]{1,0:T(8,128)}, /*index=5*/f32[8,128]{1,0:T(8,128)}) custom-call(s32[8]{0:T(128)} %stack.53.sc, f32[8,128]{1,0:T(8,128)} %get-tuple-element.39.refs_0_, f32[8,128]{1,0:T(8,128)} %copy-done.15, ...), custom_call_target="tpu_custom_call" | custom-call | tf_op jit(solution)/shard_map/pallas_call | solution.py:583
  61.9 1.3 fusion.17
  63.9 1.8 collective-permute-start.3
  65.7 2.0 %maximum_bitcast_fusion.2 = f32[1,3]{1,0:T(1,128)S(1)} fusion(f32[1]{0:T(128)} %bitcast.31, f32[1]{0:T(128)} %bitcast.29, f32[1]{0:T(128)} %bitcast.26), kind=kLoop, calls=%fused_computation.71 | loop fusion | flops 6 | bytes 24 | tf_op jit(solution)/shard_map/stack | solution.py:755
  68.3 6.2 %shard_map.197 = (f32[144,256]{1,0:T(8,128)}, bf16[144,512]{1,0:T(8,128)(2,1)}, f32[8,128]{1,0:T(8,128)}, f32[8,128]{1,0:T(8,128)}, f32[8,128]{1,0:T(8,128)}) custom-call(s32[8]{0:T(128)} %stack.53.sc, f32[8,128]{1,0:T(8,128)} %get-tuple-element.41.refs_0_, f32[8,128]{1,0:T(8,128)} %copy-done.16, f32[16,128]{1,0:T(8,128)} %copy-done.18, ...), custom_call_target="tpu_custom_call" | custom-call | tf_op jit(solution)/shard_map/pallas_call | solution.py:583
  74.7 2.0 %maximum_bitcast_fusion.1 = f32[1,3]{1,0:T(1,128)S(1)} fusion(f32[1]{0:T(128)} %bitcast.29, f32[1]{0:T(128)} %bitcast.28, f32[1]{0:T(128)} %bitcast.25), kind=kLoop, calls=%fused_computation.70 | loop fusion | flops 6 | bytes 24 | tf_op jit(solution)/shard_map/stack | solution.py:755
  77.4 1.4 collective-permute-start.5
  78.8 2.0 %maximum_bitcast_fusion = f32[1,3]{1,0:T(1,128)S(1)} fusion(f32[1]{0:T(128)} %bitcast.26, f32[1]{0:T(128)} %bitcast.25, f32[1]{0:T(128)} %bitcast.24), kind=kLoop, calls=%fused_computation.69 | loop fusion | flops 6 | bytes 24 | tf_op jit(solution)/shard_map/stack | solution.py:755
  81.6 18.5 %shard_map.198 = (f32[8,144,512]{2,1,0:T(8,128)}, f32[8,144,512]{2,1,0:T(8,128)}, f32[8,128]{1,0:T(8,128)}, f32[12,16,128]{2,1,0:T(8,128)}) custom-call(s32[8]{0:T(128)} %stack.53.sc, f32[8,128]{1,0:T(8,128)} %get-tuple-element.44.refs_0_, f32[8,128]{1,0:T(8,128)} %copy-done.9, f32[16,128]{1,0:T(8,128)} %copy-done.12, ...), custom_call_target="tpu_custom_call" | custom-call | tf_op jit(solution)/shard_map/pallas_call | solution.py:583
  100.2 1.3 collective-permute-done.6.refs_1_
  102.2 1.4 collective-permute-start.7
  103.7 0.7 slice_add_fusion
  104.4 1.5 collective-permute-done.7.refs_2_
  106.5 11.9 %shard_map.199 = (f32[8,144,512]{2,1,0:T(8,128)}, bf16[8,144,512]{2,1,0:T(8,128)(2,1)}, f32[8,128]{1,0:T(8,128)}, f32[12,16,128]{2,1,0:T(8,128)}) custom-call(s32[8]{0:T(128)} %stack.53.sc, f32[8,128]{1,0:T(8,128)} %get-tuple-element.50.refs_0_, f32[8,128]{1,0:T(8,128)} %copy-done.6, f32[16,128]{1,0:T(8,128)} %copy-done.10, ...), custom_call_target="tpu_custom_call" | custom-call | tf_op jit(solution)/shard_map/pallas_call | solution.py:583
  118.4 14.6 %shard_map.200 = (f32[32,512]{1,0:T(8,128)}, f32[8,128]{1,0:T(8,128)}, f32[8,128]{1,0:T(8,128)}) custom-call(s32[8]{0:T(128)} %stack.53.sc, bf16[8,144,512]{2,1,0:T(8,128)(2,1)} %get-tuple-element.57.pre_cot, f32[8,144,512]{2,1,0:T(8,128)} %get-tuple-element.58.d_stream, bf16[8,144,512]{2,1,0:T(8,128)(2,1)} %get-tuple-element.56.refs_10_.normed, ...), custom_call_target="tpu_custom_call" | custom-call | tf_op jit(solution)/shard_map/pallas_call | solution.py:583
  133.0 1.4 bitcast_bitcast_fusion
  134.4 3.3 %all-to-all-start.1 = ((f32[4,24,128]{2,1,0:T(8,128)}), f32[4,24,128]{2,1,0:T(8,128)S(1)}, u32[]{:S(2)}, u32[]{:S(2)}) async-start(f32[4,24,128]{2,1,0:T(8,128)} %bitcast_bitcast_fusion), calls=%async_computation.1 | async-start | bytes 98304 | tf_op jit(solution)/shard_map/all_to_all | solution.py:759
  139.6 0.8 collective-permute-done.8
  140.5 1.9 collective-permute-start.9
  142.3 1.9 collective-permute-done.9
  144.2 3.3 %all-to-all-start.4 = ((f32[4,48,128]{2,1,0:T(8,128)}), f32[4,48,128]{2,1,0:T(8,128)S(1)}, u32[]{:S(2)}, u32[]{:S(2)}) async-start(f32[4,48,128]{2,1,0:T(8,128)} %bitcast.38), calls=%async_computation.4 | async-start | bytes 196608 | tf_op jit(solution)/shard_map/all_to_all | solution.py:613
  148.2 3.6 %all-to-all-done.4 = f32[4,48,128]{2,1,0:T(8,128)S(1)} async-done(((f32[4,48,128]{2,1,0:T(8,128)}), f32[4,48,128]{2,1,0:T(8,128)S(1)}, u32[]{:S(2)}, u32[]{:S(2)}) %all-to-all-start.4) | async-done | bytes 98336 | tf_op jit(solution)/shard_map/all_to_all | solution.py:613
  151.8 3.3 %all-to-all-start.2 = ((f32[4,48,128]{2,1,0:T(8,128)}), f32[4,48,128]{2,1,0:T(8,128)S(1)}, u32[]{:S(2)}, u32[]{:S(2)}) async-start(f32[4,48,128]{2,1,0:T(8,128)} %bitcast.34), calls=%async_computation.2 | async-start | bytes 196608 | tf_op jit(solution)/shard_map/all_to_all | solution.py:613
  155.3 4.1 %all-to-all-done.2 = f32[4,48,128]{2,1,0:T(8,128)S(1)} async-done(((f32[4,48,128]{2,1,0:T(8,128)}), f32[4,48,128]{2,1,0:T(8,128)S(1)}, u32[]{:S(2)}, u32[]{:S(2)}) %all-to-all-start.2) | async-done | bytes 98336 | tf_op jit(solution)/shard_map/all_to_all | solution.py:613
  159.4 0.8 broadcast_in_dim.21
  160.2 4.6 %all-to-all-start.5 = ((bf16[32,48,128]{2,1,0:T(8,128)(2,1)}), bf16[32,48,128]{2,1,0:T(8,128)(2,1)S(1)}, u32[]{:S(2)}, u32[]{:S(2)}) async-start(bf16[32,48,128]{2,1,0:T(8,128)(2,1)} %broadcast_in_dim.21), calls=%async_computation.5 | async-start | bytes 786432 | tf_op jit(solution)/shard_map/all_to_all | solution.py:615
  166.4 12.0 %all-to-all-done.5 = bf16[32,48,128]{2,1,0:T(8,128)(2,1)S(1)} async-done(((bf16[32,48,128]{2,1,0:T(8,128)(2,1)}), bf16[32,48,128]{2,1,0:T(8,128)(2,1)S(1)}, u32[]{:S(2)}, u32[]{:S(2)}) %all-to-all-start.5) | async-done | bytes 393248 | tf_op jit(solution)/shard_map/all_to_all | solution.py:615
  178.4 0.8 broadcast_in_dim.20
  179.2 2.6 %all-to-all-start.3 = ((bf16[32,48,128]{2,1,0:T(8,128)(2,1)}), bf16[32,48,128]{2,1,0:T(8,128)(2,1)S(1)}, u32[]{:S(2)}, u32[]{:S(2)}) async-start(bf16[32,48,128]{2,1,0:T(8,128)(2,1)} %broadcast_in_dim.20), calls=%async_computation.3 | async-start | bytes 786432 | tf_op jit(solution)/shard_map/all_to_all | solution.py:615
  184.4 10.9 %all-to-all-done.3 = bf16[32,48,128]{2,1,0:T(8,128)(2,1)S(1)} async-done(((bf16[32,48,128]{2,1,0:T(8,128)(2,1)}), bf16[32,48,128]{2,1,0:T(8,128)(2,1)S(1)}, u32[]{:S(2)}, u32[]{:S(2)}) %all-to-all-start.3) | async-done | bytes 393248 | tf_op jit(solution)/shard_map/all_to_all | solution.py:615
  196.3 1.0 pad_maximum_fusion
  197.3 0.8 pad_maximum_fusion.2
  (136 shorter events, 19.0 us)
Async XLA Ops:
  0.6 16.9 %copy-start = (f32[128,128]{1,0:T(8,128)S(1)}, f32[128,128]{1,0:T(8,128)}, u32[]{:S(2)}) copy-start(f32[128,128]{1,0:T(8,128)} %param.17) | copy-start | bytes 196612
  0.7 13.0 %copy-start.2 = (bf16[2,8,128,128]{3,2,1,0:T(8,128)(2,1)S(1)}, bf16[2,8,128,128]{3,2,1,0:T(8,128)(2,1)}, u32[]{:S(2)}) copy-start(bf16[2,8,128,128]{3,2,1,0:T(8,128)(2,1)} %param.19) | copy-start | bytes 1572868
  3.0 11.0 %copy-start.4 = (bf16[2,3,128,128]{3,2,1,0:T(8,128)(2,1)S(1)}, bf16[2,3,128,128]{3,2,1,0:T(8,128)(2,1)}, u32[]{:S(2)}) copy-start(bf16[2,3,128,128]{3,2,1,0:T(8,128)(2,1)} %param.18) | copy-start | bytes 589828
  3.7 22.9 %all-to-all-start = ((f32[32,24,128]{2,1,0:T(8,128)}), f32[32,24,128]{2,1,0:T(8,128)S(1)}, u32[]{:S(2)}, u32[]{:S(2)}) async-start(f32[32,24,128]{2,1,0:T(8,128)} %broadcast_in_dim.19), calls=%async_computation | async-start | bytes 786432 | tf_op jit(solution)/shard_map/all_to_all | solution.py:641
  14.6 2.2 %copy-start.22 = (bf16[3,128]{1,0:T(4,128)(2,1)S(1)}, bf16[3,128]{1,0:T(4,128)(2,1)}, u32[]{:S(2)}) copy-start(bf16[3,128]{1,0:T(4,128)(2,1)} %param.23) | copy-start | bytes 2308
  14.6 2.2 %copy-start.13 = (f32[3,128]{1,0:T(4,128)S(1)}, f32[3,128]{1,0:T(4,128)}, u32[]{:S(2)}) copy-start(f32[3,128]{1,0:T(4,128)} %w_in.1) | copy-start | bytes 4612
  14.7 2.2 %copy-start.21 = (f32[3,128]{1,0:T(4,128)S(1)}, f32[3,128]{1,0:T(4,128)}, u32[]{:S(2)}) copy-start(f32[3,128]{1,0:T(4,128)} %param.22) | copy-start | bytes 4612
  14.7 3.0 %copy-start.23 = (f32[2,128]{1,0:T(2,128)S(1)}, f32[2,128]{1,0:T(2,128)}, u32[]{:S(2)}) copy-start(f32[2,128]{1,0:T(2,128)} %param.21) | copy-start | bytes 3076
  14.8 3.6 %copy-start.24 = (s32[2]{0:T(128)S(1)}, s32[2]{0:T(128)}, u32[]{:S(2)}) copy-start(s32[2]{0:T(128)} %param.15) | copy-start | bytes 28
  18.6 4.4 %copy-start.3 = (bf16[2,128,128]{2,1,0:T(8,128)(2,1)S(1)}, bf16[2,128,128]{2,1,0:T(8,128)(2,1)}, u32[]{:S(2)}) copy-start(bf16[2,128,128]{2,1,0:T(8,128)(2,1)} %param.20) | copy-start | bytes 196612
  26.6 0.7 copy-start.1
  41.8 1.4 collective-permute-start
  43.1 4.4 %copy-start.15 = (f32[8,128]{1,0:T(8,128)}, f32[8,128]{1,0:T(8,128)S(1)}, u32[]{:S(2)}) copy-start(f32[8,128]{1,0:T(8,128)S(1)} %collective-permute-done.refs_1_) | copy-start | bytes 12292
  43.8 3.7 %collective-permute-start.1 = (f32[16,128]{1,0:T(8,128)S(1)}, f32[16,128]{1,0:T(8,128)S(1)}, u32[]{:S(2)}, u32[]{:S(2)}) collective-permute-start(f32[16,128]{1,0:T(8,128)S(1)} %pad_maximum_fusion.4), channel_id=1, source_target_pairs={{0,16},{8,24},{16,0},{24,8},{1,17},{9,25},{17,1},{25,9},{2,18},{10... | collective-permute-start | bytes 24584 | tf_op jit(solution)/shard_map/ppermute | solution.py:595
  47.5 0.6 copy-start.17
  61.8 1.4 collective-permute-start.2
  63.2 4.5 %copy-start.16 = (f32[8,128]{1,0:T(8,128)}, f32[8,128]{1,0:T(8,128)S(1)}, u32[]{:S(2)}) copy-start(f32[8,128]{1,0:T(8,128)S(1)} %collective-permute-done.2.refs_1_) | copy-start | bytes 12292
  63.9 3.8 %collective-permute-start.3 = (f32[16,128]{1,0:T(8,128)S(1)}, f32[16,128]{1,0:T(8,128)S(1)}, u32[]{:S(2)}, u32[]{:S(2)}) collective-permute-start(f32[16,128]{1,0:T(8,128)S(1)} %pad_maximum_fusion.5), channel_id=1, source_target_pairs={{0,16},{8,24},{16,0},{24,8},{1,17},{9,25},{17,1},{25,9},{2,18},{10... | collective-permute-start | bytes 24584 | tf_op jit(solution)/shard_map/ppermute | solution.py:595
  67.7 0.6 copy-start.18
  74.5 2.2 %collective-permute-start.4 = (f32[8,128]{1,0:T(8,128)}, f32[8,128]{1,0:T(8,128)S(1)}, u32[]{:S(2)}, u32[]{:S(2)}) collective-permute-start(f32[8,128]{1,0:T(8,128)} %get-tuple-element.44.refs_0_), channel_id=1, source_target_pairs={{0,8},{8,0},{16,24},{24,16},{1,9},{9,1},{17,25},{25,17},{2,10},{10... | collective-permute-start | bytes 12296 | tf_op jit(solution)/shard_map/ppermute | solution.py:595
  76.7 4.4 %copy-start.9 = (f32[8,128]{1,0:T(8,128)}, f32[8,128]{1,0:T(8,128)S(1)}, u32[]{:S(2)}) copy-start(f32[8,128]{1,0:T(8,128)S(1)} %collective-permute-done.4.refs_1_) | copy-start | bytes 12292
  77.4 3.7 %collective-permute-start.5 = (f32[16,128]{1,0:T(8,128)S(1)}, f32[16,128]{1,0:T(8,128)S(1)}, u32[]{:S(2)}, u32[]{:S(2)}) collective-permute-start(f32[16,128]{1,0:T(8,128)S(1)} %pad_maximum_fusion.6), channel_id=1, source_target_pairs={{0,16},{8,24},{16,0},{24,8},{1,17},{9,25},{17,1},{25,9},{2,18},{10... | collective-permute-start | bytes 24584 | tf_op jit(solution)/shard_map/ppermute | solution.py:595
  81.0 0.6 copy-start.12
  81.6 22.0 %copy-start.8 = (f32[8,128]{1,0:T(8,128)S(1)}, f32[8,128]{1,0:T(8,128)}, u32[]{:S(2)}) copy-start(f32[8,128]{1,0:T(8,128)} %get-tuple-element.44.refs_0_) | copy-start | bytes 12292
  100.2 1.4 collective-permute-start.6
  101.5 4.3 %copy-start.6 = (f32[8,128]{1,0:T(8,128)}, f32[8,128]{1,0:T(8,128)S(1)}, u32[]{:S(2)}) copy-start(f32[8,128]{1,0:T(8,128)S(1)} %collective-permute-done.6.refs_1_) | copy-start | bytes 12292
  102.2 3.7 %collective-permute-start.7 = (f32[16,128]{1,0:T(8,128)S(1)}, f32[16,128]{1,0:T(8,128)S(1)}, u32[]{:S(2)}, u32[]{:S(2)}) collective-permute-start(f32[16,128]{1,0:T(8,128)S(1)} %pad_maximum_fusion.7), channel_id=1, source_target_pairs={{0,16},{8,24},{16,0},{24,8},{1,17},{9,25},{17,1},{25,9},{2,18},{10... | collective-permute-start | bytes 24584 | tf_op jit(solution)/shard_map/ppermute | solution.py:595
  105.9 0.6 copy-start.10
  118.4 20.7 %copy-start.20 = (f32[8,128]{1,0:T(8,128)S(1)}, f32[8,128]{1,0:T(8,128)}, u32[]{:S(2)}) copy-start(f32[8,128]{1,0:T(8,128)} %get-tuple-element.64) | copy-start | bytes 12292
  118.4 20.7 %copy-start.19 = (f32[8,128]{1,0:T(8,128)S(1)}, f32[8,128]{1,0:T(8,128)}, u32[]{:S(2)}) copy-start(f32[8,128]{1,0:T(8,128)} %get-tuple-element.65) | copy-start | bytes 12292
  118.4 21.2 %copy-start.5 = (f32[8,128]{1,0:T(8,128)S(1)}, f32[8,128]{1,0:T(8,128)}, u32[]{:S(2)}) copy-start(f32[8,128]{1,0:T(8,128)} %get-tuple-element.50.refs_0_) | copy-start | bytes 12292
  118.4 21.2 %copy-start.7 = (f32[8,128]{1,0:T(8,128)S(1)}, f32[8,128]{1,0:T(8,128)}, u32[]{:S(2)}) copy-start(f32[8,128]{1,0:T(8,128)} %copy-done.6) | copy-start | bytes 12292
  118.4 21.2 %copy-start.11 = (f32[16,128]{1,0:T(8,128)S(1)}, f32[16,128]{1,0:T(8,128)}, u32[]{:S(2)}) copy-start(f32[16,128]{1,0:T(8,128)} %copy-done.10) | copy-start | bytes 24580
  118.4 36.7 %copy-start.14 = (f32[3,128]{1,0:T(4,128)S(1)}, f32[3,128]{1,0:T(4,128)}, u32[]{:S(2)}) copy-start(f32[3,128]{1,0:T(4,128)} %w_in.1) | copy-start | bytes 4612
  134.4 9.8 %all-to-all-start.1 = ((f32[4,24,128]{2,1,0:T(8,128)}), f32[4,24,128]{2,1,0:T(8,128)S(1)}, u32[]{:S(2)}, u32[]{:S(2)}) async-start(f32[4,24,128]{2,1,0:T(8,128)} %bitcast_bitcast_fusion), calls=%async_computation.1 | async-start | bytes 98304 | tf_op jit(solution)/shard_map/all_to_all | solution.py:759
  139.1 1.4 collective-permute-start.8
  140.5 3.7 %collective-permute-start.9 = (f32[32,128]{1,0:T(8,128)S(1)}, f32[32,128]{1,0:T(8,128)S(1)}, u32[]{:S(2)}, u32[]{:S(2)}) collective-permute-start(f32[32,128]{1,0:T(8,128)S(1)} %add.87), channel_id=1, source_target_pairs={{0,16},{8,24},{16,0},{24,8},{1,17},{9,25},{17,1},{25,9},{2,18},{10... | collective-permute-start | bytes 49160 | tf_op jit(solution)/shard_map/ppermute | solution.py:595
  144.2 7.6 %all-to-all-start.4 = ((f32[4,48,128]{2,1,0:T(8,128)}), f32[4,48,128]{2,1,0:T(8,128)S(1)}, u32[]{:S(2)}, u32[]{:S(2)}) async-start(f32[4,48,128]{2,1,0:T(8,128)} %bitcast.38), calls=%async_computation.4 | async-start | bytes 196608 | tf_op jit(solution)/shard_map/all_to_all | solution.py:613
  151.8 7.6 %all-to-all-start.2 = ((f32[4,48,128]{2,1,0:T(8,128)}), f32[4,48,128]{2,1,0:T(8,128)S(1)}, u32[]{:S(2)}, u32[]{:S(2)}) async-start(f32[4,48,128]{2,1,0:T(8,128)} %bitcast.34), calls=%async_computation.2 | async-start | bytes 196608 | tf_op jit(solution)/shard_map/all_to_all | solution.py:613
  160.2 18.2 %all-to-all-start.5 = ((bf16[32,48,128]{2,1,0:T(8,128)(2,1)}), bf16[32,48,128]{2,1,0:T(8,128)(2,1)S(1)}, u32[]{:S(2)}, u32[]{:S(2)}) async-start(bf16[32,48,128]{2,1,0:T(8,128)(2,1)} %broadcast_in_dim.21), calls=%async_computation.5 | async-start | bytes 786432 | tf_op jit(solution)/shard_map/all_to_all | solution.py:615
  179.2 16.1 %all-to-all-start.3 = ((bf16[32,48,128]{2,1,0:T(8,128)(2,1)}), bf16[32,48,128]{2,1,0:T(8,128)(2,1)S(1)}, u32[]{:S(2)}, u32[]{:S(2)}) async-start(bf16[32,48,128]{2,1,0:T(8,128)(2,1)} %broadcast_in_dim.20), calls=%async_computation.3 | async-start | bytes 786432 | tf_op jit(solution)/shard_map/all_to_all | solution.py:615

commit v2 on v0

--- a/solution.py
+++ b/solution.py
@@ -1,16 +1,799 @@
+import functools
 import math
 
 import jax
 import jax.numpy as jnp
 from jax import lax
+from jax.experimental import pallas as pl
+from jax.experimental.pallas import tpu as pltpu
 from jax.sharding import PartitionSpec as P
 
 STEPS = 1000
-
+REACH = 256
+RIM = 4
+TILE = 16
+LIMITS = (8, 24, 24, 16, 28, 28, 28)
 
 eps_norm = 1e-05
 highest = lax.Precision.HIGHEST
+bf16 = jnp.bfloat16
+f32 = jnp.float32
 plane_offsets = ((-1, -1), (-1, 0), (-1, 1), (0, -1), (0, 1), (1, -1), (1, 0), (1, 1))
+
+
+def time_terms(timestep, w_time):
+    moment = timestep[0].astype(jnp.float32)
+    half_width = w_time.shape[0] // 2
+    alpha_bar = jnp.cos(0.5 * math.pi * (moment + 0.5) / STEPS) ** 2
+    ladder = jnp.exp(-math.log(10000.0) * jnp.arange(half_width, dtype=jnp.float32) / half_width)
+    angles = moment * ladder
+    features = jnp.concatenate([jnp.sin(angles), jnp.cos(angles)])
+    time_raw = jnp.dot(features, w_time, precision=highest)
+    return (alpha_bar, features, time_raw, jax.nn.silu(time_raw))
+
+
+def mm(left, right):
+    return lax.dot_general(left, right, (((1,), (0,)), ((), ())), preferred_element_type=f32)
+
+
+def mm_nt(left, right):
+    return lax.dot_general(left, right, (((1,), (1,)), ((), ())), preferred_element_type=f32)
+
+
+def mm_tn(left, right):
+    return lax.dot_general(left, right, (((0,), (0,)), ((), ())), preferred_element_type=f32)
+
+
+def halves(value):
+    high = value.astype(bf16)
+    return high, (value - high.astype(f32)).astype(bf16)
+
+
+def wide(vector):
+    return jnp.concatenate([vector] * 4, axis=1)
+
+
+def folded(vector):
+    channels = vector.shape[1] // 4
+    return sum(vector[:, y * channels : (y + 1) * channels] for y in range(4))
+
+
+class Place:
+    def __init__(self, sc, rows):
+        self.rows = rows
+        self.members = lax.axis_size("gz")
+        self.member = lax.axis_index("gz")
+        self.small = jnp.minimum(sc[0], sc[1])
+        self.coarse = self.small >= self.members
+        tiles = rows // TILE
+        self.tiles = tiles
+        self.stride = jnp.where(self.coarse, tiles - 1, tiles)
+        self.span = REACH // self.members + 2 * RIM
+        far = jnp.where(self.coarse, REACH // self.members, self.span)
+        near = jnp.where(self.coarse, self.small // self.members, 1)
+        self.steps = [jnp.where(sc[l] == REACH, far, near) for l in range(2)]
+
+    def index(self, shape):
+        row = lax.broadcasted_iota(jnp.int32, shape, 0)
+        return lax.rem(row, TILE) * self.stride + row // TILE, row // TILE
+
+    def own(self, shape):
+        place, tile = self.index(shape)
+        inside = lax.rem(place, self.span)
+        near = ((inside >= RIM) & (inside < self.span - RIM)).astype(jnp.int32)
+        far = (tile < self.tiles - 1).astype(jnp.int32)
+        return jnp.where(self.coarse, far, near) == 1
+
+    def pick(self, cells_z):
+        shape = (self.rows, cells_z)
+        place, _ = self.index(shape)
+        residues = jnp.minimum(self.small, self.members)
+        part, start = self.member // residues, lax.rem(self.member, residues)
+        period = place // self.span
+        inside = place - period * self.span - RIM + part * (REACH // self.members)
+        near = start + residues * inside + period * REACH
+        z = jnp.where(self.coarse, place * self.members + self.member, near)
+        z = lax.rem(z + 2 * cells_z, cells_z)
+        return z == lax.broadcasted_iota(jnp.int32, shape, 1)
+
+
+def build_taps(block_of, taps, taps_z):
+    channels = taps_z.shape[-1] // 2
+    zero = jnp.zeros((channels, channels), bf16)
+    for i in range(3):
+        for j in range(3):
+            block = block_of(i, j)
+            for q in range(2):
+                for side in range(2):
+                    y_in = 2 * q + side + j - 1
+                    if 0 <= y_in < 4:
+                        taps[
+                            q,
+                            i,
+                            y_in * channels : (y_in + 1) * channels,
+                            side * channels : (side + 1) * channels,
+                        ] = block
+        for q in range(2):
+            for side in range(2):
+                for y_in in range(4):
+                    if abs(y_in - 2 * q - side) > 1:
+                        taps[
+                            q,
+                            i,
+                            y_in * channels : (y_in + 1) * channels,
+                            side * channels : (side + 1) * channels,
+                        ] = zero
+    for m in range(2):
+        build_pair(block_of(3, m), taps_z, m)
+
+
+def build_pair(block, target, m):
+    channels = block.shape[-1]
+    zero = jnp.zeros((channels, channels), bf16)
+    target[m, :channels, :channels] = block
+    target[m, channels:, channels:] = block
+    target[m, :channels, channels:] = zero
+    target[m, channels:, :channels] = zero
+
+
+def forward_blocks(w_z, w_xy, layer):
+    def block_of(i, j):
+        if i == 3:
+            return w_z[layer, 2 * j]
+        at = i * 3 + j
+        return w_z[layer, 1] if at == 4 else w_xy[layer, at - (at > 4)]
+
+    return block_of
+
+
+def backward_blocks(w_back, layer):
+    return lambda i, j: w_back[layer, i * 3 + j]
+
+
+def kernel_prepare(w_z, w_xy, w_point, w_in, w_out, w_back, point_back, lift_in, lift_out):
+    for layer in range(2):
+        forward = forward_blocks(w_z, w_xy, layer)
+        for i in range(3):
+            for j in range(3):
+                w_back[layer, i * 3 + j] = forward(2 - i, 2 - j).T
+        for m in range(2):
+            w_back[layer, 9 + m] = forward(3, 1 - m).T
+        point_back[layer] = w_point[layer].T
+    whole = spread_rows(w_in[...], 0)
+    high, low = halves(whole)
+    lift_in[0:32] = high
+    lift_in[32:64] = high
+    lift_in[64:96] = low
+    lift_in[96:128] = jnp.zeros_like(low)
+    high = spread_rows(w_out[...].astype(f32), 3).astype(bf16)
+    lift_out[0:32] = high
+    lift_out[32:64] = high
+    lift_out[64:96] = jnp.zeros_like(high)
+    lift_out[96:128] = jnp.zeros_like(high)
+
+
+def spread_rows(weights, first):
+    channels = weights.shape[1]
+    zero = jnp.zeros((1, channels), f32)
+    rows = [jnp.zeros((1, 4 * channels), f32)] * 32
+    for k in range(3):
+        for y in range(4):
+            parts = [weights[k : k + 1] if at == y else zero for at in range(4)]
+            rows[(first + k) * 4 + y] = jnp.concatenate(parts, axis=1)
+    return jnp.concatenate(rows, axis=0)
+
+
+def fill_rims(padded, planes):
+    padded[0] = padded[planes]
+    padded[planes + 1] = padded[1]
+
+
+def fill_shifted(place, layer, padded, shifted, planes):
+    step, stride = place.steps[layer], place.stride
+    for tile in range(place.tiles):
+        for way in range(2):
+            at = tile - step if way == 0 else tile + step
+            moved = at + TILE * stride
+            source = lax.rem(moved, stride)
+            turn = lax.rem(2 * TILE - moved // stride, TILE)
+            rows = padded[1 : planes + 1, pl.ds(pl.multiple_of(source * TILE, TILE), TILE), :]
+            rows = pltpu.roll(rows.astype(f32), turn, 1)
+            shifted[way, :, tile * TILE : (tile + 1) * TILE, :] = rows.astype(bf16)
+
+
+def conv_half(padded, shifted, taps, taps_z, x0, count, q):
+    rows, lanes = padded.shape[1:]
+    half = lanes // 2
+    total = None
+    for i in range(3):
+        part = mm(padded[pl.ds(x0 + i, count)].reshape(count * rows, lanes), taps[q, i])
+        total = part if total is None else total + part
+    for m in range(2):
+        source = shifted[m, pl.ds(x0, count), :, q * half : (q + 1) * half]
+        total = total + mm(source.reshape(count * rows, half), taps_z[m])
+    return total
+
+
+def gelu_pair(value):
+    scale = math.sqrt(2.0 / math.pi)
+    square = value * value
+    bent = jnp.tanh(value * (scale + (scale * 0.044715) * square))
+    half = 0.5 + 0.5 * bent
+    slope = half + value * (0.5 - 0.5 * (bent * bent)) * (scale + (3.0 * 0.044715 * scale) * square)
+    return value * half, slope
+
+
+def members_of(parts):
+    found = []
+    for part in parts:
+        for at in range(0, part.shape[0], 8):
+            found.append(part[at : at + 8])
+    return found
+
+
+def merged_stats(parts, per_member):
+    found = members_of(parts)
+    mean = sum(one[0:1] for one in found) / (per_member * len(found))
+    spread = sum(one[1:2] for one in found)
+    for one in found:
+        gap = one[0:1] / per_member - mean
+        spread = spread + per_member * gap * gap
+    return mean, lax.rsqrt(spread / (per_member * len(found)) + eps_norm)
+
+
+def put_rows(ref, *vectors):
+    rows = list(vectors)
+    rows += [jnp.zeros((1, ref.shape[1]), f32)] * (ref.shape[0] - len(rows))
+    ref[...] = jnp.concatenate(rows, axis=0)
+
+
+def masked_total(mask, value):
+    return folded(jnp.sum(jnp.where(mask, value, 0.0), axis=0, keepdims=True))
+
+
+def layer_forward(place, layer, padded, shifted, taps, taps_z, pair, w_z, w_xy, wp, shift_bias, old,
+                  stream, act, slope, stats, acc, per_member):
+    planes, rows, lanes = stream.shape
+    half = lanes // 2
+    count = planes // 2
+    build_taps(forward_blocks(w_z, w_xy, layer), taps, taps_z)
+    build_pair(wp[layer], pair, 0)
+    fill_rims(padded, planes)
+    fill_shifted(place, layer, padded, shifted, planes)
+    acc[...] = jnp.zeros_like(acc)
+    bias = wide(shift_bias[layer : layer + 1, :])[:, :half]
+
+    def body(step, carry):
+        x0 = step * count
+        for q in range(2):
+            side = slice(q * half, (q + 1) * half)
+            pre = conv_half(padded, shifted, taps, taps_z, x0, count, q) + bias
+            value, grad = gelu_pair(pre)
+            value = value.astype(bf16)
+            act[pl.ds(x0, count), :, side] = value.reshape(count, rows, half)
+            slope[pl.ds(x0, count), :, side] = grad.astype(bf16).reshape(count, rows, half)
+            branch = mm(value, pair[0]).reshape(count, rows, half)
+            new = old[pl.ds(x0, count), :, side] + branch
+            stream[pl.ds(x0, count), :, side] = new
+            acc[:, side] += jnp.sum(new, axis=0)
+        return carry
+
+    lax.fori_loop(0, planes // count, body, 0)
+    mask = place.own((rows, lanes))
+    total = masked_total(mask, acc[...])
+    mean = wide(total / per_member)
+    spread = jnp.zeros((rows, lanes), f32)
+    for x in range(planes):
+        gap = stream[x] - mean
+        spread = spread + gap * gap
+    put_rows(stats, total, masked_total(mask, spread))
+
+
+def kernel_first(cells_z, per_member, sc, fields, lift_in, w_in, gains, shift_bias, w_z, w_xy, wp,
+                 stream, normed, act, slope, gathered, stats, consts,
+                 padded, shifted, taps, taps_z, pair, acc, old, source):
+    planes, rows, lanes = stream.shape
+    channels = lanes // 4
+    depth = fields.shape[2]
+    place = Place(sc, rows)
+    cell_count = float(planes * 4 * cells_z)
+    comps = [fields[:, 4 * k : 4 * k + 4, :] for k in range(3)]
+
+    def all_sum(value):
+        value = jnp.sum(jnp.sum(value, axis=0), axis=0, keepdims=True)
+        return jnp.sum(value, axis=1, keepdims=True)
+
+    means = [all_sum(comp) / cell_count for comp in comps]
+    gaps = [comp - mean[None] for comp, mean in zip(comps, means)]
+    covs = {}
+    for j in range(3):
+        for k in range(j, 3):
+            covs[j, k] = all_sum(gaps[j] * gaps[k]) / cell_count
+    rows_in = [w_in[k : k + 1, :] for k in range(3)]
+    mean_c = sum(means[k] * rows_in[k] for k in range(3))
+    var_c = jnp.zeros((1, channels), f32)
+    for (j, k), cov in covs.items():
+        var_c = var_c + (1.0 if j == k else 2.0) * cov * (rows_in[j] * rows_in[k])
+    inv_c = lax.rsqrt(jnp.maximum(var_c, 0.0) + eps_norm)
+    flat = [jnp.broadcast_to(value, (1, channels)) for value in means + list(covs.values())]
+    put_rows(consts, mean_c, inv_c, *flat)
+    blank = jnp.zeros((8, depth), f32)
+    for slab in range(cells_z // depth):
+        at = slice(slab * depth, (slab + 1) * depth)
+        for x in range(planes):
+            high, low = halves(jnp.concatenate([fields[slab * planes + x], blank], axis=0))
+            source[x, 0:32, at] = high
+            source[x, 32:64, at] = low
+            source[x, 64:96, at] = high
+            source[x, 96:128, at] = jnp.zeros_like(high)
+    pick = place.pick(cells_z).astype(f32).astype(bf16)
+    scale = wide(inv_c * gains[0:1, :])
+    mean_w = wide(mean_c)
+    for x in range(planes):
+        gathered[x] = mm_nt(pick, source[x]).astype(bf16)
+    for x0 in range(0, planes, planes // 2):
+        part = slice(x0, x0 + planes // 2)
+        value = mm(gathered[part].reshape(planes // 2 * rows, 128), lift_in[...])
+        unit = ((value - mean_w) * scale).astype(bf16).reshape(planes // 2, rows, lanes)
+        old[part] = value.reshape(planes // 2, rows, lanes)
+        padded[x0 + 1 : x0 + 1 + planes // 2] = unit
+        normed[part] = unit
+    layer_forward(place, 0, padded, shifted, taps, taps_z, pair, w_z, w_xy, wp, shift_bias, old, stream,
+                  act, slope, stats, acc, per_member)
+
+
+def kernel_second(per_member, sc, *refs):
+    parts, refs = refs[:3], refs[3:]
+    (old, gains, shift_bias, w_z, w_xy, wp, stream, normed, act, slope, stats, consts,
+     padded, shifted, taps, taps_z, pair, acc) = refs
+    planes, rows, _ = stream.shape
+    place = Place(sc, rows)
+    mean, inverse = merged_stats(parts, per_member)
+    put_rows(consts, mean, inverse)
+    mean_w, scale = wide(mean), wide(inverse * gains[1:2, :])
+    for x in range(planes):
+        unit = ((old[x] - mean_w) * scale).astype(bf16)
+        padded[x + 1] = unit
+        normed[x] = unit
+    layer_forward(place, 1, padded, shifted, taps, taps_z, pair, w_z, w_xy, wp, shift_bias, old, stream,
+                  act, slope, stats, acc, per_member)
+
+
+def kernel_out(per_member, sc, *refs):
+    parts, refs = refs[:3], refs[3:]
+    stream, gains, gathered, lift_out, prediction, misfit, sums, w_out_raw, consts, unit = refs
+    planes, rows, lanes = stream.shape
+    place = Place(sc, rows)
+    mean, inverse = merged_stats(parts, per_member)
+    put_rows(consts, mean, inverse)
+    mean_w, inv_w, gain_w = wide(mean), wide(inverse), wide(gains[2:3, :])
+    scale = inv_w * gain_w
+    for x in range(planes):
+        unit[x] = ((stream[x] - mean_w) * scale).astype(bf16)
+    row = lax.broadcasted_iota(jnp.int32, (128, 128), 0)
+    col = lax.broadcasted_iota(jnp.int32, (128, 128), 1)
+    slot = lax.rem(col, 32)
+    used = (col < 64) & (slot >= 12) & (slot < 24)
+    take = (used & ((row == slot) | (row == slot + 32))).astype(f32).astype(bf16)
+    total = mm_nt(unit[...].reshape(planes * rows, lanes), lift_out[...])
+    noise = mm(gathered[...].reshape(planes * rows, 128), take)
+    gap = total - noise
+    high, low = halves(gap)
+    lane = lax.broadcasted_iota(jnp.int32, gap.shape, 1)
+    both = jnp.where(lane < 32, high.astype(f32), low.astype(f32)).astype(bf16)
+    misfit[...] = both.reshape(planes, rows, 128)
+    for x in range(planes):
+        @pl.when(lax.axis_index("gx") == x)
+        def _(x=x):
+            prediction[...] = total[x * rows : (x + 1) * rows]
+    plain = jnp.zeros((rows, lanes), f32)
+    cross = jnp.zeros((rows, lanes), f32)
+    for x0 in range(0, planes, planes // 2):
+        part = slice(x0 * rows, (x0 + planes // 2) * rows)
+        d_out = mm(both[part], lift_out[...]).reshape(planes // 2, rows, lanes)
+        for x in range(planes // 2):
+            plain = plain + d_out[x]
+            cross = cross + d_out[x] * ((stream[x0 + x] - mean_w) * inv_w)
+    own = place.own((rows, 128))
+    kept = jnp.concatenate([jnp.where(own, misfit[x].astype(f32), 0.0) for x in range(planes)], axis=0)
+    raw = mm_tn(kept.astype(bf16), unit[...].reshape(planes * rows, lanes))
+    mask = place.own((rows, lanes))
+    put_rows(sums, masked_total(mask, plain), masked_total(mask, cross))
+    put_rows(w_out_raw, *by_component(raw[0:32] + raw[32:64], 3))
+
+
+def by_component(raw, first):
+    channels = raw.shape[1] // 4
+    found = []
+    for k in range(first, first + 3):
+        found.append(
+            sum(raw[k * 4 + y : k * 4 + y + 1, y * channels : (y + 1) * channels] for y in range(4))
+        )
+    return found
+
+
+def branch_backward(planes, d_stream_of, pair, slope, padded, scot, bias_acc):
+    rows, lanes = padded.shape[1:]
+    half = lanes // 2
+    count = planes // 2
+
+    def body(step, carry):
+        x0 = step * count
+        for t in range(count):
+            scot[x0 + t] = d_stream_of(x0 + t).astype(bf16)
+        for q in range(2):
+            side = slice(q * half, (q + 1) * half)
+            cot = scot[pl.ds(x0, count), :, side].reshape(count * rows, half)
+            d_act = mm(cot, pair[0]).reshape(count, rows, half)
+            pre = (d_act * slope[pl.ds(x0, count), :, side].astype(f32)).astype(bf16)
+            padded[pl.ds(x0 + 1, count), :, side] = pre
+            bias_acc[:, side] += jnp.sum(pre.astype(f32), axis=0)
+        return carry
+
+    lax.fori_loop(0, planes // count, body, 0)
+
+
+def weight_grads(place, planes, padded, shifted, scot, normed, act, grads, picked, share):
+    rows, lanes = padded.shape[1:]
+    channels = lanes // 4
+    wide_share = 4 * share
+    row = lax.broadcasted_iota(jnp.int32, (lanes, wide_share), 0)
+    col = lax.broadcasted_iota(jnp.int32, (lanes, wide_share), 1)
+    hit = (row // channels == col // share) & (
+        lax.rem(row, channels) == lax.rem(col, share) + lax.axis_index("gx") * share
+    )
+    choose = hit.astype(f32).astype(bf16)
+    mask = jnp.concatenate([place.own((rows, wide_share))] * planes, axis=0)
+
+    def turned(source):
+        got = mm(source[...].reshape(planes * rows, lanes), choose)
+        return jnp.where(mask, got, 0.0).astype(bf16)
+
+    def add_blocks(raw, j):
+        return sum(
+            raw[(y + j) * share : (y + j + 1) * share, y * channels : (y + 1) * channels]
+            for y in range(4)
+            if 0 <= y + j < 4
+        )
+
+    left = turned(normed)
+    for i in range(3):
+        raw = mm_tn(left, padded[2 - i : 2 - i + planes].reshape(planes * rows, lanes))
+        for j in range(3):
+            grads[i * 3 + j] = add_blocks(raw, j - 1)
+    for m in range(2):
+        raw = mm_tn(left, shifted[1 - m].reshape(planes * rows, lanes))
+        grads[9 + m] = add_blocks(raw, 0)
+    raw = mm_tn(turned(act), scot[...].reshape(planes * rows, lanes))
+    grads[11] = add_blocks(raw, 0)
+
+
+def conv_backward(planes, padded, shifted, taps, taps_z, emit):
+    rows, lanes = padded.shape[1:]
+    count = planes // 2
+
+    def body(step, carry):
+        x0 = step * count
+        for q in range(2):
+            emit(x0, count, q, conv_half(padded, shifted, taps, taps_z, x0, count, q))
+        return carry
+
+    lax.fori_loop(0, planes // count, body, 0)
+
+
+def kernel_back_second(share, cell_count, sc, *refs):
+    parts, refs = refs[:3], refs[3:]
+    (stream, out_consts, gains, misfit, lift_out, act, slope, normed, w_back, point_back,
+     d_stream, d_normed, sums, grads,
+     padded, shifted, taps, taps_z, pair, acc, acc2, scot) = refs
+    planes, rows, lanes = stream.shape
+    half = lanes // 2
+    place = Place(sc, rows)
+    sums_out = sum(members_of(parts))
+    gain_w = wide(gains[2:3, :])
+    mean_w, inv_w = wide(out_consts[0:1]), wide(out_consts[1:2])
+    m_plain = gain_w * wide(sums_out[0:1]) / cell_count
+    m_cross = gain_w * wide(sums_out[1:2]) / cell_count
+    build_pair(point_back[1], pair, 0)
+    build_taps(backward_blocks(w_back, 1), taps, taps_z)
+    acc[...] = jnp.zeros_like(acc)
+
+    def d_stream_of(x):
+        d_out = mm(misfit[x], lift_out[...])
+        white = (stream[x] - mean_w) * inv_w
+        value = inv_w * (gain_w * d_out - m_plain - white * m_cross)
+        d_stream[x] = value
+        return value
+
+    branch_backward(planes, d_stream_of, pair, slope, padded, scot, acc)
+    mask = place.own((rows, lanes))
+    s_bias = masked_total(mask, acc[...])
+    acc[...] = jnp.zeros_like(acc)
+    acc2[...] = jnp.zeros_like(acc2)
+    fill_rims(padded, planes)
+    fill_shifted(place, 1, padded, shifted, planes)
+
+    def emit(x0, count, q, value):
+        side = slice(q * half, (q + 1) * half)
+        value = value.reshape(count, rows, half)
+        d_normed[pl.ds(x0, count), :, side] = value
+        acc[:, side] += jnp.sum(value, axis=0)
+        acc2[:, side] += jnp.sum(value * normed[pl.ds(x0, count), :, side].astype(f32), axis=0)
+
+    conv_backward(planes, padded, shifted, taps, taps_z, emit)
+    s_plain = masked_total(mask, acc[...])
+    s_cross = masked_total(mask, acc2[...]) / gains[1:2, :]
+    put_rows(sums, s_plain, s_cross, s_bias)
+    weight_grads(place, planes, padded, shifted, scot, normed, act, grads, None, share)
+
+
+def kernel_back_first(share, cell_count, sc, *refs):
+    parts, refs = refs[:3], refs[3:]
+    (consts, d_next, d_normed, normed_next, gains, act, slope, normed, point_back,
+     d_stream, pre_cot, sums, grads,
+     padded, shifted, pair, acc, scot) = refs
+    planes, rows, lanes = d_next.shape
+    place = Place(sc, rows)
+    sums_in = sum(members_of(parts))
+    gain_w = wide(gains[1:2, :])
+    inv_w = wide(consts[1:2])
+    m_plain = gain_w * wide(sums_in[0:1]) / cell_count
+    m_cross = wide(sums_in[1:2]) / cell_count
+    build_pair(point_back[0], pair, 0)
+    acc[...] = jnp.zeros_like(acc)
+
+    def d_stream_of(x):
+        back = gain_w * d_normed[x] - m_plain - normed_next[x].astype(f32) * m_cross
+        value = d_next[x] + inv_w * back
+        d_stream[x] = value
+        return value
+
+    branch_backward(planes, d_stream_of, pair, slope, padded, scot, acc)
+    put_rows(sums, masked_total(place.own((rows, lanes)), acc[...]))
+    fill_rims(padded, planes)
+    fill_shifted(place, 0, padded, shifted, planes)
+    for x in range(planes):
+        pre_cot[x] = padded[x + 1]
+    weight_grads(place, planes, padded, shifted, scot, normed, act, grads, None, share)
+
+
+def kernel_last(cells_z, sc, pre_cot, d_stream, normed, gains, consts, gathered, lift_in, w_back,
+                prediction, ready, slab, sums, in_raw,
+                padded, shifted, taps, taps_z, acc, acc2, high, low):
+    planes, rows, lanes = d_stream.shape
+    half = lanes // 2
+    place = Place(sc, rows)
+    for x in range(planes):
+        padded[x + 1] = pre_cot[x]
+    fill_rims(padded, planes)
+    fill_shifted(place, 0, padded, shifted, planes)
+    build_taps(backward_blocks(w_back, 0), taps, taps_z)
+    acc[...] = jnp.zeros_like(acc)
+    acc2[...] = jnp.zeros_like(acc2)
+    scale = wide(consts[1:2] * gains[0:1, :])
+
+    def emit(x0, count, q, value):
+        side = slice(q * half, (q + 1) * half)
+        part = pl.ds(x0, count)
+        value = value.reshape(count, rows, half)
+        acc[:, side] += jnp.sum(value, axis=0)
+        acc2[:, side] += jnp.sum(value * normed[part, :, side].astype(f32), axis=0)
+        full = d_stream[part, :, side] + value * scale[:, side]
+        first, second = halves(full)
+        high[part, :, side] = first
+        low[part, :, side] = second
+
+    conv_backward(planes, padded, shifted, taps, taps_z, emit)
+    mask = place.own((rows, lanes))
+    s_plain = masked_total(mask, acc[...])
+    s_cross = masked_total(mask, acc2[...]) / gains[0:1, :]
+    put_rows(sums, s_plain, s_cross)
+    own = place.own((rows, 128))
+    kept = jnp.concatenate([jnp.where(own, gathered[x].astype(f32), 0.0) for x in range(planes)], axis=0)
+    kept = kept.astype(bf16)
+    raw = mm_tn(kept, high[...].reshape(planes * rows, lanes))
+    raw_low = mm_tn(kept, low[...].reshape(planes * rows, lanes))
+    put_rows(in_raw, *by_component(raw[0:32] + raw[32:64] + raw_low[0:32], 0))
+    here = lax.axis_index("gx")
+    lane = lax.broadcasted_iota(jnp.int32, (rows, 128), 1)
+    field = mm_nt(high[here], lift_in[...]) + jnp.where(lane < 32, mm_nt(low[here], lift_in[...]), 0.0)
+    field = jnp.where((lane >= 32) & (lane < 64), 0.0, field)
+    field = field + jnp.where((lane >= 12) & (lane < 24), prediction[...], 0.0)
+    pick = (place.pick(cells_z) & place.own((rows, cells_z))).astype(f32).astype(bf16)
+    first, second = halves(field)
+    out = mm_tn(first, pick) + mm_tn(second, pick)
+    slab[...] = out[0:32] + out[64:96]
+
+
+def call(kernel, outs, scratch, flops, limit, *args, scalars=True, loose=()):
+    spec = pl.BlockSpec(memory_space=pltpu.VMEM)
+    specs = [pl.BlockSpec(memory_space=pltpu.SMEM)] * scalars + [spec] * (len(args) - scalars)
+    for at in loose:
+        specs[at] = pl.BlockSpec(memory_space=pl.ANY)
+    return pl.pallas_call(
+        kernel,
+        out_shape=[jax.ShapeDtypeStruct(shape, dtype) for shape, dtype in outs],
+        in_specs=specs,
+        out_specs=[spec] * len(outs),
+        scratch_shapes=[pltpu.VMEM(shape, dtype) for shape, dtype in scratch],
+        compiler_params=pltpu.CompilerParams(vmem_limit_bytes=limit * 2**20),
+        cost_estimate=pl.CostEstimate(flops=flops, bytes_accessed=2**23, transcendentals=0),
+    )(*args)
+
+
+def swapped(value, axis, bit):
+    count = lax.axis_size(axis)
+    return lax.ppermute(value, axis, [(i, i ^ bit) for i in range(count)])
+
+
+def group_parts(value):
+    beside = swapped(value, "gz", 1)
+    pair = jnp.concatenate([value, beside], axis=0)
+    return (value, beside, swapped(pair, "gz", 2))
+
+
+def group_sum(value):
+    value = value + swapped(value, "gz", 1)
+    return value + swapped(value, "gz", 2)
+
+
+def group_grads(grads):
+    members = lax.axis_size("gz")
+    taps, share, channels = grads.shape
+    pieces = grads.reshape(members, (taps // members) * share, channels)
+    return jnp.sum(lax.all_to_all(pieces, "gz", 0, 0), axis=0).astype(bf16)
+
+
+def all_grads(mine, share):
+    members = lax.axis_size("gz")
+    total = members * lax.axis_size("gx")
+    every = lax.all_to_all(
+        jnp.broadcast_to(mine[None], (total,) + mine.shape), ("gz", "gx"), 0, 0
+    )
+    return every.reshape(members, total // members, mine.shape[0] // share, share, mine.shape[1])
+
+
+def laid_out(every):
+    members, groups, taps, share, channels = every.shape
+    return every.transpose(0, 2, 1, 3, 4).reshape(members * taps, groups * share, channels)
+
+
+def per_device_grouped(clean_field, noise_field, timestep, dilations, w_in, w_time, w_z, w_xy, w_point,
+                       biases, norm_gains, w_out):
+    members, groups = lax.axis_size("gz"), lax.axis_size("gx")
+    depth = clean_field.shape[3]
+    planes, cells_z = groups, depth * members
+    channels = w_in.shape[1]
+    lanes = 4 * channels
+    rows = (cells_z // REACH) * (REACH // members + 2 * RIM)
+    share = channels // groups
+    per_member = float(planes * 4 * depth)
+    cell_count = per_member * members
+    inv_area = 4.0 / cell_count
+
+    alpha_bar, features, time_raw, time_code = time_terms(timestep, w_time)
+    noisy = jnp.sqrt(alpha_bar) * clean_field + jnp.sqrt(1.0 - alpha_bar) * noise_field
+    block = jnp.concatenate([noisy, noise_field], axis=0).reshape(24, depth)
+    total = members * groups
+    fields = lax.all_to_all(
+        jnp.broadcast_to(block[None], (total, 24, depth)), ("gz", "gx"), 0, 0
+    )
+    shift_bias = biases + time_code
+
+    big = (planes, rows, lanes)
+    vec = ((8, channels), f32)
+    thin = ((planes, rows, 128), bf16)
+    lift = ((128, lanes), bf16)
+    conv_scratch = [
+        ((planes + 2, rows, lanes), bf16),
+        ((2,) + big, bf16),
+        ((2, 3, lanes, lanes // 2), bf16),
+        ((2, lanes // 2, lanes // 2), bf16),
+    ]
+    pair = ((1, lanes // 2, lanes // 2), bf16)
+    flat = ((rows, lanes), f32)
+    grad_out = ((12, share, channels), f32)
+
+    w_back, point_back, lift_in, lift_out = call(
+        kernel_prepare,
+        [((2, 11, channels, channels), bf16), ((2, channels, channels), bf16), lift, lift],
+        [], 10**8, LIMITS[0], w_z, w_xy, w_point, w_in, w_out, scalars=False,
+    )
+    stream1, normed0, act0, slope0, gathered, stats1, consts0 = call(
+        functools.partial(kernel_first, cells_z, per_member),
+        [(big, f32), (big, bf16), (big, bf16), (big, bf16), thin, vec, ((16, channels), f32)],
+        conv_scratch + [pair, flat, (big, f32), ((planes, 128, cells_z), bf16)],
+        4 * 10**9, LIMITS[1],
+        dilations, fields, lift_in, w_in, norm_gains, shift_bias, w_z, w_xy, w_point,
+    )
+    stream2, normed1, act1, slope1, stats2, consts1 = call(
+        functools.partial(kernel_second, per_member),
+        [(big, f32), (big, bf16), (big, bf16), (big, bf16), vec, vec],
+        conv_scratch + [pair, flat],
+        4 * 10**9, LIMITS[2],
+        dilations, *group_parts(stats1), stream1, norm_gains, shift_bias, w_z, w_xy, w_point,
+    )
+    prediction, misfit, sums2, out_raw, consts2 = call(
+        functools.partial(kernel_out, per_member),
+        [((rows, 128), f32), thin, vec, vec, vec],
+        [(big, bf16)],
+        10**9, LIMITS[3],
+        dilations, *group_parts(stats2), stream2, norm_gains, gathered, lift_out,
+    )
+    parts2 = group_parts(sums2)
+    d_stream2, d_normed1, sums1, grads1 = call(
+        functools.partial(kernel_back_second, share, cell_count),
+        [(big, f32), (big, f32), vec, grad_out],
+        conv_scratch + [pair, flat, flat, (big, bf16)],
+        6 * 10**9, LIMITS[4],
+        dilations, *parts2, stream2, consts2, norm_gains, misfit, lift_out, act1, slope1, normed1,
+        w_back, point_back,
+    )
+    parts1 = group_parts(sums1)
+    d_stream1, pre_cot0, sums_b0, grads0 = call(
+        functools.partial(kernel_back_first, share, cell_count),
+        [(big, f32), (big, bf16), vec, grad_out],
+        conv_scratch[:2] + [pair, flat, (big, bf16)],
+        4 * 10**9, LIMITS[5],
+        dilations, *parts1, consts1, d_stream2, d_normed1, normed1, norm_gains, act0, slope0, normed0,
+        point_back,
+    )
+    mine1 = group_grads(grads1)
+    slab, sums0, in_part = call(
+        functools.partial(kernel_last, cells_z),
+        [((32, cells_z), f32), vec, vec],
+        conv_scratch + [flat, flat, (big, bf16), (big, bf16)],
+        4 * 10**9, LIMITS[6],
+        dilations, pre_cot0, d_stream1, normed0, norm_gains, consts0, gathered, lift_in, w_back, prediction,
+        mine1, loose=(10,),
+    )
+    all1 = laid_out(all_grads(mine1, share))
+    all0 = laid_out(all_grads(group_grads(grads0), share))
+
+    tails = group_sum(jnp.concatenate([sums0, in_part, sums_b0, out_raw], axis=0))
+    s_plain, s_cross, in_sum = tails[0], tails[1], tails[8:11]
+    bias0, out_sum = tails[16], tails[24:27]
+    s1 = sum(members_of(parts1))
+    s2 = sum(members_of(parts2))
+    inverse = consts0[1]
+    m_plain = norm_gains[0] * s_plain / cell_count
+    m_cross = norm_gains[0] * s_cross / cell_count
+    mean_k = consts0[2:5, 0]
+    c00, c01, c02, c11, c12, c22 = (consts0[5 + at, 0] for at in range(6))
+    cov = jnp.stack([jnp.stack([c00, c01, c02]), jnp.stack([c01, c11, c12]), jnp.stack([c02, c12, c22])])
+    offset = jnp.sum(w_in * (inverse * m_plain), axis=1)
+    mix = jnp.sum(w_in[:, None, :] * (inverse * inverse * m_cross) * w_in[None, :, :], axis=2)
+    pieces = slab.reshape(32, members, depth)[:24].transpose(1, 0, 2)
+    landed = jnp.sum(lax.all_to_all(pieces, "gz", 0, 0), axis=0)
+    landed = landed.reshape(6, 1, 4, depth)
+    centered = noisy - mean_k[:, None, None, None]
+    field_grad = landed[:3] - offset[:, None, None, None] - sum(
+        mix[:, j, None, None, None] * centered[j][None] for j in range(3)
+    )
+    prediction_out = landed[3:]
+    cross_in = jnp.sum(cov[:, :, None] * w_in[None, :, :], axis=1)
+    in_raw = in_sum - cell_count * (
+        mean_k[:, None] * (inverse * m_plain) + (inverse * inverse * m_cross) * cross_in
+    )
+    bias_all = jnp.stack([bias0, s1[2]])
+    gain_all = jnp.stack([s_cross, s1[1], s2[1]])
+    weights = jnp.stack([all0, all1]).astype(f32) * inv_area
+    z_all = jnp.stack([weights[:, 9], weights[:, 4], weights[:, 10]], axis=1)
+    xy_all = jnp.concatenate([weights[:, :4], weights[:, 5:9]], axis=1)
+    time_back = jax.vjp(jax.nn.silu, time_raw)[1](jnp.sum(bias_all, axis=0))[0]
+    grad_w_time = inv_area * jnp.outer(features, time_back)
+    return (
+        prediction_out,
+        field_grad,
+        inv_area * in_raw,
+        grad_w_time,
+        z_all,
+        xy_all,
+        weights[:, 11],
+        inv_area * bias_all,
+        inv_area * gain_all,
+        inv_area * out_sum,
+    )
 
 
 def padded_2(cells, sides, width):
@@ -35,17 +818,6 @@
     return lax.ppermute(value, axis, pairs)
 
 
-def time_terms(timestep, w_time):
-    moment = timestep[0].astype(jnp.float32)
-    half_width = w_time.shape[0] // 2
-    alpha_bar = jnp.cos(0.5 * math.pi * (moment + 0.5) / STEPS) ** 2
-    ladder = jnp.exp(-math.log(10000.0) * jnp.arange(half_width, dtype=jnp.float32) / half_width)
-    angles = moment * ladder
-    features = jnp.concatenate([jnp.sin(angles), jnp.cos(angles)])
-    time_raw = jnp.dot(features, w_time, precision=highest)
-    return (alpha_bar, features, time_raw, jax.nn.silu(time_raw))
-
-
 def contract_cells(left, right):
     return lax.dot_general(
         left, right, (((0, 1, 2), (0, 1, 2)), ((), ())), preferred_element_type=jnp.float32
@@ -108,7 +880,7 @@
     return summed
 
 
-def conv_backward(pre_cot, normed, dilation, weights_z, weights_xy):
+def conv_backward_split(pre_cot, normed, dilation, weights_z, weights_xy):
     rows_x, rows_y = (normed.shape[0], normed.shape[1])
     lower_cot, upper_cot = slab_windows(pre_cot, dilation)
     padded_cot = plane_pad(pre_cot)
@@ -132,7 +904,7 @@
     return (d_normed, z_terms, jnp.stack(xy_terms))
 
 
-def per_device(
+def per_device_split(
     clean_field,
     noise_field,
     timestep,
@@ -183,7 +955,7 @@
         gelu_back = jax.vjp(jax.nn.gelu, pre_act)[1]
         pre_cot = gelu_back(d_act)[0].astype(jnp.bfloat16)
         bias_raw = jnp.sum(pre_cot, axis=(0, 1, 2), dtype=jnp.float32)
-        d_normed, z_raw, xy_raw = conv_backward(
+        d_normed, z_raw, xy_raw = conv_backward_split(
             pre_cot, normed, dilations[which_layer], w_z[which_layer], w_xy[which_layer]
         )
         d_back, gain_raw = norm_back(
@@ -225,6 +997,13 @@
     )
 
 
+def per_device(*args):
+    members, groups = lax.axis_size("gz"), lax.axis_size("gx")
+    _, rows_x, rows_y, depth = args[0].shape
+    small = rows_x == 1 and rows_y == 4 and members == 4 and groups == 8 and depth * members == 2 * REACH
+    return per_device_grouped(*args) if small else per_device_split(*args)
+
+
 def solution(mesh):
     return jax.shard_map(
         per_device,

time: 638 us -> 161 us (0.25)
  blocking collectives: 403 us -> 0 us
  waiting for transfers between devices: 145 us -> 46.6 us
  Pallas kernels: 0 us -> 41.1 us
  matrix products: 24.7 us -> 0.16 us
  local copies, waits for them, and re-layouts: 4.9 us -> 28.6 us
  between operations: 22.4 us -> 1.94 us
    psum x10 -> x0, blocking collectives: 403 us -> none  [the longest x3 122 us: normalize(): lax.psum(jnp.sum(centered * centered, axis=(0, 1, 2)), ('gz', 'gx'))]
    psum x1 -> x0, waiting for transfers between devices: 131 us -> none  [per_device(): lax.psum((jnp.stack(z_list), jnp.stack(xy_list), jnp.stack(point_list), j...]
    pallas_call x0 -> x7, Pallas kernels: none -> 41.1 us  [call(): pl.pallas_call(kernel, out_shape=[jax.ShapeDtypeStruct(shape, dtype) for...]
    all_to_all x0 -> x6, waiting for transfers between devices: none -> 36.5 us  [the longest x2 22.9 us: all_grads(): lax.all_to_all(jnp.broadcast_to(mine[None], (total,) + mine.shape), ('gz'...]
    dot_general x78 -> x0, matrix products: 24 us -> none  [the longest x24 9.32 us: contract_cells(): lax.dot_general(left, right, (((0, 1, 2), (0, 1, 2)), ((), ())), preferre...]
    all_to_all x0 -> x6, starting transfers between devices: none -> 22.4 us  [the longest x1 7.3 us: per_device_grouped(): lax.all_to_all(jnp.broadcast_to(block[None], (total, 24, depth)), ('gz',...]
    unnamed x68 -> x61, local copies, waits for them, and re-layouts: 2.78 us -> 23.2 us
    ppermute x20 -> x10, starting transfers between devices: 22.7 us -> 6.19 us  [swapped(): return lax.ppermute(value, axis, [(i, i ^ bit) for i in range(count)])]
  transfers between devices with their start and end apart: 21 -> 16, of which waited for: 5 -> 11; matrix products, arithmetic and copies ran while one was open for 2% -> 8% of each run, Pallas kernels for 0% -> 7%
where the time goes in v2:
time: 161 us; the launch traced here: 160 us
  waiting for transfers between devices  46.6 us (29%)
  Pallas kernels  41.1 us (26%)
  local copies, waits for them, and re-layouts  28.6 us (18%)
  starting transfers between devices  28.6 us (18%)
  other arithmetic  13.1 us (8%)
  between operations  1.94 us (1%)
    pallas_call x7, Pallas kernels, call(): pl.pallas_call(kernel, out_shape=[jax.ShapeDtypeStruct(shape, dtype) for...  41.1 us
    unnamed x61, local copies, waits for them, and re-layouts  23.2 us
    all_to_all x2, waiting for transfers between devices, all_grads(): lax.all_to_all(jnp.broadcast_to(mine[None], (total,) + mine.shape), ('gz'...  22.9 us
    ppermute x10, waiting for transfers between devices, swapped(): return lax.ppermute(value, axis, [(i, i ^ bit) for i in range(count)])  10 us
    all_to_all x1, waiting for transfers between devices, per_device_grouped(): lax.all_to_all(jnp.broadcast_to(block[None], (total, 24, depth)), ('gz',...  9.81 us
    all_to_all x1, starting transfers between devices, per_device_grouped(): lax.all_to_all(jnp.broadcast_to(block[None], (total, 24, depth)), ('gz',...  7.3 us
    all_to_all x2, starting transfers between devices, group_grads(): return jnp.sum(lax.all_to_all(pieces, 'gz', 0, 0), axis=0).astype(bf16)  6.62 us
    ppermute x10, starting transfers between devices, swapped(): return lax.ppermute(value, axis, [(i, i ^ bit) for i in range(count)])  6.19 us
  transfers between devices with their start and end apart: 16, of which 11 were waited for; matrix products, arithmetic and copies ran while one was open for 8% of the time, Pallas kernels for 7%

profile of v2, /device:TPU:0, one launch (start us, length us, event | category | flops | bytes accessed | tf_op | source)
XLA Modules:
  0.0 160.1 jit_solution(13417336366636417861)
XLA Ops:
  3.0 0.8 broadcast_in_dim.9
  3.8 7.3 %all-to-all-start = ((f32[32,24,128]{2,1,0:T(8,128)}), f32[32,24,128]{2,1,0:T(8,128)S(1)}, u32[]{:S(2)}, u32[]{:S(2)}) async-start(f32[32,24,128]{2,1,0:T(8,128)} %broadcast_in_dim.9), calls=%async_computation | async-start | bytes 786432 | tf_op jit(solution)/shard_map/all_to_all | solution.py:678
  11.1 0.9 copy-done.2
  12.0 0.8 copy-done.4
  14.8 9.8 %all-to-all-done.fields = f32[32,24,128]{2,1,0:T(8,128)S(1)} async-done(((f32[32,24,128]{2,1,0:T(8,128)}), f32[32,24,128]{2,1,0:T(8,128)S(1)}, u32[]{:S(2)}, u32[]{:S(2)}) %all-to-all-start) | async-done | bytes 393248 | tf_op jit(solution)/shard_map/all_to_all | solution.py:678
  24.7 9.7 %shard_map.196 = (f32[8,144,512]{2,1,0:T(8,128)S(1)}, bf16[8,144,512]{2,1,0:T(8,128)(2,1)S(1)}, bf16[8,144,512]{2,1,0:T(8,128)(2,1)S(1)}, bf16[8,144,512]{2,1,0:...) custom-call(s32[2]{0:T(128)S(1)} %copy-done.10, ...), custom_call_target="tpu_custom_call" | custom-call | flops 4000000000 | bytes 8388608 | tf_op jit(solution)/shard_map/pallas_call | solution.py:613
  34.4 1.0 copy-done.20
  35.4 1.1 copy-done.22
  36.7 1.0 collective-permute-done.refs_1_
  38.2 3.1 %collective-permute-done.1.refs_2_ = f32[16,128]{1,0:T(8,128)S(1)} collective-permute-done((f32[16,128]{1,0:T(8,128)S(1)}, f32[16,128]{1,0:T(8,128)S(1)}, u32[]{:S(2)}, u32[]{:S(2)}) %collective-permute-start.1) | collective-permute-done | bytes 8224 | tf_op jit(solution)/shard_map/ppermute | solution.py:626
  41.3 9.1 %shard_map.197 = (f32[8,144,512]{2,1,0:T(8,128)S(1)}, bf16[8,144,512]{2,1,0:T(8,128)(2,1)S(1)}, bf16[8,144,512]{2,1,0:T(8,128)(2,1)S(1)}, bf16[8,144,512]{2,1,0:...) custom-call(s32[2]{0:T(128)S(1)} %copy-done.10, f32[8,128]{1,0:T(8,128)S(1)} %get-tuple-element.44.refs_0_, ...), custom_call_target="tpu_custom_call" | custom-call | flops 4000000000 | bytes 8388608 | tf_op jit(solution)/shard_map/pallas_call | solution.py:613
  52.2 2.0 %maximum_bitcast_fusion.2 = f32[1,3]{1,0:T(1,128)S(1)} fusion(f32[1]{0:T(128)} %bitcast.18, f32[1]{0:T(128)} %bitcast.16, f32[1]{0:T(128)} %bitcast.13), kind=kLoop, calls=%fused_computation.50 | loop fusion | flops 6 | bytes 24 | tf_op jit(solution)/shard_map/stack | solution.py:763
  54.3 1.1 collective-permute-done.3.refs_2_
  55.3 2.3 %shard_map.198 = (f32[144,128]{1,0:T(8,128)S(1)}, bf16[8,144,128]{2,1,0:T(8,128)(2,1)S(1)}, f32[8,128]{1,0:T(8,128)S(1)}, f32[8,128]{1,0:T(8,128)S(1)}, f32[8,128]{1,0:T(8,128)S(1)}) custom-call(s32[2]{0:T(128)S(1)} %copy-done.10, f32[8,128]{1,0:T(8,128)S(1)} %get-tuple-element.46.refs_0_, f32[8,128]{1,0:T(8,128)S(1)} %collective-permute-done.2.refs_1_, ...), custom_call_target="tpu_custom_call" | custom-call | flops 1000000000 | bytes 8388608 | tf_op jit(solution)/shard_map/pallas_call | solution.py:613
  57.7 2.0 %maximum_bitcast_fusion.1 = f32[1,3]{1,0:T(1,128)S(1)} fusion(f32[1]{0:T(128)} %bitcast.16, f32[1]{0:T(128)} %bitcast.15, f32[1]{0:T(128)} %bitcast.12), kind=kLoop, calls=%fused_computation.49 | loop fusion | flops 6 | bytes 24 | tf_op jit(solution)/shard_map/stack | solution.py:763
  60.3 2.0 %maximum_bitcast_fusion = f32[1,3]{1,0:T(1,128)S(1)} fusion(f32[1]{0:T(128)} %bitcast.13, f32[1]{0:T(128)} %bitcast.12, f32[1]{0:T(128)} %bitcast.11), kind=kLoop, calls=%fused_computation.48 | loop fusion | flops 6 | bytes 24 | tf_op jit(solution)/shard_map/stack | solution.py:763
  62.3 1.1 collective-permute-done.5.refs_2_
  63.4 9.0 %shard_map.199 = (f32[8,144,512]{2,1,0:T(8,128)S(1)}, f32[8,144,512]{2,1,0:T(8,128)S(1)}, f32[8,128]{1,0:T(8,128)S(1)}, f32[12,16,128]{2,1,0:T(8,128)}) custom-call(s32[2]{0:T(128)S(1)} %copy-done.10, f32[8,128]{1,0:T(8,128)S(1)} %get-tuple-element.50.refs_0_, f32[8,128]{1,0:T(8,128)S(1)} %collective-permute-done.4.refs_1_, ...), custom_call_target="tpu_custom_call" | custom-call | flops 6000000000 | bytes 8388608 | tf_op jit(solution)/shard_map/pallas_call | solution.py:613
  72.5 1.4 copy-done.11
  73.9 1.4 copy-done.13
  75.3 3.3 %all-to-all-start.1 = ((f32[4,48,128]{2,1,0:T(8,128)}), f32[4,48,128]{2,1,0:T(8,128)S(1)}, u32[]{:S(2)}, u32[]{:S(2)}) async-start(f32[4,48,128]{2,1,0:T(8,128)} %bitcast.4), calls=%async_computation.1 | async-start | bytes 196608 | tf_op jit(solution)/shard_map/all_to_all | solution.py:644
  78.7 2.0 %collective-permute-start.7 = (f32[16,128]{1,0:T(8,128)S(1)}, f32[16,128]{1,0:T(8,128)S(1)}, u32[]{:S(2)}, u32[]{:S(2)}) collective-permute-start(f32[16,128]{1,0:T(8,128)S(1)} %pad_maximum_fusion.6), channel_id=1, source_target_pairs={{0,16},{8,24},{16,0},{24,8},{1,17},{9,25},{17,1},{25,9},{2,18},{10... | collective-permute-start | bytes 24584 | tf_op jit(solution)/shard_map/ppermute | solution.py:626
  80.7 2.4 %collective-permute-done.7.refs_2_ = f32[16,128]{1,0:T(8,128)S(1)} collective-permute-done((f32[16,128]{1,0:T(8,128)S(1)}, f32[16,128]{1,0:T(8,128)S(1)}, u32[]{:S(2)}, u32[]{:S(2)}) %collective-permute-start.7) | collective-permute-done | bytes 8224 | tf_op jit(solution)/shard_map/ppermute | solution.py:626
  83.1 1.7 %copy-done.12 = f32[8,144,512]{2,1,0:T(8,128)S(1)} copy-done((f32[8,144,512]{2,1,0:T(8,128)S(1)}, f32[8,144,512]{2,1,0:T(8,128)}, u32[]{:S(2)}) %copy-start.12) | copy-done | bytes 2359320
  84.7 1.7 %copy-done.14 = f32[8,144,512]{2,1,0:T(8,128)S(1)} copy-done((f32[8,144,512]{2,1,0:T(8,128)S(1)}, f32[8,144,512]{2,1,0:T(8,128)}, u32[]{:S(2)}) %copy-start.14) | copy-done | bytes 2359320
  86.4 1.3 copy-done.18
  87.7 1.3 copy-done.21
  88.9 1.3 copy-done.23
  90.2 1.3 copy-done.25
  91.5 4.8 %shard_map.200 = (f32[8,144,512]{2,1,0:T(8,128)S(1)}, bf16[8,144,512]{2,1,0:T(8,128)(2,1)S(1)}, f32[8,128]{1,0:T(8,128)S(1)}, f32[12,16,128]{2,1,0:T(8,128)}) custom-call(s32[2]{0:T(128)S(1)} %copy-done.10, f32[8,128]{1,0:T(8,128)S(1)} %get-tuple-element.58.refs_0_, f32[8,128]{1,0:T(8,128)S(1)} %collective-permute-done.6.refs_1_, ...), custom_call_target="tpu_custom_call" | custom-call | flops 4000000000 | bytes 8388608 | tf_op jit(solution)/shard_map/pallas_call | solution.py:613
  96.2 1.4 copy-done.15
  97.7 1.0 copy-done.26
  98.7 3.3 %all-to-all-start.3 = ((f32[4,48,128]{2,1,0:T(8,128)}), f32[4,48,128]{2,1,0:T(8,128)S(1)}, u32[]{:S(2)}, u32[]{:S(2)}) async-start(f32[4,48,128]{2,1,0:T(8,128)} %bitcast.21), calls=%async_computation.3 | async-start | bytes 196608 | tf_op jit(solution)/shard_map/all_to_all | solution.py:644
  102.0 1.7 %copy-done.16 = f32[8,144,512]{2,1,0:T(8,128)S(1)} copy-done((f32[8,144,512]{2,1,0:T(8,128)S(1)}, f32[8,144,512]{2,1,0:T(8,128)}, u32[]{:S(2)}) %copy-start.16) | copy-done | bytes 2359320
  103.7 1.3 copy-done.19
  105.0 1.3 copy-done.27
  106.2 6.0 %shard_map.201 = (f32[32,512]{1,0:T(8,128)S(1)}, f32[8,128]{1,0:T(8,128)S(1)}, f32[8,128]{1,0:T(8,128)S(1)}) custom-call(s32[2]{0:T(128)S(1)} %copy-done.10, bf16[8,144,512]{2,1,0:T(8,128)(2,1)S(1)} %copy-done.27, f32[8,144,512]{2,1,0:T(8,128)S(1)} %copy-done.16, bf16[8,144,512]{2,1,0:T(8,128)(2,1)S(1)} %copy-done.19, f32[3,128]{1,0:T(4,128)S(1)} %copy-done.9, ...), custom_call_target="tpu_custom_call" | custom-call | flops 4000000000 | bytes 8388608 | tf_op jit(solution)/shard_map/pallas_call | solution.py:613
  112.8 0.8 collective-permute-done.8
  113.7 1.9 %collective-permute-start.9 = (f32[32,128]{1,0:T(8,128)S(1)}, f32[32,128]{1,0:T(8,128)S(1)}, u32[]{:S(2)}, u32[]{:S(2)}) collective-permute-start(f32[32,128]{1,0:T(8,128)S(1)} %add.74), channel_id=1, source_target_pairs={{0,16},{8,24},{16,0},{24,8},{1,17},{9,25},{17,1},{25,9},{2,18},{10... | collective-permute-start | bytes 49160 | tf_op jit(solution)/shard_map/ppermute | solution.py:626
  116.1 3.3 %all-to-all-start.2 = ((f32[4,24,128]{2,1,0:T(8,128)}), f32[4,24,128]{2,1,0:T(8,128)S(1)}, u32[]{:S(2)}, u32[]{:S(2)}) async-start(f32[4,24,128]{2,1,0:T(8,128)} %bitcast_bitcast_fusion), calls=%async_computation.2 | async-start | bytes 98304 | tf_op jit(solution)/shard_map/all_to_all | solution.py:767
  119.6 3.8 %all-to-all-done.2 = f32[4,24,128]{2,1,0:T(8,128)S(1)} async-done(((f32[4,24,128]{2,1,0:T(8,128)}), f32[4,24,128]{2,1,0:T(8,128)S(1)}, u32[]{:S(2)}, u32[]{:S(2)}) %all-to-all-start.2) | async-done | bytes 49184 | tf_op jit(solution)/shard_map/all_to_all | solution.py:767
  123.4 0.8 broadcast_in_dim.11
  124.2 2.6 %all-to-all-start.5 = ((bf16[32,48,128]{2,1,0:T(8,128)(2,1)}), bf16[32,48,128]{2,1,0:T(8,128)(2,1)S(1)}, u32[]{:S(2)}, u32[]{:S(2)}) async-start(bf16[32,48,128]{2,1,0:T(8,128)(2,1)} %broadcast_in_dim.11), calls=%async_computation.5 | async-start | bytes 786432 | tf_op jit(solution)/shard_map/all_to_all | solution.py:650
  128.4 12.0 %all-to-all-done.5 = bf16[32,48,128]{2,1,0:T(8,128)(2,1)S(1)} async-done(((bf16[32,48,128]{2,1,0:T(8,128)(2,1)}), bf16[32,48,128]{2,1,0:T(8,128)(2,1)S(1)}, u32[]{:S(2)}, u32[]{:S(2)}) %all-to-all-start.5) | async-done | bytes 393248 | tf_op jit(solution)/shard_map/all_to_all | solution.py:650
  140.4 0.8 broadcast_in_dim.10
  141.2 2.6 %all-to-all-start.4 = ((bf16[32,48,128]{2,1,0:T(8,128)(2,1)}), bf16[32,48,128]{2,1,0:T(8,128)(2,1)S(1)}, u32[]{:S(2)}, u32[]{:S(2)}) async-start(bf16[32,48,128]{2,1,0:T(8,128)(2,1)} %broadcast_in_dim.10), calls=%async_computation.4 | async-start | bytes 786432 | tf_op jit(solution)/shard_map/all_to_all | solution.py:650
  146.4 10.9 %all-to-all-done.4 = bf16[32,48,128]{2,1,0:T(8,128)(2,1)S(1)} async-done(((bf16[32,48,128]{2,1,0:T(8,128)(2,1)}), bf16[32,48,128]{2,1,0:T(8,128)(2,1)S(1)}, u32[]{:S(2)}, u32[]{:S(2)}) %all-to-all-start.4) | async-done | bytes 393248 | tf_op jit(solution)/shard_map/all_to_all | solution.py:650
  158.3 1.0 pad_maximum_fusion
  (104 shorter events, 13.9 us)
Async XLA Ops:
  0.6 14.0 %copy-start = (f32[128,128]{1,0:T(8,128)S(1)}, f32[128,128]{1,0:T(8,128)}, u32[]{:S(2)}) copy-start(f32[128,128]{1,0:T(8,128)} %param.17) | copy-start | bytes 196612
  0.7 24.0 %copy-start.3 = (bf16[2,3,128,128]{3,2,1,0:T(8,128)(2,1)S(1)}, bf16[2,3,128,128]{3,2,1,0:T(8,128)(2,1)}, u32[]{:S(2)}) copy-start(bf16[2,3,128,128]{3,2,1,0:T(8,128)(2,1)} %refs_6_.1) | copy-start | bytes 589828
  0.7 10.4 %copy-start.1 = (bf16[2,8,128,128]{3,2,1,0:T(8,128)(2,1)S(1)}, bf16[2,8,128,128]{3,2,1,0:T(8,128)(2,1)}, u32[]{:S(2)}) copy-start(bf16[2,8,128,128]{3,2,1,0:T(8,128)(2,1)} %refs_7_.2) | copy-start | bytes 1572868
  0.7 24.0 %copy-start.5 = (bf16[2,128,128]{2,1,0:T(8,128)(2,1)S(1)}, bf16[2,128,128]{2,1,0:T(8,128)(2,1)}, u32[]{:S(2)}) copy-start(bf16[2,128,128]{2,1,0:T(8,128)(2,1)} %refs_8_.1) | copy-start | bytes 196612
  0.7 24.0 %copy-start.7 = (f32[3,128]{1,0:T(4,128)S(1)}, f32[3,128]{1,0:T(4,128)}, u32[]{:S(2)}) copy-start(f32[3,128]{1,0:T(4,128)} %w_in.3) | copy-start | bytes 4612
  0.7 14.1 %copy-start.28 = (f32[2,128]{1,0:T(2,128)S(1)}, f32[2,128]{1,0:T(2,128)}, u32[]{:S(2)}) copy-start(f32[2,128]{1,0:T(2,128)} %param.21) | copy-start | bytes 3076
  0.7 23.9 %copy-start.10 = (s32[2]{0:T(128)S(1)}, s32[2]{0:T(128)}, u32[]{:S(2)}) copy-start(s32[2]{0:T(128)} %sc.11) | copy-start | bytes 28
  0.7 23.9 %copy-start.9 = (f32[3,128]{1,0:T(4,128)S(1)}, f32[3,128]{1,0:T(4,128)}, u32[]{:S(2)}) copy-start(f32[3,128]{1,0:T(4,128)} %gains.3) | copy-start | bytes 4612
  3.8 20.8 %all-to-all-start = ((f32[32,24,128]{2,1,0:T(8,128)}), f32[32,24,128]{2,1,0:T(8,128)S(1)}, u32[]{:S(2)}, u32[]{:S(2)}) async-start(f32[32,24,128]{2,1,0:T(8,128)} %broadcast_in_dim.9), calls=%async_computation | async-start | bytes 786432 | tf_op jit(solution)/shard_map/all_to_all | solution.py:678
  11.1 0.9 copy-start.2
  12.0 0.8 copy-start.4
  12.9 0.7 copy-start.6
  13.6 0.7 copy-start.8
  34.4 1.0 copy-start.20
  35.4 1.1 copy-start.22
  36.5 13.9 %copy-start.17 = (bf16[8,144,512]{2,1,0:T(8,128)(2,1)}, bf16[8,144,512]{2,1,0:T(8,128)(2,1)S(1)}, u32[]{:S(2)}) copy-start(bf16[8,144,512]{2,1,0:T(8,128)(2,1)S(1)} %get-tuple-element.64.refs_10_.normed) | copy-start | bytes 3538948
  36.5 1.2 collective-permute-start
  37.7 3.7 %collective-permute-start.1 = (f32[16,128]{1,0:T(8,128)S(1)}, f32[16,128]{1,0:T(8,128)S(1)}, u32[]{:S(2)}, u32[]{:S(2)}) collective-permute-start(f32[16,128]{1,0:T(8,128)S(1)} %pad_maximum_fusion.3), channel_id=1, source_target_pairs={{0,16},{8,24},{16,0},{24,8},{1,17},{9,25},{17,1},{25,9},{2,18},{10... | collective-permute-start | bytes 24584 | tf_op jit(solution)/shard_map/ppermute | solution.py:626
  50.4 13.0 %copy-start.24 = (bf16[8,144,512]{2,1,0:T(8,128)(2,1)}, bf16[8,144,512]{2,1,0:T(8,128)(2,1)S(1)}, u32[]{:S(2)}) copy-start(bf16[8,144,512]{2,1,0:T(8,128)(2,1)S(1)} %get-tuple-element.55.refs_10_.refs_6_) | copy-start | bytes 3538948
  50.5 1.2 collective-permute-start.2
  51.7 3.7 %collective-permute-start.3 = (f32[16,128]{1,0:T(8,128)S(1)}, f32[16,128]{1,0:T(8,128)S(1)}, u32[]{:S(2)}, u32[]{:S(2)}) collective-permute-start(f32[16,128]{1,0:T(8,128)S(1)} %pad_maximum_fusion.4), channel_id=1, source_target_pairs={{0,16},{8,24},{16,0},{24,8},{1,17},{9,25},{17,1},{25,9},{2,18},{10... | collective-permute-start | bytes 24584 | tf_op jit(solution)/shard_map/ppermute | solution.py:626
  57.6 2.1 %collective-permute-start.4 = (f32[8,128]{1,0:T(8,128)S(1)}, f32[8,128]{1,0:T(8,128)S(1)}, u32[]{:S(2)}, u32[]{:S(2)}) collective-permute-start(f32[8,128]{1,0:T(8,128)S(1)} %get-tuple-element.50.refs_0_), channel_id=1, source_target_pairs={{0,8},{8,0},{16,24},{24,16},{1,9},{9,1},{17,25},{25,17},{2,10},{10... | collective-permute-start | bytes 12296 | tf_op jit(solution)/shard_map/ppermute | solution.py:626
  59.7 3.7 %collective-permute-start.5 = (f32[16,128]{1,0:T(8,128)S(1)}, f32[16,128]{1,0:T(8,128)S(1)}, u32[]{:S(2)}, u32[]{:S(2)}) collective-permute-start(f32[16,128]{1,0:T(8,128)S(1)} %pad_maximum_fusion.5), channel_id=1, source_target_pairs={{0,16},{8,24},{16,0},{24,8},{1,17},{9,25},{17,1},{25,9},{2,18},{10... | collective-permute-start | bytes 24584 | tf_op jit(solution)/shard_map/ppermute | solution.py:626
  72.5 1.4 copy-start.11
  73.9 1.4 copy-start.13
  75.3 3.3 %collective-permute-start.6 = (f32[8,128]{1,0:T(8,128)S(1)}, f32[8,128]{1,0:T(8,128)S(1)}, u32[]{:S(2)}, u32[]{:S(2)}) collective-permute-start(f32[8,128]{1,0:T(8,128)S(1)} %get-tuple-element.58.refs_0_), channel_id=1, source_target_pairs={{0,8},{8,0},{16,24},{24,16},{1,9},{9,1},{17,25},{25,17},{2,10},{10... | collective-permute-start | bytes 12296 | tf_op jit(solution)/shard_map/ppermute | solution.py:626
  75.3 23.4 %all-to-all-start.1 = ((f32[4,48,128]{2,1,0:T(8,128)}), f32[4,48,128]{2,1,0:T(8,128)S(1)}, u32[]{:S(2)}, u32[]{:S(2)}) async-start(f32[4,48,128]{2,1,0:T(8,128)} %bitcast.4), calls=%async_computation.1 | async-start | bytes 196608 | tf_op jit(solution)/shard_map/all_to_all | solution.py:644
  78.7 4.4 %collective-permute-start.7 = (f32[16,128]{1,0:T(8,128)S(1)}, f32[16,128]{1,0:T(8,128)S(1)}, u32[]{:S(2)}, u32[]{:S(2)}) collective-permute-start(f32[16,128]{1,0:T(8,128)S(1)} %pad_maximum_fusion.6), channel_id=1, source_target_pairs={{0,16},{8,24},{16,0},{24,8},{1,17},{9,25},{17,1},{25,9},{2,18},{10... | collective-permute-start | bytes 24584 | tf_op jit(solution)/shard_map/ppermute | solution.py:626
  83.1 1.7 %copy-start.12 = (f32[8,144,512]{2,1,0:T(8,128)S(1)}, f32[8,144,512]{2,1,0:T(8,128)}, u32[]{:S(2)}) copy-start(f32[8,144,512]{2,1,0:T(8,128)} %copy-done.11) | copy-start | bytes 7077892
  84.7 1.7 %copy-start.14 = (f32[8,144,512]{2,1,0:T(8,128)S(1)}, f32[8,144,512]{2,1,0:T(8,128)}, u32[]{:S(2)}) copy-start(f32[8,144,512]{2,1,0:T(8,128)} %copy-done.13) | copy-start | bytes 7077892
  86.4 1.3 copy-start.18
  87.7 1.3 copy-start.21
  88.9 1.3 copy-start.23
  90.2 1.3 copy-start.25
  96.2 1.4 copy-start.15
  97.7 1.0 copy-start.26
  98.7 17.5 %all-to-all-start.3 = ((f32[4,48,128]{2,1,0:T(8,128)}), f32[4,48,128]{2,1,0:T(8,128)S(1)}, u32[]{:S(2)}, u32[]{:S(2)}) async-start(f32[4,48,128]{2,1,0:T(8,128)} %bitcast.21), calls=%async_computation.3 | async-start | bytes 196608 | tf_op jit(solution)/shard_map/all_to_all | solution.py:644
  102.0 1.7 %copy-start.16 = (f32[8,144,512]{2,1,0:T(8,128)S(1)}, f32[8,144,512]{2,1,0:T(8,128)}, u32[]{:S(2)}) copy-start(f32[8,144,512]{2,1,0:T(8,128)} %copy-done.15) | copy-start | bytes 7077892
  103.7 1.3 copy-start.19
  105.0 1.3 copy-start.27
  112.3 1.4 collective-permute-start.8
  113.7 5.8 %collective-permute-start.9 = (f32[32,128]{1,0:T(8,128)S(1)}, f32[32,128]{1,0:T(8,128)S(1)}, u32[]{:S(2)}, u32[]{:S(2)}) collective-permute-start(f32[32,128]{1,0:T(8,128)S(1)} %add.74), channel_id=1, source_target_pairs={{0,16},{8,24},{16,0},{24,8},{1,17},{9,25},{17,1},{25,9},{2,18},{10... | collective-permute-start | bytes 49160 | tf_op jit(solution)/shard_map/ppermute | solution.py:626
  116.1 7.3 %all-to-all-start.2 = ((f32[4,24,128]{2,1,0:T(8,128)}), f32[4,24,128]{2,1,0:T(8,128)S(1)}, u32[]{:S(2)}, u32[]{:S(2)}) async-start(f32[4,24,128]{2,1,0:T(8,128)} %bitcast_bitcast_fusion), calls=%async_computation.2 | async-start | bytes 98304 | tf_op jit(solution)/shard_map/all_to_all | solution.py:767
  124.2 16.1 %all-to-all-start.5 = ((bf16[32,48,128]{2,1,0:T(8,128)(2,1)}), bf16[32,48,128]{2,1,0:T(8,128)(2,1)S(1)}, u32[]{:S(2)}, u32[]{:S(2)}) async-start(bf16[32,48,128]{2,1,0:T(8,128)(2,1)} %broadcast_in_dim.11), calls=%async_computation.5 | async-start | bytes 786432 | tf_op jit(solution)/shard_map/all_to_all | solution.py:650
  141.2 16.1 %all-to-all-start.4 = ((bf16[32,48,128]{2,1,0:T(8,128)(2,1)}), bf16[32,48,128]{2,1,0:T(8,128)(2,1)S(1)}, u32[]{:S(2)}, u32[]{:S(2)}) async-start(bf16[32,48,128]{2,1,0:T(8,128)(2,1)} %broadcast_in_dim.10), calls=%async_computation.4 | async-start | bytes 786432 | tf_op jit(solution)/shard_map/all_to_all | solution.py:650

commit v3 on v2

--- a/solution.py
+++ b/solution.py
@@ -12,7 +12,7 @@
 REACH = 256
 RIM = 4
 TILE = 16
-LIMITS = (8, 24, 24, 16, 28, 28, 28)
+LIMITS = (4, 13, 10, 7, 12, 9, 12, 2)
 
 eps_norm = 1e-05
 highest = lax.Precision.HIGHEST
@@ -86,6 +86,9 @@
 
     def pick(self, cells_z):
         shape = (self.rows, cells_z)
+        return self.z_of(shape, cells_z) == lax.broadcasted_iota(jnp.int32, shape, 1)
+
+    def z_of(self, shape, cells_z):
         place, _ = self.index(shape)
         residues = jnp.minimum(self.small, self.members)
         part, start = self.member // residues, lax.rem(self.member, residues)
@@ -93,8 +96,7 @@
         inside = place - period * self.span - RIM + part * (REACH // self.members)
         near = start + residues * inside + period * REACH
         z = jnp.where(self.coarse, place * self.members + self.member, near)
-        z = lax.rem(z + 2 * cells_z, cells_z)
-        return z == lax.broadcasted_iota(jnp.int32, shape, 1)
+        return lax.rem(z + 2 * cells_z, cells_z)
 
 
 def build_taps(block_of, taps, taps_z):
@@ -150,6 +152,15 @@
     return lambda i, j: w_back[layer, i * 3 + j]
 
 
+def kernel_mix(amounts, clean, noise, mixed):
+    parts = mixed.shape[0]
+    for k in range(3):
+        noisy = amounts[0] * clean[k, 0] + amounts[1] * noise[k, 0]
+        for part in range(parts):
+            mixed[part, 4 * k : 4 * k + 4] = noisy
+            mixed[part, 12 + 4 * k : 16 + 4 * k] = noise[k, 0]
+
+
 def kernel_prepare(w_z, w_xy, w_point, w_in, w_out, w_back, point_back, lift_in, lift_out):
     for layer in range(2):
         forward = forward_blocks(w_z, w_xy, layer)
@@ -289,15 +300,17 @@
     put_rows(stats, total, masked_total(mask, spread))
 
 
-def kernel_first(cells_z, per_member, sc, fields, lift_in, w_in, gains, shift_bias, w_z, w_xy, wp,
+def kernel_first(cells_z, per_member, sc, near, far, lift_in, w_in, gains, shift_bias, w_z, w_xy, wp,
                  stream, normed, act, slope, gathered, stats, consts,
                  padded, shifted, taps, taps_z, pair, acc, old, source):
     planes, rows, lanes = stream.shape
     channels = lanes // 4
-    depth = fields.shape[2]
+    depth = near.shape[2]
     place = Place(sc, rows)
     cell_count = float(planes * 4 * cells_z)
-    comps = [fields[:, 4 * k : 4 * k + 4, :] for k in range(3)]
+    comps = [
+        jnp.concatenate([ref[:, 4 * k : 4 * k + 4, :] for ref in (near, far)], axis=0) for k in range(3)
+    ]
 
     def all_sum(value):
         value = jnp.sum(jnp.sum(value, axis=0), axis=0, keepdims=True)
@@ -318,10 +331,12 @@
     flat = [jnp.broadcast_to(value, (1, channels)) for value in means + list(covs.values())]
     put_rows(consts, mean_c, inv_c, *flat)
     blank = jnp.zeros((8, depth), f32)
+    core = lax.rem(place.member, 2)
     for slab in range(cells_z // depth):
-        at = slice(slab * depth, (slab + 1) * depth)
+        ref, side = (near, core) if slab % 2 == 0 else (far, 1 - core)
+        at = pl.ds(pl.multiple_of((slab // 2 * 2 + side) * depth, depth), depth)
         for x in range(planes):
-            high, low = halves(jnp.concatenate([fields[slab * planes + x], blank], axis=0))
+            high, low = halves(jnp.concatenate([ref[slab // 2 * planes + x], blank], axis=0))
             source[x, 0:32, at] = high
             source[x, 32:64, at] = low
             source[x, 64:96, at] = high
@@ -343,7 +358,7 @@
 
 
 def kernel_second(per_member, sc, *refs):
-    parts, refs = refs[:3], refs[3:]
+    parts, refs = refs[:4], refs[4:]
     (old, gains, shift_bias, w_z, w_xy, wp, stream, normed, act, slope, stats, consts,
      padded, shifted, taps, taps_z, pair, acc) = refs
     planes, rows, _ = stream.shape
@@ -360,7 +375,7 @@
 
 
 def kernel_out(per_member, sc, *refs):
-    parts, refs = refs[:3], refs[3:]
+    parts, refs = refs[:4], refs[4:]
     stream, gains, gathered, lift_out, prediction, misfit, sums, w_out_raw, consts, unit = refs
     planes, rows, lanes = stream.shape
     place = Place(sc, rows)
@@ -433,7 +448,7 @@
     lax.fori_loop(0, planes // count, body, 0)
 
 
-def weight_grads(place, planes, padded, shifted, scot, normed, act, grads, picked, share):
+def weight_grads(place, planes, padded, shifted, scot, normed, act, keep, give, share):
     rows, lanes = padded.shape[1:]
     channels = lanes // 4
     wide_share = 4 * share
@@ -456,16 +471,31 @@
             if 0 <= y + j < 4
         )
 
+    odd = lax.rem(place.member, 2) == 1
+
+    def hand(tap, value):
+        late = tap >= 6
+        at = tap - 6 if late else tap
+        stays = odd if late else jnp.logical_not(odd)
+
+        @pl.when(stays)
+        def _():
+            keep[at] = value
+
+        @pl.when(jnp.logical_not(stays))
+        def _():
+            give[at] = value
+
     left = turned(normed)
     for i in range(3):
         raw = mm_tn(left, padded[2 - i : 2 - i + planes].reshape(planes * rows, lanes))
         for j in range(3):
-            grads[i * 3 + j] = add_blocks(raw, j - 1)
+            hand(i * 3 + j, add_blocks(raw, j - 1))
     for m in range(2):
         raw = mm_tn(left, shifted[1 - m].reshape(planes * rows, lanes))
-        grads[9 + m] = add_blocks(raw, 0)
+        hand(9 + m, add_blocks(raw, 0))
     raw = mm_tn(turned(act), scot[...].reshape(planes * rows, lanes))
-    grads[11] = add_blocks(raw, 0)
+    hand(11, add_blocks(raw, 0))
 
 
 def conv_backward(planes, padded, shifted, taps, taps_z, emit):
@@ -482,9 +512,9 @@
 
 
 def kernel_back_second(share, cell_count, sc, *refs):
-    parts, refs = refs[:3], refs[3:]
+    parts, refs = refs[:4], refs[4:]
     (stream, out_consts, gains, misfit, lift_out, act, slope, normed, w_back, point_back,
-     d_stream, d_normed, sums, grads,
+     d_stream, d_normed, sums, keep, give,
      padded, shifted, taps, taps_z, pair, acc, acc2, scot) = refs
     planes, rows, lanes = stream.shape
     half = lanes // 2
@@ -524,13 +554,13 @@
     s_plain = masked_total(mask, acc[...])
     s_cross = masked_total(mask, acc2[...]) / gains[1:2, :]
     put_rows(sums, s_plain, s_cross, s_bias)
-    weight_grads(place, planes, padded, shifted, scot, normed, act, grads, None, share)
+    weight_grads(place, planes, padded, shifted, scot, normed, act, keep, give, share)
 
 
 def kernel_back_first(share, cell_count, sc, *refs):
-    parts, refs = refs[:3], refs[3:]
+    parts, refs = refs[:4], refs[4:]
     (consts, d_next, d_normed, normed_next, gains, act, slope, normed, point_back,
-     d_stream, pre_cot, sums, grads,
+     d_stream, pre_cot, sums, keep, give,
      padded, shifted, pair, acc, scot) = refs
     planes, rows, lanes = d_next.shape
     place = Place(sc, rows)
@@ -554,11 +584,11 @@
     fill_shifted(place, 0, padded, shifted, planes)
     for x in range(planes):
         pre_cot[x] = padded[x + 1]
-    weight_grads(place, planes, padded, shifted, scot, normed, act, grads, None, share)
-
-
-def kernel_last(cells_z, sc, pre_cot, d_stream, normed, gains, consts, gathered, lift_in, w_back,
-                prediction, ready, slab, sums, in_raw,
+    weight_grads(place, planes, padded, shifted, scot, normed, act, keep, give, share)
+
+
+def kernel_last(depth, sc, pre_cot, d_stream, normed, gains, consts, gathered, lift_in, w_back,
+                prediction, sums_bias, out_raw, own_out, out_1, out_2, out_3,
                 padded, shifted, taps, taps_z, acc, acc2, high, low):
     planes, rows, lanes = d_stream.shape
     half = lanes // 2
@@ -587,22 +617,31 @@
     mask = place.own((rows, lanes))
     s_plain = masked_total(mask, acc[...])
     s_cross = masked_total(mask, acc2[...]) / gains[0:1, :]
-    put_rows(sums, s_plain, s_cross)
     own = place.own((rows, 128))
     kept = jnp.concatenate([jnp.where(own, gathered[x].astype(f32), 0.0) for x in range(planes)], axis=0)
     kept = kept.astype(bf16)
     raw = mm_tn(kept, high[...].reshape(planes * rows, lanes))
     raw_low = mm_tn(kept, low[...].reshape(planes * rows, lanes))
-    put_rows(in_raw, *by_component(raw[0:32] + raw[32:64] + raw_low[0:32], 0))
+    in_raw = by_component(raw[0:32] + raw[32:64] + raw_low[0:32], 0)
+    blank = jnp.zeros((1, s_plain.shape[1]), f32)
+    tail = jnp.concatenate([s_plain, s_cross] + [blank] * 6 + in_raw + [blank] * 5, axis=0)
+    tail = jnp.concatenate([tail, sums_bias[...], out_raw[...]], axis=0)
     here = lax.axis_index("gx")
     lane = lax.broadcasted_iota(jnp.int32, (rows, 128), 1)
     field = mm_nt(high[here], lift_in[...]) + jnp.where(lane < 32, mm_nt(low[here], lift_in[...]), 0.0)
     field = jnp.where((lane >= 32) & (lane < 64), 0.0, field)
     field = field + jnp.where((lane >= 12) & (lane < 24), prediction[...], 0.0)
-    pick = (place.pick(cells_z) & place.own((rows, cells_z))).astype(f32).astype(bf16)
+    cells_z = depth * place.members
+    whole = place.z_of((rows, depth), cells_z)
+    column = lax.broadcasted_iota(jnp.int32, (rows, depth), 1)
+    mask = place.own((rows, depth))
     first, second = halves(field)
-    out = mm_tn(first, pick) + mm_tn(second, pick)
-    slab[...] = out[0:32] + out[64:96]
+    for bit, target in enumerate((own_out, out_1, out_2, out_3)):
+        there = lax.bitwise_xor(place.member, bit)
+        pick = ((whole == column + there * depth) & mask).astype(f32).astype(bf16)
+        out = mm_tn(first, pick) + mm_tn(second, pick)
+        target[0:32] = out[0:32] + out[64:96]
+        target[32:64] = tail
 
 
 def call(kernel, outs, scratch, flops, limit, *args, scalars=True, loose=()):
@@ -627,35 +666,29 @@
 
 
 def group_parts(value):
-    beside = swapped(value, "gz", 1)
-    pair = jnp.concatenate([value, beside], axis=0)
-    return (value, beside, swapped(pair, "gz", 2))
-
-
-def group_sum(value):
-    value = value + swapped(value, "gz", 1)
-    return value + swapped(value, "gz", 2)
-
-
-def group_grads(grads):
-    members = lax.axis_size("gz")
-    taps, share, channels = grads.shape
-    pieces = grads.reshape(members, (taps // members) * share, channels)
-    return jnp.sum(lax.all_to_all(pieces, "gz", 0, 0), axis=0).astype(bf16)
-
-
-def all_grads(mine, share):
-    members = lax.axis_size("gz")
-    total = members * lax.axis_size("gx")
-    every = lax.all_to_all(
-        jnp.broadcast_to(mine[None], (total,) + mine.shape), ("gz", "gx"), 0, 0
-    )
-    return every.reshape(members, total // members, mine.shape[0] // share, share, mine.shape[1])
-
-
-def laid_out(every):
-    members, groups, taps, share, channels = every.shape
-    return every.transpose(0, 2, 1, 3, 4).reshape(members * taps, groups * share, channels)
+    return (value,) + tuple(swapped(value, "gz", bit) for bit in (1, 2, 3))
+
+
+def group_grads(keep, give):
+    mine = keep + swapped(give, "gz", 1)
+    return mine + swapped(mine, "gz", 2)
+
+
+def all_grads(first, second):
+    groups = lax.axis_size("gx")
+    taps, share, channels = first.shape
+    mine = jnp.concatenate([first, second], axis=0).astype(bf16)
+    mine = mine.reshape(2 * taps * share, channels)
+    near = lax.all_to_all(jnp.broadcast_to(mine[None], (groups,) + mine.shape), "gx", 0, 0)
+    far = swapped(near, "gz", 1)
+    odd = lax.rem(lax.axis_index("gz"), 2) == 1
+
+    def laid_out(every):
+        every = every.reshape(groups, 2, taps, share, channels).transpose(1, 2, 0, 3, 4)
+        return every.reshape(2, taps, groups * share, channels)
+
+    near, far = laid_out(near), laid_out(far)
+    return jnp.concatenate([jnp.where(odd, far, near), jnp.where(odd, near, far)], axis=1)
 
 
 def per_device_grouped(clean_field, noise_field, timestep, dilations, w_in, w_time, w_z, w_xy, w_point,
@@ -672,12 +705,14 @@
     inv_area = 4.0 / cell_count
 
     alpha_bar, features, time_raw, time_code = time_terms(timestep, w_time)
-    noisy = jnp.sqrt(alpha_bar) * clean_field + jnp.sqrt(1.0 - alpha_bar) * noise_field
-    block = jnp.concatenate([noisy, noise_field], axis=0).reshape(24, depth)
-    total = members * groups
-    fields = lax.all_to_all(
-        jnp.broadcast_to(block[None], (total, 24, depth)), ("gz", "gx"), 0, 0
-    )
+    parts = members // 2 * groups
+    mixed = call(
+        kernel_mix, [((parts, 24, depth), f32)], [], 10**5, LIMITS[7],
+        jnp.stack([jnp.sqrt(alpha_bar), jnp.sqrt(1.0 - alpha_bar)]), clean_field, noise_field,
+    )[0]
+    same_core = [[m * groups + g for m in range(core, members, 2) for g in range(groups)] for core in range(2)]
+    near = lax.all_to_all(mixed, ("gz", "gx"), 0, 0, axis_index_groups=same_core)
+    far = swapped(near, "gz", 1)
     shift_bias = biases + time_code
 
     big = (planes, rows, lanes)
@@ -692,7 +727,7 @@
     ]
     pair = ((1, lanes // 2, lanes // 2), bf16)
     flat = ((rows, lanes), f32)
-    grad_out = ((12, share, channels), f32)
+    grad_out = ((6, share, channels), f32)
 
     w_back, point_back, lift_in, lift_out = call(
         kernel_prepare,
@@ -704,7 +739,7 @@
         [(big, f32), (big, bf16), (big, bf16), (big, bf16), thin, vec, ((16, channels), f32)],
         conv_scratch + [pair, flat, (big, f32), ((planes, 128, cells_z), bf16)],
         4 * 10**9, LIMITS[1],
-        dilations, fields, lift_in, w_in, norm_gains, shift_bias, w_z, w_xy, w_point,
+        dilations, near, far, lift_in, w_in, norm_gains, shift_bias, w_z, w_xy, w_point,
     )
     stream2, normed1, act1, slope1, stats2, consts1 = call(
         functools.partial(kernel_second, per_member),
@@ -721,38 +756,37 @@
         dilations, *group_parts(stats2), stream2, norm_gains, gathered, lift_out,
     )
     parts2 = group_parts(sums2)
-    d_stream2, d_normed1, sums1, grads1 = call(
+    d_stream2, d_normed1, sums1, keep1, give1 = call(
         functools.partial(kernel_back_second, share, cell_count),
-        [(big, f32), (big, f32), vec, grad_out],
+        [(big, f32), (big, f32), vec, grad_out, grad_out],
         conv_scratch + [pair, flat, flat, (big, bf16)],
         6 * 10**9, LIMITS[4],
         dilations, *parts2, stream2, consts2, norm_gains, misfit, lift_out, act1, slope1, normed1,
         w_back, point_back,
     )
     parts1 = group_parts(sums1)
-    d_stream1, pre_cot0, sums_b0, grads0 = call(
+    d_stream1, pre_cot0, sums_b0, keep0, give0 = call(
         functools.partial(kernel_back_first, share, cell_count),
-        [(big, f32), (big, bf16), vec, grad_out],
+        [(big, f32), (big, bf16), vec, grad_out, grad_out],
         conv_scratch[:2] + [pair, flat, (big, bf16)],
         4 * 10**9, LIMITS[5],
         dilations, *parts1, consts1, d_stream2, d_normed1, normed1, norm_gains, act0, slope0, normed0,
         point_back,
     )
-    mine1 = group_grads(grads1)
-    slab, sums0, in_part = call(
-        functools.partial(kernel_last, cells_z),
-        [((32, cells_z), f32), vec, vec],
+    mine1 = group_grads(keep1, give1)
+    last = call(
+        functools.partial(kernel_last, depth),
+        [((64, channels), f32)] * members,
         conv_scratch + [flat, flat, (big, bf16), (big, bf16)],
         4 * 10**9, LIMITS[6],
         dilations, pre_cot0, d_stream1, normed0, norm_gains, consts0, gathered, lift_in, w_back, prediction,
-        mine1, loose=(10,),
-    )
-    all1 = laid_out(all_grads(mine1, share))
-    all0 = laid_out(all_grads(group_grads(grads0), share))
-
-    tails = group_sum(jnp.concatenate([sums0, in_part, sums_b0, out_raw], axis=0))
-    s_plain, s_cross, in_sum = tails[0], tails[1], tails[8:11]
-    bias0, out_sum = tails[16], tails[24:27]
+        sums_b0, out_raw,
+    )
+    every = all_grads(group_grads(keep0, give0), mine1)
+
+    tails = last[0] + sum(swapped(last[bit], "gz", bit) for bit in (1, 2, 3))
+    s_plain, s_cross, in_sum = tails[32], tails[33], tails[40:43]
+    bias0, out_sum = tails[48], tails[56:59]
     s1 = sum(members_of(parts1))
     s2 = sum(members_of(parts2))
     inverse = consts0[1]
@@ -763,10 +797,8 @@
     cov = jnp.stack([jnp.stack([c00, c01, c02]), jnp.stack([c01, c11, c12]), jnp.stack([c02, c12, c22])])
     offset = jnp.sum(w_in * (inverse * m_plain), axis=1)
     mix = jnp.sum(w_in[:, None, :] * (inverse * inverse * m_cross) * w_in[None, :, :], axis=2)
-    pieces = slab.reshape(32, members, depth)[:24].transpose(1, 0, 2)
-    landed = jnp.sum(lax.all_to_all(pieces, "gz", 0, 0), axis=0)
-    landed = landed.reshape(6, 1, 4, depth)
-    centered = noisy - mean_k[:, None, None, None]
+    landed = tails[:24].reshape(6, 1, 4, depth)
+    centered = mixed[0, :12].reshape(3, 1, 4, depth) - mean_k[:, None, None, None]
     field_grad = landed[:3] - offset[:, None, None, None] - sum(
         mix[:, j, None, None, None] * centered[j][None] for j in range(3)
     )
@@ -777,7 +809,7 @@
     )
     bias_all = jnp.stack([bias0, s1[2]])
     gain_all = jnp.stack([s_cross, s1[1], s2[1]])
-    weights = jnp.stack([all0, all1]).astype(f32) * inv_area
+    weights = every.astype(f32) * inv_area
     z_all = jnp.stack([weights[:, 9], weights[:, 4], weights[:, 10]], axis=1)
     xy_all = jnp.concatenate([weights[:, :4], weights[:, 5:9]], axis=1)
     time_back = jax.vjp(jax.nn.silu, time_raw)[1](jnp.sum(bias_all, axis=0))[0]

time: 161 us -> 122 us (0.76)
  waiting for transfers between devices: 46.6 us -> 23.7 us
  local copies, waits for them, and re-layouts: 28.6 us -> 14.2 us
  starting transfers between devices: 28.6 us -> 24.2 us
  Pallas kernels: 41.1 us -> 44.7 us
    all_to_all x6 -> x2, waiting for transfers between devices: 36.5 us -> 12.9 us  [the longest x1 9.92 us: all_grads(): lax.all_to_all(jnp.broadcast_to(mine[None], (groups,) + mine.shape), 'gx'...]
    unnamed x61 -> x40, local copies, waits for them, and re-layouts: 23.2 us -> 10.4 us
    all_to_all x6 -> x2, starting transfers between devices: 22.4 us -> 11.8 us  [the longest x1 8.31 us: per_device_grouped(): lax.all_to_all(mixed, ('gz', 'gx'), 0, 0, axis_index_groups=same_core)]
    ppermute x10 -> x21, starting transfers between devices: 6.19 us -> 12.4 us  [swapped(): return lax.ppermute(value, axis, [(i, i ^ bit) for i in range(count)])]
    pallas_call x7 -> x8, Pallas kernels: 41.1 us -> 44.7 us  [call(): pl.pallas_call(kernel, out_shape=[jax.ShapeDtypeStruct(shape, dtype) for...]
    ppermute x10 -> x21, waiting for transfers between devices: 10 us -> 10.8 us  [swapped(): return lax.ppermute(value, axis, [(i, i ^ bit) for i in range(count)])]
  transfers between devices with their start and end apart: 16 -> 23, of which waited for: 11 -> 12; matrix products, arithmetic and copies ran while one was open for 8% -> 10% of each run, Pallas kernels for 7% -> 10%
where the time goes in v3:
time: 122 us; the launch traced here: 121 us
  Pallas kernels  44.7 us (37%)
  starting transfers between devices  24.2 us (20%)
  waiting for transfers between devices  23.7 us (19%)
  local copies, waits for them, and re-layouts  14.2 us (12%)
  other arithmetic  12.5 us (10%)
  between operations  1.78 us (1%)
    pallas_call x8, Pallas kernels, call(): pl.pallas_call(kernel, out_shape=[jax.ShapeDtypeStruct(shape, dtype) for...  44.7 us
    ppermute x21, starting transfers between devices, swapped(): return lax.ppermute(value, axis, [(i, i ^ bit) for i in range(count)])  12.4 us
    ppermute x21, waiting for transfers between devices, swapped(): return lax.ppermute(value, axis, [(i, i ^ bit) for i in range(count)])  10.8 us
    unnamed x40, local copies, waits for them, and re-layouts  10.4 us
    all_to_all x1, waiting for transfers between devices, all_grads(): lax.all_to_all(jnp.broadcast_to(mine[None], (groups,) + mine.shape), 'gx'...  9.92 us
    all_to_all x1, starting transfers between devices, per_device_grouped(): lax.all_to_all(mixed, ('gz', 'gx'), 0, 0, axis_index_groups=same_core)  8.31 us
    another operation x4, other arithmetic, per_device_grouped(): jnp.stack([jnp.stack([c00, c01, c02]), jnp.stack([c01, c11, c12]), jnp.st...  6.05 us
    all_to_all x1, starting transfers between devices, all_grads(): lax.all_to_all(jnp.broadcast_to(mine[None], (groups,) + mine.shape), 'gx'...  3.45 us
  transfers between devices with their start and end apart: 23, of which 12 were waited for; matrix products, arithmetic and copies ran while one was open for 10% of the time, Pallas kernels for 10%

profile of v3, /device:TPU:0, one launch (start us, length us, event | category | flops | bytes accessed | tf_op | source)
XLA Modules:
  0.0 121.3 jit_solution(11802947314140485676)
XLA Ops:
  1.6 0.7 copy-done.13
  2.3 0.7 copy-done.14
  3.0 1.2 %shard_map.195 = f32[16,24,128]{2,1,0:T(8,128)} custom-call(f32[2]{0:T(128)S(1)} %pad_maximum_fusion.4.amounts, f32[3,1,4,128]{3,2,1,0:T(4,128)S(1)} %copy-done.13, f32[3,1,4,128]{3,2,1,0:T(4,128)S(1)} %copy-done.14), custom_call_target="tpu_custom_call" | custom-call | flops 100000 | bytes 8388608 | tf_op jit(solution)/shard_map/pallas_call | solution.py:652
  4.2 8.3 %all-to-all-start = ((f32[16,24,128]{2,1,0:T(8,128)}), f32[16,24,128]{2,1,0:T(8,128)S(1)}, u32[]{:S(2)}, u32[]{:S(2)}) async-start(f32[16,24,128]{2,1,0:T(8,128)} %shard_map.195), calls=%async_computation | async-start | bytes 393216 | tf_op jit(solution)/shard_map/all_to_all | solution.py:714
  12.6 0.7 slice.144
  13.3 1.0 copy-done.1
  14.3 0.9 copy-done.4
  15.3 0.8 copy-done.7
  18.0 2.9 %all-to-all-done.near = f32[16,24,128]{2,1,0:T(8,128)S(1)} async-done(((f32[16,24,128]{2,1,0:T(8,128)}), f32[16,24,128]{2,1,0:T(8,128)S(1)}, u32[]{:S(2)}, u32[]{:S(2)}) %all-to-all-start) | async-done | bytes 196640 | tf_op jit(solution)/shard_map/all_to_all | solution.py:714
  20.9 0.7 broadcast_add_fusion.shift_bias.refs_6_
  21.6 0.8 collective-permute-done.far
  22.3 1.0 copy-done.2
  23.4 0.9 copy-done.5
  24.3 0.8 copy-done.8
  27.2 9.8 %shard_map.197 = (f32[8,144,512]{2,1,0:T(8,128)S(1)}, bf16[8,144,512]{2,1,0:T(8,128)(2,1)S(1)}, bf16[8,144,512]{2,1,0:T(8,128)(2,1)S(1)}, bf16[8,144,512]{2,1,0:...) custom-call(s32[2]{0:T(128)S(1)} %copy-done.18, ...), custom_call_target="tpu_custom_call" | custom-call | flops 4000000000 | bytes 8388608 | tf_op jit(solution)/shard_map/pallas_call | solution.py:652
  37.7 1.0 collective-permute-start.3
  38.6 0.8 collective-permute-start.2
  39.6 2.0 %maximum_bitcast_fusion = f32[1,3]{1,0:T(1,128)S(1)} fusion(f32[1]{0:T(128)} %bitcast.14, f32[1]{0:T(128)} %bitcast.13, f32[1]{0:T(128)} %bitcast.12), kind=kLoop, calls=%fused_computation.39 | loop fusion | flops 6 | bytes 24 | tf_op jit(solution)/shard_map/stack | solution.py:797
  41.6 2.0 %maximum_bitcast_fusion.1 = f32[1,3]{1,0:T(1,128)S(1)} fusion(f32[1]{0:T(128)} %bitcast.17, f32[1]{0:T(128)} %bitcast.16, f32[1]{0:T(128)} %bitcast.13), kind=kLoop, calls=%fused_computation.40 | loop fusion | flops 6 | bytes 24 | tf_op jit(solution)/shard_map/stack | solution.py:797
  43.7 9.1 %shard_map.198 = (f32[8,144,512]{2,1,0:T(8,128)S(1)}, bf16[8,144,512]{2,1,0:T(8,128)(2,1)S(1)}, bf16[8,144,512]{2,1,0:T(8,128)(2,1)S(1)}, bf16[8,144,512]{2,1,0:...) custom-call(s32[2]{0:T(128)S(1)} %copy-done.19, f32[8,128]{1,0:T(8,128)S(1)} %get-tuple-element.47.refs_0_, ...), custom_call_target="tpu_custom_call" | custom-call | flops 4000000000 | bytes 8388608 | tf_op jit(solution)/shard_map/pallas_call | solution.py:652
  52.8 1.3 %collective-permute-start.6 = (f32[8,128]{1,0:T(8,128)S(1)}, f32[8,128]{1,0:T(8,128)S(1)}, u32[]{:S(2)}, u32[]{:S(2)}) collective-permute-start(f32[8,128]{1,0:T(8,128)S(1)} %get-tuple-element.49.refs_0_), channel_id=1, source_target_pairs={{0,24},{8,16},{16,8},{24,0},{1,25},{9,17},{17,9},{25,1},{2,26},{10... | collective-permute-start | bytes 12296 | tf_op jit(solution)/shard_map/ppermute | solution.py:665
  54.2 0.8 collective-permute-start.5
  55.0 2.0 %maximum_bitcast_fusion.2 = f32[1,3]{1,0:T(1,128)S(1)} fusion(f32[1]{0:T(128)} %bitcast.19, f32[1]{0:T(128)} %bitcast.17, f32[1]{0:T(128)} %bitcast.14), kind=kLoop, calls=%fused_computation.41 | loop fusion | flops 6 | bytes 24 | tf_op jit(solution)/shard_map/stack | solution.py:797
  57.0 0.8 collective-permute-done.5.refs_2_
  57.8 2.3 %shard_map.199 = (f32[144,128]{1,0:T(8,128)S(1)}, bf16[8,144,128]{2,1,0:T(8,128)(2,1)S(1)}, f32[8,128]{1,0:T(8,128)S(1)}, f32[8,128]{1,0:T(8,128)S(1)}, f32[8,128]{1,0:T(8,128)S(1)}) custom-call(s32[2]{0:T(128)S(1)} %copy-done.19, f32[8,128]{1,0:T(8,128)S(1)} %get-tuple-element.49.refs_0_, f32[8,128]{1,0:T(8,128)S(1)} %collective-permute-done.4.refs_1_, ...), custom_call_target="tpu_custom_call" | custom-call | flops 1000000000 | bytes 8388608 | tf_op jit(solution)/shard_map/pallas_call | solution.py:652
  60.7 0.8 collective-permute-start.8
  62.0 1.2 collective-permute-done.9.refs_3_
  63.2 1.1 collective-permute-done.8.refs_2_
  64.3 9.7 %shard_map.200 = (f32[8,144,512]{2,1,0:T(8,128)S(1)}, f32[8,144,512]{2,1,0:T(8,128)S(1)}, f32[8,128]{1,0:T(8,128)S(1)}, f32[6,16,128]{2,1,0:T(8,128)S(1)}, f32[6,16,128]{2,1,0:T(8,128)S(1)}) custom-call(s32[2]{0:T(128)S(1)} %copy-done.19, f32[8,128]{1,0:T(8,128)S(1)} %get-tuple-element.53.refs_0_, f32[8,128]{1,0:T(8,128)S(1)} %collective-permute-done.7.refs_1_, ...), custom_call_target="tpu_custom_call" | custom-call | flops 6000000000 | bytes 8388608 | tf_op jit(solution)/shard_map/pallas_call | solution.py:652
  74.1 0.8 collective-permute-start.11
  75.0 1.0 collective-permute-start.10
  76.1 1.1 collective-permute-done.12.refs_3_
  77.8 6.2 %shard_map.201 = (f32[8,144,512]{2,1,0:T(8,128)S(1)}, bf16[8,144,512]{2,1,0:T(8,128)(2,1)S(1)}, f32[8,128]{1,0:T(8,128)S(1)}, f32[6,16,128]{2,1,0:T(8,128)S(1)}, f32[6,16,128]{2,1,0:T(8,128)S(1)}) custom-call(s32[2]{0:T(128)S(1)} %copy-done.19, f32[8,128]{1,0:T(8,128)S(1)} %get-tuple-element.61.refs_0_, f32[8,128]{1,0:T(8,128)S(1)} %collective-permute-done.10.refs_1_, ...), custom_call_target="tpu_custom_call" | custom-call | flops 4000000000 | bytes 8388608 | tf_op jit(solution)/shard_map/pallas_call | solution.py:652
  84.0 6.1 %shard_map.202 = (f32[64,128]{1,0:T(8,128)S(1)}, f32[64,128]{1,0:T(8,128)S(1)}, f32[64,128]{1,0:T(8,128)S(1)}, f32[64,128]{1,0:T(8,128)S(1)}) custom-call(s32[2]{0:T(128)S(1)} %copy-done.19, bf16[8,144,512]{2,1,0:T(8,128)(2,1)S(1)} %get-tuple-element.68.pre_cot, f32[8,144,512]{2,1,0:T(8,128)S(1)} %get-tuple-element.69.d_stream, ...), custom_call_target="tpu_custom_call" | custom-call | flops 4000000000 | bytes 8388608 | tf_op jit(solution)/shard_map/pallas_call | solution.py:652
  90.2 0.9 collective-permute-start.14
  91.1 1.0 collective-permute-start.15
  92.4 1.8 %collective-permute-done.14 = f32[64,128]{1,0:T(8,128)S(1)} collective-permute-done((f32[64,128]{1,0:T(8,128)S(1)}, f32[64,128]{1,0:T(8,128)S(1)}, u32[]{:S(2)}, u32[]{:S(2)}) %collective-permute-start.14) | collective-permute-done | bytes 32800 | tf_op jit(solution)/shard_map/ppermute | solution.py:665
  94.8 1.1 collective-permute-start.19
  96.0 1.1 collective-permute-start.17
  97.1 2.3 %collective-permute-done.19 = f32[6,16,128]{2,1,0:T(8,128)S(1)} collective-permute-done((f32[6,16,128]{2,1,0:T(8,128)S(1)}, f32[6,16,128]{2,1,0:T(8,128)S(1)}, u32[]{:S(2)}, u32[]{:S(2)}) %collective-permute-start.19) | collective-permute-done | bytes 49184 | tf_op jit(solution)/shard_map/ppermute | solution.py:665
  99.4 0.7 collective-permute-done.17
  100.2 0.8 broadcast_in_dim.2
  100.9 3.5 %all-to-all-start.1 = ((bf16[8,192,128]{2,1,0:T(8,128)(2,1)}), bf16[8,192,128]{2,1,0:T(8,128)(2,1)S(1)}, u32[]{:S(2)}, u32[]{:S(2)}) async-start(bf16[8,192,128]{2,1,0:T(8,128)(2,1)} %broadcast_in_dim.2), calls=%async_computation.1 | async-start | bytes 786432 | tf_op jit(solution)/shard_map/all_to_all | solution.py:682
  105.9 9.9 %all-to-all-done.1 = bf16[8,192,128]{2,1,0:T(8,128)(2,1)S(1)} async-done(((bf16[8,192,128]{2,1,0:T(8,128)(2,1)}), bf16[8,192,128]{2,1,0:T(8,128)(2,1)S(1)}, u32[]{:S(2)}, u32[]{:S(2)}) %all-to-all-start.1) | async-done | bytes 393248 | tf_op jit(solution)/shard_map/all_to_all | solution.py:682
  117.6 0.7 multiply_multiply_fusion
  118.7 0.7 slice_bitcast_fusion
  119.5 1.0 pad_maximum_fusion
  120.5 0.8 pad_maximum_fusion.1
  (93 shorter events, 11.7 us)
Async XLA Ops:
  0.6 17.2 %copy-start = (f32[128,128]{1,0:T(8,128)S(1)}, f32[128,128]{1,0:T(8,128)}, u32[]{:S(2)}) copy-start(f32[128,128]{1,0:T(8,128)} %param.17) | copy-start | bytes 196612
  1.6 0.7 copy-start.13
  2.3 0.7 copy-start.14
  4.2 16.7 %all-to-all-start = ((f32[16,24,128]{2,1,0:T(8,128)}), f32[16,24,128]{2,1,0:T(8,128)S(1)}, u32[]{:S(2)}, u32[]{:S(2)}) async-start(f32[16,24,128]{2,1,0:T(8,128)} %shard_map.195), calls=%async_computation | async-start | bytes 393216 | tf_op jit(solution)/shard_map/all_to_all | solution.py:714
  13.3 1.0 copy-start.1
  14.3 0.9 copy-start.4
  15.3 0.8 copy-start.7
  16.1 0.7 copy-start.10
  16.8 0.7 copy-start.15
  20.9 1.4 %collective-permute-start = (f32[16,24,128]{2,1,0:T(8,128)S(1)}, f32[16,24,128]{2,1,0:T(8,128)S(1)}, u32[]{:S(2)}, u32[]{:S(2)}) collective-permute-start(f32[16,24,128]{2,1,0:T(8,128)S(1)} %all-to-all-done.near), channel_id=1, source_target_pairs={{0,8},{8,0},{16,24},{24,16},{1,9},{9,1},{17,25},{25,17},{2,10},{10... | collective-permute-start | bytes 589832 | tf_op jit(solution)/shard_map/ppermute | solution.py:665
  22.3 1.0 copy-start.2
  23.4 0.9 copy-start.5
  24.3 0.8 copy-start.8
  25.2 0.7 copy-start.11
  25.8 0.7 copy-start.16
  26.5 0.7 copy-start.18
  27.2 16.5 %copy-start.3 = (bf16[2,8,128,128]{3,2,1,0:T(8,128)(2,1)S(1)}, bf16[2,8,128,128]{3,2,1,0:T(8,128)(2,1)}, u32[]{:S(2)}) copy-start(bf16[2,8,128,128]{3,2,1,0:T(8,128)(2,1)} %refs_8_.2) | copy-start | bytes 1572868
  27.2 16.5 %copy-start.6 = (bf16[2,3,128,128]{3,2,1,0:T(8,128)(2,1)S(1)}, bf16[2,3,128,128]{3,2,1,0:T(8,128)(2,1)}, u32[]{:S(2)}) copy-start(bf16[2,3,128,128]{3,2,1,0:T(8,128)(2,1)} %refs_7_.1) | copy-start | bytes 589828
  27.2 16.5 %copy-start.9 = (bf16[2,128,128]{2,1,0:T(8,128)(2,1)S(1)}, bf16[2,128,128]{2,1,0:T(8,128)(2,1)}, u32[]{:S(2)}) copy-start(bf16[2,128,128]{2,1,0:T(8,128)(2,1)} %refs_9_.1) | copy-start | bytes 196612
  27.2 16.5 %copy-start.19 = (s32[2]{0:T(128)S(1)}, s32[2]{0:T(128)}, u32[]{:S(2)}) copy-start(s32[2]{0:T(128)} %sc.11) | copy-start | bytes 28
  37.7 6.0 %collective-permute-start.3 = (f32[8,128]{1,0:T(8,128)S(1)}, f32[8,128]{1,0:T(8,128)S(1)}, u32[]{:S(2)}, u32[]{:S(2)}) collective-permute-start(f32[8,128]{1,0:T(8,128)S(1)} %get-tuple-element.47.refs_0_), channel_id=1, source_target_pairs={{0,24},{8,16},{16,8},{24,0},{1,25},{9,17},{17,9},{25,1},{2,26},{10... | collective-permute-start | bytes 12296 | tf_op jit(solution)/shard_map/ppermute | solution.py:665
  38.6 5.0 %collective-permute-start.2 = (f32[8,128]{1,0:T(8,128)S(1)}, f32[8,128]{1,0:T(8,128)S(1)}, u32[]{:S(2)}, u32[]{:S(2)}) collective-permute-start(f32[8,128]{1,0:T(8,128)S(1)} %get-tuple-element.47.refs_0_), channel_id=1, source_target_pairs={{0,16},{8,24},{16,0},{24,8},{1,17},{9,25},{17,1},{25,9},{2,18},{10... | collective-permute-start | bytes 12296 | tf_op jit(solution)/shard_map/ppermute | solution.py:665
  39.5 4.2 %collective-permute-start.1 = (f32[8,128]{1,0:T(8,128)S(1)}, f32[8,128]{1,0:T(8,128)S(1)}, u32[]{:S(2)}, u32[]{:S(2)}) collective-permute-start(f32[8,128]{1,0:T(8,128)S(1)} %get-tuple-element.47.refs_0_), channel_id=1, source_target_pairs={{0,8},{8,0},{16,24},{24,16},{1,9},{9,1},{17,25},{25,17},{2,10},{10... | collective-permute-start | bytes 12296 | tf_op jit(solution)/shard_map/ppermute | solution.py:665
  52.8 4.2 %collective-permute-start.6 = (f32[8,128]{1,0:T(8,128)S(1)}, f32[8,128]{1,0:T(8,128)S(1)}, u32[]{:S(2)}, u32[]{:S(2)}) collective-permute-start(f32[8,128]{1,0:T(8,128)S(1)} %get-tuple-element.49.refs_0_), channel_id=1, source_target_pairs={{0,24},{8,16},{16,8},{24,0},{1,25},{9,17},{17,9},{25,1},{2,26},{10... | collective-permute-start | bytes 12296 | tf_op jit(solution)/shard_map/ppermute | solution.py:665
  54.2 3.6 %collective-permute-start.5 = (f32[8,128]{1,0:T(8,128)S(1)}, f32[8,128]{1,0:T(8,128)S(1)}, u32[]{:S(2)}, u32[]{:S(2)}) collective-permute-start(f32[8,128]{1,0:T(8,128)S(1)} %get-tuple-element.49.refs_0_), channel_id=1, source_target_pairs={{0,16},{8,24},{16,0},{24,8},{1,17},{9,25},{17,1},{25,9},{2,18},{10... | collective-permute-start | bytes 12296 | tf_op jit(solution)/shard_map/ppermute | solution.py:665
  54.9 2.8 %collective-permute-start.4 = (f32[8,128]{1,0:T(8,128)S(1)}, f32[8,128]{1,0:T(8,128)S(1)}, u32[]{:S(2)}, u32[]{:S(2)}) collective-permute-start(f32[8,128]{1,0:T(8,128)S(1)} %get-tuple-element.49.refs_0_), channel_id=1, source_target_pairs={{0,8},{8,0},{16,24},{24,16},{1,9},{9,1},{17,25},{25,17},{2,10},{10... | collective-permute-start | bytes 12296 | tf_op jit(solution)/shard_map/ppermute | solution.py:665
  57.8 6.6 %copy-start.17 = (f32[3,128]{1,0:T(4,128)S(1)}, f32[3,128]{1,0:T(4,128)}, u32[]{:S(2)}) copy-start(f32[3,128]{1,0:T(4,128)} %gains.3) | copy-start | bytes 4612
  60.1 3.1 %collective-permute-start.9 = (f32[8,128]{1,0:T(8,128)S(1)}, f32[8,128]{1,0:T(8,128)S(1)}, u32[]{:S(2)}, u32[]{:S(2)}) collective-permute-start(f32[8,128]{1,0:T(8,128)S(1)} %get-tuple-element.53.refs_0_), channel_id=1, source_target_pairs={{0,24},{8,16},{16,8},{24,0},{1,25},{9,17},{17,9},{25,1},{2,26},{10... | collective-permute-start | bytes 12296 | tf_op jit(solution)/shard_map/ppermute | solution.py:665
  60.7 3.6 %collective-permute-start.8 = (f32[8,128]{1,0:T(8,128)S(1)}, f32[8,128]{1,0:T(8,128)S(1)}, u32[]{:S(2)}, u32[]{:S(2)}) collective-permute-start(f32[8,128]{1,0:T(8,128)S(1)} %get-tuple-element.53.refs_0_), channel_id=1, source_target_pairs={{0,16},{8,24},{16,0},{24,8},{1,17},{9,25},{17,1},{25,9},{2,18},{10... | collective-permute-start | bytes 12296 | tf_op jit(solution)/shard_map/ppermute | solution.py:665
  61.5 2.8 %collective-permute-start.7 = (f32[8,128]{1,0:T(8,128)S(1)}, f32[8,128]{1,0:T(8,128)S(1)}, u32[]{:S(2)}, u32[]{:S(2)}) collective-permute-start(f32[8,128]{1,0:T(8,128)S(1)} %get-tuple-element.53.refs_0_), channel_id=1, source_target_pairs={{0,8},{8,0},{16,24},{24,16},{1,9},{9,1},{17,25},{25,17},{2,10},{10... | collective-permute-start | bytes 12296 | tf_op jit(solution)/shard_map/ppermute | solution.py:665
  74.0 3.1 %collective-permute-start.12 = (f32[8,128]{1,0:T(8,128)S(1)}, f32[8,128]{1,0:T(8,128)S(1)}, u32[]{:S(2)}, u32[]{:S(2)}) collective-permute-start(f32[8,128]{1,0:T(8,128)S(1)} %get-tuple-element.61.refs_0_), channel_id=1, source_target_pairs={{0,24},{8,16},{16,8},{24,0},{1,25},{9,17},{17,9},{25,1},{2,26},{10... | collective-permute-start | bytes 12296 | tf_op jit(solution)/shard_map/ppermute | solution.py:665
  74.1 3.7 %collective-permute-start.11 = (f32[8,128]{1,0:T(8,128)S(1)}, f32[8,128]{1,0:T(8,128)S(1)}, u32[]{:S(2)}, u32[]{:S(2)}) collective-permute-start(f32[8,128]{1,0:T(8,128)S(1)} %get-tuple-element.61.refs_0_), channel_id=1, source_target_pairs={{0,16},{8,24},{16,0},{24,8},{1,17},{9,25},{17,1},{25,9},{2,18},{10... | collective-permute-start | bytes 12296 | tf_op jit(solution)/shard_map/ppermute | solution.py:665
  75.0 2.8 %collective-permute-start.10 = (f32[8,128]{1,0:T(8,128)S(1)}, f32[8,128]{1,0:T(8,128)S(1)}, u32[]{:S(2)}, u32[]{:S(2)}) collective-permute-start(f32[8,128]{1,0:T(8,128)S(1)} %get-tuple-element.61.refs_0_), channel_id=1, source_target_pairs={{0,8},{8,0},{16,24},{24,16},{1,9},{9,1},{17,25},{25,17},{2,10},{10... | collective-permute-start | bytes 12296 | tf_op jit(solution)/shard_map/ppermute | solution.py:665
  76.0 18.8 %collective-permute-start.18 = (f32[6,16,128]{2,1,0:T(8,128)S(1)}, f32[6,16,128]{2,1,0:T(8,128)S(1)}, u32[]{:S(2)}, u32[]{:S(2)}) collective-permute-start(f32[6,16,128]{2,1,0:T(8,128)S(1)} %get-tuple-element.81), channel_id=1, source_target_pairs={{0,8},{8,0},{16,24},{24,16},{1,9},{9,1},{17,25},{25,17},{2,10},{10... | collective-permute-start | bytes 147464 | tf_op jit(solution)/shard_map/ppermute | solution.py:665
  84.0 10.7 %copy-start.12 = (f32[3,128]{1,0:T(4,128)S(1)}, f32[3,128]{1,0:T(4,128)}, u32[]{:S(2)}) copy-start(f32[3,128]{1,0:T(4,128)} %w_in.3) | copy-start | bytes 4612
  90.1 2.4 %collective-permute-start.13 = (f32[64,128]{1,0:T(8,128)S(1)}, f32[64,128]{1,0:T(8,128)S(1)}, u32[]{:S(2)}, u32[]{:S(2)}) collective-permute-start(f32[64,128]{1,0:T(8,128)S(1)} %get-tuple-element.75), channel_id=1, source_target_pairs={{0,8},{8,0},{16,24},{24,16},{1,9},{9,1},{17,25},{25,17},{2,10},{10... | collective-permute-start | bytes 98312 | tf_op jit(solution)/shard_map/ppermute | solution.py:665
  90.2 4.1 %collective-permute-start.14 = (f32[64,128]{1,0:T(8,128)S(1)}, f32[64,128]{1,0:T(8,128)S(1)}, u32[]{:S(2)}, u32[]{:S(2)}) collective-permute-start(f32[64,128]{1,0:T(8,128)S(1)} %get-tuple-element.76), channel_id=1, source_target_pairs={{0,16},{8,24},{16,0},{24,8},{1,17},{9,25},{17,1},{25,9},{2,18},{10... | collective-permute-start | bytes 98312 | tf_op jit(solution)/shard_map/ppermute | solution.py:665
  91.1 3.5 %collective-permute-start.15 = (f32[64,128]{1,0:T(8,128)S(1)}, f32[64,128]{1,0:T(8,128)S(1)}, u32[]{:S(2)}, u32[]{:S(2)}) collective-permute-start(f32[64,128]{1,0:T(8,128)S(1)} %get-tuple-element.77), channel_id=1, source_target_pairs={{0,24},{8,16},{16,8},{24,0},{1,25},{9,17},{17,9},{25,1},{2,26},{10... | collective-permute-start | bytes 98312 | tf_op jit(solution)/shard_map/ppermute | solution.py:665
  92.0 3.9 %collective-permute-start.16 = (f32[6,16,128]{2,1,0:T(8,128)S(1)}, f32[6,16,128]{2,1,0:T(8,128)S(1)}, u32[]{:S(2)}, u32[]{:S(2)}) collective-permute-start(f32[6,16,128]{2,1,0:T(8,128)S(1)} %get-tuple-element.79), channel_id=1, source_target_pairs={{0,8},{8,0},{16,24},{24,16},{1,9},{9,1},{17,25},{25,17},{2,10},{10... | collective-permute-start | bytes 147464 | tf_op jit(solution)/shard_map/ppermute | solution.py:665
  94.8 4.6 %collective-permute-start.19 = (f32[6,16,128]{2,1,0:T(8,128)S(1)}, f32[6,16,128]{2,1,0:T(8,128)S(1)}, u32[]{:S(2)}, u32[]{:S(2)}) collective-permute-start(f32[6,16,128]{2,1,0:T(8,128)S(1)} %add.96), channel_id=1, source_target_pairs={{0,16},{8,24},{16,0},{24,8},{1,17},{9,25},{17,1},{25,9},{2,18},{10... | collective-permute-start | bytes 147464 | tf_op jit(solution)/shard_map/ppermute | solution.py:665
  96.0 4.2 %collective-permute-start.17 = (f32[6,16,128]{2,1,0:T(8,128)S(1)}, f32[6,16,128]{2,1,0:T(8,128)S(1)}, u32[]{:S(2)}, u32[]{:S(2)}) collective-permute-start(f32[6,16,128]{2,1,0:T(8,128)S(1)} %add.94), channel_id=1, source_target_pairs={{0,16},{8,24},{16,0},{24,8},{1,17},{9,25},{17,1},{25,9},{2,18},{10... | collective-permute-start | bytes 147464 | tf_op jit(solution)/shard_map/ppermute | solution.py:665
  100.9 14.9 %all-to-all-start.1 = ((bf16[8,192,128]{2,1,0:T(8,128)(2,1)}), bf16[8,192,128]{2,1,0:T(8,128)(2,1)S(1)}, u32[]{:S(2)}, u32[]{:S(2)}) async-start(bf16[8,192,128]{2,1,0:T(8,128)(2,1)} %broadcast_in_dim.2), calls=%async_computation.1 | async-start | bytes 786432 | tf_op jit(solution)/shard_map/all_to_all | solution.py:682
  115.9 2.5 %collective-permute-start.20 = (bf16[8,192,128]{2,1,0:T(8,128)(2,1)S(1)}, bf16[8,192,128]{2,1,0:T(8,128)(2,1)S(1)}, u32[]{:S(2)}, u32[]{:S(2)}) collective-permute-start(bf16[8,192,128]{2,1,0:T(8,128)(2,1)S(1)} %all-to-all-done.1), channel_id=1, source_target_pairs={{0,8},{8,0},{16,24},{24,16},{1,9},{9,1},{17,25},{25,17},{2,10},{10... | collective-permute-start | bytes 1179656 | tf_op jit(solution)/shard_map/ppermute | solution.py:665

commit v4 on v3

--- a/solution.py
+++ b/solution.py
@@ -12,7 +12,7 @@
 REACH = 256
 RIM = 4
 TILE = 16
-LIMITS = (4, 13, 10, 7, 12, 9, 12, 2)
+LIMITS = (4, 14, 10, 7, 10, 8, 10, 2, 6)
 
 eps_norm = 1e-05
 highest = lax.Precision.HIGHEST
@@ -148,12 +148,20 @@
     return block_of
 
 
-def backward_blocks(w_back, layer):
-    return lambda i, j: w_back[layer, i * 3 + j]
-
-
-def kernel_mix(amounts, clean, noise, mixed):
+def taken(weights, layer):
+    return lambda i, j: weights[layer, i * 3 + j]
+
+
+def kernel_mix(amounts, clean_far, noise_far, mixed, clean, noise, sems):
     parts = mixed.shape[0]
+    copies = [
+        pltpu.make_async_copy(clean_far, clean, sems.at[0]),
+        pltpu.make_async_copy(noise_far, noise, sems.at[1]),
+    ]
+    for copy in copies:
+        copy.start()
+    for copy in copies:
+        copy.wait()
     for k in range(3):
         noisy = amounts[0] * clean[k, 0] + amounts[1] * noise[k, 0]
         for part in range(parts):
@@ -161,9 +169,18 @@
             mixed[part, 12 + 4 * k : 16 + 4 * k] = noise[k, 0]
 
 
-def kernel_prepare(w_z, w_xy, w_point, w_in, w_out, w_back, point_back, lift_in, lift_out):
+def kernel_prepare(w_z, w_xy, w_point, w_in, w_out, gains, w_front, point, w_back, point_back, lift_in,
+                   lift_out, w_in_on, gains_on):
+    w_in_on[...] = w_in[...]
+    gains_on[...] = gains[...]
+    point[...] = w_point[...]
     for layer in range(2):
         forward = forward_blocks(w_z, w_xy, layer)
+        for i in range(3):
+            for j in range(3):
+                w_front[layer, i * 3 + j] = forward(i, j)
+        for m in range(2):
+            w_front[layer, 9 + m] = forward(3, m)
         for i in range(3):
             for j in range(3):
                 w_back[layer, i * 3 + j] = forward(2 - i, 2 - j).T
@@ -217,10 +234,10 @@
     half = lanes // 2
     total = None
     for i in range(3):
-        part = mm(padded[pl.ds(x0 + i, count)].reshape(count * rows, lanes), taps[q, i])
+        part = mm(padded[x0 + i : x0 + i + count].reshape(count * rows, lanes), taps[q, i])
         total = part if total is None else total + part
     for m in range(2):
-        source = shifted[m, pl.ds(x0, count), :, q * half : (q + 1) * half]
+        source = shifted[m, x0 : x0 + count, :, q * half : (q + 1) * half]
         total = total + mm(source.reshape(count * rows, half), taps_z[m])
     return total
 
@@ -262,34 +279,34 @@
     return folded(jnp.sum(jnp.where(mask, value, 0.0), axis=0, keepdims=True))
 
 
-def layer_forward(place, layer, padded, shifted, taps, taps_z, pair, w_z, w_xy, wp, shift_bias, old,
+def layer_forward(place, layer, padded, shifted, taps, taps_z, pair, w_front, wp, shift_bias, old,
                   stream, act, slope, stats, acc, per_member):
     planes, rows, lanes = stream.shape
     half = lanes // 2
-    count = planes // 2
-    build_taps(forward_blocks(w_z, w_xy, layer), taps, taps_z)
+    count = planes // 4
+    build_taps(taken(w_front, layer), taps, taps_z)
     build_pair(wp[layer], pair, 0)
     fill_rims(padded, planes)
     fill_shifted(place, layer, padded, shifted, planes)
     acc[...] = jnp.zeros_like(acc)
     bias = wide(shift_bias[layer : layer + 1, :])[:, :half]
 
-    def body(step, carry):
-        x0 = step * count
+    for x0 in range(0, planes, count):
+        part = slice(x0, x0 + count)
         for q in range(2):
             side = slice(q * half, (q + 1) * half)
             pre = conv_half(padded, shifted, taps, taps_z, x0, count, q) + bias
             value, grad = gelu_pair(pre)
-            value = value.astype(bf16)
-            act[pl.ds(x0, count), :, side] = value.reshape(count, rows, half)
-            slope[pl.ds(x0, count), :, side] = grad.astype(bf16).reshape(count, rows, half)
-            branch = mm(value, pair[0]).reshape(count, rows, half)
-            new = old[pl.ds(x0, count), :, side] + branch
-            stream[pl.ds(x0, count), :, side] = new
+            act[part, :, side] = value.astype(bf16).reshape(count, rows, half)
+            slope[part, :, side] = grad.astype(bf16).reshape(count, rows, half)
+    for x0 in range(0, planes, count):
+        part = slice(x0, x0 + count)
+        for q in range(2):
+            side = slice(q * half, (q + 1) * half)
+            branch = mm(act[part, :, side].reshape(count * rows, half), pair[0])
+            new = old[part, :, side] + branch.reshape(count, rows, half)
+            stream[part, :, side] = new
             acc[:, side] += jnp.sum(new, axis=0)
-        return carry
-
-    lax.fori_loop(0, planes // count, body, 0)
     mask = place.own((rows, lanes))
     total = masked_total(mask, acc[...])
     mean = wide(total / per_member)
@@ -300,7 +317,7 @@
     put_rows(stats, total, masked_total(mask, spread))
 
 
-def kernel_first(cells_z, per_member, sc, near, far, lift_in, w_in, gains, shift_bias, w_z, w_xy, wp,
+def kernel_first(cells_z, per_member, sc, near, far, lift_in, w_in, gains, shift_bias, w_front, wp,
                  stream, normed, act, slope, gathered, stats, consts,
                  padded, shifted, taps, taps_z, pair, acc, old, source):
     planes, rows, lanes = stream.shape
@@ -353,13 +370,13 @@
         old[part] = value.reshape(planes // 2, rows, lanes)
         padded[x0 + 1 : x0 + 1 + planes // 2] = unit
         normed[part] = unit
-    layer_forward(place, 0, padded, shifted, taps, taps_z, pair, w_z, w_xy, wp, shift_bias, old, stream,
+    layer_forward(place, 0, padded, shifted, taps, taps_z, pair, w_front, wp, shift_bias, old, stream,
                   act, slope, stats, acc, per_member)
 
 
 def kernel_second(per_member, sc, *refs):
     parts, refs = refs[:4], refs[4:]
-    (old, gains, shift_bias, w_z, w_xy, wp, stream, normed, act, slope, stats, consts,
+    (old, gains, shift_bias, w_front, wp, stream, normed, act, slope, stats, consts,
      padded, shifted, taps, taps_z, pair, acc) = refs
     planes, rows, _ = stream.shape
     place = Place(sc, rows)
@@ -370,7 +387,7 @@
         unit = ((old[x] - mean_w) * scale).astype(bf16)
         padded[x + 1] = unit
         normed[x] = unit
-    layer_forward(place, 1, padded, shifted, taps, taps_z, pair, w_z, w_xy, wp, shift_bias, old, stream,
+    layer_forward(place, 1, padded, shifted, taps, taps_z, pair, w_front, wp, shift_bias, old, stream,
                   act, slope, stats, acc, per_member)
 
 
@@ -432,23 +449,20 @@
     half = lanes // 2
     count = planes // 2
 
-    def body(step, carry):
-        x0 = step * count
-        for t in range(count):
-            scot[x0 + t] = d_stream_of(x0 + t).astype(bf16)
+    for x0 in range(0, planes, count):
+        part = slice(x0, x0 + count)
+        for x in range(x0, x0 + count):
+            scot[x] = d_stream_of(x).astype(bf16)
         for q in range(2):
             side = slice(q * half, (q + 1) * half)
-            cot = scot[pl.ds(x0, count), :, side].reshape(count * rows, half)
+            cot = scot[part, :, side].reshape(count * rows, half)
             d_act = mm(cot, pair[0]).reshape(count, rows, half)
-            pre = (d_act * slope[pl.ds(x0, count), :, side].astype(f32)).astype(bf16)
-            padded[pl.ds(x0 + 1, count), :, side] = pre
+            pre = (d_act * slope[part, :, side].astype(f32)).astype(bf16)
+            padded[x0 + 1 : x0 + 1 + count, :, side] = pre
             bias_acc[:, side] += jnp.sum(pre.astype(f32), axis=0)
-        return carry
-
-    lax.fori_loop(0, planes // count, body, 0)
-
-
-def weight_grads(place, planes, padded, shifted, scot, normed, act, keep, give, share):
+
+
+def weight_grads(place, planes, padded, shifted, scot, normed, act, keep, give, taps_all, share):
     rows, lanes = padded.shape[1:]
     channels = lanes // 4
     wide_share = 4 * share
@@ -471,51 +485,34 @@
             if 0 <= y + j < 4
         )
 
-    odd = lax.rem(place.member, 2) == 1
-
-    def hand(tap, value):
-        late = tap >= 6
-        at = tap - 6 if late else tap
-        stays = odd if late else jnp.logical_not(odd)
-
-        @pl.when(stays)
-        def _():
-            keep[at] = value
-
-        @pl.when(jnp.logical_not(stays))
-        def _():
-            give[at] = value
-
     left = turned(normed)
     for i in range(3):
         raw = mm_tn(left, padded[2 - i : 2 - i + planes].reshape(planes * rows, lanes))
         for j in range(3):
-            hand(i * 3 + j, add_blocks(raw, j - 1))
+            taps_all[i * 3 + j] = add_blocks(raw, j - 1)
     for m in range(2):
         raw = mm_tn(left, shifted[1 - m].reshape(planes * rows, lanes))
-        hand(9 + m, add_blocks(raw, 0))
+        taps_all[9 + m] = add_blocks(raw, 0)
     raw = mm_tn(turned(act), scot[...].reshape(planes * rows, lanes))
-    hand(11, add_blocks(raw, 0))
+    taps_all[11] = add_blocks(raw, 0)
+    odd, half = lax.rem(place.member, 2), keep.shape[0]
+    keep[...] = taps_all[pl.ds(odd * half, half)]
+    give[...] = taps_all[pl.ds((1 - odd) * half, half)]
 
 
 def conv_backward(planes, padded, shifted, taps, taps_z, emit):
-    rows, lanes = padded.shape[1:]
-    count = planes // 2
-
-    def body(step, carry):
-        x0 = step * count
+    count = planes // 4
+
+    for x0 in range(0, planes, count):
         for q in range(2):
             emit(x0, count, q, conv_half(padded, shifted, taps, taps_z, x0, count, q))
-        return carry
-
-    lax.fori_loop(0, planes // count, body, 0)
-
-
-def kernel_back_second(share, cell_count, sc, *refs):
+
+
+def kernel_back_second(cell_count, sc, *refs):
     parts, refs = refs[:4], refs[4:]
-    (stream, out_consts, gains, misfit, lift_out, act, slope, normed, w_back, point_back,
-     d_stream, d_normed, sums, keep, give,
-     padded, shifted, taps, taps_z, pair, acc, acc2, scot) = refs
+    (stream, out_consts, gains, misfit, lift_out, slope, normed, w_back, point_back,
+     d_stream, d_normed, sums, padded, shifted, scot,
+     taps, taps_z, pair, acc, acc2) = refs
     planes, rows, lanes = stream.shape
     half = lanes // 2
     place = Place(sc, rows)
@@ -525,7 +522,7 @@
     m_plain = gain_w * wide(sums_out[0:1]) / cell_count
     m_cross = gain_w * wide(sums_out[1:2]) / cell_count
     build_pair(point_back[1], pair, 0)
-    build_taps(backward_blocks(w_back, 1), taps, taps_z)
+    build_taps(taken(w_back, 1), taps, taps_z)
     acc[...] = jnp.zeros_like(acc)
 
     def d_stream_of(x):
@@ -546,22 +543,26 @@
     def emit(x0, count, q, value):
         side = slice(q * half, (q + 1) * half)
         value = value.reshape(count, rows, half)
-        d_normed[pl.ds(x0, count), :, side] = value
+        d_normed[x0 : x0 + count, :, side] = value
         acc[:, side] += jnp.sum(value, axis=0)
-        acc2[:, side] += jnp.sum(value * normed[pl.ds(x0, count), :, side].astype(f32), axis=0)
+        acc2[:, side] += jnp.sum(value * normed[x0 : x0 + count, :, side].astype(f32), axis=0)
 
     conv_backward(planes, padded, shifted, taps, taps_z, emit)
     s_plain = masked_total(mask, acc[...])
     s_cross = masked_total(mask, acc2[...]) / gains[1:2, :]
     put_rows(sums, s_plain, s_cross, s_bias)
-    weight_grads(place, planes, padded, shifted, scot, normed, act, keep, give, share)
+
+
+def kernel_weights_second(share, sc, padded, shifted, scot, normed, act, keep, give, taps_all):
+    planes, rows, _ = scot.shape
+    weight_grads(Place(sc, rows), planes, padded, shifted, scot, normed, act, keep, give, taps_all, share)
 
 
 def kernel_back_first(share, cell_count, sc, *refs):
     parts, refs = refs[:4], refs[4:]
     (consts, d_next, d_normed, normed_next, gains, act, slope, normed, point_back,
-     d_stream, pre_cot, sums, keep, give,
-     padded, shifted, pair, acc, scot) = refs
+     d_stream, sums, keep, give, padded, shifted,
+     pair, acc, scot, taps_all) = refs
     planes, rows, lanes = d_next.shape
     place = Place(sc, rows)
     sums_in = sum(members_of(parts))
@@ -582,29 +583,23 @@
     put_rows(sums, masked_total(place.own((rows, lanes)), acc[...]))
     fill_rims(padded, planes)
     fill_shifted(place, 0, padded, shifted, planes)
-    for x in range(planes):
-        pre_cot[x] = padded[x + 1]
-    weight_grads(place, planes, padded, shifted, scot, normed, act, keep, give, share)
-
-
-def kernel_last(depth, sc, pre_cot, d_stream, normed, gains, consts, gathered, lift_in, w_back,
+    weight_grads(place, planes, padded, shifted, scot, normed, act, keep, give, taps_all, share)
+
+
+def kernel_last(depth, sc, padded, shifted, d_stream, normed, gains, consts, gathered, lift_in, w_back,
                 prediction, sums_bias, out_raw, own_out, out_1, out_2, out_3,
-                padded, shifted, taps, taps_z, acc, acc2, high, low):
+                taps, taps_z, acc, acc2, high, low):
     planes, rows, lanes = d_stream.shape
     half = lanes // 2
     place = Place(sc, rows)
-    for x in range(planes):
-        padded[x + 1] = pre_cot[x]
-    fill_rims(padded, planes)
-    fill_shifted(place, 0, padded, shifted, planes)
-    build_taps(backward_blocks(w_back, 0), taps, taps_z)
+    build_taps(taken(w_back, 0), taps, taps_z)
     acc[...] = jnp.zeros_like(acc)
     acc2[...] = jnp.zeros_like(acc2)
     scale = wide(consts[1:2] * gains[0:1, :])
 
     def emit(x0, count, q, value):
         side = slice(q * half, (q + 1) * half)
-        part = pl.ds(x0, count)
+        part = slice(x0, x0 + count)
         value = value.reshape(count, rows, half)
         acc[:, side] += jnp.sum(value, axis=0)
         acc2[:, side] += jnp.sum(value * normed[part, :, side].astype(f32), axis=0)
@@ -654,7 +649,7 @@
         out_shape=[jax.ShapeDtypeStruct(shape, dtype) for shape, dtype in outs],
         in_specs=specs,
         out_specs=[spec] * len(outs),
-        scratch_shapes=[pltpu.VMEM(shape, dtype) for shape, dtype in scratch],
+        scratch_shapes=[pltpu.VMEM(*one) if isinstance(one, tuple) else one for one in scratch],
         compiler_params=pltpu.CompilerParams(vmem_limit_bytes=limit * 2**20),
         cost_estimate=pl.CostEstimate(flops=flops, bytes_accessed=2**23, transcendentals=0),
     )(*args)
@@ -707,8 +702,9 @@
     alpha_bar, features, time_raw, time_code = time_terms(timestep, w_time)
     parts = members // 2 * groups
     mixed = call(
-        kernel_mix, [((parts, 24, depth), f32)], [], 10**5, LIMITS[7],
-        jnp.stack([jnp.sqrt(alpha_bar), jnp.sqrt(1.0 - alpha_bar)]), clean_field, noise_field,
+        kernel_mix, [((parts, 24, depth), f32)],
+        [(clean_field.shape, f32), (clean_field.shape, f32), pltpu.SemaphoreType.DMA((2,))], 10**5, LIMITS[7],
+        jnp.stack([jnp.sqrt(alpha_bar), jnp.sqrt(1.0 - alpha_bar)]), clean_field, noise_field, loose=(1, 2),
     )[0]
     same_core = [[m * groups + g for m in range(core, members, 2) for g in range(groups)] for core in range(2)]
     near = lax.all_to_all(mixed, ("gz", "gx"), 0, 0, axis_index_groups=same_core)
@@ -729,57 +725,63 @@
     flat = ((rows, lanes), f32)
     grad_out = ((6, share, channels), f32)
 
-    w_back, point_back, lift_in, lift_out = call(
+    taps_out, point_out = ((2, 11, channels, channels), bf16), ((2, channels, channels), bf16)
+    w_front, point, w_back, point_back, lift_in, lift_out, w_in_on, gains_on = call(
         kernel_prepare,
-        [((2, 11, channels, channels), bf16), ((2, channels, channels), bf16), lift, lift],
-        [], 10**8, LIMITS[0], w_z, w_xy, w_point, w_in, w_out, scalars=False,
+        [taps_out, point_out, taps_out, point_out, lift, lift, ((3, channels), f32), ((3, channels), f32)],
+        [], 10**8, LIMITS[0], w_z, w_xy, w_point, w_in, w_out, norm_gains, scalars=False,
     )
     stream1, normed0, act0, slope0, gathered, stats1, consts0 = call(
         functools.partial(kernel_first, cells_z, per_member),
         [(big, f32), (big, bf16), (big, bf16), (big, bf16), thin, vec, ((16, channels), f32)],
         conv_scratch + [pair, flat, (big, f32), ((planes, 128, cells_z), bf16)],
         4 * 10**9, LIMITS[1],
-        dilations, near, far, lift_in, w_in, norm_gains, shift_bias, w_z, w_xy, w_point,
+        dilations, near, far, lift_in, w_in_on, gains_on, shift_bias, w_front, point,
     )
     stream2, normed1, act1, slope1, stats2, consts1 = call(
         functools.partial(kernel_second, per_member),
         [(big, f32), (big, bf16), (big, bf16), (big, bf16), vec, vec],
         conv_scratch + [pair, flat],
         4 * 10**9, LIMITS[2],
-        dilations, *group_parts(stats1), stream1, norm_gains, shift_bias, w_z, w_xy, w_point,
+        dilations, *group_parts(stats1), stream1, gains_on, shift_bias, w_front, point,
     )
     prediction, misfit, sums2, out_raw, consts2 = call(
         functools.partial(kernel_out, per_member),
         [((rows, 128), f32), thin, vec, vec, vec],
         [(big, bf16)],
         10**9, LIMITS[3],
-        dilations, *group_parts(stats2), stream2, norm_gains, gathered, lift_out,
+        dilations, *group_parts(stats2), stream2, gains_on, gathered, lift_out,
     )
     parts2 = group_parts(sums2)
-    d_stream2, d_normed1, sums1, keep1, give1 = call(
-        functools.partial(kernel_back_second, share, cell_count),
-        [(big, f32), (big, f32), vec, grad_out, grad_out],
-        conv_scratch + [pair, flat, flat, (big, bf16)],
+    d_stream2, d_normed1, sums1, rimmed1, shifted1, scot1 = call(
+        functools.partial(kernel_back_second, cell_count),
+        [(big, f32), (big, f32), vec] + conv_scratch[:2] + [(big, bf16)],
+        conv_scratch[2:] + [pair, flat, flat],
         6 * 10**9, LIMITS[4],
-        dilations, *parts2, stream2, consts2, norm_gains, misfit, lift_out, act1, slope1, normed1,
+        dilations, *parts2, stream2, consts2, gains_on, misfit, lift_out, slope1, normed1,
         w_back, point_back,
     )
     parts1 = group_parts(sums1)
-    d_stream1, pre_cot0, sums_b0, keep0, give0 = call(
+    keep1, give1 = call(
+        functools.partial(kernel_weights_second, share),
+        [grad_out, grad_out], [((12, share, channels), f32)], 2 * 10**9, LIMITS[8],
+        dilations, rimmed1, shifted1, scot1, normed1, act1,
+    )
+    d_stream1, sums_b0, keep0, give0, rimmed0, shifted0 = call(
         functools.partial(kernel_back_first, share, cell_count),
-        [(big, f32), (big, bf16), vec, grad_out, grad_out],
-        conv_scratch[:2] + [pair, flat, (big, bf16)],
+        [(big, f32), vec, grad_out, grad_out] + conv_scratch[:2],
+        [pair, flat, (big, bf16), ((12, share, channels), f32)],
         4 * 10**9, LIMITS[5],
-        dilations, *parts1, consts1, d_stream2, d_normed1, normed1, norm_gains, act0, slope0, normed0,
+        dilations, *parts1, consts1, d_stream2, d_normed1, normed1, gains_on, act0, slope0, normed0,
         point_back,
     )
     mine1 = group_grads(keep1, give1)
     last = call(
         functools.partial(kernel_last, depth),
         [((64, channels), f32)] * members,
-        conv_scratch + [flat, flat, (big, bf16), (big, bf16)],
+        conv_scratch[2:] + [flat, flat, (big, bf16), (big, bf16)],
         4 * 10**9, LIMITS[6],
-        dilations, pre_cot0, d_stream1, normed0, norm_gains, consts0, gathered, lift_in, w_back, prediction,
+        dilations, rimmed0, shifted0, d_stream1, normed0, gains_on, consts0, gathered, lift_in, w_back, prediction,
         sums_b0, out_raw,
     )
     every = all_grads(group_grads(keep0, give0), mine1)

time: 122 us -> 104 us (0.85)
  Pallas kernels: 44.7 us -> 31.3 us
  local copies, waits for them, and re-layouts: 14.2 us -> 10.7 us
  waiting for transfers between devices: 23.7 us -> 20.7 us
    pallas_call x8 -> x9, Pallas kernels: 44.7 us -> 31.3 us  [call(): pl.pallas_call(kernel, out_shape=[jax.ShapeDtypeStruct(shape, dtype) for...]
    unnamed x40 -> x24, local copies, waits for them, and re-layouts: 10.4 us -> 6.9 us
    ppermute x21, waiting for transfers between devices: 10.8 us -> 9.43 us  [swapped(): return lax.ppermute(value, axis, [(i, i ^ bit) for i in range(count)])]
  transfers between devices with their start and end apart: 23 -> 23, of which waited for: 12 -> 10; matrix products, arithmetic and copies ran while one was open for 10% -> 12% of each run, Pallas kernels for 10% -> 11%
where the time goes in v4:
time: 104 us; the launch traced here: 103 us
  Pallas kernels  31.3 us (30%)
  starting transfers between devices  25.2 us (24%)
  waiting for transfers between devices  20.7 us (20%)
  other arithmetic  13.2 us (13%)
  local copies, waits for them, and re-layouts  10.7 us (10%)
  between operations  1.76 us (2%)
    pallas_call x9, Pallas kernels, call(): pl.pallas_call(kernel, out_shape=[jax.ShapeDtypeStruct(shape, dtype) for...  31.3 us
    ppermute x21, starting transfers between devices, swapped(): return lax.ppermute(value, axis, [(i, i ^ bit) for i in range(count)])  12.8 us
    ppermute x21, waiting for transfers between devices, swapped(): return lax.ppermute(value, axis, [(i, i ^ bit) for i in range(count)])  9.43 us
    all_to_all x1, waiting for transfers between devices, all_grads(): lax.all_to_all(jnp.broadcast_to(mine[None], (groups,) + mine.shape), 'gx'...  9.03 us
    all_to_all x1, starting transfers between devices, per_device_grouped(): lax.all_to_all(mixed, ('gz', 'gx'), 0, 0, axis_index_groups=same_core)  8.32 us
    unnamed x24, local copies, waits for them, and re-layouts  6.9 us
    another operation x4, other arithmetic, per_device_grouped(): jnp.stack([jnp.stack([c00, c01, c02]), jnp.stack([c01, c11, c12]), jnp.st...  6.05 us
    all_to_all x1, starting transfers between devices, all_grads(): lax.all_to_all(jnp.broadcast_to(mine[None], (groups,) + mine.shape), 'gx'...  4.04 us
  transfers between devices with their start and end apart: 23, of which 10 were waited for; matrix products, arithmetic and copies ran while one was open for 12% of the time, Pallas kernels for 11%

profile of v4, /device:TPU:0, one launch (start us, length us, event | category | flops | bytes accessed | tf_op | source)
XLA Modules:
  0.0 103.0 jit_solution(12348140564696176151)
XLA Ops:
  1.6 0.7 copy-done.6
  2.3 0.7 copy-done.7
  3.0 1.3 %shard_map.195 = f32[16,24,128]{2,1,0:T(8,128)} custom-call(f32[2]{0:T(128)S(1)} %pad_maximum_fusion.4.amounts, f32[3,1,4,128]{3,2,1,0:T(4,128)S(1)} %copy-done.6, f32[3,1,4,128]{3,2,1,0:T(4,128)S(1)} %copy-done.7), custom_call_target="tpu_custom_call" | custom-call | flops 100000 | bytes 8388608 | tf_op jit(solution)/shard_map/pallas_call | solution.py:647
  4.2 8.3 %all-to-all-start = ((f32[16,24,128]{2,1,0:T(8,128)}), f32[16,24,128]{2,1,0:T(8,128)S(1)}, u32[]{:S(2)}, u32[]{:S(2)}) async-start(f32[16,24,128]{2,1,0:T(8,128)} %shard_map.195), calls=%async_computation | async-start | bytes 393216 | tf_op jit(solution)/shard_map/all_to_all | solution.py:710
  12.6 0.7 slice.144
  13.4 1.0 %copy-done.1 = bf16[2,8,128,128]{3,2,1,0:T(8,128)(2,1)S(1)} copy-done((bf16[2,8,128,128]{3,2,1,0:T(8,128)(2,1)S(1)}, bf16[2,8,128,128]{3,2,1,0:T(8,128)(2,1)}, u32[]{:S(2)}) %copy-start.1) | copy-done | bytes 524312
  14.4 0.9 copy-done.2
  15.3 0.8 copy-done.3
  16.2 0.7 copy-done.4
  16.8 0.7 copy-done.8
  18.7 2.2 %all-to-all-done.near = f32[16,24,128]{2,1,0:T(8,128)S(1)} async-done(((f32[16,24,128]{2,1,0:T(8,128)}), f32[16,24,128]{2,1,0:T(8,128)S(1)}, u32[]{:S(2)}, u32[]{:S(2)}) %all-to-all-start) | async-done | bytes 196640 | tf_op jit(solution)/shard_map/all_to_all | solution.py:710
  21.0 0.7 broadcast_add_fusion.shift_bias.refs_6_
  21.6 0.8 collective-permute-done.far
  23.1 6.3 %shard_map.197 = (f32[8,144,512]{2,1,0:T(8,128)S(1)}, bf16[8,144,512]{2,1,0:T(8,128)(2,1)S(1)}, bf16[8,144,512]{2,1,0:T(8,128)(2,1)S(1)}, bf16[8,144,512]{2,1,0:...) custom-call(s32[2]{0:T(128)S(1)} %copy-done.10, ...), custom_call_target="tpu_custom_call" | custom-call | flops 4000000000 | bytes 8388608 | tf_op jit(solution)/shard_map/pallas_call | solution.py:647
  30.0 0.9 collective-permute-start.3
  30.9 0.8 collective-permute-start.2
  32.0 2.0 %maximum_bitcast_fusion = f32[1,3]{1,0:T(1,128)S(1)} fusion(f32[1]{0:T(128)} %bitcast.14, f32[1]{0:T(128)} %bitcast.13, f32[1]{0:T(128)} %bitcast.12), kind=kLoop, calls=%fused_computation.39 | loop fusion | flops 6 | bytes 24 | tf_op jit(solution)/shard_map/stack | solution.py:799
  34.0 2.0 %maximum_bitcast_fusion.1 = f32[1,3]{1,0:T(1,128)S(1)} fusion(f32[1]{0:T(128)} %bitcast.17, f32[1]{0:T(128)} %bitcast.16, f32[1]{0:T(128)} %bitcast.13), kind=kLoop, calls=%fused_computation.40 | loop fusion | flops 6 | bytes 24 | tf_op jit(solution)/shard_map/stack | solution.py:799
  36.0 5.3 %shard_map.198 = (f32[8,144,512]{2,1,0:T(8,128)S(1)}, bf16[8,144,512]{2,1,0:T(8,128)(2,1)S(1)}, bf16[8,144,512]{2,1,0:T(8,128)(2,1)S(1)}, bf16[8,144,512]{2,1,0:...) custom-call(s32[2]{0:T(128)S(1)} %copy-done.11, f32[8,128]{1,0:T(8,128)S(1)} %get-tuple-element.59.refs_0_, ...), custom_call_target="tpu_custom_call" | custom-call | flops 4000000000 | bytes 8388608 | tf_op jit(solution)/shard_map/pallas_call | solution.py:647
  41.4 1.3 %collective-permute-start.6 = (f32[8,128]{1,0:T(8,128)S(1)}, f32[8,128]{1,0:T(8,128)S(1)}, u32[]{:S(2)}, u32[]{:S(2)}) collective-permute-start(f32[8,128]{1,0:T(8,128)S(1)} %get-tuple-element.61.refs_0_), channel_id=1, source_target_pairs={{0,24},{8,16},{16,8},{24,0},{1,25},{9,17},{17,9},{25,1},{2,26},{10... | collective-permute-start | bytes 12296 | tf_op jit(solution)/shard_map/ppermute | solution.py:660
  42.7 0.8 collective-permute-start.5
  43.4 2.0 %maximum_bitcast_fusion.2 = f32[1,3]{1,0:T(1,128)S(1)} fusion(f32[1]{0:T(128)} %bitcast.19, f32[1]{0:T(128)} %bitcast.17, f32[1]{0:T(128)} %bitcast.14), kind=kLoop, calls=%fused_computation.41 | loop fusion | flops 6 | bytes 24 | tf_op jit(solution)/shard_map/stack | solution.py:799
  45.5 0.8 collective-permute-done.5.refs_2_
  46.3 2.3 %shard_map.199 = (f32[144,128]{1,0:T(8,128)S(1)}, bf16[8,144,128]{2,1,0:T(8,128)(2,1)S(1)}, f32[8,128]{1,0:T(8,128)S(1)}, f32[8,128]{1,0:T(8,128)S(1)}, f32[8,128]{1,0:T(8,128)S(1)}) custom-call(s32[2]{0:T(128)S(1)} %copy-done.11, f32[8,128]{1,0:T(8,128)S(1)} %get-tuple-element.61.refs_0_, f32[8,128]{1,0:T(8,128)S(1)} %collective-permute-done.4.refs_1_, ...), custom_call_target="tpu_custom_call" | custom-call | flops 1000000000 | bytes 8388608 | tf_op jit(solution)/shard_map/pallas_call | solution.py:647
  49.2 0.8 collective-permute-start.8
  50.5 1.2 %collective-permute-done.9.refs_3_ = f32[8,128]{1,0:T(8,128)S(1)} collective-permute-done((f32[8,128]{1,0:T(8,128)S(1)}, f32[8,128]{1,0:T(8,128)S(1)}, u32[]{:S(2)}, u32[]{:S(2)}) %collective-permute-start.9) | collective-permute-done | bytes 4128 | tf_op jit(solution)/shard_map/ppermute | solution.py:660
  51.6 1.1 %collective-permute-done.8.refs_2_ = f32[8,128]{1,0:T(8,128)S(1)} collective-permute-done((f32[8,128]{1,0:T(8,128)S(1)}, f32[8,128]{1,0:T(8,128)S(1)}, u32[]{:S(2)}, u32[]{:S(2)}) %collective-permute-start.8) | collective-permute-done | bytes 4128 | tf_op jit(solution)/shard_map/ppermute | solution.py:660
  52.8 4.8 %shard_map.200 = (f32[8,144,512]{2,1,0:T(8,128)S(1)}, f32[8,144,512]{2,1,0:T(8,128)S(1)}, f32[8,128]{1,0:T(8,128)S(1)}, bf16[10,144,512]{2,1,0:T(8,128)(2,1)S(1)...) custom-call(s32[2]{0:T(128)S(1)} %copy-done.11, f32[8,128]{1,0:T(8,128)S(1)} %get-tuple-element.65.refs_0_, ...), custom_call_target="tpu_custom_call" | custom-call | flops 6000000000 | bytes 8388608 | tf_op jit(solution)/shard_map/pallas_call | solution.py:647
  57.6 0.8 collective-permute-start.11
  58.5 1.0 collective-permute-start.10
  59.5 2.8 %shard_map.203 = (f32[6,16,128]{2,1,0:T(8,128)S(1)}, f32[6,16,128]{2,1,0:T(8,128)S(1)}) custom-call(s32[2]{0:T(128)S(1)} %copy-done.11, bf16[10,144,512]{2,1,0:T(8,128)(2,1)S(1)} %get-tuple-element.92.padded, bf16[2,8,144,512]{3,2,1,0:T(8,128)(2,1)S(1)} %get-tuple-element.93.shifted, bf16[8,144,512]{2,1,0:T(8,128)(2,1)S(1)} %get-tuple-element.94.scot, ...), custom_call_target="tpu_custom_call" | custom-call | flops 2000000000 | bytes 8388608 | tf_op jit(solution)/shard_map/pallas_call | solution.py:647
  62.4 3.9 %shard_map.201 = (f32[8,144,512]{2,1,0:T(8,128)S(1)}, f32[8,128]{1,0:T(8,128)S(1)}, f32[6,16,128]{2,1,0:T(8,128)S(1)}, f32[6,16,128]{2,1,0:T(8,128)S(1)}, bf16[1...) custom-call(s32[2]{0:T(128)S(1)} %copy-done.11, f32[8,128]{1,0:T(8,128)S(1)} %get-tuple-element.72.refs_0_, ...), custom_call_target="tpu_custom_call" | custom-call | flops 4000000000 | bytes 8388608 | tf_op jit(solution)/shard_map/pallas_call | solution.py:647
  66.3 4.4 %shard_map.202 = (f32[64,128]{1,0:T(8,128)S(1)}, f32[64,128]{1,0:T(8,128)S(1)}, f32[64,128]{1,0:T(8,128)S(1)}, f32[64,128]{1,0:T(8,128)S(1)}) custom-call(s32[2]{0:T(128)S(1)} %copy-done.11, bf16[10,144,512]{2,1,0:T(8,128)(2,1)S(1)} %get-tuple-element.79.padded, bf16[2,8,144,512]{3,2,1,0:T(8,128)(2,1)S(1)} %get-tuple-element.80.shifted, ...), custom_call_target="tpu_custom_call" | custom-call | flops 4000000000 | bytes 8388608 | tf_op jit(solution)/shard_map/pallas_call | solution.py:647
  71.3 0.8 collective-permute-start.14
  72.7 0.8 collective-permute-start.16
  73.5 1.8 %collective-permute-done.14 = f32[64,128]{1,0:T(8,128)S(1)} collective-permute-done((f32[64,128]{1,0:T(8,128)S(1)}, f32[64,128]{1,0:T(8,128)S(1)}, u32[]{:S(2)}, u32[]{:S(2)}) %collective-permute-start.14) | collective-permute-done | bytes 32800 | tf_op jit(solution)/shard_map/ppermute | solution.py:660
  75.8 0.7 fusion.12
  76.6 1.3 %collective-permute-start.19 = (f32[6,16,128]{2,1,0:T(8,128)S(1)}, f32[6,16,128]{2,1,0:T(8,128)S(1)}, u32[]{:S(2)}, u32[]{:S(2)}) collective-permute-start(f32[6,16,128]{2,1,0:T(8,128)S(1)} %add.96), channel_id=1, source_target_pairs={{0,16},{8,24},{16,0},{24,8},{1,17},{9,25},{17,1},{25,9},{2,18},{10... | collective-permute-start | bytes 147464 | tf_op jit(solution)/shard_map/ppermute | solution.py:660
  78.0 0.9 collective-permute-start.17
  78.9 2.1 %collective-permute-done.19 = f32[6,16,128]{2,1,0:T(8,128)S(1)} collective-permute-done((f32[6,16,128]{2,1,0:T(8,128)S(1)}, f32[6,16,128]{2,1,0:T(8,128)S(1)}, u32[]{:S(2)}, u32[]{:S(2)}) %collective-permute-start.19) | collective-permute-done | bytes 49184 | tf_op jit(solution)/shard_map/ppermute | solution.py:660
  81.0 1.1 %collective-permute-done.17 = f32[6,16,128]{2,1,0:T(8,128)S(1)} collective-permute-done((f32[6,16,128]{2,1,0:T(8,128)S(1)}, f32[6,16,128]{2,1,0:T(8,128)S(1)}, u32[]{:S(2)}, u32[]{:S(2)}) %collective-permute-start.17) | collective-permute-done | bytes 49184 | tf_op jit(solution)/shard_map/ppermute | solution.py:660
  82.2 0.8 broadcast_in_dim.2
  83.0 4.0 %all-to-all-start.1 = ((bf16[8,192,128]{2,1,0:T(8,128)(2,1)}), bf16[8,192,128]{2,1,0:T(8,128)(2,1)S(1)}, u32[]{:S(2)}, u32[]{:S(2)}) async-start(bf16[8,192,128]{2,1,0:T(8,128)(2,1)} %broadcast_in_dim.2), calls=%async_computation.1 | async-start | bytes 786432 | tf_op jit(solution)/shard_map/all_to_all | solution.py:677
  88.6 9.0 %all-to-all-done.1 = bf16[8,192,128]{2,1,0:T(8,128)(2,1)S(1)} async-done(((bf16[8,192,128]{2,1,0:T(8,128)(2,1)}), bf16[8,192,128]{2,1,0:T(8,128)(2,1)S(1)}, u32[]{:S(2)}, u32[]{:S(2)}) %all-to-all-start.1) | async-done | bytes 393248 | tf_op jit(solution)/shard_map/all_to_all | solution.py:677
  99.4 0.7 multiply_multiply_fusion
  100.4 0.7 slice_bitcast_fusion
  101.2 1.0 %pad_maximum_fusion = f32[2,8,128,128]{3,2,1,0:T(8,128)} fusion(f32[2,4,128,128]{3,2,1,0:T(8,128)S(1)} %get-tuple-element.160, f32[2,4,128,128]{3,2,1,0:T(8,128)S(1)} %get-tuple-element.159), kind=kLoop, calls=%fused_computation.2 | loop fusion | flops 262144 | bytes 2097152 | tf_op jit(solution)/shard_map/concatenate | solution.py:816
  102.2 0.8 pad_maximum_fusion.1
  (78 shorter events, 9.8 us)
Async XLA Ops:
  0.6 17.9 %copy-start = (f32[128,128]{1,0:T(8,128)S(1)}, f32[128,128]{1,0:T(8,128)}, u32[]{:S(2)}) copy-start(f32[128,128]{1,0:T(8,128)} %param.17) | copy-start | bytes 196612
  1.6 0.7 copy-start.6
  2.3 0.7 copy-start.7
  4.2 16.7 %all-to-all-start = ((f32[16,24,128]{2,1,0:T(8,128)}), f32[16,24,128]{2,1,0:T(8,128)S(1)}, u32[]{:S(2)}, u32[]{:S(2)}) async-start(f32[16,24,128]{2,1,0:T(8,128)} %shard_map.195), calls=%async_computation | async-start | bytes 393216 | tf_op jit(solution)/shard_map/all_to_all | solution.py:710
  13.3 1.0 %copy-start.1 = (bf16[2,8,128,128]{3,2,1,0:T(8,128)(2,1)S(1)}, bf16[2,8,128,128]{3,2,1,0:T(8,128)(2,1)}, u32[]{:S(2)}) copy-start(bf16[2,8,128,128]{3,2,1,0:T(8,128)(2,1)} %w_xy.1) | copy-start | bytes 1572868
  14.4 0.9 copy-start.2
  15.3 0.8 copy-start.3
  16.2 0.7 copy-start.4
  16.8 0.7 copy-start.8
  17.5 0.7 copy-start.9
  20.9 1.4 %collective-permute-start = (f32[16,24,128]{2,1,0:T(8,128)S(1)}, f32[16,24,128]{2,1,0:T(8,128)S(1)}, u32[]{:S(2)}, u32[]{:S(2)}) collective-permute-start(f32[16,24,128]{2,1,0:T(8,128)S(1)} %all-to-all-done.near), channel_id=1, source_target_pairs={{0,8},{8,0},{16,24},{24,16},{1,9},{9,1},{17,25},{25,17},{2,10},{10... | collective-permute-start | bytes 589832 | tf_op jit(solution)/shard_map/ppermute | solution.py:660
  22.4 0.7 copy-start.10
  23.0 13.0 %copy-start.11 = (s32[2]{0:T(128)S(1)}, s32[2]{0:T(128)}, u32[]{:S(2)}) copy-start(s32[2]{0:T(128)} %sc.13) | copy-start | bytes 28
  30.0 6.0 %collective-permute-start.3 = (f32[8,128]{1,0:T(8,128)S(1)}, f32[8,128]{1,0:T(8,128)S(1)}, u32[]{:S(2)}, u32[]{:S(2)}) collective-permute-start(f32[8,128]{1,0:T(8,128)S(1)} %get-tuple-element.59.refs_0_), channel_id=1, source_target_pairs={{0,24},{8,16},{16,8},{24,0},{1,25},{9,17},{17,9},{25,1},{2,26},{10... | collective-permute-start | bytes 12296 | tf_op jit(solution)/shard_map/ppermute | solution.py:660
  30.9 5.1 %collective-permute-start.2 = (f32[8,128]{1,0:T(8,128)S(1)}, f32[8,128]{1,0:T(8,128)S(1)}, u32[]{:S(2)}, u32[]{:S(2)}) collective-permute-start(f32[8,128]{1,0:T(8,128)S(1)} %get-tuple-element.59.refs_0_), channel_id=1, source_target_pairs={{0,16},{8,24},{16,0},{24,8},{1,17},{9,25},{17,1},{25,9},{2,18},{10... | collective-permute-start | bytes 12296 | tf_op jit(solution)/shard_map/ppermute | solution.py:660
  31.7 4.3 %collective-permute-start.1 = (f32[8,128]{1,0:T(8,128)S(1)}, f32[8,128]{1,0:T(8,128)S(1)}, u32[]{:S(2)}, u32[]{:S(2)}) collective-permute-start(f32[8,128]{1,0:T(8,128)S(1)} %get-tuple-element.59.refs_0_), channel_id=1, source_target_pairs={{0,8},{8,0},{16,24},{24,16},{1,9},{9,1},{17,25},{25,17},{2,10},{10... | collective-permute-start | bytes 12296 | tf_op jit(solution)/shard_map/ppermute | solution.py:660
  41.4 4.1 %collective-permute-start.6 = (f32[8,128]{1,0:T(8,128)S(1)}, f32[8,128]{1,0:T(8,128)S(1)}, u32[]{:S(2)}, u32[]{:S(2)}) collective-permute-start(f32[8,128]{1,0:T(8,128)S(1)} %get-tuple-element.61.refs_0_), channel_id=1, source_target_pairs={{0,24},{8,16},{16,8},{24,0},{1,25},{9,17},{17,9},{25,1},{2,26},{10... | collective-permute-start | bytes 12296 | tf_op jit(solution)/shard_map/ppermute | solution.py:660
  42.7 3.6 %collective-permute-start.5 = (f32[8,128]{1,0:T(8,128)S(1)}, f32[8,128]{1,0:T(8,128)S(1)}, u32[]{:S(2)}, u32[]{:S(2)}) collective-permute-start(f32[8,128]{1,0:T(8,128)S(1)} %get-tuple-element.61.refs_0_), channel_id=1, source_target_pairs={{0,16},{8,24},{16,0},{24,8},{1,17},{9,25},{17,1},{25,9},{2,18},{10... | collective-permute-start | bytes 12296 | tf_op jit(solution)/shard_map/ppermute | solution.py:660
  43.4 2.8 %collective-permute-start.4 = (f32[8,128]{1,0:T(8,128)S(1)}, f32[8,128]{1,0:T(8,128)S(1)}, u32[]{:S(2)}, u32[]{:S(2)}) collective-permute-start(f32[8,128]{1,0:T(8,128)S(1)} %get-tuple-element.61.refs_0_), channel_id=1, source_target_pairs={{0,8},{8,0},{16,24},{24,16},{1,9},{9,1},{17,25},{25,17},{2,10},{10... | collective-permute-start | bytes 12296 | tf_op jit(solution)/shard_map/ppermute | solution.py:660
  48.5 3.1 %collective-permute-start.9 = (f32[8,128]{1,0:T(8,128)S(1)}, f32[8,128]{1,0:T(8,128)S(1)}, u32[]{:S(2)}, u32[]{:S(2)}) collective-permute-start(f32[8,128]{1,0:T(8,128)S(1)} %get-tuple-element.65.refs_0_), channel_id=1, source_target_pairs={{0,24},{8,16},{16,8},{24,0},{1,25},{9,17},{17,9},{25,1},{2,26},{10... | collective-permute-start | bytes 12296 | tf_op jit(solution)/shard_map/ppermute | solution.py:660
  49.2 3.6 %collective-permute-start.8 = (f32[8,128]{1,0:T(8,128)S(1)}, f32[8,128]{1,0:T(8,128)S(1)}, u32[]{:S(2)}, u32[]{:S(2)}) collective-permute-start(f32[8,128]{1,0:T(8,128)S(1)} %get-tuple-element.65.refs_0_), channel_id=1, source_target_pairs={{0,16},{8,24},{16,0},{24,8},{1,17},{9,25},{17,1},{25,9},{2,18},{10... | collective-permute-start | bytes 12296 | tf_op jit(solution)/shard_map/ppermute | solution.py:660
  49.9 2.8 %collective-permute-start.7 = (f32[8,128]{1,0:T(8,128)S(1)}, f32[8,128]{1,0:T(8,128)S(1)}, u32[]{:S(2)}, u32[]{:S(2)}) collective-permute-start(f32[8,128]{1,0:T(8,128)S(1)} %get-tuple-element.65.refs_0_), channel_id=1, source_target_pairs={{0,8},{8,0},{16,24},{24,16},{1,9},{9,1},{17,25},{25,17},{2,10},{10... | collective-permute-start | bytes 12296 | tf_op jit(solution)/shard_map/ppermute | solution.py:660
  57.5 4.9 %collective-permute-start.12 = (f32[8,128]{1,0:T(8,128)S(1)}, f32[8,128]{1,0:T(8,128)S(1)}, u32[]{:S(2)}, u32[]{:S(2)}) collective-permute-start(f32[8,128]{1,0:T(8,128)S(1)} %get-tuple-element.72.refs_0_), channel_id=1, source_target_pairs={{0,24},{8,16},{16,8},{24,0},{1,25},{9,17},{17,9},{25,1},{2,26},{10... | collective-permute-start | bytes 12296 | tf_op jit(solution)/shard_map/ppermute | solution.py:660
  57.6 4.8 %collective-permute-start.11 = (f32[8,128]{1,0:T(8,128)S(1)}, f32[8,128]{1,0:T(8,128)S(1)}, u32[]{:S(2)}, u32[]{:S(2)}) collective-permute-start(f32[8,128]{1,0:T(8,128)S(1)} %get-tuple-element.72.refs_0_), channel_id=1, source_target_pairs={{0,16},{8,24},{16,0},{24,8},{1,17},{9,25},{17,1},{25,9},{2,18},{10... | collective-permute-start | bytes 12296 | tf_op jit(solution)/shard_map/ppermute | solution.py:660
  58.5 4.0 %collective-permute-start.10 = (f32[8,128]{1,0:T(8,128)S(1)}, f32[8,128]{1,0:T(8,128)S(1)}, u32[]{:S(2)}, u32[]{:S(2)}) collective-permute-start(f32[8,128]{1,0:T(8,128)S(1)} %get-tuple-element.72.refs_0_), channel_id=1, source_target_pairs={{0,8},{8,0},{16,24},{24,16},{1,9},{9,1},{17,25},{25,17},{2,10},{10... | collective-permute-start | bytes 12296 | tf_op jit(solution)/shard_map/ppermute | solution.py:660
  62.3 14.3 %collective-permute-start.18 = (f32[6,16,128]{2,1,0:T(8,128)S(1)}, f32[6,16,128]{2,1,0:T(8,128)S(1)}, u32[]{:S(2)}, u32[]{:S(2)}) collective-permute-start(f32[6,16,128]{2,1,0:T(8,128)S(1)} %get-tuple-element.97), channel_id=1, source_target_pairs={{0,8},{8,0},{16,24},{24,16},{1,9},{9,1},{17,25},{25,17},{2,10},{10... | collective-permute-start | bytes 147464 | tf_op jit(solution)/shard_map/ppermute | solution.py:660
  66.3 10.1 %copy-start.5 = (f32[3,128]{1,0:T(4,128)S(1)}, f32[3,128]{1,0:T(4,128)}, u32[]{:S(2)}) copy-start(f32[3,128]{1,0:T(4,128)} %w_in.1) | copy-start | bytes 4612
  70.7 2.8 %collective-permute-start.13 = (f32[64,128]{1,0:T(8,128)S(1)}, f32[64,128]{1,0:T(8,128)S(1)}, u32[]{:S(2)}, u32[]{:S(2)}) collective-permute-start(f32[64,128]{1,0:T(8,128)S(1)} %get-tuple-element.87), channel_id=1, source_target_pairs={{0,8},{8,0},{16,24},{24,16},{1,9},{9,1},{17,25},{25,17},{2,10},{10... | collective-permute-start | bytes 98312 | tf_op jit(solution)/shard_map/ppermute | solution.py:660
  71.3 4.1 %collective-permute-start.14 = (f32[64,128]{1,0:T(8,128)S(1)}, f32[64,128]{1,0:T(8,128)S(1)}, u32[]{:S(2)}, u32[]{:S(2)}) collective-permute-start(f32[64,128]{1,0:T(8,128)S(1)} %get-tuple-element.88), channel_id=1, source_target_pairs={{0,16},{8,24},{16,0},{24,8},{1,17},{9,25},{17,1},{25,9},{2,18},{10... | collective-permute-start | bytes 98312 | tf_op jit(solution)/shard_map/ppermute | solution.py:660
  72.1 3.7 %collective-permute-start.15 = (f32[64,128]{1,0:T(8,128)S(1)}, f32[64,128]{1,0:T(8,128)S(1)}, u32[]{:S(2)}, u32[]{:S(2)}) collective-permute-start(f32[64,128]{1,0:T(8,128)S(1)} %get-tuple-element.89), channel_id=1, source_target_pairs={{0,24},{8,16},{16,8},{24,0},{1,25},{9,17},{17,9},{25,1},{2,26},{10... | collective-permute-start | bytes 98312 | tf_op jit(solution)/shard_map/ppermute | solution.py:660
  72.7 5.3 %collective-permute-start.16 = (f32[6,16,128]{2,1,0:T(8,128)S(1)}, f32[6,16,128]{2,1,0:T(8,128)S(1)}, u32[]{:S(2)}, u32[]{:S(2)}) collective-permute-start(f32[6,16,128]{2,1,0:T(8,128)S(1)} %get-tuple-element.91), channel_id=1, source_target_pairs={{0,8},{8,0},{16,24},{24,16},{1,9},{9,1},{17,25},{25,17},{2,10},{10... | collective-permute-start | bytes 147464 | tf_op jit(solution)/shard_map/ppermute | solution.py:660
  76.6 4.4 %collective-permute-start.19 = (f32[6,16,128]{2,1,0:T(8,128)S(1)}, f32[6,16,128]{2,1,0:T(8,128)S(1)}, u32[]{:S(2)}, u32[]{:S(2)}) collective-permute-start(f32[6,16,128]{2,1,0:T(8,128)S(1)} %add.96), channel_id=1, source_target_pairs={{0,16},{8,24},{16,0},{24,8},{1,17},{9,25},{17,1},{25,9},{2,18},{10... | collective-permute-start | bytes 147464 | tf_op jit(solution)/shard_map/ppermute | solution.py:660
  78.0 4.2 %collective-permute-start.17 = (f32[6,16,128]{2,1,0:T(8,128)S(1)}, f32[6,16,128]{2,1,0:T(8,128)S(1)}, u32[]{:S(2)}, u32[]{:S(2)}) collective-permute-start(f32[6,16,128]{2,1,0:T(8,128)S(1)} %add.94), channel_id=1, source_target_pairs={{0,16},{8,24},{16,0},{24,8},{1,17},{9,25},{17,1},{25,9},{2,18},{10... | collective-permute-start | bytes 147464 | tf_op jit(solution)/shard_map/ppermute | solution.py:660
  83.0 14.6 %all-to-all-start.1 = ((bf16[8,192,128]{2,1,0:T(8,128)(2,1)}), bf16[8,192,128]{2,1,0:T(8,128)(2,1)S(1)}, u32[]{:S(2)}, u32[]{:S(2)}) async-start(bf16[8,192,128]{2,1,0:T(8,128)(2,1)} %broadcast_in_dim.2), calls=%async_computation.1 | async-start | bytes 786432 | tf_op jit(solution)/shard_map/all_to_all | solution.py:677
  97.6 2.5 %collective-permute-start.20 = (bf16[8,192,128]{2,1,0:T(8,128)(2,1)S(1)}, bf16[8,192,128]{2,1,0:T(8,128)(2,1)S(1)}, u32[]{:S(2)}, u32[]{:S(2)}) collective-permute-start(bf16[8,192,128]{2,1,0:T(8,128)(2,1)S(1)} %all-to-all-done.1), channel_id=1, source_target_pairs={{0,8},{8,0},{16,24},{24,16},{1,9},{9,1},{17,25},{25,17},{2,10},{10... | collective-permute-start | bytes 1179656 | tf_op jit(solution)/shard_map/ppermute | solution.py:660

commit v5 on v4

--- a/solution.py
+++ b/solution.py
@@ -12,7 +12,7 @@
 REACH = 256
 RIM = 4
 TILE = 16
-LIMITS = (4, 14, 10, 7, 10, 8, 10, 2, 6)
+LIMITS = (4, 14, 10, 7, 10, 8, 10, 2, 6, 2, 2, 3)
 
 eps_norm = 1e-05
 highest = lax.Precision.HIGHEST
@@ -152,7 +152,7 @@
     return lambda i, j: weights[layer, i * 3 + j]
 
 
-def kernel_mix(amounts, clean_far, noise_far, mixed, clean, noise, sems):
+def kernel_mix(timestep, clean_far, noise_far, mixed, mixed_own, clean, noise, sems):
     parts = mixed.shape[0]
     copies = [
         pltpu.make_async_copy(clean_far, clean, sems.at[0]),
@@ -160,10 +160,14 @@
     ]
     for copy in copies:
         copy.start()
+    moment = jnp.full((1, clean.shape[3]), timestep[0], jnp.int32).astype(f32)
+    alpha_bar = jnp.cos(0.5 * math.pi * (moment + 0.5) / STEPS) ** 2
+    keep, add = jnp.sqrt(alpha_bar), jnp.sqrt(1.0 - alpha_bar)
     for copy in copies:
         copy.wait()
     for k in range(3):
-        noisy = amounts[0] * clean[k, 0] + amounts[1] * noise[k, 0]
+        noisy = keep * clean[k, 0] + add * noise[k, 0]
+        mixed_own[4 * k : 4 * k + 4] = noisy
         for part in range(parts):
             mixed[part, 4 * k : 4 * k + 4] = noisy
             mixed[part, 12 + 4 * k : 16 + 4 * k] = noise[k, 0]
@@ -587,7 +591,7 @@
 
 
 def kernel_last(depth, sc, padded, shifted, d_stream, normed, gains, consts, gathered, lift_in, w_back,
-                prediction, sums_bias, out_raw, own_out, out_1, out_2, out_3,
+                prediction, sums_bias, out_raw, ready0, ready1, own_out, out_1, out_2, out_3,
                 taps, taps_z, acc, acc2, high, low):
     planes, rows, lanes = d_stream.shape
     half = lanes // 2
@@ -639,11 +643,13 @@
         target[32:64] = tail
 
 
-def call(kernel, outs, scratch, flops, limit, *args, scalars=True, loose=()):
+def call(kernel, outs, scratch, flops, limit, *args, scalars=True, loose=(), ready=()):
     spec = pl.BlockSpec(memory_space=pltpu.VMEM)
     specs = [pl.BlockSpec(memory_space=pltpu.SMEM)] * scalars + [spec] * (len(args) - scalars)
+    for at in ready:
+        specs[at] = pl.BlockSpec(memory_space=pl.ANY)
     for at in loose:
-        specs[at] = pl.BlockSpec(memory_space=pl.ANY)
+        specs[at] = pl.BlockSpec(memory_space=pltpu.HBM)
     return pl.pallas_call(
         kernel,
         out_shape=[jax.ShapeDtypeStruct(shape, dtype) for shape, dtype in outs],
@@ -664,26 +670,72 @@
     return (value,) + tuple(swapped(value, "gz", bit) for bit in (1, 2, 3))
 
 
-def group_grads(keep, give):
-    mine = keep + swapped(give, "gz", 1)
-    return mine + swapped(mine, "gz", 2)
-
-
-def all_grads(first, second):
-    groups = lax.axis_size("gx")
+def kernel_spread(first, first_far, second, second_far, ready, spread):
     taps, share, channels = first.shape
-    mine = jnp.concatenate([first, second], axis=0).astype(bf16)
-    mine = mine.reshape(2 * taps * share, channels)
-    near = lax.all_to_all(jnp.broadcast_to(mine[None], (groups,) + mine.shape), "gx", 0, 0)
-    far = swapped(near, "gz", 1)
+    for layer, (own, other) in enumerate(((first, first_far), (second, second_far))):
+        value = (own[...] + other[...]).reshape(taps * share, channels).astype(bf16)
+        for part in range(spread.shape[0]):
+            spread[part, layer * taps * share : (layer + 1) * taps * share] = value
+
+
+def kernel_layout(scale, share, near, far, grad_w_z, grad_w_xy, grad_w_point):
+    groups = near.shape[0]
+    taps = near.shape[1] // share // 2
     odd = lax.rem(lax.axis_index("gz"), 2) == 1
-
-    def laid_out(every):
-        every = every.reshape(groups, 2, taps, share, channels).transpose(1, 2, 0, 3, 4)
-        return every.reshape(2, taps, groups * share, channels)
-
-    near, far = laid_out(near), laid_out(far)
-    return jnp.concatenate([jnp.where(odd, far, near), jnp.where(odd, near, far)], axis=1)
+    for layer in range(2):
+        for tap in range(taps):
+            at = (layer * taps + tap) * share
+            one = near[:, at : at + share].astype(f32) * scale
+            two = far[:, at : at + share].astype(f32) * scale
+            for side in range(2):
+                value = jnp.where(odd, one if side else two, two if side else one)
+                value = value.reshape(groups * share, value.shape[2])
+                whole = side * taps + tap
+                if whole == 4:
+                    grad_w_z[layer, 1] = value
+                elif whole < 9:
+                    grad_w_xy[layer, whole - (whole > 4)] = value
+                elif whole < 11:
+                    grad_w_z[layer, 2 * (whole - 9)] = value
+                else:
+                    grad_w_point[layer] = value
+
+
+def kernel_tail(cell_count, inv_area, *refs):
+    tails, parts1, parts2, refs = refs[:4], refs[4:8], refs[8:12], refs[12:]
+    (consts, w_in, gains, mixed, features, time_raw,
+     prediction, field_grad, grad_w_in, grad_w_time, grad_biases, grad_gains, grad_w_out) = refs
+    tail = sum(ref[...] for ref in tails)
+    s1, s2 = sum(ref[...] for ref in parts1), sum(ref[...] for ref in parts2)
+    inverse = consts[1:2]
+    m_plain = inverse * (gains[0:1] * tail[32:33] / cell_count)
+    m_cross = inverse * inverse * (gains[0:1] * tail[33:34] / cell_count)
+    at = {(0, 0): 5, (0, 1): 6, (0, 2): 7, (1, 1): 8, (1, 2): 9, (2, 2): 10}
+    rows_in = [w_in[k : k + 1] for k in range(3)]
+    depth = mixed.shape[1]
+    gaps = [mixed[4 * k : 4 * k + 4] - consts[2 + k : 3 + k, 0:1] for k in range(3)]
+    for k in range(3):
+        offset = jnp.sum(rows_in[k] * m_plain, axis=1, keepdims=True)
+        value = tail[4 * k : 4 * k + 4] - offset
+        cross = jnp.zeros_like(m_plain)
+        for j in range(3):
+            mix = jnp.sum(rows_in[k] * m_cross * rows_in[j], axis=1, keepdims=True)
+            value = value - mix * gaps[j]
+            row = at[min(j, k), max(j, k)]
+            cross = cross + consts[row : row + 1] * rows_in[j]
+        field_grad[k, 0] = value
+        prediction[k, 0] = tail[12 + 4 * k : 16 + 4 * k]
+        in_sum = tail[40 + k : 41 + k] - cell_count * (consts[2 + k : 3 + k] * m_plain + m_cross * cross)
+        grad_w_in[k : k + 1] = inv_area * in_sum
+    bias0, bias1 = tail[48:49], s1[2:3]
+    grad_biases[...] = inv_area * jnp.concatenate([bias0, bias1], axis=0)
+    grad_gains[...] = inv_area * jnp.concatenate([tail[33:34], s1[1:2], s2[1:2]], axis=0)
+    grad_w_out[...] = inv_area * tail[56:59]
+    raw = time_raw[...]
+    gate = 1.0 / (1.0 + jnp.exp(-raw))
+    back = (bias0 + bias1) * (gate * (1.0 + raw * (1.0 - gate)))
+    spread = jnp.broadcast_to(features[...], grad_w_time.shape).T
+    grad_w_time[...] = inv_area * (spread * back)
 
 
 def per_device_grouped(clean_field, noise_field, timestep, dilations, w_in, w_time, w_z, w_xy, w_point,
@@ -699,13 +751,13 @@
     cell_count = per_member * members
     inv_area = 4.0 / cell_count
 
-    alpha_bar, features, time_raw, time_code = time_terms(timestep, w_time)
+    _, features, time_raw, time_code = time_terms(timestep, w_time)
     parts = members // 2 * groups
-    mixed = call(
-        kernel_mix, [((parts, 24, depth), f32)],
+    mixed, mixed_own = call(
+        kernel_mix, [((parts, 24, depth), f32), ((12, depth), f32)],
         [(clean_field.shape, f32), (clean_field.shape, f32), pltpu.SemaphoreType.DMA((2,))], 10**5, LIMITS[7],
-        jnp.stack([jnp.sqrt(alpha_bar), jnp.sqrt(1.0 - alpha_bar)]), clean_field, noise_field, loose=(1, 2),
-    )[0]
+        timestep, clean_field, noise_field, loose=(1, 2),
+    )
     same_core = [[m * groups + g for m in range(core, members, 2) for g in range(groups)] for core in range(2)]
     near = lax.all_to_all(mixed, ("gz", "gx"), 0, 0, axis_index_groups=same_core)
     far = swapped(near, "gz", 1)
@@ -775,58 +827,48 @@
         dilations, *parts1, consts1, d_stream2, d_normed1, normed1, gains_on, act0, slope0, normed0,
         point_back,
     )
-    mine1 = group_grads(keep1, give1)
+    chip0 = keep0 + swapped(give0, "gz", 1)
+    chip1 = keep1 + swapped(give1, "gz", 1)
     last = call(
         functools.partial(kernel_last, depth),
         [((64, channels), f32)] * members,
         conv_scratch[2:] + [flat, flat, (big, bf16), (big, bf16)],
         4 * 10**9, LIMITS[6],
         dilations, rimmed0, shifted0, d_stream1, normed0, gains_on, consts0, gathered, lift_in, w_back, prediction,
-        sums_b0, out_raw,
-    )
-    every = all_grads(group_grads(keep0, give0), mine1)
-
-    tails = last[0] + sum(swapped(last[bit], "gz", bit) for bit in (1, 2, 3))
-    s_plain, s_cross, in_sum = tails[32], tails[33], tails[40:43]
-    bias0, out_sum = tails[48], tails[56:59]
-    s1 = sum(members_of(parts1))
-    s2 = sum(members_of(parts2))
-    inverse = consts0[1]
-    m_plain = norm_gains[0] * s_plain / cell_count
-    m_cross = norm_gains[0] * s_cross / cell_count
-    mean_k = consts0[2:5, 0]
-    c00, c01, c02, c11, c12, c22 = (consts0[5 + at, 0] for at in range(6))
-    cov = jnp.stack([jnp.stack([c00, c01, c02]), jnp.stack([c01, c11, c12]), jnp.stack([c02, c12, c22])])
-    offset = jnp.sum(w_in * (inverse * m_plain), axis=1)
-    mix = jnp.sum(w_in[:, None, :] * (inverse * inverse * m_cross) * w_in[None, :, :], axis=2)
-    landed = tails[:24].reshape(6, 1, 4, depth)
-    centered = mixed[0, :12].reshape(3, 1, 4, depth) - mean_k[:, None, None, None]
-    field_grad = landed[:3] - offset[:, None, None, None] - sum(
-        mix[:, j, None, None, None] * centered[j][None] for j in range(3)
-    )
-    prediction_out = landed[3:]
-    cross_in = jnp.sum(cov[:, :, None] * w_in[None, :, :], axis=1)
-    in_raw = in_sum - cell_count * (
-        mean_k[:, None] * (inverse * m_plain) + (inverse * inverse * m_cross) * cross_in
-    )
-    bias_all = jnp.stack([bias0, s1[2]])
-    gain_all = jnp.stack([s_cross, s1[1], s2[1]])
-    weights = every.astype(f32) * inv_area
-    z_all = jnp.stack([weights[:, 9], weights[:, 4], weights[:, 10]], axis=1)
-    xy_all = jnp.concatenate([weights[:, :4], weights[:, 5:9]], axis=1)
-    time_back = jax.vjp(jax.nn.silu, time_raw)[1](jnp.sum(bias_all, axis=0))[0]
-    grad_w_time = inv_area * jnp.outer(features, time_back)
+        sums_b0, out_raw, chip0, chip1, ready=(13, 14),
+    )
+    spread = call(
+        kernel_spread, [((groups, 12 * share, channels), bf16)], [], 10**5, LIMITS[9],
+        chip0, swapped(chip0, "gz", 2), chip1, swapped(chip1, "gz", 2), last[0], scalars=False, ready=(4,),
+    )[0]
+    near_grads = lax.all_to_all(spread, "gx", 0, 0)
+
+    prediction, field_grad, grad_w_in, grad_w_time, grad_biases, grad_gains, grad_w_out = call(
+        functools.partial(kernel_tail, cell_count, inv_area),
+        [(clean_field.shape, f32), (clean_field.shape, f32), ((3, channels), f32), (w_time.shape, f32),
+         ((2, channels), f32), ((3, channels), f32), ((3, channels), f32)],
+        [], 10**6, LIMITS[10],
+        last[0], *(swapped(last[bit], "gz", bit) for bit in (1, 2, 3)), *parts1, *parts2, consts0, w_in_on,
+        gains_on, mixed_own, features[None], time_raw[None], scalars=False,
+    )
+    tied, _ = lax.optimization_barrier((near_grads, field_grad))
+    far_grads = swapped(tied, "gz", 1)
+    grad_w_z, grad_w_xy, grad_w_point = call(
+        functools.partial(kernel_layout, inv_area, share),
+        [(w_z.shape, f32), (w_xy.shape, f32), (w_point.shape, f32)],
+        [], 10**6, LIMITS[11], near_grads, far_grads, scalars=False,
+    )
     return (
-        prediction_out,
+        prediction,
         field_grad,
-        inv_area * in_raw,
+        grad_w_in,
         grad_w_time,
-        z_all,
-        xy_all,
-        weights[:, 11],
-        inv_area * bias_all,
-        inv_area * gain_all,
-        inv_area * out_sum,
+        grad_w_z,
+        grad_w_xy,
+        grad_w_point,
+        grad_biases,
+        grad_gains,
+        grad_w_out,
     )
 
 

time: 104 us -> 89.5 us (0.86)
  other arithmetic: 13.2 us -> 0.82 us
  local copies, waits for them, and re-layouts: 10.7 us -> 6.89 us
  Pallas kernels: 31.3 us -> 34 us
    another operation x8 -> x0, other arithmetic: 6.92 us -> none  [the longest x4 6.05 us: per_device_grouped(): jnp.stack([jnp.stack([c00, c01, c02]), jnp.stack([c01, c11, c12]), jnp.st...]
    mul x5 -> x0, other arithmetic: 2.7 us -> none  [the longest x1 0.71 us: per_device_grouped(): grad_w_time = inv_area * jnp.outer(features, time_back)]
    pallas_call x9 -> x12, Pallas kernels: 31.3 us -> 34 us  [call(): pl.pallas_call(kernel, out_shape=[jax.ShapeDtypeStruct(shape, dtype) for...]
    all_to_all x1, waiting for transfers between devices: 9.03 us -> 6.48 us  [per_device_grouped(): near_grads = lax.all_to_all(spread, 'gx', 0, 0)]
    ppermute x21, waiting for transfers between devices: 9.43 us -> 11.8 us  [swapped(): return lax.ppermute(value, axis, [(i, i ^ bit) for i in range(count)])]
    slice x11 -> x0, local copies, waits for them, and re-layouts: 2.25 us -> none  [the longest x1 0.7 us: per_device_grouped(): mixed[0, :12].reshape(3, 1, 4, depth) - mean_k[:, None, None, None]]
    concatenate x3 -> x0, other arithmetic: 1.13 us -> none  [the longest x1 1.04 us: per_device_grouped(): xy_all = jnp.concatenate([weights[:, :4], weights[:, 5:9]], axis=1)]
    unnamed x24 -> x22, local copies, waits for them, and re-layouts: 6.9 us -> 6.89 us
  transfers between devices with their start and end apart: 23 -> 23, of which waited for: 10 -> 12; matrix products, arithmetic and copies ran while one was open for 12% -> 1% of each run, Pallas kernels for 11% -> 14%
where the time goes in v5:
time: 89.5 us; the launch traced here: 88.8 us
  Pallas kernels  34 us (38%)
  starting transfers between devices  24.2 us (27%)
  waiting for transfers between devices  21.2 us (24%)
  local copies, waits for them, and re-layouts  6.89 us (8%)
  between operations  1.53 us (2%)
    pallas_call x12, Pallas kernels, call(): pl.pallas_call(kernel, out_shape=[jax.ShapeDtypeStruct(shape, dtype) for...  34 us
    ppermute x21, starting transfers between devices, swapped(): return lax.ppermute(value, axis, [(i, i ^ bit) for i in range(count)])  12.4 us
    ppermute x21, waiting for transfers between devices, swapped(): return lax.ppermute(value, axis, [(i, i ^ bit) for i in range(count)])  11.8 us
    all_to_all x1, starting transfers between devices, per_device_grouped(): lax.all_to_all(mixed, ('gz', 'gx'), 0, 0, axis_index_groups=same_core)  8.32 us
    unnamed x22, local copies, waits for them, and re-layouts  6.89 us
    all_to_all x1, waiting for transfers between devices, per_device_grouped(): near_grads = lax.all_to_all(spread, 'gx', 0, 0)  6.48 us
    all_to_all x1, starting transfers between devices, per_device_grouped(): near_grads = lax.all_to_all(spread, 'gx', 0, 0)  3.45 us
    all_to_all x1, waiting for transfers between devices, per_device_grouped(): lax.all_to_all(mixed, ('gz', 'gx'), 0, 0, axis_index_groups=same_core)  2.94 us
  transfers between devices with their start and end apart: 23, of which 12 were waited for; matrix products, arithmetic and copies ran while one was open for 1% of the time, Pallas kernels for 14%

profile of v5, /device:TPU:0, one launch (start us, length us, event | category | flops | bytes accessed | tf_op | source)
XLA Modules:
  0.0 88.8 jit_solution(2249880661635023684)
XLA Ops:
  1.3 0.7 copy-done.4
  2.0 0.7 copy-done.5
  2.7 0.8 shard_map.195
  3.5 8.3 %all-to-all-start = ((f32[16,24,128]{2,1,0:T(8,128)}), f32[16,24,128]{2,1,0:T(8,128)S(1)}, u32[]{:S(2)}, u32[]{:S(2)}) async-start(f32[16,24,128]{2,1,0:T(8,128)} %get-tuple-element.67), calls=%async_computation | async-start | bytes 393216 | tf_op jit(solution)/shard_map/all_to_all | solution.py:762
  11.9 1.0 %copy-done.1 = bf16[2,8,128,128]{3,2,1,0:T(8,128)(2,1)S(1)} copy-done((bf16[2,8,128,128]{3,2,1,0:T(8,128)(2,1)S(1)}, bf16[2,8,128,128]{3,2,1,0:T(8,128)(2,1)}, u32[]{:S(2)}) %copy-start.1) | copy-done | bytes 524312
  12.9 0.9 %copy-done.2 = bf16[2,3,128,128]{3,2,1,0:T(8,128)(2,1)S(1)} copy-done((bf16[2,3,128,128]{3,2,1,0:T(8,128)(2,1)S(1)}, bf16[2,3,128,128]{3,2,1,0:T(8,128)(2,1)}, u32[]{:S(2)}) %copy-start.2) | copy-done | bytes 196632
  13.8 0.8 copy-done.3
  14.7 0.7 copy-done.6
  15.3 0.7 copy-done.7
  16.0 0.7 copy-done.8
  17.3 2.9 %all-to-all-done.near = f32[16,24,128]{2,1,0:T(8,128)S(1)} async-done(((f32[16,24,128]{2,1,0:T(8,128)}), f32[16,24,128]{2,1,0:T(8,128)S(1)}, u32[]{:S(2)}, u32[]{:S(2)}) %all-to-all-start) | async-done | bytes 196640 | tf_op jit(solution)/shard_map/all_to_all | solution.py:762
  20.2 0.7 broadcast_add_fusion.shift_bias.refs_6_
  20.9 0.8 collective-permute-done.far
  21.7 0.7 copy-done.9
  22.3 6.3 %shard_map.197 = (f32[8,144,512]{2,1,0:T(8,128)S(1)}, bf16[8,144,512]{2,1,0:T(8,128)(2,1)S(1)}, bf16[8,144,512]{2,1,0:T(8,128)(2,1)S(1)}, bf16[8,144,512]{2,1,0:...) custom-call(s32[2]{0:T(128)S(1)} %copy-done.9, ...), custom_call_target="tpu_custom_call" | custom-call | flops 4000000000 | bytes 8388608 | tf_op jit(solution)/shard_map/pallas_call | solution.py:653
  28.6 1.1 %collective-permute-start.3 = (f32[8,128]{1,0:T(8,128)S(1)}, f32[8,128]{1,0:T(8,128)S(1)}, u32[]{:S(2)}, u32[]{:S(2)}) collective-permute-start(f32[8,128]{1,0:T(8,128)S(1)} %get-tuple-element.73.refs_0_), channel_id=1, source_target_pairs={{0,24},{8,16},{16,8},{24,0},{1,25},{9,17},{17,9},{25,1},{2,26},{10... | collective-permute-start | bytes 12296 | tf_op jit(solution)/shard_map/ppermute | solution.py:666
  29.7 0.8 collective-permute-start.2
  30.6 1.2 %collective-permute-done.3.refs_3_ = f32[8,128]{1,0:T(8,128)S(1)} collective-permute-done((f32[8,128]{1,0:T(8,128)S(1)}, f32[8,128]{1,0:T(8,128)S(1)}, u32[]{:S(2)}, u32[]{:S(2)}) %collective-permute-start.3) | collective-permute-done | bytes 4128 | tf_op jit(solution)/shard_map/ppermute | solution.py:666
  31.7 1.6 %collective-permute-done.2.refs_2_ = f32[8,128]{1,0:T(8,128)S(1)} collective-permute-done((f32[8,128]{1,0:T(8,128)S(1)}, f32[8,128]{1,0:T(8,128)S(1)}, u32[]{:S(2)}, u32[]{:S(2)}) %collective-permute-start.2) | collective-permute-done | bytes 4128 | tf_op jit(solution)/shard_map/ppermute | solution.py:666
  33.3 5.4 %shard_map.198 = (f32[8,144,512]{2,1,0:T(8,128)S(1)}, bf16[8,144,512]{2,1,0:T(8,128)(2,1)S(1)}, bf16[8,144,512]{2,1,0:T(8,128)(2,1)S(1)}, bf16[8,144,512]{2,1,0:...) custom-call(s32[2]{0:T(128)S(1)} %copy-done.9, f32[8,128]{1,0:T(8,128)S(1)} %get-tuple-element.73.refs_0_, ...), custom_call_target="tpu_custom_call" | custom-call | flops 4000000000 | bytes 8388608 | tf_op jit(solution)/shard_map/pallas_call | solution.py:653
  38.8 0.9 collective-permute-start.5
  39.7 1.0 %collective-permute-start.4 = (f32[8,128]{1,0:T(8,128)S(1)}, f32[8,128]{1,0:T(8,128)S(1)}, u32[]{:S(2)}, u32[]{:S(2)}) collective-permute-start(f32[8,128]{1,0:T(8,128)S(1)} %get-tuple-element.75.refs_0_), channel_id=1, source_target_pairs={{0,8},{8,0},{16,24},{24,16},{1,9},{9,1},{17,25},{25,17},{2,10},{10... | collective-permute-start | bytes 12296 | tf_op jit(solution)/shard_map/ppermute | solution.py:666
  40.7 1.2 %collective-permute-done.6.refs_3_ = f32[8,128]{1,0:T(8,128)S(1)} collective-permute-done((f32[8,128]{1,0:T(8,128)S(1)}, f32[8,128]{1,0:T(8,128)S(1)}, u32[]{:S(2)}, u32[]{:S(2)}) %collective-permute-start.6) | collective-permute-done | bytes 4128 | tf_op jit(solution)/shard_map/ppermute | solution.py:666
  41.8 0.7 collective-permute-done.5.refs_2_
  42.5 2.3 %shard_map.199 = (f32[144,128]{1,0:T(8,128)S(1)}, bf16[8,144,128]{2,1,0:T(8,128)(2,1)S(1)}, f32[8,128]{1,0:T(8,128)S(1)}, f32[8,128]{1,0:T(8,128)S(1)}, f32[8,128]{1,0:T(8,128)S(1)}) custom-call(s32[2]{0:T(128)S(1)} %copy-done.9, f32[8,128]{1,0:T(8,128)S(1)} %get-tuple-element.75.refs_0_, f32[8,128]{1,0:T(8,128)S(1)} %collective-permute-done.4.refs_1_, ...), custom_call_target="tpu_custom_call" | custom-call | flops 1000000000 | bytes 8388608 | tf_op jit(solution)/shard_map/pallas_call | solution.py:653
  44.8 0.6 collective-permute-start.9
  45.4 0.8 collective-permute-start.8
  46.2 0.5 collective-permute-start.7
  46.7 1.2 %collective-permute-done.9.refs_3_.refs_11_ = f32[8,128]{1,0:T(8,128)S(1)} collective-permute-done((f32[8,128]{1,0:T(8,128)S(1)}, f32[8,128]{1,0:T(8,128)S(1)}, u32[]{:S(2)}, u32[]{:S(2)}) %collective-permute-start.9) | collective-permute-done | bytes 4128 | tf_op jit(solution)/shard_map/ppermute | solution.py:666
  47.9 1.1 %collective-permute-done.8.refs_2_.refs_10_ = f32[8,128]{1,0:T(8,128)S(1)} collective-permute-done((f32[8,128]{1,0:T(8,128)S(1)}, f32[8,128]{1,0:T(8,128)S(1)}, u32[]{:S(2)}, u32[]{:S(2)}) %collective-permute-start.8) | collective-permute-done | bytes 4128 | tf_op jit(solution)/shard_map/ppermute | solution.py:666
  49.0 4.9 %shard_map.200 = (f32[8,144,512]{2,1,0:T(8,128)S(1)}, f32[8,144,512]{2,1,0:T(8,128)S(1)}, f32[8,128]{1,0:T(8,128)S(1)}, bf16[10,144,512]{2,1,0:T(8,128)(2,1)S(1)...) custom-call(s32[2]{0:T(128)S(1)} %copy-done.10, ...), custom_call_target="tpu_custom_call" | custom-call | flops 6000000000 | bytes 8388608 | tf_op jit(solution)/shard_map/pallas_call | solution.py:653
  54.1 0.8 collective-permute-start.11
  54.9 0.9 %collective-permute-start.10 = (f32[8,128]{1,0:T(8,128)S(1)}, f32[8,128]{1,0:T(8,128)S(1)}, u32[]{:S(2)}, u32[]{:S(2)}) collective-permute-start(f32[8,128]{1,0:T(8,128)S(1)} %get-tuple-element.86.refs_0_.refs_4_), channel_id=1, source_target_pairs={{0,8},{8,0},{16,24},{24,16},{1,9},{9,1},{17,25},{25,17},{2,10},{10... | collective-permute-start | bytes 12296 | tf_op jit(solution)/shard_map/ppermute | solution.py:666
  55.9 2.8 %shard_map.202 = (f32[6,16,128]{2,1,0:T(8,128)S(1)}, f32[6,16,128]{2,1,0:T(8,128)S(1)}) custom-call(s32[2]{0:T(128)S(1)} %copy-done.10, bf16[10,144,512]{2,1,0:T(8,128)(2,1)S(1)} %get-tuple-element.102.padded, bf16[2,8,144,512]{3,2,1,0:T(8,128)(2,1)S(1)} %get-tuple-element.103.shifted, bf16[8,144,512]{2,1,0:T(8,128)(2,1)S(1)} %get-tuple-element.104.scot, ...), custom_call_target="tpu_custom_call" | custom-call | flops 2000000000 | bytes 8388608 | tf_op jit(solution)/shard_map/pallas_call | solution.py:653
  58.8 3.9 %shard_map.201 = (f32[8,144,512]{2,1,0:T(8,128)S(1)}, f32[8,128]{1,0:T(8,128)S(1)}, f32[6,16,128]{2,1,0:T(8,128)S(1)}, f32[6,16,128]{2,1,0:T(8,128)S(1)}, bf16[1...) custom-call(s32[2]{0:T(128)S(1)} %copy-done.10, f32[8,128]{1,0:T(8,128)S(1)} %get-tuple-element.86.refs_0_.refs_4_, ...), custom_call_target="tpu_custom_call" | custom-call | flops 4000000000 | bytes 8388608 | tf_op jit(solution)/shard_map/pallas_call | solution.py:653
  62.7 0.6 collective-permute-start.13
  63.3 0.9 collective-permute-start.19
  64.2 1.3 %collective-permute-start.18 = (f32[6,16,128]{2,1,0:T(8,128)S(1)}, f32[6,16,128]{2,1,0:T(8,128)S(1)}, u32[]{:S(2)}, u32[]{:S(2)}) collective-permute-start(f32[6,16,128]{2,1,0:T(8,128)S(1)} %add.21.ready0.first), channel_id=1, source_target_pairs={{0,16},{8,24},{16,0},{24,8},{1,17},{9,25},{17,1},{25,9},{2,18},{10... | collective-permute-start | bytes 147464 | tf_op jit(solution)/shard_map/ppermute | solution.py:666
  65.4 4.4 %shard_map.203 = (f32[64,128]{1,0:T(8,128)S(1)}, f32[64,128]{1,0:T(8,128)S(1)}, f32[64,128]{1,0:T(8,128)S(1)}, f32[64,128]{1,0:T(8,128)S(1)}) custom-call(s32[2]{0:T(128)S(1)} %copy-done.10, bf16[10,144,512]{2,1,0:T(8,128)(2,1)S(1)} %get-tuple-element.93.padded, bf16[2,8,144,512]{3,2,1,0:T(8,128)(2,1)S(1)} %get-tuple-element.94.shifted, ...), custom_call_target="tpu_custom_call" | custom-call | flops 4000000000 | bytes 8388608 | tf_op jit(solution)/shard_map/pallas_call | solution.py:653
  69.9 0.8 shard_map.205
  70.6 3.5 %all-to-all-start.1 = ((bf16[8,192,128]{2,1,0:T(8,128)(2,1)}), bf16[8,192,128]{2,1,0:T(8,128)(2,1)S(1)}, u32[]{:S(2)}, u32[]{:S(2)}) async-start(bf16[8,192,128]{2,1,0:T(8,128)(2,1)} %shard_map.205), calls=%async_computation.1 | async-start | bytes 786432 | tf_op jit(solution)/shard_map/all_to_all | solution.py:844
  74.2 1.1 %collective-permute-start.16 = (f32[64,128]{1,0:T(8,128)S(1)}, f32[64,128]{1,0:T(8,128)S(1)}, u32[]{:S(2)}, u32[]{:S(2)}) collective-permute-start(f32[64,128]{1,0:T(8,128)S(1)} %get-tuple-element.110), channel_id=1, source_target_pairs={{0,16},{8,24},{16,0},{24,8},{1,17},{9,25},{17,1},{25,9},{2,18},{10... | collective-permute-start | bytes 98312 | tf_op jit(solution)/shard_map/ppermute | solution.py:666
  75.2 0.8 collective-permute-start.17
  76.1 2.0 %collective-permute-done.16.refs_2_ = f32[64,128]{1,0:T(8,128)S(1)} collective-permute-done((f32[64,128]{1,0:T(8,128)S(1)}, f32[64,128]{1,0:T(8,128)S(1)}, u32[]{:S(2)}, u32[]{:S(2)}) %collective-permute-start.16) | collective-permute-done | bytes 32800 | tf_op jit(solution)/shard_map/ppermute | solution.py:666
  78.6 0.8 shard_map.204
  79.4 6.5 %all-to-all-done.1.near = bf16[8,192,128]{2,1,0:T(8,128)(2,1)S(1)} async-done(((bf16[8,192,128]{2,1,0:T(8,128)(2,1)}), bf16[8,192,128]{2,1,0:T(8,128)(2,1)S(1)}, u32[]{:S(2)}, u32[]{:S(2)}) %all-to-all-start.1) | async-done | bytes 393248 | tf_op jit(solution)/shard_map/all_to_all | solution.py:844
  85.9 1.7 %collective-permute-done.20.far = bf16[8,192,128]{2,1,0:T(8,128)(2,1)S(1)} collective-permute-done((bf16[8,192,128]{2,1,0:T(8,128)(2,1)S(1)}, bf16[8,192,128]{2,1,0:T(8,128)(2,1)S(1)}, u32[]{:S(2)}, u32[]{:S(2)}) %collective-permute-start.20) | collective-permute-done | bytes 393248 | tf_op jit(solution)/shard_map/ppermute | solution.py:666
  87.6 1.3 %shard_map.206 = (f32[2,3,128,128]{3,2,1,0:T(8,128)}, f32[2,8,128,128]{3,2,1,0:T(8,128)}, f32[2,128,128]{2,1,0:T(8,128)}) custom-call(bf16[8,192,128]{2,1,0:T(8,128)(2,1)S(1)} %all-to-all-done.1.near, bf16[8,192,128]{2,1,0:T(8,128)(2,1)S(1)} %collective-permute-done.20.far), custom_call_target="tpu_custom_call" | custom-call | flops 1000000 | bytes 8388608 | tf_op jit(solution)/shard_map/pallas_call | solution.py:653
  (38 shorter events, 1.6 us)
Async XLA Ops:
  0.6 16.4 %copy-start = (f32[128,128]{1,0:T(8,128)S(1)}, f32[128,128]{1,0:T(8,128)}, u32[]{:S(2)}) copy-start(f32[128,128]{1,0:T(8,128)} %param.17) | copy-start | bytes 196612
  1.3 0.7 copy-start.4
  2.0 0.7 copy-start.5
  3.5 16.7 %all-to-all-start = ((f32[16,24,128]{2,1,0:T(8,128)}), f32[16,24,128]{2,1,0:T(8,128)S(1)}, u32[]{:S(2)}, u32[]{:S(2)}) async-start(f32[16,24,128]{2,1,0:T(8,128)} %get-tuple-element.67), calls=%async_computation | async-start | bytes 393216 | tf_op jit(solution)/shard_map/all_to_all | solution.py:762
  11.8 1.0 %copy-start.1 = (bf16[2,8,128,128]{3,2,1,0:T(8,128)(2,1)S(1)}, bf16[2,8,128,128]{3,2,1,0:T(8,128)(2,1)}, u32[]{:S(2)}) copy-start(bf16[2,8,128,128]{3,2,1,0:T(8,128)(2,1)} %w_xy.1) | copy-start | bytes 1572868
  12.9 0.9 %copy-start.2 = (bf16[2,3,128,128]{3,2,1,0:T(8,128)(2,1)S(1)}, bf16[2,3,128,128]{3,2,1,0:T(8,128)(2,1)}, u32[]{:S(2)}) copy-start(bf16[2,3,128,128]{3,2,1,0:T(8,128)(2,1)} %w_z.1) | copy-start | bytes 589828
  13.8 0.8 copy-start.3
  14.7 0.7 copy-start.6
  15.3 0.7 copy-start.7
  16.0 0.7 copy-start.8
  20.2 1.4 %collective-permute-start = (f32[16,24,128]{2,1,0:T(8,128)S(1)}, f32[16,24,128]{2,1,0:T(8,128)S(1)}, u32[]{:S(2)}, u32[]{:S(2)}) collective-permute-start(f32[16,24,128]{2,1,0:T(8,128)S(1)} %all-to-all-done.near), channel_id=1, source_target_pairs={{0,8},{8,0},{16,24},{24,16},{1,9},{9,1},{17,25},{25,17},{2,10},{10... | collective-permute-start | bytes 589832 | tf_op jit(solution)/shard_map/ppermute | solution.py:666
  21.7 0.7 copy-start.9
  28.6 3.1 %collective-permute-start.3 = (f32[8,128]{1,0:T(8,128)S(1)}, f32[8,128]{1,0:T(8,128)S(1)}, u32[]{:S(2)}, u32[]{:S(2)}) collective-permute-start(f32[8,128]{1,0:T(8,128)S(1)} %get-tuple-element.73.refs_0_), channel_id=1, source_target_pairs={{0,24},{8,16},{16,8},{24,0},{1,25},{9,17},{17,9},{25,1},{2,26},{10... | collective-permute-start | bytes 12296 | tf_op jit(solution)/shard_map/ppermute | solution.py:666
  29.7 3.6 %collective-permute-start.2 = (f32[8,128]{1,0:T(8,128)S(1)}, f32[8,128]{1,0:T(8,128)S(1)}, u32[]{:S(2)}, u32[]{:S(2)}) collective-permute-start(f32[8,128]{1,0:T(8,128)S(1)} %get-tuple-element.73.refs_0_), channel_id=1, source_target_pairs={{0,16},{8,24},{16,0},{24,8},{1,17},{9,25},{17,1},{25,9},{2,18},{10... | collective-permute-start | bytes 12296 | tf_op jit(solution)/shard_map/ppermute | solution.py:666
  30.5 2.8 %collective-permute-start.1 = (f32[8,128]{1,0:T(8,128)S(1)}, f32[8,128]{1,0:T(8,128)S(1)}, u32[]{:S(2)}, u32[]{:S(2)}) collective-permute-start(f32[8,128]{1,0:T(8,128)S(1)} %get-tuple-element.73.refs_0_), channel_id=1, source_target_pairs={{0,8},{8,0},{16,24},{24,16},{1,9},{9,1},{17,25},{25,17},{2,10},{10... | collective-permute-start | bytes 12296 | tf_op jit(solution)/shard_map/ppermute | solution.py:666
  38.7 3.1 %collective-permute-start.6 = (f32[8,128]{1,0:T(8,128)S(1)}, f32[8,128]{1,0:T(8,128)S(1)}, u32[]{:S(2)}, u32[]{:S(2)}) collective-permute-start(f32[8,128]{1,0:T(8,128)S(1)} %get-tuple-element.75.refs_0_), channel_id=1, source_target_pairs={{0,24},{8,16},{16,8},{24,0},{1,25},{9,17},{17,9},{25,1},{2,26},{10... | collective-permute-start | bytes 12296 | tf_op jit(solution)/shard_map/ppermute | solution.py:666
  38.8 3.7 %collective-permute-start.5 = (f32[8,128]{1,0:T(8,128)S(1)}, f32[8,128]{1,0:T(8,128)S(1)}, u32[]{:S(2)}, u32[]{:S(2)}) collective-permute-start(f32[8,128]{1,0:T(8,128)S(1)} %get-tuple-element.75.refs_0_), channel_id=1, source_target_pairs={{0,16},{8,24},{16,0},{24,8},{1,17},{9,25},{17,1},{25,9},{2,18},{10... | collective-permute-start | bytes 12296 | tf_op jit(solution)/shard_map/ppermute | solution.py:666
  39.7 2.8 %collective-permute-start.4 = (f32[8,128]{1,0:T(8,128)S(1)}, f32[8,128]{1,0:T(8,128)S(1)}, u32[]{:S(2)}, u32[]{:S(2)}) collective-permute-start(f32[8,128]{1,0:T(8,128)S(1)} %get-tuple-element.75.refs_0_), channel_id=1, source_target_pairs={{0,8},{8,0},{16,24},{24,16},{1,9},{9,1},{17,25},{25,17},{2,10},{10... | collective-permute-start | bytes 12296 | tf_op jit(solution)/shard_map/ppermute | solution.py:666
  42.5 6.5 %copy-start.10 = (s32[2]{0:T(128)S(1)}, s32[2]{0:T(128)}, u32[]{:S(2)}) copy-start(s32[2]{0:T(128)} %sc.13) | copy-start | bytes 28
  44.8 3.1 %collective-permute-start.9 = (f32[8,128]{1,0:T(8,128)S(1)}, f32[8,128]{1,0:T(8,128)S(1)}, u32[]{:S(2)}, u32[]{:S(2)}) collective-permute-start(f32[8,128]{1,0:T(8,128)S(1)} %get-tuple-element.79.refs_0_.refs_8_), channel_id=1, source_target_pairs={{0,24},{8,16},{16,8},{24,0},{1,25},{9,17},{17,9},{25,1},{2,26},{10... | collective-permute-start | bytes 12296 | tf_op jit(solution)/shard_map/ppermute | solution.py:666
  45.4 3.6 %collective-permute-start.8 = (f32[8,128]{1,0:T(8,128)S(1)}, f32[8,128]{1,0:T(8,128)S(1)}, u32[]{:S(2)}, u32[]{:S(2)}) collective-permute-start(f32[8,128]{1,0:T(8,128)S(1)} %get-tuple-element.79.refs_0_.refs_8_), channel_id=1, source_target_pairs={{0,16},{8,24},{16,0},{24,8},{1,17},{9,25},{17,1},{25,9},{2,18},{10... | collective-permute-start | bytes 12296 | tf_op jit(solution)/shard_map/ppermute | solution.py:666
  46.2 2.8 %collective-permute-start.7 = (f32[8,128]{1,0:T(8,128)S(1)}, f32[8,128]{1,0:T(8,128)S(1)}, u32[]{:S(2)}, u32[]{:S(2)}) collective-permute-start(f32[8,128]{1,0:T(8,128)S(1)} %get-tuple-element.79.refs_0_.refs_8_), channel_id=1, source_target_pairs={{0,8},{8,0},{16,24},{24,16},{1,9},{9,1},{17,25},{25,17},{2,10},{10... | collective-permute-start | bytes 12296 | tf_op jit(solution)/shard_map/ppermute | solution.py:666
  54.0 4.8 %collective-permute-start.12 = (f32[8,128]{1,0:T(8,128)S(1)}, f32[8,128]{1,0:T(8,128)S(1)}, u32[]{:S(2)}, u32[]{:S(2)}) collective-permute-start(f32[8,128]{1,0:T(8,128)S(1)} %get-tuple-element.86.refs_0_.refs_4_), channel_id=1, source_target_pairs={{0,24},{8,16},{16,8},{24,0},{1,25},{9,17},{17,9},{25,1},{2,26},{10... | collective-permute-start | bytes 12296 | tf_op jit(solution)/shard_map/ppermute | solution.py:666
  54.1 4.7 %collective-permute-start.11 = (f32[8,128]{1,0:T(8,128)S(1)}, f32[8,128]{1,0:T(8,128)S(1)}, u32[]{:S(2)}, u32[]{:S(2)}) collective-permute-start(f32[8,128]{1,0:T(8,128)S(1)} %get-tuple-element.86.refs_0_.refs_4_), channel_id=1, source_target_pairs={{0,16},{8,24},{16,0},{24,8},{1,17},{9,25},{17,1},{25,9},{2,18},{10... | collective-permute-start | bytes 12296 | tf_op jit(solution)/shard_map/ppermute | solution.py:666
  54.9 3.9 %collective-permute-start.10 = (f32[8,128]{1,0:T(8,128)S(1)}, f32[8,128]{1,0:T(8,128)S(1)}, u32[]{:S(2)}, u32[]{:S(2)}) collective-permute-start(f32[8,128]{1,0:T(8,128)S(1)} %get-tuple-element.86.refs_0_.refs_4_), channel_id=1, source_target_pairs={{0,8},{8,0},{16,24},{24,16},{1,9},{9,1},{17,25},{25,17},{2,10},{10... | collective-permute-start | bytes 12296 | tf_op jit(solution)/shard_map/ppermute | solution.py:666
  58.7 4.6 %collective-permute-start.14 = (f32[6,16,128]{2,1,0:T(8,128)S(1)}, f32[6,16,128]{2,1,0:T(8,128)S(1)}, u32[]{:S(2)}, u32[]{:S(2)}) collective-permute-start(f32[6,16,128]{2,1,0:T(8,128)S(1)} %get-tuple-element.107), channel_id=1, source_target_pairs={{0,8},{8,0},{16,24},{24,16},{1,9},{9,1},{17,25},{25,17},{2,10},{10... | collective-permute-start | bytes 147464 | tf_op jit(solution)/shard_map/ppermute | solution.py:666
  62.7 1.4 %collective-permute-start.13 = (f32[6,16,128]{2,1,0:T(8,128)S(1)}, f32[6,16,128]{2,1,0:T(8,128)S(1)}, u32[]{:S(2)}, u32[]{:S(2)}) collective-permute-start(f32[6,16,128]{2,1,0:T(8,128)S(1)} %get-tuple-element.101), channel_id=1, source_target_pairs={{0,8},{8,0},{16,24},{24,16},{1,9},{9,1},{17,25},{25,17},{2,10},{10... | collective-permute-start | bytes 147464 | tf_op jit(solution)/shard_map/ppermute | solution.py:666
  63.3 6.6 %collective-permute-start.19 = (f32[6,16,128]{2,1,0:T(8,128)S(1)}, f32[6,16,128]{2,1,0:T(8,128)S(1)}, u32[]{:S(2)}, u32[]{:S(2)}) collective-permute-start(f32[6,16,128]{2,1,0:T(8,128)S(1)} %add.22.ready1.second), channel_id=1, source_target_pairs={{0,16},{8,24},{16,0},{24,8},{1,17},{9,25},{17,1},{25,9},{2,18},{10... | collective-permute-start | bytes 147464 | tf_op jit(solution)/shard_map/ppermute | solution.py:666
  64.2 5.7 %collective-permute-start.18 = (f32[6,16,128]{2,1,0:T(8,128)S(1)}, f32[6,16,128]{2,1,0:T(8,128)S(1)}, u32[]{:S(2)}, u32[]{:S(2)}) collective-permute-start(f32[6,16,128]{2,1,0:T(8,128)S(1)} %add.21.ready0.first), channel_id=1, source_target_pairs={{0,16},{8,24},{16,0},{24,8},{1,17},{9,25},{17,1},{25,9},{2,18},{10... | collective-permute-start | bytes 147464 | tf_op jit(solution)/shard_map/ppermute | solution.py:666
  70.6 15.2 %all-to-all-start.1 = ((bf16[8,192,128]{2,1,0:T(8,128)(2,1)}), bf16[8,192,128]{2,1,0:T(8,128)(2,1)S(1)}, u32[]{:S(2)}, u32[]{:S(2)}) async-start(bf16[8,192,128]{2,1,0:T(8,128)(2,1)} %shard_map.205), calls=%async_computation.1 | async-start | bytes 786432 | tf_op jit(solution)/shard_map/all_to_all | solution.py:844
  74.1 2.0 %collective-permute-start.15 = (f32[64,128]{1,0:T(8,128)S(1)}, f32[64,128]{1,0:T(8,128)S(1)}, u32[]{:S(2)}, u32[]{:S(2)}) collective-permute-start(f32[64,128]{1,0:T(8,128)S(1)} %get-tuple-element.109), channel_id=1, source_target_pairs={{0,8},{8,0},{16,24},{24,16},{1,9},{9,1},{17,25},{25,17},{2,10},{10... | collective-permute-start | bytes 98312 | tf_op jit(solution)/shard_map/ppermute | solution.py:666
  74.2 4.0 %collective-permute-start.16 = (f32[64,128]{1,0:T(8,128)S(1)}, f32[64,128]{1,0:T(8,128)S(1)}, u32[]{:S(2)}, u32[]{:S(2)}) collective-permute-start(f32[64,128]{1,0:T(8,128)S(1)} %get-tuple-element.110), channel_id=1, source_target_pairs={{0,16},{8,24},{16,0},{24,8},{1,17},{9,25},{17,1},{25,9},{2,18},{10... | collective-permute-start | bytes 98312 | tf_op jit(solution)/shard_map/ppermute | solution.py:666
  75.2 3.4 %collective-permute-start.17 = (f32[64,128]{1,0:T(8,128)S(1)}, f32[64,128]{1,0:T(8,128)S(1)}, u32[]{:S(2)}, u32[]{:S(2)}) collective-permute-start(f32[64,128]{1,0:T(8,128)S(1)} %get-tuple-element.111), channel_id=1, source_target_pairs={{0,24},{8,16},{16,8},{24,0},{1,25},{9,17},{17,9},{25,1},{2,26},{10... | collective-permute-start | bytes 98312 | tf_op jit(solution)/shard_map/ppermute | solution.py:666
  85.8 1.7 %collective-permute-start.20 = (bf16[8,192,128]{2,1,0:T(8,128)(2,1)S(1)}, bf16[8,192,128]{2,1,0:T(8,128)(2,1)S(1)}, u32[]{:S(2)}, u32[]{:S(2)}) collective-permute-start(bf16[8,192,128]{2,1,0:T(8,128)(2,1)S(1)} %all-to-all-done.1.near), channel_id=1, source_target_pairs={{0,8},{8,0},{16,24},{24,16},{1,9},{9,1},{17,25},{25,17},{2,10},{10... | collective-permute-start | bytes 1179656 | tf_op jit(solution)/shard_map/ppermute | solution.py:666

commit v6 on v5

--- a/solution.py
+++ b/solution.py
@@ -12,7 +12,7 @@
 REACH = 256
 RIM = 4
 TILE = 16
-LIMITS = (4, 14, 10, 7, 10, 8, 10, 2, 6, 2, 2, 3)
+LIMITS = (4, 13, 9, 7, 9, 8, 10, 2, 6, 2, 2, 3)
 
 eps_norm = 1e-05
 highest = lax.Precision.HIGHEST
@@ -99,34 +99,22 @@
         return lax.rem(z + 2 * cells_z, cells_z)
 
 
-def build_taps(block_of, taps, taps_z):
-    channels = taps_z.shape[-1] // 2
+def build_taps(block_of, taps):
+    channels = taps.shape[-1] // 2
     zero = jnp.zeros((channels, channels), bf16)
+    near, far = slice(0, channels), slice(channels, 2 * channels)
     for i in range(3):
-        for j in range(3):
-            block = block_of(i, j)
-            for q in range(2):
-                for side in range(2):
-                    y_in = 2 * q + side + j - 1
-                    if 0 <= y_in < 4:
-                        taps[
-                            q,
-                            i,
-                            y_in * channels : (y_in + 1) * channels,
-                            side * channels : (side + 1) * channels,
-                        ] = block
-        for q in range(2):
-            for side in range(2):
-                for y_in in range(4):
-                    if abs(y_in - 2 * q - side) > 1:
-                        taps[
-                            q,
-                            i,
-                            y_in * channels : (y_in + 1) * channels,
-                            side * channels : (side + 1) * channels,
-                        ] = zero
+        down, here, up = (block_of(i, j) for j in range(3))
+        taps[i, near, near] = here
+        taps[i, far, far] = here
+        taps[i, near, far] = down
+        taps[i, far, near] = up
+        taps[3 + i, near, near] = zero
+        taps[3 + i, far, far] = zero
+        taps[3 + i, near, far] = down
+        taps[3 + i, far, near] = up
     for m in range(2):
-        build_pair(block_of(3, m), taps_z, m)
+        build_pair(block_of(3, m), taps, 6 + m)
 
 
 def build_pair(block, target, m):
@@ -152,31 +140,22 @@
     return lambda i, j: weights[layer, i * 3 + j]
 
 
-def kernel_mix(timestep, clean_far, noise_far, mixed, mixed_own, clean, noise, sems):
+def kernel_mix(block, mixed, mixed_own):
     parts = mixed.shape[0]
-    copies = [
-        pltpu.make_async_copy(clean_far, clean, sems.at[0]),
-        pltpu.make_async_copy(noise_far, noise, sems.at[1]),
-    ]
-    for copy in copies:
-        copy.start()
-    moment = jnp.full((1, clean.shape[3]), timestep[0], jnp.int32).astype(f32)
-    alpha_bar = jnp.cos(0.5 * math.pi * (moment + 0.5) / STEPS) ** 2
+    alpha_bar = jnp.cos(0.5 * math.pi * (block[6, 0, 0:1] + 0.5) / STEPS) ** 2
     keep, add = jnp.sqrt(alpha_bar), jnp.sqrt(1.0 - alpha_bar)
-    for copy in copies:
-        copy.wait()
     for k in range(3):
-        noisy = keep * clean[k, 0] + add * noise[k, 0]
+        noise = block[3 + k, 0]
+        noisy = keep * block[k, 0] + add * noise
         mixed_own[4 * k : 4 * k + 4] = noisy
         for part in range(parts):
             mixed[part, 4 * k : 4 * k + 4] = noisy
-            mixed[part, 12 + 4 * k : 16 + 4 * k] = noise[k, 0]
-
-
-def kernel_prepare(w_z, w_xy, w_point, w_in, w_out, gains, w_front, point, w_back, point_back, lift_in,
-                   lift_out, w_in_on, gains_on):
-    w_in_on[...] = w_in[...]
-    gains_on[...] = gains[...]
+            mixed[part, 12 + 4 * k : 16 + 4 * k] = noise
+
+
+def kernel_prepare(steps, w_z, w_xy, w_point, small, w_front, point, w_back, point_back, lift_in, lift_out,
+                   steps_on):
+    steps_on[0], steps_on[1] = steps[0], steps[1]
     point[...] = w_point[...]
     for layer in range(2):
         forward = forward_blocks(w_z, w_xy, layer)
@@ -191,13 +170,13 @@
         for m in range(2):
             w_back[layer, 9 + m] = forward(3, 1 - m).T
         point_back[layer] = w_point[layer].T
-    whole = spread_rows(w_in[...], 0)
+    whole = spread_rows(small[0:3], 0)
     high, low = halves(whole)
     lift_in[0:32] = high
     lift_in[32:64] = high
     lift_in[64:96] = low
     lift_in[96:128] = jnp.zeros_like(low)
-    high = spread_rows(w_out[...].astype(f32), 3).astype(bf16)
+    high = spread_rows(small[6:9], 3).astype(bf16)
     lift_out[0:32] = high
     lift_out[32:64] = high
     lift_out[64:96] = jnp.zeros_like(high)
@@ -233,17 +212,27 @@
             shifted[way, :, tile * TILE : (tile + 1) * TILE, :] = rows.astype(bf16)
 
 
-def conv_half(padded, shifted, taps, taps_z, x0, count, q):
+def conv_pair(padded, shifted, taps, x0, count):
     rows, lanes = padded.shape[1:]
-    half = lanes // 2
-    total = None
+    half, quarter = lanes // 2, lanes // 4
+    totals = [None, None, None]
+
+    def add(at, left, right):
+        part = mm(left.reshape(count * rows, half), right)
+        totals[at] = part if totals[at] is None else totals[at] + part
+
+    for q in range(2):
+        side = slice(q * half, (q + 1) * half)
+        for i in range(3):
+            add(q, padded[x0 + i : x0 + i + count, :, side], taps[i])
+        for m in range(2):
+            add(q, shifted[m, x0 : x0 + count, :, side], taps[6 + m])
     for i in range(3):
-        part = mm(padded[x0 + i : x0 + i + count].reshape(count * rows, lanes), taps[q, i])
-        total = part if total is None else total + part
-    for m in range(2):
-        source = shifted[m, x0 : x0 + count, :, q * half : (q + 1) * half]
-        total = total + mm(source.reshape(count * rows, half), taps_z[m])
-    return total
+        add(2, padded[x0 + i : x0 + i + count, :, quarter : 3 * quarter], taps[3 + i])
+    first, second, middle = totals
+    first = jnp.concatenate([first[:, :quarter], first[:, quarter:] + middle[:, :quarter]], axis=1)
+    second = jnp.concatenate([second[:, :quarter] + middle[:, quarter:], second[:, quarter:]], axis=1)
+    return first, second
 
 
 def gelu_pair(value):
@@ -283,12 +272,12 @@
     return folded(jnp.sum(jnp.where(mask, value, 0.0), axis=0, keepdims=True))
 
 
-def layer_forward(place, layer, padded, shifted, taps, taps_z, pair, w_front, wp, shift_bias, old,
+def layer_forward(place, layer, padded, shifted, taps, pair, w_front, wp, shift_bias, old,
                   stream, act, slope, stats, acc, per_member):
     planes, rows, lanes = stream.shape
     half = lanes // 2
     count = planes // 4
-    build_taps(taken(w_front, layer), taps, taps_z)
+    build_taps(taken(w_front, layer), taps)
     build_pair(wp[layer], pair, 0)
     fill_rims(padded, planes)
     fill_shifted(place, layer, padded, shifted, planes)
@@ -297,10 +286,9 @@
 
     for x0 in range(0, planes, count):
         part = slice(x0, x0 + count)
-        for q in range(2):
+        for q, total in enumerate(conv_pair(padded, shifted, taps, x0, count)):
             side = slice(q * half, (q + 1) * half)
-            pre = conv_half(padded, shifted, taps, taps_z, x0, count, q) + bias
-            value, grad = gelu_pair(pre)
+            value, grad = gelu_pair(total + bias)
             act[part, :, side] = value.astype(bf16).reshape(count, rows, half)
             slope[part, :, side] = grad.astype(bf16).reshape(count, rows, half)
     for x0 in range(0, planes, count):
@@ -321,9 +309,9 @@
     put_rows(stats, total, masked_total(mask, spread))
 
 
-def kernel_first(cells_z, per_member, sc, near, far, lift_in, w_in, gains, shift_bias, w_front, wp,
-                 stream, normed, act, slope, gathered, stats, consts,
-                 padded, shifted, taps, taps_z, pair, acc, old, source):
+def kernel_first(cells_z, per_member, sc, near, far, lift_in, small, shift_bias, w_front, wp,
+                 stream, padded, act, slope, gathered, stats, consts,
+                 shifted, taps, pair, acc, old, source):
     planes, rows, lanes = stream.shape
     channels = lanes // 4
     depth = near.shape[2]
@@ -343,7 +331,7 @@
     for j in range(3):
         for k in range(j, 3):
             covs[j, k] = all_sum(gaps[j] * gaps[k]) / cell_count
-    rows_in = [w_in[k : k + 1, :] for k in range(3)]
+    rows_in = [small[k : k + 1, :] for k in range(3)]
     mean_c = sum(means[k] * rows_in[k] for k in range(3))
     var_c = jnp.zeros((1, channels), f32)
     for (j, k), cov in covs.items():
@@ -363,7 +351,7 @@
             source[x, 64:96, at] = high
             source[x, 96:128, at] = jnp.zeros_like(high)
     pick = place.pick(cells_z).astype(f32).astype(bf16)
-    scale = wide(inv_c * gains[0:1, :])
+    scale = wide(inv_c * small[3:4, :])
     mean_w = wide(mean_c)
     for x in range(planes):
         gathered[x] = mm_nt(pick, source[x]).astype(bf16)
@@ -373,36 +361,33 @@
         unit = ((value - mean_w) * scale).astype(bf16).reshape(planes // 2, rows, lanes)
         old[part] = value.reshape(planes // 2, rows, lanes)
         padded[x0 + 1 : x0 + 1 + planes // 2] = unit
-        normed[part] = unit
-    layer_forward(place, 0, padded, shifted, taps, taps_z, pair, w_front, wp, shift_bias, old, stream,
+    layer_forward(place, 0, padded, shifted, taps, pair, w_front, wp, shift_bias, old, stream,
                   act, slope, stats, acc, per_member)
 
 
 def kernel_second(per_member, sc, *refs):
     parts, refs = refs[:4], refs[4:]
-    (old, gains, shift_bias, w_front, wp, stream, normed, act, slope, stats, consts,
-     padded, shifted, taps, taps_z, pair, acc) = refs
+    (old, small, shift_bias, w_front, wp, stream, padded, act, slope, stats, consts,
+     shifted, taps, pair, acc) = refs
     planes, rows, _ = stream.shape
     place = Place(sc, rows)
     mean, inverse = merged_stats(parts, per_member)
     put_rows(consts, mean, inverse)
-    mean_w, scale = wide(mean), wide(inverse * gains[1:2, :])
+    mean_w, scale = wide(mean), wide(inverse * small[4:5, :])
     for x in range(planes):
-        unit = ((old[x] - mean_w) * scale).astype(bf16)
-        padded[x + 1] = unit
-        normed[x] = unit
-    layer_forward(place, 1, padded, shifted, taps, taps_z, pair, w_front, wp, shift_bias, old, stream,
+        padded[x + 1] = ((old[x] - mean_w) * scale).astype(bf16)
+    layer_forward(place, 1, padded, shifted, taps, pair, w_front, wp, shift_bias, old, stream,
                   act, slope, stats, acc, per_member)
 
 
 def kernel_out(per_member, sc, *refs):
     parts, refs = refs[:4], refs[4:]
-    stream, gains, gathered, lift_out, prediction, misfit, sums, w_out_raw, consts, unit = refs
+    stream, small, gathered, lift_out, prediction, misfit, sums, w_out_raw, consts, unit = refs
     planes, rows, lanes = stream.shape
     place = Place(sc, rows)
     mean, inverse = merged_stats(parts, per_member)
     put_rows(consts, mean, inverse)
-    mean_w, inv_w, gain_w = wide(mean), wide(inverse), wide(gains[2:3, :])
+    mean_w, inv_w, gain_w = wide(mean), wide(inverse), wide(small[5:6, :])
     scale = inv_w * gain_w
     for x in range(planes):
         unit[x] = ((stream[x] - mean_w) * scale).astype(bf16)
@@ -479,7 +464,7 @@
     mask = jnp.concatenate([place.own((rows, wide_share))] * planes, axis=0)
 
     def turned(source):
-        got = mm(source[...].reshape(planes * rows, lanes), choose)
+        got = mm(source.reshape(planes * rows, lanes), choose)
         return jnp.where(mask, got, 0.0).astype(bf16)
 
     def add_blocks(raw, j):
@@ -489,7 +474,7 @@
             if 0 <= y + j < 4
         )
 
-    left = turned(normed)
+    left = turned(normed[1 : planes + 1])
     for i in range(3):
         raw = mm_tn(left, padded[2 - i : 2 - i + planes].reshape(planes * rows, lanes))
         for j in range(3):
@@ -497,36 +482,36 @@
     for m in range(2):
         raw = mm_tn(left, shifted[1 - m].reshape(planes * rows, lanes))
         taps_all[9 + m] = add_blocks(raw, 0)
-    raw = mm_tn(turned(act), scot[...].reshape(planes * rows, lanes))
+    raw = mm_tn(turned(act[...]), scot[...].reshape(planes * rows, lanes))
     taps_all[11] = add_blocks(raw, 0)
     odd, half = lax.rem(place.member, 2), keep.shape[0]
     keep[...] = taps_all[pl.ds(odd * half, half)]
     give[...] = taps_all[pl.ds((1 - odd) * half, half)]
 
 
-def conv_backward(planes, padded, shifted, taps, taps_z, emit):
+def conv_backward(planes, padded, shifted, taps, emit):
     count = planes // 4
 
     for x0 in range(0, planes, count):
-        for q in range(2):
-            emit(x0, count, q, conv_half(padded, shifted, taps, taps_z, x0, count, q))
+        for q, total in enumerate(conv_pair(padded, shifted, taps, x0, count)):
+            emit(x0, count, q, total)
 
 
 def kernel_back_second(cell_count, sc, *refs):
     parts, refs = refs[:4], refs[4:]
-    (stream, out_consts, gains, misfit, lift_out, slope, normed, w_back, point_back,
+    (stream, out_consts, small, misfit, lift_out, slope, normed, w_back, point_back,
      d_stream, d_normed, sums, padded, shifted, scot,
-     taps, taps_z, pair, acc, acc2) = refs
+     taps, pair, acc, acc2) = refs
     planes, rows, lanes = stream.shape
     half = lanes // 2
     place = Place(sc, rows)
     sums_out = sum(members_of(parts))
-    gain_w = wide(gains[2:3, :])
+    gain_w = wide(small[5:6, :])
     mean_w, inv_w = wide(out_consts[0:1]), wide(out_consts[1:2])
     m_plain = gain_w * wide(sums_out[0:1]) / cell_count
     m_cross = gain_w * wide(sums_out[1:2]) / cell_count
     build_pair(point_back[1], pair, 0)
-    build_taps(taken(w_back, 1), taps, taps_z)
+    build_taps(taken(w_back, 1), taps)
     acc[...] = jnp.zeros_like(acc)
 
     def d_stream_of(x):
@@ -549,11 +534,11 @@
         value = value.reshape(count, rows, half)
         d_normed[x0 : x0 + count, :, side] = value
         acc[:, side] += jnp.sum(value, axis=0)
-        acc2[:, side] += jnp.sum(value * normed[x0 : x0 + count, :, side].astype(f32), axis=0)
-
-    conv_backward(planes, padded, shifted, taps, taps_z, emit)
+        acc2[:, side] += jnp.sum(value * normed[x0 + 1 : x0 + 1 + count, :, side].astype(f32), axis=0)
+
+    conv_backward(planes, padded, shifted, taps, emit)
     s_plain = masked_total(mask, acc[...])
-    s_cross = masked_total(mask, acc2[...]) / gains[1:2, :]
+    s_cross = masked_total(mask, acc2[...]) / small[4:5, :]
     put_rows(sums, s_plain, s_cross, s_bias)
 
 
@@ -564,13 +549,13 @@
 
 def kernel_back_first(share, cell_count, sc, *refs):
     parts, refs = refs[:4], refs[4:]
-    (consts, d_next, d_normed, normed_next, gains, act, slope, normed, point_back,
+    (consts, d_next, d_normed, normed_next, small, act, slope, normed, point_back,
      d_stream, sums, keep, give, padded, shifted,
      pair, acc, scot, taps_all) = refs
     planes, rows, lanes = d_next.shape
     place = Place(sc, rows)
     sums_in = sum(members_of(parts))
-    gain_w = wide(gains[1:2, :])
+    gain_w = wide(small[4:5, :])
     inv_w = wide(consts[1:2])
     m_plain = gain_w * wide(sums_in[0:1]) / cell_count
     m_cross = wide(sums_in[1:2]) / cell_count
@@ -578,7 +563,7 @@
     acc[...] = jnp.zeros_like(acc)
 
     def d_stream_of(x):
-        back = gain_w * d_normed[x] - m_plain - normed_next[x].astype(f32) * m_cross
+        back = gain_w * d_normed[x] - m_plain - normed_next[x + 1].astype(f32) * m_cross
         value = d_next[x] + inv_w * back
         d_stream[x] = value
         return value
@@ -590,32 +575,32 @@
     weight_grads(place, planes, padded, shifted, scot, normed, act, keep, give, taps_all, share)
 
 
-def kernel_last(depth, sc, padded, shifted, d_stream, normed, gains, consts, gathered, lift_in, w_back,
+def kernel_last(depth, sc, padded, shifted, d_stream, normed, small, consts, gathered, lift_in, w_back,
                 prediction, sums_bias, out_raw, ready0, ready1, own_out, out_1, out_2, out_3,
-                taps, taps_z, acc, acc2, high, low):
+                taps, acc, acc2, high, low):
     planes, rows, lanes = d_stream.shape
     half = lanes // 2
     place = Place(sc, rows)
-    build_taps(taken(w_back, 0), taps, taps_z)
+    build_taps(taken(w_back, 0), taps)
     acc[...] = jnp.zeros_like(acc)
     acc2[...] = jnp.zeros_like(acc2)
-    scale = wide(consts[1:2] * gains[0:1, :])
+    scale = wide(consts[1:2] * small[3:4, :])
 
     def emit(x0, count, q, value):
         side = slice(q * half, (q + 1) * half)
         part = slice(x0, x0 + count)
         value = value.reshape(count, rows, half)
         acc[:, side] += jnp.sum(value, axis=0)
-        acc2[:, side] += jnp.sum(value * normed[part, :, side].astype(f32), axis=0)
+        acc2[:, side] += jnp.sum(value * normed[x0 + 1 : x0 + 1 + count, :, side].astype(f32), axis=0)
         full = d_stream[part, :, side] + value * scale[:, side]
         first, second = halves(full)
         high[part, :, side] = first
         low[part, :, side] = second
 
-    conv_backward(planes, padded, shifted, taps, taps_z, emit)
+    conv_backward(planes, padded, shifted, taps, emit)
     mask = place.own((rows, lanes))
     s_plain = masked_total(mask, acc[...])
-    s_cross = masked_total(mask, acc2[...]) / gains[0:1, :]
+    s_cross = masked_total(mask, acc2[...]) / small[3:4, :]
     own = place.own((rows, 128))
     kept = jnp.concatenate([jnp.where(own, gathered[x].astype(f32), 0.0) for x in range(planes)], axis=0)
     kept = kept.astype(bf16)
@@ -643,18 +628,17 @@
         target[32:64] = tail
 
 
-def call(kernel, outs, scratch, flops, limit, *args, scalars=True, loose=(), ready=()):
+def call(kernel, outs, scratch, flops, limit, *args, scalars=True, scalar_out=0, ready=()):
     spec = pl.BlockSpec(memory_space=pltpu.VMEM)
     specs = [pl.BlockSpec(memory_space=pltpu.SMEM)] * scalars + [spec] * (len(args) - scalars)
     for at in ready:
         specs[at] = pl.BlockSpec(memory_space=pl.ANY)
-    for at in loose:
-        specs[at] = pl.BlockSpec(memory_space=pltpu.HBM)
+    smem = pl.BlockSpec(memory_space=pltpu.SMEM)
     return pl.pallas_call(
         kernel,
         out_shape=[jax.ShapeDtypeStruct(shape, dtype) for shape, dtype in outs],
         in_specs=specs,
-        out_specs=[spec] * len(outs),
+        out_specs=[spec] * (len(outs) - scalar_out) + [smem] * scalar_out,
         scratch_shapes=[pltpu.VMEM(*one) if isinstance(one, tuple) else one for one in scratch],
         compiler_params=pltpu.CompilerParams(vmem_limit_bytes=limit * 2**20),
         cost_estimate=pl.CostEstimate(flops=flops, bytes_accessed=2**23, transcendentals=0),
@@ -703,15 +687,15 @@
 
 def kernel_tail(cell_count, inv_area, *refs):
     tails, parts1, parts2, refs = refs[:4], refs[4:8], refs[8:12], refs[12:]
-    (consts, w_in, gains, mixed, features, time_raw,
+    (consts, small, mixed, features, time_raw,
      prediction, field_grad, grad_w_in, grad_w_time, grad_biases, grad_gains, grad_w_out) = refs
     tail = sum(ref[...] for ref in tails)
     s1, s2 = sum(ref[...] for ref in parts1), sum(ref[...] for ref in parts2)
     inverse = consts[1:2]
-    m_plain = inverse * (gains[0:1] * tail[32:33] / cell_count)
-    m_cross = inverse * inverse * (gains[0:1] * tail[33:34] / cell_count)
+    m_plain = inverse * (small[3:4] * tail[32:33] / cell_count)
+    m_cross = inverse * inverse * (small[3:4] * tail[33:34] / cell_count)
     at = {(0, 0): 5, (0, 1): 6, (0, 2): 7, (1, 1): 8, (1, 2): 9, (2, 2): 10}
-    rows_in = [w_in[k : k + 1] for k in range(3)]
+    rows_in = [small[k : k + 1] for k in range(3)]
     depth = mixed.shape[1]
     gaps = [mixed[4 * k : 4 * k + 4] - consts[2 + k : 3 + k, 0:1] for k in range(3)]
     for k in range(3):
@@ -753,10 +737,10 @@
 
     _, features, time_raw, time_code = time_terms(timestep, w_time)
     parts = members // 2 * groups
+    moment = jnp.broadcast_to(timestep.astype(f32).reshape(1, 1, 1, 1), (1,) + clean_field.shape[1:])
+    block = jnp.concatenate([clean_field, noise_field, moment], axis=0)
     mixed, mixed_own = call(
-        kernel_mix, [((parts, 24, depth), f32), ((12, depth), f32)],
-        [(clean_field.shape, f32), (clean_field.shape, f32), pltpu.SemaphoreType.DMA((2,))], 10**5, LIMITS[7],
-        timestep, clean_field, noise_field, loose=(1, 2),
+        kernel_mix, [((parts, 24, depth), f32), ((12, depth), f32)], [], 10**5, LIMITS[7], block, scalars=False,
     )
     same_core = [[m * groups + g for m in range(core, members, 2) for g in range(groups)] for core in range(2)]
     near = lax.all_to_all(mixed, ("gz", "gx"), 0, 0, axis_index_groups=same_core)
@@ -770,39 +754,39 @@
     conv_scratch = [
         ((planes + 2, rows, lanes), bf16),
         ((2,) + big, bf16),
-        ((2, 3, lanes, lanes // 2), bf16),
-        ((2, lanes // 2, lanes // 2), bf16),
+        ((8, lanes // 2, lanes // 2), bf16),
     ]
     pair = ((1, lanes // 2, lanes // 2), bf16)
     flat = ((rows, lanes), f32)
     grad_out = ((6, share, channels), f32)
 
     taps_out, point_out = ((2, 11, channels, channels), bf16), ((2, channels, channels), bf16)
-    w_front, point, w_back, point_back, lift_in, lift_out, w_in_on, gains_on = call(
+    small = jnp.concatenate([w_in, norm_gains, w_out.astype(f32)], axis=0)
+    w_front, point, w_back, point_back, lift_in, lift_out, steps_on = call(
         kernel_prepare,
-        [taps_out, point_out, taps_out, point_out, lift, lift, ((3, channels), f32), ((3, channels), f32)],
-        [], 10**8, LIMITS[0], w_z, w_xy, w_point, w_in, w_out, norm_gains, scalars=False,
+        [taps_out, point_out, taps_out, point_out, lift, lift, ((2,), jnp.int32)],
+        [], 10**8, LIMITS[0], dilations, w_z, w_xy, w_point, small, scalar_out=1,
     )
     stream1, normed0, act0, slope0, gathered, stats1, consts0 = call(
         functools.partial(kernel_first, cells_z, per_member),
-        [(big, f32), (big, bf16), (big, bf16), (big, bf16), thin, vec, ((16, channels), f32)],
-        conv_scratch + [pair, flat, (big, f32), ((planes, 128, cells_z), bf16)],
+        [(big, f32), conv_scratch[0], (big, bf16), (big, bf16), thin, vec, ((16, channels), f32)],
+        conv_scratch[1:] + [pair, flat, (big, f32), ((planes, 128, cells_z), bf16)],
         4 * 10**9, LIMITS[1],
-        dilations, near, far, lift_in, w_in_on, gains_on, shift_bias, w_front, point,
+        steps_on, near, far, lift_in, small, shift_bias, w_front, point,
     )
     stream2, normed1, act1, slope1, stats2, consts1 = call(
         functools.partial(kernel_second, per_member),
-        [(big, f32), (big, bf16), (big, bf16), (big, bf16), vec, vec],
-        conv_scratch + [pair, flat],
+        [(big, f32), conv_scratch[0], (big, bf16), (big, bf16), vec, vec],
+        conv_scratch[1:] + [pair, flat],
         4 * 10**9, LIMITS[2],
-        dilations, *group_parts(stats1), stream1, gains_on, shift_bias, w_front, point,
+        steps_on, *group_parts(stats1), stream1, small, shift_bias, w_front, point,
     )
     prediction, misfit, sums2, out_raw, consts2 = call(
         functools.partial(kernel_out, per_member),
         [((rows, 128), f32), thin, vec, vec, vec],
         [(big, bf16)],
         10**9, LIMITS[3],
-        dilations, *group_parts(stats2), stream2, gains_on, gathered, lift_out,
+        steps_on, *group_parts(stats2), stream2, small, gathered, lift_out,
     )
     parts2 = group_parts(sums2)
     d_stream2, d_normed1, sums1, rimmed1, shifted1, scot1 = call(
@@ -810,21 +794,21 @@
         [(big, f32), (big, f32), vec] + conv_scratch[:2] + [(big, bf16)],
         conv_scratch[2:] + [pair, flat, flat],
         6 * 10**9, LIMITS[4],
-        dilations, *parts2, stream2, consts2, gains_on, misfit, lift_out, slope1, normed1,
+        steps_on, *parts2, stream2, consts2, small, misfit, lift_out, slope1, normed1,
         w_back, point_back,
     )
     parts1 = group_parts(sums1)
     keep1, give1 = call(
         functools.partial(kernel_weights_second, share),
         [grad_out, grad_out], [((12, share, channels), f32)], 2 * 10**9, LIMITS[8],
-        dilations, rimmed1, shifted1, scot1, normed1, act1,
+        steps_on, rimmed1, shifted1, scot1, normed1, act1,
     )
     d_stream1, sums_b0, keep0, give0, rimmed0, shifted0 = call(
         functools.partial(kernel_back_first, share, cell_count),
         [(big, f32), vec, grad_out, grad_out] + conv_scratch[:2],
         [pair, flat, (big, bf16), ((12, share, channels), f32)],
         4 * 10**9, LIMITS[5],
-        dilations, *parts1, consts1, d_stream2, d_normed1, normed1, gains_on, act0, slope0, normed0,
+        steps_on, *parts1, consts1, d_stream2, d_normed1, normed1, small, act0, slope0, normed0,
         point_back,
     )
     chip0 = keep0 + swapped(give0, "gz", 1)
@@ -834,7 +818,7 @@
         [((64, channels), f32)] * members,
         conv_scratch[2:] + [flat, flat, (big, bf16), (big, bf16)],
         4 * 10**9, LIMITS[6],
-        dilations, rimmed0, shifted0, d_stream1, normed0, gains_on, consts0, gathered, lift_in, w_back, prediction,
+        steps_on, rimmed0, shifted0, d_stream1, normed0, small, consts0, gathered, lift_in, w_back, prediction,
         sums_b0, out_raw, chip0, chip1, ready=(13, 14),
     )
     spread = call(
@@ -848,8 +832,8 @@
         [(clean_field.shape, f32), (clean_field.shape, f32), ((3, channels), f32), (w_time.shape, f32),
          ((2, channels), f32), ((3, channels), f32), ((3, channels), f32)],
         [], 10**6, LIMITS[10],
-        last[0], *(swapped(last[bit], "gz", bit) for bit in (1, 2, 3)), *parts1, *parts2, consts0, w_in_on,
-        gains_on, mixed_own, features[None], time_raw[None], scalars=False,
+        last[0], *(swapped(last[bit], "gz", bit) for bit in (1, 2, 3)), *parts1, *parts2, consts0, small,
+        mixed_own, features[None], time_raw[None], scalars=False,
     )
     tied, _ = lax.optimization_barrier((near_grads, field_grad))
     far_grads = swapped(tied, "gz", 1)

time: 89.5 us -> 86.1 us (0.962)
  local copies, waits for them, and re-layouts: 6.89 us -> 3.54 us
  other arithmetic: 0.82 us -> 3 us
  Pallas kernels: 34 us -> 32.4 us
  waiting for transfers between devices: 21.2 us -> 20.1 us
    unnamed x22 -> x10, local copies, waits for them, and re-layouts: 6.89 us -> 3.47 us
    pallas_call x12, Pallas kernels: 34 us -> 32.4 us  [call(): pl.pallas_call(kernel, out_shape=[jax.ShapeDtypeStruct(shape, dtype) for...]
    concatenate x0 -> x2, other arithmetic: none -> 1.49 us  [the longest x1 0.78 us: per_device_grouped(): block = jnp.concatenate([clean_field, noise_field, moment], axis=0)]
  transfers between devices with their start and end apart: 23 -> 23, of which waited for: 12 -> 12; matrix products, arithmetic and copies ran while one was open for 1% -> 3% of each run, Pallas kernels for 14% -> 15%
where the time goes in v6:
time: 86.1 us; the launch traced here: 85.5 us
  Pallas kernels  32.4 us (38%)
  starting transfers between devices  24.8 us (29%)
  waiting for transfers between devices  20.1 us (23%)
  local copies, waits for them, and re-layouts  3.54 us (4%)
  other arithmetic  3 us (3%)
  between operations  1.48 us (2%)
    pallas_call x12, Pallas kernels, call(): pl.pallas_call(kernel, out_shape=[jax.ShapeDtypeStruct(shape, dtype) for...  32.4 us
    ppermute x21, starting transfers between devices, swapped(): return lax.ppermute(value, axis, [(i, i ^ bit) for i in range(count)])  12.3 us
    ppermute x21, waiting for transfers between devices, swapped(): return lax.ppermute(value, axis, [(i, i ^ bit) for i in range(count)])  11.9 us
    all_to_all x1, starting transfers between devices, per_device_grouped(): lax.all_to_all(mixed, ('gz', 'gx'), 0, 0, axis_index_groups=same_core)  8.31 us
    all_to_all x1, waiting for transfers between devices, per_device_grouped(): near_grads = lax.all_to_all(spread, 'gx', 0, 0)  6.06 us
    all_to_all x1, starting transfers between devices, per_device_grouped(): near_grads = lax.all_to_all(spread, 'gx', 0, 0)  4.13 us
    unnamed x10, local copies, waits for them, and re-layouts  3.47 us
    all_to_all x1, waiting for transfers between devices, per_device_grouped(): lax.all_to_all(mixed, ('gz', 'gx'), 0, 0, axis_index_groups=same_core)  2.09 us
  transfers between devices with their start and end apart: 23, of which 12 were waited for; matrix products, arithmetic and copies ran while one was open for 3% of the time, Pallas kernels for 15%

profile of v6, /device:TPU:0, one launch (start us, length us, event | category | flops | bytes accessed | tf_op | source)
XLA Modules:
  0.0 85.5 jit_solution(11620669012411162960)
XLA Ops:
  1.4 0.8 maximum_maximum_fusion.block
  2.2 0.8 shard_map.196
  3.0 8.3 %all-to-all-start = ((f32[16,24,128]{2,1,0:T(8,128)}), f32[16,24,128]{2,1,0:T(8,128)S(1)}, u32[]{:S(2)}, u32[]{:S(2)}) async-start(f32[16,24,128]{2,1,0:T(8,128)} %get-tuple-element.67), calls=%async_computation | async-start | bytes 393216 | tf_op jit(solution)/shard_map/all_to_all | solution.py:746
  11.3 0.7 convert_element_type.8
  12.0 0.7 pad_maximum_fusion.small.refs_5_.refs_6_.refs_8_.refs_13_
  12.7 1.0 %copy-done.1 = bf16[2,8,128,128]{3,2,1,0:T(8,128)(2,1)S(1)} copy-done((bf16[2,8,128,128]{3,2,1,0:T(8,128)(2,1)S(1)}, bf16[2,8,128,128]{3,2,1,0:T(8,128)(2,1)}, u32[]{:S(2)}) %copy-start.1) | copy-done | bytes 524312
  13.7 0.9 %copy-done.2 = bf16[2,3,128,128]{3,2,1,0:T(8,128)(2,1)S(1)} copy-done((bf16[2,3,128,128]{3,2,1,0:T(8,128)(2,1)S(1)}, bf16[2,3,128,128]{3,2,1,0:T(8,128)(2,1)}, u32[]{:S(2)}) %copy-start.2) | copy-done | bytes 196632
  14.6 0.8 copy-done.3
  15.5 0.7 copy-done.4
  16.1 1.1 %shard_map.195 = (bf16[2,11,128,128]{3,2,1,0:T(8,128)(2,1)S(1)}, bf16[2,128,128]{2,1,0:T(8,128)(2,1)S(1)}, bf16[2,11,128,128]{3,2,1,0:T(8,128)(2,1)S(1)}, bf16[2...) custom-call(s32[2]{0:T(128)S(1)} %copy-done.4, ...), custom_call_target="tpu_custom_call" | custom-call | flops 100000000 | bytes 8388608 | tf_op jit(solution)/shard_map/pallas_call | solution.py:637
  17.6 2.1 %all-to-all-done.near = f32[16,24,128]{2,1,0:T(8,128)S(1)} async-done(((f32[16,24,128]{2,1,0:T(8,128)}), f32[16,24,128]{2,1,0:T(8,128)S(1)}, u32[]{:S(2)}, u32[]{:S(2)}) %all-to-all-start) | async-done | bytes 196640 | tf_op jit(solution)/shard_map/all_to_all | solution.py:746
  19.7 0.7 broadcast_add_fusion.shift_bias.refs_6_
  20.3 0.8 collective-permute-done.far
  21.1 5.3 %shard_map.197 = (f32[8,144,512]{2,1,0:T(8,128)S(1)}, bf16[10,144,512]{2,1,0:T(8,128)(2,1)S(1)}, bf16[8,144,512]{2,1,0:T(8,128)(2,1)S(1)}, bf16[8,144,512]{2,1,0...) custom-call(s32[2]{0:T(128)S(1)} %get-tuple-element.66.sc, ...), custom_call_target="tpu_custom_call" | custom-call | flops 4000000000 | bytes 8388608 | tf_op jit(solution)/shard_map/pallas_call | solution.py:637
  26.4 1.0 %collective-permute-start.3 = (f32[8,128]{1,0:T(8,128)S(1)}, f32[8,128]{1,0:T(8,128)S(1)}, u32[]{:S(2)}, u32[]{:S(2)}) collective-permute-start(f32[8,128]{1,0:T(8,128)S(1)} %get-tuple-element.71.refs_0_), channel_id=1, source_target_pairs={{0,24},{8,16},{16,8},{24,0},{1,25},{9,17},{17,9},{25,1},{2,26},{10... | collective-permute-start | bytes 12296 | tf_op jit(solution)/shard_map/ppermute | solution.py:650
  27.5 0.8 collective-permute-start.2
  28.4 1.2 %collective-permute-done.3.refs_3_ = f32[8,128]{1,0:T(8,128)S(1)} collective-permute-done((f32[8,128]{1,0:T(8,128)S(1)}, f32[8,128]{1,0:T(8,128)S(1)}, u32[]{:S(2)}, u32[]{:S(2)}) %collective-permute-start.3) | collective-permute-done | bytes 4128 | tf_op jit(solution)/shard_map/ppermute | solution.py:650
  29.5 1.6 %collective-permute-done.2.refs_2_ = f32[8,128]{1,0:T(8,128)S(1)} collective-permute-done((f32[8,128]{1,0:T(8,128)S(1)}, f32[8,128]{1,0:T(8,128)S(1)}, u32[]{:S(2)}, u32[]{:S(2)}) %collective-permute-start.2) | collective-permute-done | bytes 4128 | tf_op jit(solution)/shard_map/ppermute | solution.py:650
  31.1 4.6 %shard_map.198 = (f32[8,144,512]{2,1,0:T(8,128)S(1)}, bf16[10,144,512]{2,1,0:T(8,128)(2,1)S(1)}, bf16[8,144,512]{2,1,0:T(8,128)(2,1)S(1)}, bf16[8,144,512]{2,1,0...) custom-call(s32[2]{0:T(128)S(1)} %get-tuple-element.66.sc, f32[8,128]{1,0:T(8,128)S(1)} %get-tuple-element.71.refs_0_, ...), custom_call_target="tpu_custom_call" | custom-call | flops 4000000000 | bytes 8388608 | tf_op jit(solution)/shard_map/pallas_call | solution.py:637
  35.8 0.9 %collective-permute-start.5 = (f32[8,128]{1,0:T(8,128)S(1)}, f32[8,128]{1,0:T(8,128)S(1)}, u32[]{:S(2)}, u32[]{:S(2)}) collective-permute-start(f32[8,128]{1,0:T(8,128)S(1)} %get-tuple-element.73.refs_0_), channel_id=1, source_target_pairs={{0,16},{8,24},{16,0},{24,8},{1,17},{9,25},{17,1},{25,9},{2,18},{10... | collective-permute-start | bytes 12296 | tf_op jit(solution)/shard_map/ppermute | solution.py:650
  36.6 1.0 %collective-permute-start.4 = (f32[8,128]{1,0:T(8,128)S(1)}, f32[8,128]{1,0:T(8,128)S(1)}, u32[]{:S(2)}, u32[]{:S(2)}) collective-permute-start(f32[8,128]{1,0:T(8,128)S(1)} %get-tuple-element.73.refs_0_), channel_id=1, source_target_pairs={{0,8},{8,0},{16,24},{24,16},{1,9},{9,1},{17,25},{25,17},{2,10},{10... | collective-permute-start | bytes 12296 | tf_op jit(solution)/shard_map/ppermute | solution.py:650
  37.6 1.2 %collective-permute-done.6.refs_3_ = f32[8,128]{1,0:T(8,128)S(1)} collective-permute-done((f32[8,128]{1,0:T(8,128)S(1)}, f32[8,128]{1,0:T(8,128)S(1)}, u32[]{:S(2)}, u32[]{:S(2)}) %collective-permute-start.6) | collective-permute-done | bytes 4128 | tf_op jit(solution)/shard_map/ppermute | solution.py:650
  38.8 0.7 collective-permute-done.5.refs_2_
  39.5 2.3 %shard_map.199 = (f32[144,128]{1,0:T(8,128)S(1)}, bf16[8,144,128]{2,1,0:T(8,128)(2,1)S(1)}, f32[8,128]{1,0:T(8,128)S(1)}, f32[8,128]{1,0:T(8,128)S(1)}, f32[8,128]{1,0:T(8,128)S(1)}) custom-call(s32[2]{0:T(128)S(1)} %get-tuple-element.66.sc, f32[8,128]{1,0:T(8,128)S(1)} %get-tuple-element.73.refs_0_, f32[8,128]{1,0:T(8,128)S(1)} %collective-permute-done.4.refs_1_, ...), custom_call_target="tpu_custom_call" | custom-call | flops 1000000000 | bytes 8388608 | tf_op jit(solution)/shard_map/pallas_call | solution.py:637
  41.8 0.6 collective-permute-start.9
  42.4 0.8 collective-permute-start.8
  43.2 0.5 collective-permute-start.7
  43.7 1.2 %collective-permute-done.9.refs_3_.refs_11_ = f32[8,128]{1,0:T(8,128)S(1)} collective-permute-done((f32[8,128]{1,0:T(8,128)S(1)}, f32[8,128]{1,0:T(8,128)S(1)}, u32[]{:S(2)}, u32[]{:S(2)}) %collective-permute-start.9) | collective-permute-done | bytes 4128 | tf_op jit(solution)/shard_map/ppermute | solution.py:650
  44.9 1.1 %collective-permute-done.8.refs_2_.refs_10_ = f32[8,128]{1,0:T(8,128)S(1)} collective-permute-done((f32[8,128]{1,0:T(8,128)S(1)}, f32[8,128]{1,0:T(8,128)S(1)}, u32[]{:S(2)}, u32[]{:S(2)}) %collective-permute-start.8) | collective-permute-done | bytes 4128 | tf_op jit(solution)/shard_map/ppermute | solution.py:650
  46.0 4.6 %shard_map.200 = (f32[8,144,512]{2,1,0:T(8,128)S(1)}, f32[8,144,512]{2,1,0:T(8,128)S(1)}, f32[8,128]{1,0:T(8,128)S(1)}, bf16[10,144,512]{2,1,0:T(8,128)(2,1)S(1)...) custom-call(s32[2]{0:T(128)S(1)} %get-tuple-element.66.sc, ...), custom_call_target="tpu_custom_call" | custom-call | flops 6000000000 | bytes 8388608 | tf_op jit(solution)/shard_map/pallas_call | solution.py:637
  50.7 0.8 collective-permute-start.11
  51.5 1.0 %collective-permute-start.10 = (f32[8,128]{1,0:T(8,128)S(1)}, f32[8,128]{1,0:T(8,128)S(1)}, u32[]{:S(2)}, u32[]{:S(2)}) collective-permute-start(f32[8,128]{1,0:T(8,128)S(1)} %get-tuple-element.84.refs_0_.refs_4_), channel_id=1, source_target_pairs={{0,8},{8,0},{16,24},{24,16},{1,9},{9,1},{17,25},{25,17},{2,10},{10... | collective-permute-start | bytes 12296 | tf_op jit(solution)/shard_map/ppermute | solution.py:650
  52.5 2.8 %shard_map.202 = (f32[6,16,128]{2,1,0:T(8,128)S(1)}, f32[6,16,128]{2,1,0:T(8,128)S(1)}) custom-call(s32[2]{0:T(128)S(1)} %get-tuple-element.66.sc, bf16[10,144,512]{2,1,0:T(8,128)(2,1)S(1)} %get-tuple-element.100.padded, bf16[2,8,144,512]{3,2,1,0:T(8,128)(2,1)S(1)} %get-tuple-element.101.shifted, bf16[8,144,512]{2,1,0:T(8,128)(2,1)S(1)} %get-tuple-element.102.scot, ...), custom_call_target="tpu_custom_call" | custom-call | flops 2000000000 | bytes 8388608 | tf_op jit(solution)/shard_map/pallas_call | solution.py:637
  55.4 4.0 %shard_map.201 = (f32[8,144,512]{2,1,0:T(8,128)S(1)}, f32[8,128]{1,0:T(8,128)S(1)}, f32[6,16,128]{2,1,0:T(8,128)S(1)}, f32[6,16,128]{2,1,0:T(8,128)S(1)}, bf16[1...) custom-call(s32[2]{0:T(128)S(1)} %get-tuple-element.66.sc, ...), custom_call_target="tpu_custom_call" | custom-call | flops 4000000000 | bytes 8388608 | tf_op jit(solution)/shard_map/pallas_call | solution.py:637
  59.5 0.5 collective-permute-start.13
  60.0 0.8 collective-permute-start.19
  60.9 1.3 %collective-permute-start.18 = (f32[6,16,128]{2,1,0:T(8,128)S(1)}, f32[6,16,128]{2,1,0:T(8,128)S(1)}, u32[]{:S(2)}, u32[]{:S(2)}) collective-permute-start(f32[6,16,128]{2,1,0:T(8,128)S(1)} %add.21.ready0.first), channel_id=1, source_target_pairs={{0,16},{8,24},{16,0},{24,8},{1,17},{9,25},{17,1},{25,9},{2,18},{10... | collective-permute-start | bytes 147464 | tf_op jit(solution)/shard_map/ppermute | solution.py:650
  62.2 4.0 %shard_map.203 = (f32[64,128]{1,0:T(8,128)S(1)}, f32[64,128]{1,0:T(8,128)S(1)}, f32[64,128]{1,0:T(8,128)S(1)}, f32[64,128]{1,0:T(8,128)S(1)}) custom-call(s32[2]{0:T(128)S(1)} %get-tuple-element.66.sc, bf16[10,144,512]{2,1,0:T(8,128)(2,1)S(1)} %get-tuple-element.91.padded, bf16[2,8,144,512]{3,2,1,0:T(8,128)(2,1)S(1)} %get-tuple-element.92.shifted, ...), custom_call_target="tpu_custom_call" | custom-call | flops 4000000000 | bytes 8388608 | tf_op jit(solution)/shard_map/pallas_call | solution.py:637
  66.3 0.8 shard_map.205
  67.0 4.1 %all-to-all-start.1 = ((bf16[8,192,128]{2,1,0:T(8,128)(2,1)}), bf16[8,192,128]{2,1,0:T(8,128)(2,1)S(1)}, u32[]{:S(2)}, u32[]{:S(2)}) async-start(bf16[8,192,128]{2,1,0:T(8,128)(2,1)} %shard_map.205), calls=%async_computation.1 | async-start | bytes 786432 | tf_op jit(solution)/shard_map/all_to_all | solution.py:828
  71.2 0.8 collective-permute-start.16
  72.0 1.0 %collective-permute-start.17 = (f32[64,128]{1,0:T(8,128)S(1)}, f32[64,128]{1,0:T(8,128)S(1)}, u32[]{:S(2)}, u32[]{:S(2)}) collective-permute-start(f32[64,128]{1,0:T(8,128)S(1)} %get-tuple-element.109), channel_id=1, source_target_pairs={{0,24},{8,16},{16,8},{24,0},{1,25},{9,17},{17,9},{25,1},{2,26},{10... | collective-permute-start | bytes 98312 | tf_op jit(solution)/shard_map/ppermute | solution.py:650
  73.1 2.2 %collective-permute-done.16.refs_2_ = f32[64,128]{1,0:T(8,128)S(1)} collective-permute-done((f32[64,128]{1,0:T(8,128)S(1)}, f32[64,128]{1,0:T(8,128)S(1)}, u32[]{:S(2)}, u32[]{:S(2)}) %collective-permute-start.16) | collective-permute-done | bytes 32800 | tf_op jit(solution)/shard_map/ppermute | solution.py:650
  75.3 0.4 collective-permute-done.17.refs_3_
  75.7 0.8 shard_map.204
  76.5 6.1 %all-to-all-done.1.near = bf16[8,192,128]{2,1,0:T(8,128)(2,1)S(1)} async-done(((bf16[8,192,128]{2,1,0:T(8,128)(2,1)}), bf16[8,192,128]{2,1,0:T(8,128)(2,1)S(1)}, u32[]{:S(2)}, u32[]{:S(2)}) %all-to-all-start.1) | async-done | bytes 393248 | tf_op jit(solution)/shard_map/all_to_all | solution.py:828
  82.5 1.7 %collective-permute-done.20.far = bf16[8,192,128]{2,1,0:T(8,128)(2,1)S(1)} collective-permute-done((bf16[8,192,128]{2,1,0:T(8,128)(2,1)S(1)}, bf16[8,192,128]{2,1,0:T(8,128)(2,1)S(1)}, u32[]{:S(2)}, u32[]{:S(2)}) %collective-permute-start.20) | collective-permute-done | bytes 393248 | tf_op jit(solution)/shard_map/ppermute | solution.py:650
  84.3 1.3 %shard_map.206 = (f32[2,3,128,128]{3,2,1,0:T(8,128)}, f32[2,8,128,128]{3,2,1,0:T(8,128)}, f32[2,128,128]{2,1,0:T(8,128)}) custom-call(bf16[8,192,128]{2,1,0:T(8,128)(2,1)S(1)} %all-to-all-done.1.near, bf16[8,192,128]{2,1,0:T(8,128)(2,1)S(1)} %collective-permute-done.20.far), custom_call_target="tpu_custom_call" | custom-call | flops 1000000 | bytes 8388608 | tf_op jit(solution)/shard_map/pallas_call | solution.py:637
  (30 shorter events, 0.9 us)
Async XLA Ops:
  0.6 16.7 %copy-start = (f32[128,128]{1,0:T(8,128)S(1)}, f32[128,128]{1,0:T(8,128)}, u32[]{:S(2)}) copy-start(f32[128,128]{1,0:T(8,128)} %param.17) | copy-start | bytes 196612
  3.0 16.7 %all-to-all-start = ((f32[16,24,128]{2,1,0:T(8,128)}), f32[16,24,128]{2,1,0:T(8,128)S(1)}, u32[]{:S(2)}, u32[]{:S(2)}) async-start(f32[16,24,128]{2,1,0:T(8,128)} %get-tuple-element.67), calls=%async_computation | async-start | bytes 393216 | tf_op jit(solution)/shard_map/all_to_all | solution.py:746
  12.7 1.0 %copy-start.1 = (bf16[2,8,128,128]{3,2,1,0:T(8,128)(2,1)S(1)}, bf16[2,8,128,128]{3,2,1,0:T(8,128)(2,1)}, u32[]{:S(2)}) copy-start(bf16[2,8,128,128]{3,2,1,0:T(8,128)(2,1)} %w_xy.1) | copy-start | bytes 1572868
  13.7 0.9 %copy-start.2 = (bf16[2,3,128,128]{3,2,1,0:T(8,128)(2,1)S(1)}, bf16[2,3,128,128]{3,2,1,0:T(8,128)(2,1)}, u32[]{:S(2)}) copy-start(bf16[2,3,128,128]{3,2,1,0:T(8,128)(2,1)} %w_z.1) | copy-start | bytes 589828
  14.6 0.8 copy-start.3
  15.5 0.7 copy-start.4
  19.7 1.4 %collective-permute-start = (f32[16,24,128]{2,1,0:T(8,128)S(1)}, f32[16,24,128]{2,1,0:T(8,128)S(1)}, u32[]{:S(2)}, u32[]{:S(2)}) collective-permute-start(f32[16,24,128]{2,1,0:T(8,128)S(1)} %all-to-all-done.near), channel_id=1, source_target_pairs={{0,8},{8,0},{16,24},{24,16},{1,9},{9,1},{17,25},{25,17},{2,10},{10... | collective-permute-start | bytes 589832 | tf_op jit(solution)/shard_map/ppermute | solution.py:650
  26.4 3.1 %collective-permute-start.3 = (f32[8,128]{1,0:T(8,128)S(1)}, f32[8,128]{1,0:T(8,128)S(1)}, u32[]{:S(2)}, u32[]{:S(2)}) collective-permute-start(f32[8,128]{1,0:T(8,128)S(1)} %get-tuple-element.71.refs_0_), channel_id=1, source_target_pairs={{0,24},{8,16},{16,8},{24,0},{1,25},{9,17},{17,9},{25,1},{2,26},{10... | collective-permute-start | bytes 12296 | tf_op jit(solution)/shard_map/ppermute | solution.py:650
  27.5 3.6 %collective-permute-start.2 = (f32[8,128]{1,0:T(8,128)S(1)}, f32[8,128]{1,0:T(8,128)S(1)}, u32[]{:S(2)}, u32[]{:S(2)}) collective-permute-start(f32[8,128]{1,0:T(8,128)S(1)} %get-tuple-element.71.refs_0_), channel_id=1, source_target_pairs={{0,16},{8,24},{16,0},{24,8},{1,17},{9,25},{17,1},{25,9},{2,18},{10... | collective-permute-start | bytes 12296 | tf_op jit(solution)/shard_map/ppermute | solution.py:650
  28.3 2.8 %collective-permute-start.1 = (f32[8,128]{1,0:T(8,128)S(1)}, f32[8,128]{1,0:T(8,128)S(1)}, u32[]{:S(2)}, u32[]{:S(2)}) collective-permute-start(f32[8,128]{1,0:T(8,128)S(1)} %get-tuple-element.71.refs_0_), channel_id=1, source_target_pairs={{0,8},{8,0},{16,24},{24,16},{1,9},{9,1},{17,25},{25,17},{2,10},{10... | collective-permute-start | bytes 12296 | tf_op jit(solution)/shard_map/ppermute | solution.py:650
  35.7 3.1 %collective-permute-start.6 = (f32[8,128]{1,0:T(8,128)S(1)}, f32[8,128]{1,0:T(8,128)S(1)}, u32[]{:S(2)}, u32[]{:S(2)}) collective-permute-start(f32[8,128]{1,0:T(8,128)S(1)} %get-tuple-element.73.refs_0_), channel_id=1, source_target_pairs={{0,24},{8,16},{16,8},{24,0},{1,25},{9,17},{17,9},{25,1},{2,26},{10... | collective-permute-start | bytes 12296 | tf_op jit(solution)/shard_map/ppermute | solution.py:650
  35.8 3.7 %collective-permute-start.5 = (f32[8,128]{1,0:T(8,128)S(1)}, f32[8,128]{1,0:T(8,128)S(1)}, u32[]{:S(2)}, u32[]{:S(2)}) collective-permute-start(f32[8,128]{1,0:T(8,128)S(1)} %get-tuple-element.73.refs_0_), channel_id=1, source_target_pairs={{0,16},{8,24},{16,0},{24,8},{1,17},{9,25},{17,1},{25,9},{2,18},{10... | collective-permute-start | bytes 12296 | tf_op jit(solution)/shard_map/ppermute | solution.py:650
  36.6 2.8 %collective-permute-start.4 = (f32[8,128]{1,0:T(8,128)S(1)}, f32[8,128]{1,0:T(8,128)S(1)}, u32[]{:S(2)}, u32[]{:S(2)}) collective-permute-start(f32[8,128]{1,0:T(8,128)S(1)} %get-tuple-element.73.refs_0_), channel_id=1, source_target_pairs={{0,8},{8,0},{16,24},{24,16},{1,9},{9,1},{17,25},{25,17},{2,10},{10... | collective-permute-start | bytes 12296 | tf_op jit(solution)/shard_map/ppermute | solution.py:650
  41.8 3.1 %collective-permute-start.9 = (f32[8,128]{1,0:T(8,128)S(1)}, f32[8,128]{1,0:T(8,128)S(1)}, u32[]{:S(2)}, u32[]{:S(2)}) collective-permute-start(f32[8,128]{1,0:T(8,128)S(1)} %get-tuple-element.77.refs_0_.refs_8_), channel_id=1, source_target_pairs={{0,24},{8,16},{16,8},{24,0},{1,25},{9,17},{17,9},{25,1},{2,26},{10... | collective-permute-start | bytes 12296 | tf_op jit(solution)/shard_map/ppermute | solution.py:650
  42.4 3.6 %collective-permute-start.8 = (f32[8,128]{1,0:T(8,128)S(1)}, f32[8,128]{1,0:T(8,128)S(1)}, u32[]{:S(2)}, u32[]{:S(2)}) collective-permute-start(f32[8,128]{1,0:T(8,128)S(1)} %get-tuple-element.77.refs_0_.refs_8_), channel_id=1, source_target_pairs={{0,16},{8,24},{16,0},{24,8},{1,17},{9,25},{17,1},{25,9},{2,18},{10... | collective-permute-start | bytes 12296 | tf_op jit(solution)/shard_map/ppermute | solution.py:650
  43.2 2.8 %collective-permute-start.7 = (f32[8,128]{1,0:T(8,128)S(1)}, f32[8,128]{1,0:T(8,128)S(1)}, u32[]{:S(2)}, u32[]{:S(2)}) collective-permute-start(f32[8,128]{1,0:T(8,128)S(1)} %get-tuple-element.77.refs_0_.refs_8_), channel_id=1, source_target_pairs={{0,8},{8,0},{16,24},{24,16},{1,9},{9,1},{17,25},{25,17},{2,10},{10... | collective-permute-start | bytes 12296 | tf_op jit(solution)/shard_map/ppermute | solution.py:650
  50.6 4.8 %collective-permute-start.12 = (f32[8,128]{1,0:T(8,128)S(1)}, f32[8,128]{1,0:T(8,128)S(1)}, u32[]{:S(2)}, u32[]{:S(2)}) collective-permute-start(f32[8,128]{1,0:T(8,128)S(1)} %get-tuple-element.84.refs_0_.refs_4_), channel_id=1, source_target_pairs={{0,24},{8,16},{16,8},{24,0},{1,25},{9,17},{17,9},{25,1},{2,26},{10... | collective-permute-start | bytes 12296 | tf_op jit(solution)/shard_map/ppermute | solution.py:650
  50.7 4.7 %collective-permute-start.11 = (f32[8,128]{1,0:T(8,128)S(1)}, f32[8,128]{1,0:T(8,128)S(1)}, u32[]{:S(2)}, u32[]{:S(2)}) collective-permute-start(f32[8,128]{1,0:T(8,128)S(1)} %get-tuple-element.84.refs_0_.refs_4_), channel_id=1, source_target_pairs={{0,16},{8,24},{16,0},{24,8},{1,17},{9,25},{17,1},{25,9},{2,18},{10... | collective-permute-start | bytes 12296 | tf_op jit(solution)/shard_map/ppermute | solution.py:650
  51.5 3.9 %collective-permute-start.10 = (f32[8,128]{1,0:T(8,128)S(1)}, f32[8,128]{1,0:T(8,128)S(1)}, u32[]{:S(2)}, u32[]{:S(2)}) collective-permute-start(f32[8,128]{1,0:T(8,128)S(1)} %get-tuple-element.84.refs_0_.refs_4_), channel_id=1, source_target_pairs={{0,8},{8,0},{16,24},{24,16},{1,9},{9,1},{17,25},{25,17},{2,10},{10... | collective-permute-start | bytes 12296 | tf_op jit(solution)/shard_map/ppermute | solution.py:650
  55.3 4.7 %collective-permute-start.14 = (f32[6,16,128]{2,1,0:T(8,128)S(1)}, f32[6,16,128]{2,1,0:T(8,128)S(1)}, u32[]{:S(2)}, u32[]{:S(2)}) collective-permute-start(f32[6,16,128]{2,1,0:T(8,128)S(1)} %get-tuple-element.105), channel_id=1, source_target_pairs={{0,8},{8,0},{16,24},{24,16},{1,9},{9,1},{17,25},{25,17},{2,10},{10... | collective-permute-start | bytes 147464 | tf_op jit(solution)/shard_map/ppermute | solution.py:650
  59.5 1.4 %collective-permute-start.13 = (f32[6,16,128]{2,1,0:T(8,128)S(1)}, f32[6,16,128]{2,1,0:T(8,128)S(1)}, u32[]{:S(2)}, u32[]{:S(2)}) collective-permute-start(f32[6,16,128]{2,1,0:T(8,128)S(1)} %get-tuple-element.99), channel_id=1, source_target_pairs={{0,8},{8,0},{16,24},{24,16},{1,9},{9,1},{17,25},{25,17},{2,10},{10... | collective-permute-start | bytes 147464 | tf_op jit(solution)/shard_map/ppermute | solution.py:650
  60.0 6.2 %collective-permute-start.19 = (f32[6,16,128]{2,1,0:T(8,128)S(1)}, f32[6,16,128]{2,1,0:T(8,128)S(1)}, u32[]{:S(2)}, u32[]{:S(2)}) collective-permute-start(f32[6,16,128]{2,1,0:T(8,128)S(1)} %add.22.ready1.second), channel_id=1, source_target_pairs={{0,16},{8,24},{16,0},{24,8},{1,17},{9,25},{17,1},{25,9},{2,18},{10... | collective-permute-start | bytes 147464 | tf_op jit(solution)/shard_map/ppermute | solution.py:650
  60.9 5.3 %collective-permute-start.18 = (f32[6,16,128]{2,1,0:T(8,128)S(1)}, f32[6,16,128]{2,1,0:T(8,128)S(1)}, u32[]{:S(2)}, u32[]{:S(2)}) collective-permute-start(f32[6,16,128]{2,1,0:T(8,128)S(1)} %add.21.ready0.first), channel_id=1, source_target_pairs={{0,16},{8,24},{16,0},{24,8},{1,17},{9,25},{17,1},{25,9},{2,18},{10... | collective-permute-start | bytes 147464 | tf_op jit(solution)/shard_map/ppermute | solution.py:650
  67.0 15.5 %all-to-all-start.1 = ((bf16[8,192,128]{2,1,0:T(8,128)(2,1)}), bf16[8,192,128]{2,1,0:T(8,128)(2,1)S(1)}, u32[]{:S(2)}, u32[]{:S(2)}) async-start(bf16[8,192,128]{2,1,0:T(8,128)(2,1)} %shard_map.205), calls=%async_computation.1 | async-start | bytes 786432 | tf_op jit(solution)/shard_map/all_to_all | solution.py:828
  71.2 1.9 %collective-permute-start.15 = (f32[64,128]{1,0:T(8,128)S(1)}, f32[64,128]{1,0:T(8,128)S(1)}, u32[]{:S(2)}, u32[]{:S(2)}) collective-permute-start(f32[64,128]{1,0:T(8,128)S(1)} %get-tuple-element.107), channel_id=1, source_target_pairs={{0,8},{8,0},{16,24},{24,16},{1,9},{9,1},{17,25},{25,17},{2,10},{10... | collective-permute-start | bytes 98312 | tf_op jit(solution)/shard_map/ppermute | solution.py:650
  71.2 4.1 %collective-permute-start.16 = (f32[64,128]{1,0:T(8,128)S(1)}, f32[64,128]{1,0:T(8,128)S(1)}, u32[]{:S(2)}, u32[]{:S(2)}) collective-permute-start(f32[64,128]{1,0:T(8,128)S(1)} %get-tuple-element.108), channel_id=1, source_target_pairs={{0,16},{8,24},{16,0},{24,8},{1,17},{9,25},{17,1},{25,9},{2,18},{10... | collective-permute-start | bytes 98312 | tf_op jit(solution)/shard_map/ppermute | solution.py:650
  72.0 3.7 %collective-permute-start.17 = (f32[64,128]{1,0:T(8,128)S(1)}, f32[64,128]{1,0:T(8,128)S(1)}, u32[]{:S(2)}, u32[]{:S(2)}) collective-permute-start(f32[64,128]{1,0:T(8,128)S(1)} %get-tuple-element.109), channel_id=1, source_target_pairs={{0,24},{8,16},{16,8},{24,0},{1,25},{9,17},{17,9},{25,1},{2,26},{10... | collective-permute-start | bytes 98312 | tf_op jit(solution)/shard_map/ppermute | solution.py:650
  82.5 1.7 %collective-permute-start.20 = (bf16[8,192,128]{2,1,0:T(8,128)(2,1)S(1)}, bf16[8,192,128]{2,1,0:T(8,128)(2,1)S(1)}, u32[]{:S(2)}, u32[]{:S(2)}) collective-permute-start(bf16[8,192,128]{2,1,0:T(8,128)(2,1)S(1)} %all-to-all-done.1.near), channel_id=1, source_target_pairs={{0,8},{8,0},{16,24},{24,16},{1,9},{9,1},{17,25},{25,17},{2,10},{10... | collective-permute-start | bytes 1179656 | tf_op jit(solution)/shard_map/ppermute | solution.py:650

commit v7 on v6

--- a/solution.py
+++ b/solution.py
@@ -12,7 +12,7 @@
 REACH = 256
 RIM = 4
 TILE = 16
-LIMITS = (4, 13, 9, 7, 9, 8, 10, 2, 6, 2, 2, 3)
+LIMITS = (4, 14, 9, 7, 9, 8, 10, 2, 6, 2, 2, 3)
 
 eps_norm = 1e-05
 highest = lax.Precision.HIGHEST
@@ -126,50 +126,34 @@
     target[m, channels:, :channels] = zero
 
 
-def forward_blocks(w_z, w_xy, layer):
-    def block_of(i, j):
-        if i == 3:
-            return w_z[layer, 2 * j]
-        at = i * 3 + j
-        return w_z[layer, 1] if at == 4 else w_xy[layer, at - (at > 4)]
-
-    return block_of
-
-
 def taken(weights, layer):
     return lambda i, j: weights[layer, i * 3 + j]
 
 
-def kernel_mix(block, mixed, mixed_own):
-    parts = mixed.shape[0]
-    alpha_bar = jnp.cos(0.5 * math.pi * (block[6, 0, 0:1] + 0.5) / STEPS) ** 2
-    keep, add = jnp.sqrt(alpha_bar), jnp.sqrt(1.0 - alpha_bar)
-    for k in range(3):
-        noise = block[3 + k, 0]
-        noisy = keep * block[k, 0] + add * noise
-        mixed_own[4 * k : 4 * k + 4] = noisy
-        for part in range(parts):
-            mixed[part, 4 * k : 4 * k + 4] = noisy
-            mixed[part, 12 + 4 * k : 16 + 4 * k] = noise
-
-
-def kernel_prepare(steps, w_z, w_xy, w_point, small, w_front, point, w_back, point_back, lift_in, lift_out,
-                   steps_on):
-    steps_on[0], steps_on[1] = steps[0], steps[1]
-    point[...] = w_point[...]
+def fetch(pairs, sems):
+    copies = [pltpu.make_async_copy(one, two, sems.at[at]) for at, (one, two) in enumerate(pairs)]
+    for copy in copies:
+        copy.start()
+    for copy in copies:
+        copy.wait()
+
+
+def kernel_prepare(steps, w_z, w_xy, w_point, w_in_far, gains_far, w_out_far, w_front, point, w_back, point_back,
+                   lift_in, lift_out, small, steps_on, w_in, gains, w_out, sems):
+    pairs = [(w_point, point), (w_in_far, w_in), (gains_far, gains), (w_out_far, w_out), (steps, steps_on)]
     for layer in range(2):
-        forward = forward_blocks(w_z, w_xy, layer)
-        for i in range(3):
-            for j in range(3):
-                w_front[layer, i * 3 + j] = forward(i, j)
-        for m in range(2):
-            w_front[layer, 9 + m] = forward(3, m)
-        for i in range(3):
-            for j in range(3):
-                w_back[layer, i * 3 + j] = forward(2 - i, 2 - j).T
-        for m in range(2):
-            w_back[layer, 9 + m] = forward(3, 1 - m).T
-        point_back[layer] = w_point[layer].T
+        pairs.append((w_xy.at[layer, pl.ds(0, 4)], w_front.at[layer, pl.ds(0, 4)]))
+        pairs.append((w_xy.at[layer, pl.ds(4, 4)], w_front.at[layer, pl.ds(5, 4)]))
+        for m, at in ((1, 4), (0, 9), (2, 10)):
+            pairs.append((w_z.at[layer, m], w_front.at[layer, at]))
+    fetch(pairs, sems)
+    small[...] = jnp.concatenate([w_in[...], gains[...], w_out[...].astype(f32)], axis=0)
+    for layer in range(2):
+        for at in range(9):
+            w_back[layer, at] = w_front[layer, 8 - at].T
+        w_back[layer, 9] = w_front[layer, 10].T
+        w_back[layer, 10] = w_front[layer, 9].T
+        point_back[layer] = point[layer].T
     whole = spread_rows(small[0:3], 0)
     high, low = halves(whole)
     lift_in[0:32] = high
@@ -240,8 +224,9 @@
     square = value * value
     bent = jnp.tanh(value * (scale + (scale * 0.044715) * square))
     half = 0.5 + 0.5 * bent
-    slope = half + value * (0.5 - 0.5 * (bent * bent)) * (scale + (3.0 * 0.044715 * scale) * square)
-    return value * half, slope
+    result = value * half
+    slope = half + result * (1.0 - half) * (2.0 * scale + (6.0 * 0.044715 * scale) * square)
+    return result, slope
 
 
 def members_of(parts):
@@ -309,16 +294,21 @@
     put_rows(stats, total, masked_total(mask, spread))
 
 
-def kernel_first(cells_z, per_member, sc, near, far, lift_in, small, shift_bias, w_front, wp,
-                 stream, padded, act, slope, gathered, stats, consts,
-                 shifted, taps, pair, acc, old, source):
+def kernel_first(cells_z, per_member, sc, near, far, amounts, lift_in, small, shift_bias, w_front, wp,
+                 stream, padded, act, slope, gathered, stats, consts, mixed_own,
+                 shifted, taps, pair, acc, old, source, fields):
     planes, rows, lanes = stream.shape
     channels = lanes // 4
     depth = near.shape[2]
     place = Place(sc, rows)
+    keep, add = amounts[0:1], amounts[1:2]
+    for at, ref in enumerate((near, far)):
+        fields[at, :, 12:24] = ref[:, 12:24]
+        fields[at, :, 0:12] = keep * ref[:, 0:12] + add * ref[:, 12:24]
+    mixed_own[...] = fields[0, place.member // 2 * planes + lax.axis_index("gx"), 0:12]
     cell_count = float(planes * 4 * cells_z)
     comps = [
-        jnp.concatenate([ref[:, 4 * k : 4 * k + 4, :] for ref in (near, far)], axis=0) for k in range(3)
+        jnp.concatenate([fields[at, :, 4 * k : 4 * k + 4, :] for at in range(2)], axis=0) for k in range(3)
     ]
 
     def all_sum(value):
@@ -342,10 +332,10 @@
     blank = jnp.zeros((8, depth), f32)
     core = lax.rem(place.member, 2)
     for slab in range(cells_z // depth):
-        ref, side = (near, core) if slab % 2 == 0 else (far, 1 - core)
+        side = core if slab % 2 == 0 else 1 - core
         at = pl.ds(pl.multiple_of((slab // 2 * 2 + side) * depth, depth), depth)
         for x in range(planes):
-            high, low = halves(jnp.concatenate([ref[slab // 2 * planes + x], blank], axis=0))
+            high, low = halves(jnp.concatenate([fields[slab % 2, slab // 2 * planes + x], blank], axis=0))
             source[x, 0:32, at] = high
             source[x, 32:64, at] = low
             source[x, 64:96, at] = high
@@ -628,11 +618,15 @@
         target[32:64] = tail
 
 
-def call(kernel, outs, scratch, flops, limit, *args, scalars=True, scalar_out=0, ready=()):
+def call(kernel, outs, scratch, flops, limit, *args, scalars=True, scalar_out=0, ready=(), far=()):
     spec = pl.BlockSpec(memory_space=pltpu.VMEM)
     specs = [pl.BlockSpec(memory_space=pltpu.SMEM)] * scalars + [spec] * (len(args) - scalars)
     for at in ready:
         specs[at] = pl.BlockSpec(memory_space=pl.ANY)
+    args = list(args)
+    for at in far:
+        specs[at] = pl.BlockSpec(memory_space=pltpu.HBM)
+        args[at] = pltpu.with_memory_space_constraint(args[at], pltpu.HBM)
     smem = pl.BlockSpec(memory_space=pltpu.SMEM)
     return pl.pallas_call(
         kernel,
@@ -735,15 +729,14 @@
     cell_count = per_member * members
     inv_area = 4.0 / cell_count
 
-    _, features, time_raw, time_code = time_terms(timestep, w_time)
+    alpha_bar, features, time_raw, time_code = time_terms(timestep, w_time)
     parts = members // 2 * groups
-    moment = jnp.broadcast_to(timestep.astype(f32).reshape(1, 1, 1, 1), (1,) + clean_field.shape[1:])
-    block = jnp.concatenate([clean_field, noise_field, moment], axis=0)
-    mixed, mixed_own = call(
-        kernel_mix, [((parts, 24, depth), f32), ((12, depth), f32)], [], 10**5, LIMITS[7], block, scalars=False,
-    )
+    block = jnp.concatenate([clean_field, noise_field], axis=0).reshape(24, depth)
+    block = jnp.broadcast_to(block[None], (parts, 24, depth))
+    amounts = jnp.stack([jnp.sqrt(alpha_bar), jnp.sqrt(1.0 - alpha_bar)])
+    amounts = jnp.broadcast_to(amounts[:, None], (2, depth))
     same_core = [[m * groups + g for m in range(core, members, 2) for g in range(groups)] for core in range(2)]
-    near = lax.all_to_all(mixed, ("gz", "gx"), 0, 0, axis_index_groups=same_core)
+    near = lax.all_to_all(block, ("gz", "gx"), 0, 0, axis_index_groups=same_core)
     far = swapped(near, "gz", 1)
     shift_bias = biases + time_code
 
@@ -761,18 +754,19 @@
     grad_out = ((6, share, channels), f32)
 
     taps_out, point_out = ((2, 11, channels, channels), bf16), ((2, channels, channels), bf16)
-    small = jnp.concatenate([w_in, norm_gains, w_out.astype(f32)], axis=0)
-    w_front, point, w_back, point_back, lift_in, lift_out, steps_on = call(
+    w_front, point, w_back, point_back, lift_in, lift_out, small, steps_on = call(
         kernel_prepare,
-        [taps_out, point_out, taps_out, point_out, lift, lift, ((2,), jnp.int32)],
-        [], 10**8, LIMITS[0], dilations, w_z, w_xy, w_point, small, scalar_out=1,
-    )
-    stream1, normed0, act0, slope0, gathered, stats1, consts0 = call(
+        [taps_out, point_out, taps_out, point_out, lift, lift, ((9, channels), f32), ((2,), jnp.int32)],
+        [((3, channels), f32), ((3, channels), f32), ((3, channels), bf16), pltpu.SemaphoreType.DMA((15,))],
+        10**8, LIMITS[0], dilations, w_z, w_xy, w_point, w_in, norm_gains, w_out, scalar_out=1,
+        far=tuple(range(7)),
+    )
+    stream1, normed0, act0, slope0, gathered, stats1, consts0, mixed_own = call(
         functools.partial(kernel_first, cells_z, per_member),
-        [(big, f32), conv_scratch[0], (big, bf16), (big, bf16), thin, vec, ((16, channels), f32)],
-        conv_scratch[1:] + [pair, flat, (big, f32), ((planes, 128, cells_z), bf16)],
+        [(big, f32), conv_scratch[0], (big, bf16), (big, bf16), thin, vec, ((16, channels), f32), ((12, depth), f32)],
+        conv_scratch[1:] + [pair, flat, (big, f32), ((planes, 128, cells_z), bf16), ((2, parts, 24, depth), f32)],
         4 * 10**9, LIMITS[1],
-        steps_on, near, far, lift_in, small, shift_bias, w_front, point,
+        steps_on, near, far, amounts, lift_in, small, shift_bias, w_front, point,
     )
     stream2, normed1, act1, slope1, stats2, consts1 = call(
         functools.partial(kernel_second, per_member),

time: 86.1 us -> 84.5 us (0.981)
  waiting for transfers between devices: 20.1 us -> 24.1 us
  local copies, waits for them, and re-layouts: 3.54 us -> 0.77 us
  other arithmetic: 3 us -> 0.97 us
    unnamed x10 -> x4, local copies, waits for them, and re-layouts: 3.47 us -> 0.01 us
    all_to_all x1, waiting for transfers between devices: 2.09 us -> 5.24 us  [per_device_grouped(): lax.all_to_all(block, ('gz', 'gx'), 0, 0, axis_index_groups=same_core)]
    pallas_call x12 -> x11, Pallas kernels: 32.4 us -> 32.2 us  [call(): pl.pallas_call(kernel, out_shape=[jax.ShapeDtypeStruct(shape, dtype) for...]
  transfers between devices with their start and end apart: 23 -> 23, of which waited for: 12 -> 12; matrix products, arithmetic and copies ran while one was open for 3% -> 1% of each run, Pallas kernels for 15% -> 16%
where the time goes in v7:
time: 84.5 us; the launch traced here: 84.1 us
  Pallas kernels  32.2 us (38%)
  starting transfers between devices  24.2 us (29%)
  waiting for transfers between devices  24.1 us (29%)
  between operations  1.63 us (2%)
  other arithmetic  0.97 us (1%)
    pallas_call x11, Pallas kernels, call(): pl.pallas_call(kernel, out_shape=[jax.ShapeDtypeStruct(shape, dtype) for...  32.2 us
    ppermute x21, waiting for transfers between devices, swapped(): return lax.ppermute(value, axis, [(i, i ^ bit) for i in range(count)])  12.6 us
    ppermute x21, starting transfers between devices, swapped(): return lax.ppermute(value, axis, [(i, i ^ bit) for i in range(count)])  12.4 us
    all_to_all x1, starting transfers between devices, per_device_grouped(): lax.all_to_all(block, ('gz', 'gx'), 0, 0, axis_index_groups=same_core)  8.31 us
    all_to_all x1, waiting for transfers between devices, per_device_grouped(): near_grads = lax.all_to_all(spread, 'gx', 0, 0)  6.31 us
    all_to_all x1, waiting for transfers between devices, per_device_grouped(): lax.all_to_all(block, ('gz', 'gx'), 0, 0, axis_index_groups=same_core)  5.24 us
    all_to_all x1, starting transfers between devices, per_device_grouped(): near_grads = lax.all_to_all(spread, 'gx', 0, 0)  3.45 us
  transfers between devices with their start and end apart: 23, of which 12 were waited for; matrix products, arithmetic and copies ran while one was open for 1% of the time, Pallas kernels for 16%

profile of v7, /device:TPU:0, one launch (start us, length us, event | category | flops | bytes accessed | tf_op | source)
XLA Modules:
  0.0 84.1 jit_solution(11693379946821194476)
XLA Ops:
  0.7 0.7 pad_maximum_fusion
  1.4 0.7 broadcast_in_dim.21
  2.1 8.3 %all-to-all-start = ((f32[16,24,128]{2,1,0:T(8,128)}), f32[16,24,128]{2,1,0:T(8,128)S(1)}, u32[]{:S(2)}, u32[]{:S(2)}) async-start(f32[16,24,128]{2,1,0:T(8,128)} %broadcast_in_dim.21), calls=%async_computation | async-start | bytes 393216 | tf_op jit(solution)/shard_map/all_to_all | solution.py:739
  11.2 0.1 pad_maximum_fusion.1
  11.3 2.0 %shard_map.195 = (bf16[2,11,128,128]{3,2,1,0:T(8,128)(2,1)S(1)}, bf16[2,128,128]{2,1,0:T(8,128)(2,1)S(1)}, bf16[2,11,128,128]{3,2,1,0:T(8,128)(2,1)S(1)}, bf16[2...) custom-call(s32[2]{0:T(128)} %steps.1, ...), custom_call_target="tpu_custom_call" | custom-call | flops 100000000 | bytes 8388608 | tf_op jit(solution)/shard_map/pallas_call | solution.py:631
  13.3 0.2 divide_multiply_fusion
  13.6 5.2 %all-to-all-done.near = f32[16,24,128]{2,1,0:T(8,128)S(1)} async-done(((f32[16,24,128]{2,1,0:T(8,128)}), f32[16,24,128]{2,1,0:T(8,128)S(1)}, u32[]{:S(2)}, u32[]{:S(2)}) %all-to-all-start) | async-done | bytes 196640 | tf_op jit(solution)/shard_map/all_to_all | solution.py:739
  18.8 1.4 %collective-permute-done.far = f32[16,24,128]{2,1,0:T(8,128)S(1)} collective-permute-done((f32[16,24,128]{2,1,0:T(8,128)S(1)}, f32[16,24,128]{2,1,0:T(8,128)S(1)}, u32[]{:S(2)}, u32[]{:S(2)}) %collective-permute-start) | collective-permute-done | bytes 196640 | tf_op jit(solution)/shard_map/ppermute | solution.py:644
  20.3 5.3 %shard_map.196 = (f32[8,144,512]{2,1,0:T(8,128)S(1)}, bf16[10,144,512]{2,1,0:T(8,128)(2,1)S(1)}, bf16[8,144,512]{2,1,0:T(8,128)(2,1)S(1)}, bf16[8,144,512]{2,1,0...) custom-call(s32[2]{0:T(128)S(1)} %get-tuple-element.66.sc, ...), custom_call_target="tpu_custom_call" | custom-call | flops 4000000000 | bytes 8388608 | tf_op jit(solution)/shard_map/pallas_call | solution.py:631
  25.6 1.0 %collective-permute-start.3 = (f32[8,128]{1,0:T(8,128)S(1)}, f32[8,128]{1,0:T(8,128)S(1)}, u32[]{:S(2)}, u32[]{:S(2)}) collective-permute-start(f32[8,128]{1,0:T(8,128)S(1)} %get-tuple-element.71.refs_0_), channel_id=1, source_target_pairs={{0,24},{8,16},{16,8},{24,0},{1,25},{9,17},{17,9},{25,1},{2,26},{10... | collective-permute-start | bytes 12296 | tf_op jit(solution)/shard_map/ppermute | solution.py:644
  26.6 0.8 collective-permute-start.2
  27.4 0.1 collective-permute-start.1
  27.5 1.2 %collective-permute-done.3.refs_3_ = f32[8,128]{1,0:T(8,128)S(1)} collective-permute-done((f32[8,128]{1,0:T(8,128)S(1)}, f32[8,128]{1,0:T(8,128)S(1)}, u32[]{:S(2)}, u32[]{:S(2)}) %collective-permute-start.3) | collective-permute-done | bytes 4128 | tf_op jit(solution)/shard_map/ppermute | solution.py:644
  28.7 1.6 %collective-permute-done.2.refs_2_ = f32[8,128]{1,0:T(8,128)S(1)} collective-permute-done((f32[8,128]{1,0:T(8,128)S(1)}, f32[8,128]{1,0:T(8,128)S(1)}, u32[]{:S(2)}, u32[]{:S(2)}) %collective-permute-start.2) | collective-permute-done | bytes 4128 | tf_op jit(solution)/shard_map/ppermute | solution.py:644
  30.2 4.5 %shard_map.197 = (f32[8,144,512]{2,1,0:T(8,128)S(1)}, bf16[10,144,512]{2,1,0:T(8,128)(2,1)S(1)}, bf16[8,144,512]{2,1,0:T(8,128)(2,1)S(1)}, bf16[8,144,512]{2,1,0...) custom-call(s32[2]{0:T(128)S(1)} %get-tuple-element.66.sc, f32[8,128]{1,0:T(8,128)S(1)} %get-tuple-element.71.refs_0_, ...), custom_call_target="tpu_custom_call" | custom-call | flops 4000000000 | bytes 8388608 | tf_op jit(solution)/shard_map/pallas_call | solution.py:631
  34.7 0.1 collective-permute-start.6
  34.8 0.9 %collective-permute-start.5 = (f32[8,128]{1,0:T(8,128)S(1)}, f32[8,128]{1,0:T(8,128)S(1)}, u32[]{:S(2)}, u32[]{:S(2)}) collective-permute-start(f32[8,128]{1,0:T(8,128)S(1)} %get-tuple-element.73.refs_0_), channel_id=1, source_target_pairs={{0,16},{8,24},{16,0},{24,8},{1,17},{9,25},{17,1},{25,9},{2,18},{10... | collective-permute-start | bytes 12296 | tf_op jit(solution)/shard_map/ppermute | solution.py:644
  35.6 1.0 %collective-permute-start.4 = (f32[8,128]{1,0:T(8,128)S(1)}, f32[8,128]{1,0:T(8,128)S(1)}, u32[]{:S(2)}, u32[]{:S(2)}) collective-permute-start(f32[8,128]{1,0:T(8,128)S(1)} %get-tuple-element.73.refs_0_), channel_id=1, source_target_pairs={{0,8},{8,0},{16,24},{24,16},{1,9},{9,1},{17,25},{25,17},{2,10},{10... | collective-permute-start | bytes 12296 | tf_op jit(solution)/shard_map/ppermute | solution.py:644
  36.6 1.2 %collective-permute-done.6.refs_3_ = f32[8,128]{1,0:T(8,128)S(1)} collective-permute-done((f32[8,128]{1,0:T(8,128)S(1)}, f32[8,128]{1,0:T(8,128)S(1)}, u32[]{:S(2)}, u32[]{:S(2)}) %collective-permute-start.6) | collective-permute-done | bytes 4128 | tf_op jit(solution)/shard_map/ppermute | solution.py:644
  37.8 0.7 collective-permute-done.5.refs_2_
  38.5 2.3 %shard_map.198 = (f32[144,128]{1,0:T(8,128)S(1)}, bf16[8,144,128]{2,1,0:T(8,128)(2,1)S(1)}, f32[8,128]{1,0:T(8,128)S(1)}, f32[8,128]{1,0:T(8,128)S(1)}, f32[8,128]{1,0:T(8,128)S(1)}) custom-call(s32[2]{0:T(128)S(1)} %get-tuple-element.66.sc, f32[8,128]{1,0:T(8,128)S(1)} %get-tuple-element.73.refs_0_, f32[8,128]{1,0:T(8,128)S(1)} %collective-permute-done.4.refs_1_, ...), custom_call_target="tpu_custom_call" | custom-call | flops 1000000000 | bytes 8388608 | tf_op jit(solution)/shard_map/pallas_call | solution.py:631
  40.8 0.6 collective-permute-start.9
  41.4 0.8 collective-permute-start.8
  42.2 0.6 collective-permute-start.7
  42.7 1.2 %collective-permute-done.9.refs_3_.refs_11_ = f32[8,128]{1,0:T(8,128)S(1)} collective-permute-done((f32[8,128]{1,0:T(8,128)S(1)}, f32[8,128]{1,0:T(8,128)S(1)}, u32[]{:S(2)}, u32[]{:S(2)}) %collective-permute-start.9) | collective-permute-done | bytes 4128 | tf_op jit(solution)/shard_map/ppermute | solution.py:644
  43.9 1.1 %collective-permute-done.8.refs_2_.refs_10_ = f32[8,128]{1,0:T(8,128)S(1)} collective-permute-done((f32[8,128]{1,0:T(8,128)S(1)}, f32[8,128]{1,0:T(8,128)S(1)}, u32[]{:S(2)}, u32[]{:S(2)}) %collective-permute-start.8) | collective-permute-done | bytes 4128 | tf_op jit(solution)/shard_map/ppermute | solution.py:644
  45.0 4.6 %shard_map.199 = (f32[8,144,512]{2,1,0:T(8,128)S(1)}, f32[8,144,512]{2,1,0:T(8,128)S(1)}, f32[8,128]{1,0:T(8,128)S(1)}, bf16[10,144,512]{2,1,0:T(8,128)(2,1)S(1)...) custom-call(s32[2]{0:T(128)S(1)} %get-tuple-element.66.sc, ...), custom_call_target="tpu_custom_call" | custom-call | flops 6000000000 | bytes 8388608 | tf_op jit(solution)/shard_map/pallas_call | solution.py:631
  49.6 0.1 collective-permute-start.12
  49.7 0.8 collective-permute-start.11
  50.5 1.0 %collective-permute-start.10 = (f32[8,128]{1,0:T(8,128)S(1)}, f32[8,128]{1,0:T(8,128)S(1)}, u32[]{:S(2)}, u32[]{:S(2)}) collective-permute-start(f32[8,128]{1,0:T(8,128)S(1)} %get-tuple-element.84.refs_0_.refs_4_), channel_id=1, source_target_pairs={{0,8},{8,0},{16,24},{24,16},{1,9},{9,1},{17,25},{25,17},{2,10},{10... | collective-permute-start | bytes 12296 | tf_op jit(solution)/shard_map/ppermute | solution.py:644
  51.5 2.8 %shard_map.201 = (f32[6,16,128]{2,1,0:T(8,128)S(1)}, f32[6,16,128]{2,1,0:T(8,128)S(1)}) custom-call(s32[2]{0:T(128)S(1)} %get-tuple-element.66.sc, bf16[10,144,512]{2,1,0:T(8,128)(2,1)S(1)} %get-tuple-element.100.padded, bf16[2,8,144,512]{3,2,1,0:T(8,128)(2,1)S(1)} %get-tuple-element.101.shifted, bf16[8,144,512]{2,1,0:T(8,128)(2,1)S(1)} %get-tuple-element.102.scot, ...), custom_call_target="tpu_custom_call" | custom-call | flops 2000000000 | bytes 8388608 | tf_op jit(solution)/shard_map/pallas_call | solution.py:631
  54.3 0.1 collective-permute-start.14
  54.4 4.0 %shard_map.200 = (f32[8,144,512]{2,1,0:T(8,128)S(1)}, f32[8,128]{1,0:T(8,128)S(1)}, f32[6,16,128]{2,1,0:T(8,128)S(1)}, f32[6,16,128]{2,1,0:T(8,128)S(1)}, bf16[1...) custom-call(s32[2]{0:T(128)S(1)} %get-tuple-element.66.sc, ...), custom_call_target="tpu_custom_call" | custom-call | flops 4000000000 | bytes 8388608 | tf_op jit(solution)/shard_map/pallas_call | solution.py:631
  58.5 0.5 collective-permute-start.13
  59.0 0.8 collective-permute-start.19
  59.9 1.3 %collective-permute-start.18 = (f32[6,16,128]{2,1,0:T(8,128)S(1)}, f32[6,16,128]{2,1,0:T(8,128)S(1)}, u32[]{:S(2)}, u32[]{:S(2)}) collective-permute-start(f32[6,16,128]{2,1,0:T(8,128)S(1)} %add.25.ready0.first), channel_id=1, source_target_pairs={{0,16},{8,24},{16,0},{24,8},{1,17},{9,25},{17,1},{25,9},{2,18},{10... | collective-permute-start | bytes 147464 | tf_op jit(solution)/shard_map/ppermute | solution.py:644
  61.2 4.0 %shard_map.202 = (f32[64,128]{1,0:T(8,128)S(1)}, f32[64,128]{1,0:T(8,128)S(1)}, f32[64,128]{1,0:T(8,128)S(1)}, f32[64,128]{1,0:T(8,128)S(1)}) custom-call(s32[2]{0:T(128)S(1)} %get-tuple-element.66.sc, bf16[10,144,512]{2,1,0:T(8,128)(2,1)S(1)} %get-tuple-element.91.padded, bf16[2,8,144,512]{3,2,1,0:T(8,128)(2,1)S(1)} %get-tuple-element.92.shifted, ...), custom_call_target="tpu_custom_call" | custom-call | flops 4000000000 | bytes 8388608 | tf_op jit(solution)/shard_map/pallas_call | solution.py:631
  65.3 0.8 shard_map.204
  66.0 3.5 %all-to-all-start.1 = ((bf16[8,192,128]{2,1,0:T(8,128)(2,1)}), bf16[8,192,128]{2,1,0:T(8,128)(2,1)S(1)}, u32[]{:S(2)}, u32[]{:S(2)}) async-start(bf16[8,192,128]{2,1,0:T(8,128)(2,1)} %shard_map.204), calls=%async_computation.1 | async-start | bytes 786432 | tf_op jit(solution)/shard_map/all_to_all | solution.py:822
  69.6 0.9 %collective-permute-start.16 = (f32[64,128]{1,0:T(8,128)S(1)}, f32[64,128]{1,0:T(8,128)S(1)}, u32[]{:S(2)}, u32[]{:S(2)}) collective-permute-start(f32[64,128]{1,0:T(8,128)S(1)} %get-tuple-element.108), channel_id=1, source_target_pairs={{0,16},{8,24},{16,0},{24,8},{1,17},{9,25},{17,1},{25,9},{2,18},{10... | collective-permute-start | bytes 98312 | tf_op jit(solution)/shard_map/ppermute | solution.py:644
  70.4 1.0 %collective-permute-start.17 = (f32[64,128]{1,0:T(8,128)S(1)}, f32[64,128]{1,0:T(8,128)S(1)}, u32[]{:S(2)}, u32[]{:S(2)}) collective-permute-start(f32[64,128]{1,0:T(8,128)S(1)} %get-tuple-element.109), channel_id=1, source_target_pairs={{0,24},{8,16},{16,8},{24,0},{1,25},{9,17},{17,9},{25,1},{2,26},{10... | collective-permute-start | bytes 98312 | tf_op jit(solution)/shard_map/ppermute | solution.py:644
  71.4 0.1 fusion.6.refs_15_
  71.5 2.2 %collective-permute-done.16.refs_2_ = f32[64,128]{1,0:T(8,128)S(1)} collective-permute-done((f32[64,128]{1,0:T(8,128)S(1)}, f32[64,128]{1,0:T(8,128)S(1)}, u32[]{:S(2)}, u32[]{:S(2)}) %collective-permute-start.16) | collective-permute-done | bytes 32800 | tf_op jit(solution)/shard_map/ppermute | solution.py:644
  73.7 0.4 collective-permute-done.17.refs_3_
  74.0 0.8 shard_map.203
  74.8 6.3 %all-to-all-done.1.near = bf16[8,192,128]{2,1,0:T(8,128)(2,1)S(1)} async-done(((bf16[8,192,128]{2,1,0:T(8,128)(2,1)}), bf16[8,192,128]{2,1,0:T(8,128)(2,1)S(1)}, u32[]{:S(2)}, u32[]{:S(2)}) %all-to-all-start.1) | async-done | bytes 393248 | tf_op jit(solution)/shard_map/all_to_all | solution.py:822
  81.1 1.7 %collective-permute-done.20.far = bf16[8,192,128]{2,1,0:T(8,128)(2,1)S(1)} collective-permute-done((bf16[8,192,128]{2,1,0:T(8,128)(2,1)S(1)}, bf16[8,192,128]{2,1,0:T(8,128)(2,1)S(1)}, u32[]{:S(2)}, u32[]{:S(2)}) %collective-permute-start.20) | collective-permute-done | bytes 393248 | tf_op jit(solution)/shard_map/ppermute | solution.py:644
  82.9 1.3 %shard_map.205 = (f32[2,3,128,128]{3,2,1,0:T(8,128)}, f32[2,8,128,128]{3,2,1,0:T(8,128)}, f32[2,128,128]{2,1,0:T(8,128)}) custom-call(bf16[8,192,128]{2,1,0:T(8,128)(2,1)S(1)} %all-to-all-done.1.near, bf16[8,192,128]{2,1,0:T(8,128)(2,1)S(1)} %collective-permute-done.20.far), custom_call_target="tpu_custom_call" | custom-call | flops 1000000 | bytes 8388608 | tf_op jit(solution)/shard_map/pallas_call | solution.py:631
  (23 shorter events, 0.3 us)
Async XLA Ops:
  0.6 12.7 %copy-start = (f32[128,128]{1,0:T(8,128)S(1)}, f32[128,128]{1,0:T(8,128)}, u32[]{:S(2)}) copy-start(f32[128,128]{1,0:T(8,128)} %param.17) | copy-start | bytes 196612
  0.7 18.2 %copy-start.1 = (f32[2,128]{1,0:T(2,128)S(1)}, f32[2,128]{1,0:T(2,128)}, u32[]{:S(2)}) copy-start(f32[2,128]{1,0:T(2,128)} %param.21) | copy-start | bytes 3076
  2.1 16.7 %all-to-all-start = ((f32[16,24,128]{2,1,0:T(8,128)}), f32[16,24,128]{2,1,0:T(8,128)S(1)}, u32[]{:S(2)}, u32[]{:S(2)}) async-start(f32[16,24,128]{2,1,0:T(8,128)} %broadcast_in_dim.21), calls=%async_computation | async-start | bytes 393216 | tf_op jit(solution)/shard_map/all_to_all | solution.py:739
  18.8 1.4 %collective-permute-start = (f32[16,24,128]{2,1,0:T(8,128)S(1)}, f32[16,24,128]{2,1,0:T(8,128)S(1)}, u32[]{:S(2)}, u32[]{:S(2)}) collective-permute-start(f32[16,24,128]{2,1,0:T(8,128)S(1)} %all-to-all-done.near), channel_id=1, source_target_pairs={{0,8},{8,0},{16,24},{24,16},{1,9},{9,1},{17,25},{25,17},{2,10},{10... | collective-permute-start | bytes 589832 | tf_op jit(solution)/shard_map/ppermute | solution.py:644
  25.6 3.1 %collective-permute-start.3 = (f32[8,128]{1,0:T(8,128)S(1)}, f32[8,128]{1,0:T(8,128)S(1)}, u32[]{:S(2)}, u32[]{:S(2)}) collective-permute-start(f32[8,128]{1,0:T(8,128)S(1)} %get-tuple-element.71.refs_0_), channel_id=1, source_target_pairs={{0,24},{8,16},{16,8},{24,0},{1,25},{9,17},{17,9},{25,1},{2,26},{10... | collective-permute-start | bytes 12296 | tf_op jit(solution)/shard_map/ppermute | solution.py:644
  26.6 3.6 %collective-permute-start.2 = (f32[8,128]{1,0:T(8,128)S(1)}, f32[8,128]{1,0:T(8,128)S(1)}, u32[]{:S(2)}, u32[]{:S(2)}) collective-permute-start(f32[8,128]{1,0:T(8,128)S(1)} %get-tuple-element.71.refs_0_), channel_id=1, source_target_pairs={{0,16},{8,24},{16,0},{24,8},{1,17},{9,25},{17,1},{25,9},{2,18},{10... | collective-permute-start | bytes 12296 | tf_op jit(solution)/shard_map/ppermute | solution.py:644
  27.4 2.8 %collective-permute-start.1 = (f32[8,128]{1,0:T(8,128)S(1)}, f32[8,128]{1,0:T(8,128)S(1)}, u32[]{:S(2)}, u32[]{:S(2)}) collective-permute-start(f32[8,128]{1,0:T(8,128)S(1)} %get-tuple-element.71.refs_0_), channel_id=1, source_target_pairs={{0,8},{8,0},{16,24},{24,16},{1,9},{9,1},{17,25},{25,17},{2,10},{10... | collective-permute-start | bytes 12296 | tf_op jit(solution)/shard_map/ppermute | solution.py:644
  34.7 3.1 %collective-permute-start.6 = (f32[8,128]{1,0:T(8,128)S(1)}, f32[8,128]{1,0:T(8,128)S(1)}, u32[]{:S(2)}, u32[]{:S(2)}) collective-permute-start(f32[8,128]{1,0:T(8,128)S(1)} %get-tuple-element.73.refs_0_), channel_id=1, source_target_pairs={{0,24},{8,16},{16,8},{24,0},{1,25},{9,17},{17,9},{25,1},{2,26},{10... | collective-permute-start | bytes 12296 | tf_op jit(solution)/shard_map/ppermute | solution.py:644
  34.8 3.7 %collective-permute-start.5 = (f32[8,128]{1,0:T(8,128)S(1)}, f32[8,128]{1,0:T(8,128)S(1)}, u32[]{:S(2)}, u32[]{:S(2)}) collective-permute-start(f32[8,128]{1,0:T(8,128)S(1)} %get-tuple-element.73.refs_0_), channel_id=1, source_target_pairs={{0,16},{8,24},{16,0},{24,8},{1,17},{9,25},{17,1},{25,9},{2,18},{10... | collective-permute-start | bytes 12296 | tf_op jit(solution)/shard_map/ppermute | solution.py:644
  35.6 2.8 %collective-permute-start.4 = (f32[8,128]{1,0:T(8,128)S(1)}, f32[8,128]{1,0:T(8,128)S(1)}, u32[]{:S(2)}, u32[]{:S(2)}) collective-permute-start(f32[8,128]{1,0:T(8,128)S(1)} %get-tuple-element.73.refs_0_), channel_id=1, source_target_pairs={{0,8},{8,0},{16,24},{24,16},{1,9},{9,1},{17,25},{25,17},{2,10},{10... | collective-permute-start | bytes 12296 | tf_op jit(solution)/shard_map/ppermute | solution.py:644
  40.8 3.1 %collective-permute-start.9 = (f32[8,128]{1,0:T(8,128)S(1)}, f32[8,128]{1,0:T(8,128)S(1)}, u32[]{:S(2)}, u32[]{:S(2)}) collective-permute-start(f32[8,128]{1,0:T(8,128)S(1)} %get-tuple-element.77.refs_0_.refs_8_), channel_id=1, source_target_pairs={{0,24},{8,16},{16,8},{24,0},{1,25},{9,17},{17,9},{25,1},{2,26},{10... | collective-permute-start | bytes 12296 | tf_op jit(solution)/shard_map/ppermute | solution.py:644
  41.4 3.6 %collective-permute-start.8 = (f32[8,128]{1,0:T(8,128)S(1)}, f32[8,128]{1,0:T(8,128)S(1)}, u32[]{:S(2)}, u32[]{:S(2)}) collective-permute-start(f32[8,128]{1,0:T(8,128)S(1)} %get-tuple-element.77.refs_0_.refs_8_), channel_id=1, source_target_pairs={{0,16},{8,24},{16,0},{24,8},{1,17},{9,25},{17,1},{25,9},{2,18},{10... | collective-permute-start | bytes 12296 | tf_op jit(solution)/shard_map/ppermute | solution.py:644
  42.2 2.8 %collective-permute-start.7 = (f32[8,128]{1,0:T(8,128)S(1)}, f32[8,128]{1,0:T(8,128)S(1)}, u32[]{:S(2)}, u32[]{:S(2)}) collective-permute-start(f32[8,128]{1,0:T(8,128)S(1)} %get-tuple-element.77.refs_0_.refs_8_), channel_id=1, source_target_pairs={{0,8},{8,0},{16,24},{24,16},{1,9},{9,1},{17,25},{25,17},{2,10},{10... | collective-permute-start | bytes 12296 | tf_op jit(solution)/shard_map/ppermute | solution.py:644
  49.6 4.8 %collective-permute-start.12 = (f32[8,128]{1,0:T(8,128)S(1)}, f32[8,128]{1,0:T(8,128)S(1)}, u32[]{:S(2)}, u32[]{:S(2)}) collective-permute-start(f32[8,128]{1,0:T(8,128)S(1)} %get-tuple-element.84.refs_0_.refs_4_), channel_id=1, source_target_pairs={{0,24},{8,16},{16,8},{24,0},{1,25},{9,17},{17,9},{25,1},{2,26},{10... | collective-permute-start | bytes 12296 | tf_op jit(solution)/shard_map/ppermute | solution.py:644
  49.7 4.7 %collective-permute-start.11 = (f32[8,128]{1,0:T(8,128)S(1)}, f32[8,128]{1,0:T(8,128)S(1)}, u32[]{:S(2)}, u32[]{:S(2)}) collective-permute-start(f32[8,128]{1,0:T(8,128)S(1)} %get-tuple-element.84.refs_0_.refs_4_), channel_id=1, source_target_pairs={{0,16},{8,24},{16,0},{24,8},{1,17},{9,25},{17,1},{25,9},{2,18},{10... | collective-permute-start | bytes 12296 | tf_op jit(solution)/shard_map/ppermute | solution.py:644
  50.5 3.9 %collective-permute-start.10 = (f32[8,128]{1,0:T(8,128)S(1)}, f32[8,128]{1,0:T(8,128)S(1)}, u32[]{:S(2)}, u32[]{:S(2)}) collective-permute-start(f32[8,128]{1,0:T(8,128)S(1)} %get-tuple-element.84.refs_0_.refs_4_), channel_id=1, source_target_pairs={{0,8},{8,0},{16,24},{24,16},{1,9},{9,1},{17,25},{25,17},{2,10},{10... | collective-permute-start | bytes 12296 | tf_op jit(solution)/shard_map/ppermute | solution.py:644
  54.3 4.7 %collective-permute-start.14 = (f32[6,16,128]{2,1,0:T(8,128)S(1)}, f32[6,16,128]{2,1,0:T(8,128)S(1)}, u32[]{:S(2)}, u32[]{:S(2)}) collective-permute-start(f32[6,16,128]{2,1,0:T(8,128)S(1)} %get-tuple-element.105), channel_id=1, source_target_pairs={{0,8},{8,0},{16,24},{24,16},{1,9},{9,1},{17,25},{25,17},{2,10},{10... | collective-permute-start | bytes 147464 | tf_op jit(solution)/shard_map/ppermute | solution.py:644
  58.5 1.4 %collective-permute-start.13 = (f32[6,16,128]{2,1,0:T(8,128)S(1)}, f32[6,16,128]{2,1,0:T(8,128)S(1)}, u32[]{:S(2)}, u32[]{:S(2)}) collective-permute-start(f32[6,16,128]{2,1,0:T(8,128)S(1)} %get-tuple-element.99), channel_id=1, source_target_pairs={{0,8},{8,0},{16,24},{24,16},{1,9},{9,1},{17,25},{25,17},{2,10},{10... | collective-permute-start | bytes 147464 | tf_op jit(solution)/shard_map/ppermute | solution.py:644
  59.0 6.2 %collective-permute-start.19 = (f32[6,16,128]{2,1,0:T(8,128)S(1)}, f32[6,16,128]{2,1,0:T(8,128)S(1)}, u32[]{:S(2)}, u32[]{:S(2)}) collective-permute-start(f32[6,16,128]{2,1,0:T(8,128)S(1)} %add.26.ready1.second), channel_id=1, source_target_pairs={{0,16},{8,24},{16,0},{24,8},{1,17},{9,25},{17,1},{25,9},{2,18},{10... | collective-permute-start | bytes 147464 | tf_op jit(solution)/shard_map/ppermute | solution.py:644
  59.9 5.3 %collective-permute-start.18 = (f32[6,16,128]{2,1,0:T(8,128)S(1)}, f32[6,16,128]{2,1,0:T(8,128)S(1)}, u32[]{:S(2)}, u32[]{:S(2)}) collective-permute-start(f32[6,16,128]{2,1,0:T(8,128)S(1)} %add.25.ready0.first), channel_id=1, source_target_pairs={{0,16},{8,24},{16,0},{24,8},{1,17},{9,25},{17,1},{25,9},{2,18},{10... | collective-permute-start | bytes 147464 | tf_op jit(solution)/shard_map/ppermute | solution.py:644
  66.0 15.1 %all-to-all-start.1 = ((bf16[8,192,128]{2,1,0:T(8,128)(2,1)}), bf16[8,192,128]{2,1,0:T(8,128)(2,1)S(1)}, u32[]{:S(2)}, u32[]{:S(2)}) async-start(bf16[8,192,128]{2,1,0:T(8,128)(2,1)} %shard_map.204), calls=%async_computation.1 | async-start | bytes 786432 | tf_op jit(solution)/shard_map/all_to_all | solution.py:822
  69.5 2.0 %collective-permute-start.15 = (f32[64,128]{1,0:T(8,128)S(1)}, f32[64,128]{1,0:T(8,128)S(1)}, u32[]{:S(2)}, u32[]{:S(2)}) collective-permute-start(f32[64,128]{1,0:T(8,128)S(1)} %get-tuple-element.107), channel_id=1, source_target_pairs={{0,8},{8,0},{16,24},{24,16},{1,9},{9,1},{17,25},{25,17},{2,10},{10... | collective-permute-start | bytes 98312 | tf_op jit(solution)/shard_map/ppermute | solution.py:644
  69.6 4.1 %collective-permute-start.16 = (f32[64,128]{1,0:T(8,128)S(1)}, f32[64,128]{1,0:T(8,128)S(1)}, u32[]{:S(2)}, u32[]{:S(2)}) collective-permute-start(f32[64,128]{1,0:T(8,128)S(1)} %get-tuple-element.108), channel_id=1, source_target_pairs={{0,16},{8,24},{16,0},{24,8},{1,17},{9,25},{17,1},{25,9},{2,18},{10... | collective-permute-start | bytes 98312 | tf_op jit(solution)/shard_map/ppermute | solution.py:644
  70.4 3.6 %collective-permute-start.17 = (f32[64,128]{1,0:T(8,128)S(1)}, f32[64,128]{1,0:T(8,128)S(1)}, u32[]{:S(2)}, u32[]{:S(2)}) collective-permute-start(f32[64,128]{1,0:T(8,128)S(1)} %get-tuple-element.109), channel_id=1, source_target_pairs={{0,24},{8,16},{16,8},{24,0},{1,25},{9,17},{17,9},{25,1},{2,26},{10... | collective-permute-start | bytes 98312 | tf_op jit(solution)/shard_map/ppermute | solution.py:644
  81.1 1.7 %collective-permute-start.20 = (bf16[8,192,128]{2,1,0:T(8,128)(2,1)S(1)}, bf16[8,192,128]{2,1,0:T(8,128)(2,1)S(1)}, u32[]{:S(2)}, u32[]{:S(2)}) collective-permute-start(bf16[8,192,128]{2,1,0:T(8,128)(2,1)S(1)} %all-to-all-done.1.near), channel_id=1, source_target_pairs={{0,8},{8,0},{16,24},{24,16},{1,9},{9,1},{17,25},{25,17},{2,10},{10... | collective-permute-start | bytes 1179656 | tf_op jit(solution)/shard_map/ppermute | solution.py:644

commit v8 on v7

--- a/solution.py
+++ b/solution.py
@@ -317,6 +317,9 @@
 
     means = [all_sum(comp) / cell_count for comp in comps]
     gaps = [comp - mean[None] for comp, mean in zip(comps, means)]
+    for k in range(3):
+        for at in range(2):
+            fields[at, :, 4 * k : 4 * k + 4, :] = gaps[k][at * near.shape[0] : (at + 1) * near.shape[0]]
     covs = {}
     for j in range(3):
         for k in range(j, 3):
@@ -342,13 +345,12 @@
             source[x, 96:128, at] = jnp.zeros_like(high)
     pick = place.pick(cells_z).astype(f32).astype(bf16)
     scale = wide(inv_c * small[3:4, :])
-    mean_w = wide(mean_c)
     for x in range(planes):
         gathered[x] = mm_nt(pick, source[x]).astype(bf16)
     for x0 in range(0, planes, planes // 2):
         part = slice(x0, x0 + planes // 2)
         value = mm(gathered[part].reshape(planes // 2 * rows, 128), lift_in[...])
-        unit = ((value - mean_w) * scale).astype(bf16).reshape(planes // 2, rows, lanes)
+        unit = (value * scale).astype(bf16).reshape(planes // 2, rows, lanes)
         old[part] = value.reshape(planes // 2, rows, lanes)
         padded[x0 + 1 : x0 + 1 + planes // 2] = unit
     layer_forward(place, 0, padded, shifted, taps, pair, w_front, wp, shift_bias, old, stream,
@@ -703,7 +705,7 @@
             cross = cross + consts[row : row + 1] * rows_in[j]
         field_grad[k, 0] = value
         prediction[k, 0] = tail[12 + 4 * k : 16 + 4 * k]
-        in_sum = tail[40 + k : 41 + k] - cell_count * (consts[2 + k : 3 + k] * m_plain + m_cross * cross)
+        in_sum = tail[40 + k : 41 + k] - cell_count * (m_cross * cross)
         grad_w_in[k : k + 1] = inv_area * in_sum
     bias0, bias1 = tail[48:49], s1[2:3]
     grad_biases[...] = inv_area * jnp.concatenate([bias0, bias1], axis=0)

time: 84.5 us -> 84.6 us (level)
  no operation moved by 1% of the time
where the time goes in v8:
time: 84.6 us; the launch traced here: 84.2 us
  Pallas kernels  32.4 us (38%)
  starting transfers between devices  24.2 us (29%)
  waiting for transfers between devices  24.1 us (28%)
  between operations  1.63 us (2%)
  other arithmetic  0.97 us (1%)
    pallas_call x11, Pallas kernels, call(): pl.pallas_call(kernel, out_shape=[jax.ShapeDtypeStruct(shape, dtype) for...  32.4 us
    ppermute x21, waiting for transfers between devices, swapped(): return lax.ppermute(value, axis, [(i, i ^ bit) for i in range(count)])  12.6 us
    ppermute x21, starting transfers between devices, swapped(): return lax.ppermute(value, axis, [(i, i ^ bit) for i in range(count)])  12.4 us
    all_to_all x1, starting transfers between devices, per_device_grouped(): lax.all_to_all(block, ('gz', 'gx'), 0, 0, axis_index_groups=same_core)  8.31 us
    all_to_all x1, waiting for transfers between devices, per_device_grouped(): near_grads = lax.all_to_all(spread, 'gx', 0, 0)  6.31 us
    all_to_all x1, waiting for transfers between devices, per_device_grouped(): lax.all_to_all(block, ('gz', 'gx'), 0, 0, axis_index_groups=same_core)  5.24 us
    all_to_all x1, starting transfers between devices, per_device_grouped(): near_grads = lax.all_to_all(spread, 'gx', 0, 0)  3.45 us
  transfers between devices with their start and end apart: 23, of which 12 were waited for; matrix products, arithmetic and copies ran while one was open for 1% of the time, Pallas kernels for 16%

profile of v8, /device:TPU:0, one launch (start us, length us, event | category | flops | bytes accessed | tf_op | source)
XLA Modules:
  0.0 84.2 jit_solution(18180586364641523457)
XLA Ops:
  0.7 0.7 pad_maximum_fusion
  1.4 0.7 broadcast_in_dim.21
  2.1 8.3 %all-to-all-start = ((f32[16,24,128]{2,1,0:T(8,128)}), f32[16,24,128]{2,1,0:T(8,128)S(1)}, u32[]{:S(2)}, u32[]{:S(2)}) async-start(f32[16,24,128]{2,1,0:T(8,128)} %broadcast_in_dim.21), calls=%async_computation | async-start | bytes 393216 | tf_op jit(solution)/shard_map/all_to_all | solution.py:741
  11.2 0.1 pad_maximum_fusion.1
  11.3 2.0 %shard_map.195 = (bf16[2,11,128,128]{3,2,1,0:T(8,128)(2,1)S(1)}, bf16[2,128,128]{2,1,0:T(8,128)(2,1)S(1)}, bf16[2,11,128,128]{3,2,1,0:T(8,128)(2,1)S(1)}, bf16[2...) custom-call(s32[2]{0:T(128)} %steps.1, ...), custom_call_target="tpu_custom_call" | custom-call | flops 100000000 | bytes 8388608 | tf_op jit(solution)/shard_map/pallas_call | solution.py:633
  13.3 0.2 divide_multiply_fusion
  13.6 5.2 %all-to-all-done.near = f32[16,24,128]{2,1,0:T(8,128)S(1)} async-done(((f32[16,24,128]{2,1,0:T(8,128)}), f32[16,24,128]{2,1,0:T(8,128)S(1)}, u32[]{:S(2)}, u32[]{:S(2)}) %all-to-all-start) | async-done | bytes 196640 | tf_op jit(solution)/shard_map/all_to_all | solution.py:741
  18.8 1.4 %collective-permute-done.far = f32[16,24,128]{2,1,0:T(8,128)S(1)} collective-permute-done((f32[16,24,128]{2,1,0:T(8,128)S(1)}, f32[16,24,128]{2,1,0:T(8,128)S(1)}, u32[]{:S(2)}, u32[]{:S(2)}) %collective-permute-start) | collective-permute-done | bytes 196640 | tf_op jit(solution)/shard_map/ppermute | solution.py:646
  20.3 5.3 %shard_map.196 = (f32[8,144,512]{2,1,0:T(8,128)S(1)}, bf16[10,144,512]{2,1,0:T(8,128)(2,1)S(1)}, bf16[8,144,512]{2,1,0:T(8,128)(2,1)S(1)}, bf16[8,144,512]{2,1,0...) custom-call(s32[2]{0:T(128)S(1)} %get-tuple-element.66.sc, ...), custom_call_target="tpu_custom_call" | custom-call | flops 4000000000 | bytes 8388608 | tf_op jit(solution)/shard_map/pallas_call | solution.py:633
  25.7 1.0 %collective-permute-start.3 = (f32[8,128]{1,0:T(8,128)S(1)}, f32[8,128]{1,0:T(8,128)S(1)}, u32[]{:S(2)}, u32[]{:S(2)}) collective-permute-start(f32[8,128]{1,0:T(8,128)S(1)} %get-tuple-element.71.refs_0_), channel_id=1, source_target_pairs={{0,24},{8,16},{16,8},{24,0},{1,25},{9,17},{17,9},{25,1},{2,26},{10... | collective-permute-start | bytes 12296 | tf_op jit(solution)/shard_map/ppermute | solution.py:646
  26.7 0.8 collective-permute-start.2
  27.5 0.1 collective-permute-start.1
  27.6 1.2 %collective-permute-done.3.refs_3_ = f32[8,128]{1,0:T(8,128)S(1)} collective-permute-done((f32[8,128]{1,0:T(8,128)S(1)}, f32[8,128]{1,0:T(8,128)S(1)}, u32[]{:S(2)}, u32[]{:S(2)}) %collective-permute-start.3) | collective-permute-done | bytes 4128 | tf_op jit(solution)/shard_map/ppermute | solution.py:646
  28.8 1.5 %collective-permute-done.2.refs_2_ = f32[8,128]{1,0:T(8,128)S(1)} collective-permute-done((f32[8,128]{1,0:T(8,128)S(1)}, f32[8,128]{1,0:T(8,128)S(1)}, u32[]{:S(2)}, u32[]{:S(2)}) %collective-permute-start.2) | collective-permute-done | bytes 4128 | tf_op jit(solution)/shard_map/ppermute | solution.py:646
  30.3 4.5 %shard_map.197 = (f32[8,144,512]{2,1,0:T(8,128)S(1)}, bf16[10,144,512]{2,1,0:T(8,128)(2,1)S(1)}, bf16[8,144,512]{2,1,0:T(8,128)(2,1)S(1)}, bf16[8,144,512]{2,1,0...) custom-call(s32[2]{0:T(128)S(1)} %get-tuple-element.66.sc, f32[8,128]{1,0:T(8,128)S(1)} %get-tuple-element.71.refs_0_, ...), custom_call_target="tpu_custom_call" | custom-call | flops 4000000000 | bytes 8388608 | tf_op jit(solution)/shard_map/pallas_call | solution.py:633
  34.8 0.1 collective-permute-start.6
  34.9 0.9 %collective-permute-start.5 = (f32[8,128]{1,0:T(8,128)S(1)}, f32[8,128]{1,0:T(8,128)S(1)}, u32[]{:S(2)}, u32[]{:S(2)}) collective-permute-start(f32[8,128]{1,0:T(8,128)S(1)} %get-tuple-element.73.refs_0_), channel_id=1, source_target_pairs={{0,16},{8,24},{16,0},{24,8},{1,17},{9,25},{17,1},{25,9},{2,18},{10... | collective-permute-start | bytes 12296 | tf_op jit(solution)/shard_map/ppermute | solution.py:646
  35.7 1.0 %collective-permute-start.4 = (f32[8,128]{1,0:T(8,128)S(1)}, f32[8,128]{1,0:T(8,128)S(1)}, u32[]{:S(2)}, u32[]{:S(2)}) collective-permute-start(f32[8,128]{1,0:T(8,128)S(1)} %get-tuple-element.73.refs_0_), channel_id=1, source_target_pairs={{0,8},{8,0},{16,24},{24,16},{1,9},{9,1},{17,25},{25,17},{2,10},{10... | collective-permute-start | bytes 12296 | tf_op jit(solution)/shard_map/ppermute | solution.py:646
  36.7 1.2 %collective-permute-done.6.refs_3_ = f32[8,128]{1,0:T(8,128)S(1)} collective-permute-done((f32[8,128]{1,0:T(8,128)S(1)}, f32[8,128]{1,0:T(8,128)S(1)}, u32[]{:S(2)}, u32[]{:S(2)}) %collective-permute-start.6) | collective-permute-done | bytes 4128 | tf_op jit(solution)/shard_map/ppermute | solution.py:646
  37.9 0.7 collective-permute-done.5.refs_2_
  38.5 2.3 %shard_map.198 = (f32[144,128]{1,0:T(8,128)S(1)}, bf16[8,144,128]{2,1,0:T(8,128)(2,1)S(1)}, f32[8,128]{1,0:T(8,128)S(1)}, f32[8,128]{1,0:T(8,128)S(1)}, f32[8,128]{1,0:T(8,128)S(1)}) custom-call(s32[2]{0:T(128)S(1)} %get-tuple-element.66.sc, f32[8,128]{1,0:T(8,128)S(1)} %get-tuple-element.73.refs_0_, f32[8,128]{1,0:T(8,128)S(1)} %collective-permute-done.4.refs_1_, ...), custom_call_target="tpu_custom_call" | custom-call | flops 1000000000 | bytes 8388608 | tf_op jit(solution)/shard_map/pallas_call | solution.py:633
  40.9 0.6 collective-permute-start.9
  41.4 0.8 collective-permute-start.8
  42.2 0.5 collective-permute-start.7
  42.8 1.2 %collective-permute-done.9.refs_3_.refs_11_ = f32[8,128]{1,0:T(8,128)S(1)} collective-permute-done((f32[8,128]{1,0:T(8,128)S(1)}, f32[8,128]{1,0:T(8,128)S(1)}, u32[]{:S(2)}, u32[]{:S(2)}) %collective-permute-start.9) | collective-permute-done | bytes 4128 | tf_op jit(solution)/shard_map/ppermute | solution.py:646
  44.0 1.1 %collective-permute-done.8.refs_2_.refs_10_ = f32[8,128]{1,0:T(8,128)S(1)} collective-permute-done((f32[8,128]{1,0:T(8,128)S(1)}, f32[8,128]{1,0:T(8,128)S(1)}, u32[]{:S(2)}, u32[]{:S(2)}) %collective-permute-start.8) | collective-permute-done | bytes 4128 | tf_op jit(solution)/shard_map/ppermute | solution.py:646
  45.1 4.6 %shard_map.199 = (f32[8,144,512]{2,1,0:T(8,128)S(1)}, f32[8,144,512]{2,1,0:T(8,128)S(1)}, f32[8,128]{1,0:T(8,128)S(1)}, bf16[10,144,512]{2,1,0:T(8,128)(2,1)S(1)...) custom-call(s32[2]{0:T(128)S(1)} %get-tuple-element.66.sc, ...), custom_call_target="tpu_custom_call" | custom-call | flops 6000000000 | bytes 8388608 | tf_op jit(solution)/shard_map/pallas_call | solution.py:633
  49.7 0.1 collective-permute-start.12
  49.8 0.8 collective-permute-start.11
  50.6 1.0 %collective-permute-start.10 = (f32[8,128]{1,0:T(8,128)S(1)}, f32[8,128]{1,0:T(8,128)S(1)}, u32[]{:S(2)}, u32[]{:S(2)}) collective-permute-start(f32[8,128]{1,0:T(8,128)S(1)} %get-tuple-element.84.refs_0_.refs_4_), channel_id=1, source_target_pairs={{0,8},{8,0},{16,24},{24,16},{1,9},{9,1},{17,25},{25,17},{2,10},{10... | collective-permute-start | bytes 12296 | tf_op jit(solution)/shard_map/ppermute | solution.py:646
  51.6 2.8 %shard_map.201 = (f32[6,16,128]{2,1,0:T(8,128)S(1)}, f32[6,16,128]{2,1,0:T(8,128)S(1)}) custom-call(s32[2]{0:T(128)S(1)} %get-tuple-element.66.sc, bf16[10,144,512]{2,1,0:T(8,128)(2,1)S(1)} %get-tuple-element.100.padded, bf16[2,8,144,512]{3,2,1,0:T(8,128)(2,1)S(1)} %get-tuple-element.101.shifted, bf16[8,144,512]{2,1,0:T(8,128)(2,1)S(1)} %get-tuple-element.102.scot, ...), custom_call_target="tpu_custom_call" | custom-call | flops 2000000000 | bytes 8388608 | tf_op jit(solution)/shard_map/pallas_call | solution.py:633
  54.4 0.1 collective-permute-start.14
  54.5 4.0 %shard_map.200 = (f32[8,144,512]{2,1,0:T(8,128)S(1)}, f32[8,128]{1,0:T(8,128)S(1)}, f32[6,16,128]{2,1,0:T(8,128)S(1)}, f32[6,16,128]{2,1,0:T(8,128)S(1)}, bf16[1...) custom-call(s32[2]{0:T(128)S(1)} %get-tuple-element.66.sc, ...), custom_call_target="tpu_custom_call" | custom-call | flops 4000000000 | bytes 8388608 | tf_op jit(solution)/shard_map/pallas_call | solution.py:633
  58.6 0.5 collective-permute-start.13
  59.1 0.8 collective-permute-start.19
  60.0 1.3 %collective-permute-start.18 = (f32[6,16,128]{2,1,0:T(8,128)S(1)}, f32[6,16,128]{2,1,0:T(8,128)S(1)}, u32[]{:S(2)}, u32[]{:S(2)}) collective-permute-start(f32[6,16,128]{2,1,0:T(8,128)S(1)} %add.25.ready0.first), channel_id=1, source_target_pairs={{0,16},{8,24},{16,0},{24,8},{1,17},{9,25},{17,1},{25,9},{2,18},{10... | collective-permute-start | bytes 147464 | tf_op jit(solution)/shard_map/ppermute | solution.py:646
  61.3 4.0 %shard_map.202 = (f32[64,128]{1,0:T(8,128)S(1)}, f32[64,128]{1,0:T(8,128)S(1)}, f32[64,128]{1,0:T(8,128)S(1)}, f32[64,128]{1,0:T(8,128)S(1)}) custom-call(s32[2]{0:T(128)S(1)} %get-tuple-element.66.sc, bf16[10,144,512]{2,1,0:T(8,128)(2,1)S(1)} %get-tuple-element.91.padded, bf16[2,8,144,512]{3,2,1,0:T(8,128)(2,1)S(1)} %get-tuple-element.92.shifted, ...), custom_call_target="tpu_custom_call" | custom-call | flops 4000000000 | bytes 8388608 | tf_op jit(solution)/shard_map/pallas_call | solution.py:633
  65.3 0.8 shard_map.204
  66.1 3.5 %all-to-all-start.1 = ((bf16[8,192,128]{2,1,0:T(8,128)(2,1)}), bf16[8,192,128]{2,1,0:T(8,128)(2,1)S(1)}, u32[]{:S(2)}, u32[]{:S(2)}) async-start(bf16[8,192,128]{2,1,0:T(8,128)(2,1)} %shard_map.204), calls=%async_computation.1 | async-start | bytes 786432 | tf_op jit(solution)/shard_map/all_to_all | solution.py:824
  69.7 0.9 %collective-permute-start.16 = (f32[64,128]{1,0:T(8,128)S(1)}, f32[64,128]{1,0:T(8,128)S(1)}, u32[]{:S(2)}, u32[]{:S(2)}) collective-permute-start(f32[64,128]{1,0:T(8,128)S(1)} %get-tuple-element.108), channel_id=1, source_target_pairs={{0,16},{8,24},{16,0},{24,8},{1,17},{9,25},{17,1},{25,9},{2,18},{10... | collective-permute-start | bytes 98312 | tf_op jit(solution)/shard_map/ppermute | solution.py:646
  70.5 1.0 %collective-permute-start.17 = (f32[64,128]{1,0:T(8,128)S(1)}, f32[64,128]{1,0:T(8,128)S(1)}, u32[]{:S(2)}, u32[]{:S(2)}) collective-permute-start(f32[64,128]{1,0:T(8,128)S(1)} %get-tuple-element.109), channel_id=1, source_target_pairs={{0,24},{8,16},{16,8},{24,0},{1,25},{9,17},{17,9},{25,1},{2,26},{10... | collective-permute-start | bytes 98312 | tf_op jit(solution)/shard_map/ppermute | solution.py:646
  71.5 0.1 fusion.6.refs_15_
  71.6 2.2 %collective-permute-done.16.refs_2_ = f32[64,128]{1,0:T(8,128)S(1)} collective-permute-done((f32[64,128]{1,0:T(8,128)S(1)}, f32[64,128]{1,0:T(8,128)S(1)}, u32[]{:S(2)}, u32[]{:S(2)}) %collective-permute-start.16) | collective-permute-done | bytes 32800 | tf_op jit(solution)/shard_map/ppermute | solution.py:646
  73.8 0.4 collective-permute-done.17.refs_3_
  74.1 0.8 shard_map.203
  74.9 6.3 %all-to-all-done.1.near = bf16[8,192,128]{2,1,0:T(8,128)(2,1)S(1)} async-done(((bf16[8,192,128]{2,1,0:T(8,128)(2,1)}), bf16[8,192,128]{2,1,0:T(8,128)(2,1)S(1)}, u32[]{:S(2)}, u32[]{:S(2)}) %all-to-all-start.1) | async-done | bytes 393248 | tf_op jit(solution)/shard_map/all_to_all | solution.py:824
  81.2 1.7 %collective-permute-done.20.far = bf16[8,192,128]{2,1,0:T(8,128)(2,1)S(1)} collective-permute-done((bf16[8,192,128]{2,1,0:T(8,128)(2,1)S(1)}, bf16[8,192,128]{2,1,0:T(8,128)(2,1)S(1)}, u32[]{:S(2)}, u32[]{:S(2)}) %collective-permute-start.20) | collective-permute-done | bytes 393248 | tf_op jit(solution)/shard_map/ppermute | solution.py:646
  82.9 1.3 %shard_map.205 = (f32[2,3,128,128]{3,2,1,0:T(8,128)}, f32[2,8,128,128]{3,2,1,0:T(8,128)}, f32[2,128,128]{2,1,0:T(8,128)}) custom-call(bf16[8,192,128]{2,1,0:T(8,128)(2,1)S(1)} %all-to-all-done.1.near, bf16[8,192,128]{2,1,0:T(8,128)(2,1)S(1)} %collective-permute-done.20.far), custom_call_target="tpu_custom_call" | custom-call | flops 1000000 | bytes 8388608 | tf_op jit(solution)/shard_map/pallas_call | solution.py:633
  (23 shorter events, 0.3 us)
Async XLA Ops:
  0.6 12.7 %copy-start = (f32[128,128]{1,0:T(8,128)S(1)}, f32[128,128]{1,0:T(8,128)}, u32[]{:S(2)}) copy-start(f32[128,128]{1,0:T(8,128)} %param.17) | copy-start | bytes 196612
  0.7 18.2 %copy-start.1 = (f32[2,128]{1,0:T(2,128)S(1)}, f32[2,128]{1,0:T(2,128)}, u32[]{:S(2)}) copy-start(f32[2,128]{1,0:T(2,128)} %param.21) | copy-start | bytes 3076
  2.1 16.7 %all-to-all-start = ((f32[16,24,128]{2,1,0:T(8,128)}), f32[16,24,128]{2,1,0:T(8,128)S(1)}, u32[]{:S(2)}, u32[]{:S(2)}) async-start(f32[16,24,128]{2,1,0:T(8,128)} %broadcast_in_dim.21), calls=%async_computation | async-start | bytes 393216 | tf_op jit(solution)/shard_map/all_to_all | solution.py:741
  18.8 1.4 %collective-permute-start = (f32[16,24,128]{2,1,0:T(8,128)S(1)}, f32[16,24,128]{2,1,0:T(8,128)S(1)}, u32[]{:S(2)}, u32[]{:S(2)}) collective-permute-start(f32[16,24,128]{2,1,0:T(8,128)S(1)} %all-to-all-done.near), channel_id=1, source_target_pairs={{0,8},{8,0},{16,24},{24,16},{1,9},{9,1},{17,25},{25,17},{2,10},{10... | collective-permute-start | bytes 589832 | tf_op jit(solution)/shard_map/ppermute | solution.py:646
  25.7 3.1 %collective-permute-start.3 = (f32[8,128]{1,0:T(8,128)S(1)}, f32[8,128]{1,0:T(8,128)S(1)}, u32[]{:S(2)}, u32[]{:S(2)}) collective-permute-start(f32[8,128]{1,0:T(8,128)S(1)} %get-tuple-element.71.refs_0_), channel_id=1, source_target_pairs={{0,24},{8,16},{16,8},{24,0},{1,25},{9,17},{17,9},{25,1},{2,26},{10... | collective-permute-start | bytes 12296 | tf_op jit(solution)/shard_map/ppermute | solution.py:646
  26.7 3.6 %collective-permute-start.2 = (f32[8,128]{1,0:T(8,128)S(1)}, f32[8,128]{1,0:T(8,128)S(1)}, u32[]{:S(2)}, u32[]{:S(2)}) collective-permute-start(f32[8,128]{1,0:T(8,128)S(1)} %get-tuple-element.71.refs_0_), channel_id=1, source_target_pairs={{0,16},{8,24},{16,0},{24,8},{1,17},{9,25},{17,1},{25,9},{2,18},{10... | collective-permute-start | bytes 12296 | tf_op jit(solution)/shard_map/ppermute | solution.py:646
  27.5 2.8 %collective-permute-start.1 = (f32[8,128]{1,0:T(8,128)S(1)}, f32[8,128]{1,0:T(8,128)S(1)}, u32[]{:S(2)}, u32[]{:S(2)}) collective-permute-start(f32[8,128]{1,0:T(8,128)S(1)} %get-tuple-element.71.refs_0_), channel_id=1, source_target_pairs={{0,8},{8,0},{16,24},{24,16},{1,9},{9,1},{17,25},{25,17},{2,10},{10... | collective-permute-start | bytes 12296 | tf_op jit(solution)/shard_map/ppermute | solution.py:646
  34.8 3.1 %collective-permute-start.6 = (f32[8,128]{1,0:T(8,128)S(1)}, f32[8,128]{1,0:T(8,128)S(1)}, u32[]{:S(2)}, u32[]{:S(2)}) collective-permute-start(f32[8,128]{1,0:T(8,128)S(1)} %get-tuple-element.73.refs_0_), channel_id=1, source_target_pairs={{0,24},{8,16},{16,8},{24,0},{1,25},{9,17},{17,9},{25,1},{2,26},{10... | collective-permute-start | bytes 12296 | tf_op jit(solution)/shard_map/ppermute | solution.py:646
  34.9 3.7 %collective-permute-start.5 = (f32[8,128]{1,0:T(8,128)S(1)}, f32[8,128]{1,0:T(8,128)S(1)}, u32[]{:S(2)}, u32[]{:S(2)}) collective-permute-start(f32[8,128]{1,0:T(8,128)S(1)} %get-tuple-element.73.refs_0_), channel_id=1, source_target_pairs={{0,16},{8,24},{16,0},{24,8},{1,17},{9,25},{17,1},{25,9},{2,18},{10... | collective-permute-start | bytes 12296 | tf_op jit(solution)/shard_map/ppermute | solution.py:646
  35.7 2.8 %collective-permute-start.4 = (f32[8,128]{1,0:T(8,128)S(1)}, f32[8,128]{1,0:T(8,128)S(1)}, u32[]{:S(2)}, u32[]{:S(2)}) collective-permute-start(f32[8,128]{1,0:T(8,128)S(1)} %get-tuple-element.73.refs_0_), channel_id=1, source_target_pairs={{0,8},{8,0},{16,24},{24,16},{1,9},{9,1},{17,25},{25,17},{2,10},{10... | collective-permute-start | bytes 12296 | tf_op jit(solution)/shard_map/ppermute | solution.py:646
  40.9 3.1 %collective-permute-start.9 = (f32[8,128]{1,0:T(8,128)S(1)}, f32[8,128]{1,0:T(8,128)S(1)}, u32[]{:S(2)}, u32[]{:S(2)}) collective-permute-start(f32[8,128]{1,0:T(8,128)S(1)} %get-tuple-element.77.refs_0_.refs_8_), channel_id=1, source_target_pairs={{0,24},{8,16},{16,8},{24,0},{1,25},{9,17},{17,9},{25,1},{2,26},{10... | collective-permute-start | bytes 12296 | tf_op jit(solution)/shard_map/ppermute | solution.py:646
  41.4 3.6 %collective-permute-start.8 = (f32[8,128]{1,0:T(8,128)S(1)}, f32[8,128]{1,0:T(8,128)S(1)}, u32[]{:S(2)}, u32[]{:S(2)}) collective-permute-start(f32[8,128]{1,0:T(8,128)S(1)} %get-tuple-element.77.refs_0_.refs_8_), channel_id=1, source_target_pairs={{0,16},{8,24},{16,0},{24,8},{1,17},{9,25},{17,1},{25,9},{2,18},{10... | collective-permute-start | bytes 12296 | tf_op jit(solution)/shard_map/ppermute | solution.py:646
  42.2 2.8 %collective-permute-start.7 = (f32[8,128]{1,0:T(8,128)S(1)}, f32[8,128]{1,0:T(8,128)S(1)}, u32[]{:S(2)}, u32[]{:S(2)}) collective-permute-start(f32[8,128]{1,0:T(8,128)S(1)} %get-tuple-element.77.refs_0_.refs_8_), channel_id=1, source_target_pairs={{0,8},{8,0},{16,24},{24,16},{1,9},{9,1},{17,25},{25,17},{2,10},{10... | collective-permute-start | bytes 12296 | tf_op jit(solution)/shard_map/ppermute | solution.py:646
  49.7 4.8 %collective-permute-start.12 = (f32[8,128]{1,0:T(8,128)S(1)}, f32[8,128]{1,0:T(8,128)S(1)}, u32[]{:S(2)}, u32[]{:S(2)}) collective-permute-start(f32[8,128]{1,0:T(8,128)S(1)} %get-tuple-element.84.refs_0_.refs_4_), channel_id=1, source_target_pairs={{0,24},{8,16},{16,8},{24,0},{1,25},{9,17},{17,9},{25,1},{2,26},{10... | collective-permute-start | bytes 12296 | tf_op jit(solution)/shard_map/ppermute | solution.py:646
  49.8 4.7 %collective-permute-start.11 = (f32[8,128]{1,0:T(8,128)S(1)}, f32[8,128]{1,0:T(8,128)S(1)}, u32[]{:S(2)}, u32[]{:S(2)}) collective-permute-start(f32[8,128]{1,0:T(8,128)S(1)} %get-tuple-element.84.refs_0_.refs_4_), channel_id=1, source_target_pairs={{0,16},{8,24},{16,0},{24,8},{1,17},{9,25},{17,1},{25,9},{2,18},{10... | collective-permute-start | bytes 12296 | tf_op jit(solution)/shard_map/ppermute | solution.py:646
  50.6 3.9 %collective-permute-start.10 = (f32[8,128]{1,0:T(8,128)S(1)}, f32[8,128]{1,0:T(8,128)S(1)}, u32[]{:S(2)}, u32[]{:S(2)}) collective-permute-start(f32[8,128]{1,0:T(8,128)S(1)} %get-tuple-element.84.refs_0_.refs_4_), channel_id=1, source_target_pairs={{0,8},{8,0},{16,24},{24,16},{1,9},{9,1},{17,25},{25,17},{2,10},{10... | collective-permute-start | bytes 12296 | tf_op jit(solution)/shard_map/ppermute | solution.py:646
  54.4 4.7 %collective-permute-start.14 = (f32[6,16,128]{2,1,0:T(8,128)S(1)}, f32[6,16,128]{2,1,0:T(8,128)S(1)}, u32[]{:S(2)}, u32[]{:S(2)}) collective-permute-start(f32[6,16,128]{2,1,0:T(8,128)S(1)} %get-tuple-element.105), channel_id=1, source_target_pairs={{0,8},{8,0},{16,24},{24,16},{1,9},{9,1},{17,25},{25,17},{2,10},{10... | collective-permute-start | bytes 147464 | tf_op jit(solution)/shard_map/ppermute | solution.py:646
  58.6 1.4 %collective-permute-start.13 = (f32[6,16,128]{2,1,0:T(8,128)S(1)}, f32[6,16,128]{2,1,0:T(8,128)S(1)}, u32[]{:S(2)}, u32[]{:S(2)}) collective-permute-start(f32[6,16,128]{2,1,0:T(8,128)S(1)} %get-tuple-element.99), channel_id=1, source_target_pairs={{0,8},{8,0},{16,24},{24,16},{1,9},{9,1},{17,25},{25,17},{2,10},{10... | collective-permute-start | bytes 147464 | tf_op jit(solution)/shard_map/ppermute | solution.py:646
  59.1 6.2 %collective-permute-start.19 = (f32[6,16,128]{2,1,0:T(8,128)S(1)}, f32[6,16,128]{2,1,0:T(8,128)S(1)}, u32[]{:S(2)}, u32[]{:S(2)}) collective-permute-start(f32[6,16,128]{2,1,0:T(8,128)S(1)} %add.26.ready1.second), channel_id=1, source_target_pairs={{0,16},{8,24},{16,0},{24,8},{1,17},{9,25},{17,1},{25,9},{2,18},{10... | collective-permute-start | bytes 147464 | tf_op jit(solution)/shard_map/ppermute | solution.py:646
  60.0 5.3 %collective-permute-start.18 = (f32[6,16,128]{2,1,0:T(8,128)S(1)}, f32[6,16,128]{2,1,0:T(8,128)S(1)}, u32[]{:S(2)}, u32[]{:S(2)}) collective-permute-start(f32[6,16,128]{2,1,0:T(8,128)S(1)} %add.25.ready0.first), channel_id=1, source_target_pairs={{0,16},{8,24},{16,0},{24,8},{1,17},{9,25},{17,1},{25,9},{2,18},{10... | collective-permute-start | bytes 147464 | tf_op jit(solution)/shard_map/ppermute | solution.py:646
  66.1 15.1 %all-to-all-start.1 = ((bf16[8,192,128]{2,1,0:T(8,128)(2,1)}), bf16[8,192,128]{2,1,0:T(8,128)(2,1)S(1)}, u32[]{:S(2)}, u32[]{:S(2)}) async-start(bf16[8,192,128]{2,1,0:T(8,128)(2,1)} %shard_map.204), calls=%async_computation.1 | async-start | bytes 786432 | tf_op jit(solution)/shard_map/all_to_all | solution.py:824
  69.6 2.0 %collective-permute-start.15 = (f32[64,128]{1,0:T(8,128)S(1)}, f32[64,128]{1,0:T(8,128)S(1)}, u32[]{:S(2)}, u32[]{:S(2)}) collective-permute-start(f32[64,128]{1,0:T(8,128)S(1)} %get-tuple-element.107), channel_id=1, source_target_pairs={{0,8},{8,0},{16,24},{24,16},{1,9},{9,1},{17,25},{25,17},{2,10},{10... | collective-permute-start | bytes 98312 | tf_op jit(solution)/shard_map/ppermute | solution.py:646
  69.7 4.1 %collective-permute-start.16 = (f32[64,128]{1,0:T(8,128)S(1)}, f32[64,128]{1,0:T(8,128)S(1)}, u32[]{:S(2)}, u32[]{:S(2)}) collective-permute-start(f32[64,128]{1,0:T(8,128)S(1)} %get-tuple-element.108), channel_id=1, source_target_pairs={{0,16},{8,24},{16,0},{24,8},{1,17},{9,25},{17,1},{25,9},{2,18},{10... | collective-permute-start | bytes 98312 | tf_op jit(solution)/shard_map/ppermute | solution.py:646
  70.5 3.6 %collective-permute-start.17 = (f32[64,128]{1,0:T(8,128)S(1)}, f32[64,128]{1,0:T(8,128)S(1)}, u32[]{:S(2)}, u32[]{:S(2)}) collective-permute-start(f32[64,128]{1,0:T(8,128)S(1)} %get-tuple-element.109), channel_id=1, source_target_pairs={{0,24},{8,16},{16,8},{24,0},{1,25},{9,17},{17,9},{25,1},{2,26},{10... | collective-permute-start | bytes 98312 | tf_op jit(solution)/shard_map/ppermute | solution.py:646
  81.2 1.7 %collective-permute-start.20 = (bf16[8,192,128]{2,1,0:T(8,128)(2,1)S(1)}, bf16[8,192,128]{2,1,0:T(8,128)(2,1)S(1)}, u32[]{:S(2)}, u32[]{:S(2)}) collective-permute-start(bf16[8,192,128]{2,1,0:T(8,128)(2,1)S(1)} %all-to-all-done.1.near), channel_id=1, source_target_pairs={{0,8},{8,0},{16,24},{24,16},{1,9},{9,1},{17,25},{25,17},{2,10},{10... | collective-permute-start | bytes 1179656 | tf_op jit(solution)/shard_map/ppermute | solution.py:646

commit v9 on v8

--- a/solution.py
+++ b/solution.py
@@ -147,7 +147,7 @@
         for m, at in ((1, 4), (0, 9), (2, 10)):
             pairs.append((w_z.at[layer, m], w_front.at[layer, at]))
     fetch(pairs, sems)
-    small[...] = jnp.concatenate([w_in[...], gains[...], w_out[...].astype(f32)], axis=0)
+    small[...] = jnp.concatenate([w_in[...], gains[...], w_out[...]], axis=0)
     for layer in range(2):
         for at in range(9):
             w_back[layer, at] = w_front[layer, 8 - at].T
@@ -759,8 +759,9 @@
     w_front, point, w_back, point_back, lift_in, lift_out, small, steps_on = call(
         kernel_prepare,
         [taps_out, point_out, taps_out, point_out, lift, lift, ((9, channels), f32), ((2,), jnp.int32)],
-        [((3, channels), f32), ((3, channels), f32), ((3, channels), bf16), pltpu.SemaphoreType.DMA((15,))],
-        10**8, LIMITS[0], dilations, w_z, w_xy, w_point, w_in, norm_gains, w_out, scalar_out=1,
+        [((3, channels), f32), ((3, channels), f32), ((3, channels), f32), pltpu.SemaphoreType.DMA((15,))],
+        10**8, LIMITS[0], dilations, w_z, w_xy, w_point, w_in, norm_gains, w_out.astype(f32),
+        scalar_out=1,
         far=tuple(range(7)),
     )
     stream1, normed0, act0, slope0, gathered, stats1, consts0, mixed_own = call(

time: 84.6 us -> 84.6 us (level)
  other arithmetic: 0.97 us -> 2.22 us
  waiting for transfers between devices: 24.1 us -> 22.9 us
    convert_element_type x0 -> x1, other arithmetic: none -> 1.26 us  [per_device_grouped(): w_out.astype(f32)]
    all_to_all x1, waiting for transfers between devices: 5.24 us -> 3.98 us  [per_device_grouped(): lax.all_to_all(block, ('gz', 'gx'), 0, 0, axis_index_groups=same_core)]
  transfers between devices with their start and end apart: 23 -> 23, of which waited for: 12 -> 12; matrix products, arithmetic and copies ran while one was open for 1% -> 2% of each run, Pallas kernels for 16% -> 16%
where the time goes in v9:
time: 84.6 us; the launch traced here: 84.2 us
  Pallas kernels  32.4 us (38%)
  starting transfers between devices  24.2 us (29%)
  waiting for transfers between devices  22.9 us (27%)
  other arithmetic  2.22 us (3%)
  between operations  1.63 us (2%)
    pallas_call x11, Pallas kernels, call(): pl.pallas_call(kernel, out_shape=[jax.ShapeDtypeStruct(shape, dtype) for...  32.4 us
    ppermute x21, waiting for transfers between devices, swapped(): return lax.ppermute(value, axis, [(i, i ^ bit) for i in range(count)])  12.6 us
    ppermute x21, starting transfers between devices, swapped(): return lax.ppermute(value, axis, [(i, i ^ bit) for i in range(count)])  12.4 us
    all_to_all x1, starting transfers between devices, per_device_grouped(): lax.all_to_all(block, ('gz', 'gx'), 0, 0, axis_index_groups=same_core)  8.31 us
    all_to_all x1, waiting for transfers between devices, per_device_grouped(): near_grads = lax.all_to_all(spread, 'gx', 0, 0)  6.31 us
    all_to_all x1, waiting for transfers between devices, per_device_grouped(): lax.all_to_all(block, ('gz', 'gx'), 0, 0, axis_index_groups=same_core)  3.98 us
    all_to_all x1, starting transfers between devices, per_device_grouped(): near_grads = lax.all_to_all(spread, 'gx', 0, 0)  3.45 us
  transfers between devices with their start and end apart: 23, of which 12 were waited for; matrix products, arithmetic and copies ran while one was open for 2% of the time, Pallas kernels for 16%

profile of v9, /device:TPU:0, one launch (start us, length us, event | category | flops | bytes accessed | tf_op | source)
XLA Modules:
  0.0 84.2 jit_solution(12971371503494798344)
XLA Ops:
  0.7 0.7 pad_maximum_fusion
  1.4 0.7 broadcast_in_dim.21
  2.1 8.3 %all-to-all-start = ((f32[16,24,128]{2,1,0:T(8,128)}), f32[16,24,128]{2,1,0:T(8,128)S(1)}, u32[]{:S(2)}, u32[]{:S(2)}) async-start(f32[16,24,128]{2,1,0:T(8,128)} %broadcast_in_dim.21), calls=%async_computation | async-start | bytes 393216 | tf_op jit(solution)/shard_map/all_to_all | solution.py:741
  11.2 0.1 pad_maximum_fusion.1
  11.3 1.3 %convert_element_type.9.w_out_far = f32[3,128]{1,0:T(4,128)} convert(bf16[3,128]{1,0:T(4,128)(2,1)} %param.23) | non-fusion elementwise | flops 384 | bytes 2304 | tf_op jit(solution)/shard_map/convert_element_type | solution.py:763
  12.6 2.0 %shard_map.195 = (bf16[2,11,128,128]{3,2,1,0:T(8,128)(2,1)S(1)}, bf16[2,128,128]{2,1,0:T(8,128)(2,1)S(1)}, bf16[2,11,128,128]{3,2,1,0:T(8,128)(2,1)S(1)}, bf16[2...) custom-call(s32[2]{0:T(128)} %steps.1, ...), custom_call_target="tpu_custom_call" | custom-call | flops 100000000 | bytes 8388608 | tf_op jit(solution)/shard_map/pallas_call | solution.py:633
  14.6 0.2 divide_multiply_fusion
  14.8 4.0 %all-to-all-done.near = f32[16,24,128]{2,1,0:T(8,128)S(1)} async-done(((f32[16,24,128]{2,1,0:T(8,128)}), f32[16,24,128]{2,1,0:T(8,128)S(1)}, u32[]{:S(2)}, u32[]{:S(2)}) %all-to-all-start) | async-done | bytes 196640 | tf_op jit(solution)/shard_map/all_to_all | solution.py:741
  18.8 1.4 %collective-permute-done.far = f32[16,24,128]{2,1,0:T(8,128)S(1)} collective-permute-done((f32[16,24,128]{2,1,0:T(8,128)S(1)}, f32[16,24,128]{2,1,0:T(8,128)S(1)}, u32[]{:S(2)}, u32[]{:S(2)}) %collective-permute-start) | collective-permute-done | bytes 196640 | tf_op jit(solution)/shard_map/ppermute | solution.py:646
  20.3 5.3 %shard_map.196 = (f32[8,144,512]{2,1,0:T(8,128)S(1)}, bf16[10,144,512]{2,1,0:T(8,128)(2,1)S(1)}, bf16[8,144,512]{2,1,0:T(8,128)(2,1)S(1)}, bf16[8,144,512]{2,1,0...) custom-call(s32[2]{0:T(128)S(1)} %get-tuple-element.66.sc, ...), custom_call_target="tpu_custom_call" | custom-call | flops 4000000000 | bytes 8388608 | tf_op jit(solution)/shard_map/pallas_call | solution.py:633
  25.7 1.0 %collective-permute-start.3 = (f32[8,128]{1,0:T(8,128)S(1)}, f32[8,128]{1,0:T(8,128)S(1)}, u32[]{:S(2)}, u32[]{:S(2)}) collective-permute-start(f32[8,128]{1,0:T(8,128)S(1)} %get-tuple-element.71.refs_0_), channel_id=1, source_target_pairs={{0,24},{8,16},{16,8},{24,0},{1,25},{9,17},{17,9},{25,1},{2,26},{10... | collective-permute-start | bytes 12296 | tf_op jit(solution)/shard_map/ppermute | solution.py:646
  26.7 0.8 collective-permute-start.2
  27.5 0.1 collective-permute-start.1
  27.6 1.2 %collective-permute-done.3.refs_3_ = f32[8,128]{1,0:T(8,128)S(1)} collective-permute-done((f32[8,128]{1,0:T(8,128)S(1)}, f32[8,128]{1,0:T(8,128)S(1)}, u32[]{:S(2)}, u32[]{:S(2)}) %collective-permute-start.3) | collective-permute-done | bytes 4128 | tf_op jit(solution)/shard_map/ppermute | solution.py:646
  28.8 1.5 %collective-permute-done.2.refs_2_ = f32[8,128]{1,0:T(8,128)S(1)} collective-permute-done((f32[8,128]{1,0:T(8,128)S(1)}, f32[8,128]{1,0:T(8,128)S(1)}, u32[]{:S(2)}, u32[]{:S(2)}) %collective-permute-start.2) | collective-permute-done | bytes 4128 | tf_op jit(solution)/shard_map/ppermute | solution.py:646
  30.3 4.5 %shard_map.197 = (f32[8,144,512]{2,1,0:T(8,128)S(1)}, bf16[10,144,512]{2,1,0:T(8,128)(2,1)S(1)}, bf16[8,144,512]{2,1,0:T(8,128)(2,1)S(1)}, bf16[8,144,512]{2,1,0...) custom-call(s32[2]{0:T(128)S(1)} %get-tuple-element.66.sc, f32[8,128]{1,0:T(8,128)S(1)} %get-tuple-element.71.refs_0_, ...), custom_call_target="tpu_custom_call" | custom-call | flops 4000000000 | bytes 8388608 | tf_op jit(solution)/shard_map/pallas_call | solution.py:633
  34.9 0.9 %collective-permute-start.5 = (f32[8,128]{1,0:T(8,128)S(1)}, f32[8,128]{1,0:T(8,128)S(1)}, u32[]{:S(2)}, u32[]{:S(2)}) collective-permute-start(f32[8,128]{1,0:T(8,128)S(1)} %get-tuple-element.73.refs_0_), channel_id=1, source_target_pairs={{0,16},{8,24},{16,0},{24,8},{1,17},{9,25},{17,1},{25,9},{2,18},{10... | collective-permute-start | bytes 12296 | tf_op jit(solution)/shard_map/ppermute | solution.py:646
  35.7 1.0 %collective-permute-start.4 = (f32[8,128]{1,0:T(8,128)S(1)}, f32[8,128]{1,0:T(8,128)S(1)}, u32[]{:S(2)}, u32[]{:S(2)}) collective-permute-start(f32[8,128]{1,0:T(8,128)S(1)} %get-tuple-element.73.refs_0_), channel_id=1, source_target_pairs={{0,8},{8,0},{16,24},{24,16},{1,9},{9,1},{17,25},{25,17},{2,10},{10... | collective-permute-start | bytes 12296 | tf_op jit(solution)/shard_map/ppermute | solution.py:646
  36.7 1.2 %collective-permute-done.6.refs_3_ = f32[8,128]{1,0:T(8,128)S(1)} collective-permute-done((f32[8,128]{1,0:T(8,128)S(1)}, f32[8,128]{1,0:T(8,128)S(1)}, u32[]{:S(2)}, u32[]{:S(2)}) %collective-permute-start.6) | collective-permute-done | bytes 4128 | tf_op jit(solution)/shard_map/ppermute | solution.py:646
  37.9 0.7 collective-permute-done.5.refs_2_
  38.5 2.3 %shard_map.198 = (f32[144,128]{1,0:T(8,128)S(1)}, bf16[8,144,128]{2,1,0:T(8,128)(2,1)S(1)}, f32[8,128]{1,0:T(8,128)S(1)}, f32[8,128]{1,0:T(8,128)S(1)}, f32[8,128]{1,0:T(8,128)S(1)}) custom-call(s32[2]{0:T(128)S(1)} %get-tuple-element.66.sc, f32[8,128]{1,0:T(8,128)S(1)} %get-tuple-element.73.refs_0_, f32[8,128]{1,0:T(8,128)S(1)} %collective-permute-done.4.refs_1_, ...), custom_call_target="tpu_custom_call" | custom-call | flops 1000000000 | bytes 8388608 | tf_op jit(solution)/shard_map/pallas_call | solution.py:633
  40.9 0.6 collective-permute-start.9
  41.4 0.8 collective-permute-start.8
  42.2 0.5 collective-permute-start.7
  42.8 1.2 %collective-permute-done.9.refs_3_.refs_11_ = f32[8,128]{1,0:T(8,128)S(1)} collective-permute-done((f32[8,128]{1,0:T(8,128)S(1)}, f32[8,128]{1,0:T(8,128)S(1)}, u32[]{:S(2)}, u32[]{:S(2)}) %collective-permute-start.9) | collective-permute-done | bytes 4128 | tf_op jit(solution)/shard_map/ppermute | solution.py:646
  44.0 1.1 %collective-permute-done.8.refs_2_.refs_10_ = f32[8,128]{1,0:T(8,128)S(1)} collective-permute-done((f32[8,128]{1,0:T(8,128)S(1)}, f32[8,128]{1,0:T(8,128)S(1)}, u32[]{:S(2)}, u32[]{:S(2)}) %collective-permute-start.8) | collective-permute-done | bytes 4128 | tf_op jit(solution)/shard_map/ppermute | solution.py:646
  45.1 4.6 %shard_map.199 = (f32[8,144,512]{2,1,0:T(8,128)S(1)}, f32[8,144,512]{2,1,0:T(8,128)S(1)}, f32[8,128]{1,0:T(8,128)S(1)}, bf16[10,144,512]{2,1,0:T(8,128)(2,1)S(1)...) custom-call(s32[2]{0:T(128)S(1)} %get-tuple-element.66.sc, ...), custom_call_target="tpu_custom_call" | custom-call | flops 6000000000 | bytes 8388608 | tf_op jit(solution)/shard_map/pallas_call | solution.py:633
  49.7 0.1 collective-permute-start.12
  49.8 0.8 collective-permute-start.11
  50.6 1.0 %collective-permute-start.10 = (f32[8,128]{1,0:T(8,128)S(1)}, f32[8,128]{1,0:T(8,128)S(1)}, u32[]{:S(2)}, u32[]{:S(2)}) collective-permute-start(f32[8,128]{1,0:T(8,128)S(1)} %get-tuple-element.84.refs_0_.refs_4_), channel_id=1, source_target_pairs={{0,8},{8,0},{16,24},{24,16},{1,9},{9,1},{17,25},{25,17},{2,10},{10... | collective-permute-start | bytes 12296 | tf_op jit(solution)/shard_map/ppermute | solution.py:646
  51.6 2.8 %shard_map.201 = (f32[6,16,128]{2,1,0:T(8,128)S(1)}, f32[6,16,128]{2,1,0:T(8,128)S(1)}) custom-call(s32[2]{0:T(128)S(1)} %get-tuple-element.66.sc, bf16[10,144,512]{2,1,0:T(8,128)(2,1)S(1)} %get-tuple-element.100.padded, bf16[2,8,144,512]{3,2,1,0:T(8,128)(2,1)S(1)} %get-tuple-element.101.shifted, bf16[8,144,512]{2,1,0:T(8,128)(2,1)S(1)} %get-tuple-element.102.scot, ...), custom_call_target="tpu_custom_call" | custom-call | flops 2000000000 | bytes 8388608 | tf_op jit(solution)/shard_map/pallas_call | solution.py:633
  54.4 0.1 collective-permute-start.14
  54.5 4.0 %shard_map.200 = (f32[8,144,512]{2,1,0:T(8,128)S(1)}, f32[8,128]{1,0:T(8,128)S(1)}, f32[6,16,128]{2,1,0:T(8,128)S(1)}, f32[6,16,128]{2,1,0:T(8,128)S(1)}, bf16[1...) custom-call(s32[2]{0:T(128)S(1)} %get-tuple-element.66.sc, ...), custom_call_target="tpu_custom_call" | custom-call | flops 4000000000 | bytes 8388608 | tf_op jit(solution)/shard_map/pallas_call | solution.py:633
  58.6 0.5 collective-permute-start.13
  59.1 0.8 collective-permute-start.19
  60.0 1.3 %collective-permute-start.18 = (f32[6,16,128]{2,1,0:T(8,128)S(1)}, f32[6,16,128]{2,1,0:T(8,128)S(1)}, u32[]{:S(2)}, u32[]{:S(2)}) collective-permute-start(f32[6,16,128]{2,1,0:T(8,128)S(1)} %add.25.ready0.first), channel_id=1, source_target_pairs={{0,16},{8,24},{16,0},{24,8},{1,17},{9,25},{17,1},{25,9},{2,18},{10... | collective-permute-start | bytes 147464 | tf_op jit(solution)/shard_map/ppermute | solution.py:646
  61.3 4.0 %shard_map.202 = (f32[64,128]{1,0:T(8,128)S(1)}, f32[64,128]{1,0:T(8,128)S(1)}, f32[64,128]{1,0:T(8,128)S(1)}, f32[64,128]{1,0:T(8,128)S(1)}) custom-call(s32[2]{0:T(128)S(1)} %get-tuple-element.66.sc, bf16[10,144,512]{2,1,0:T(8,128)(2,1)S(1)} %get-tuple-element.91.padded, bf16[2,8,144,512]{3,2,1,0:T(8,128)(2,1)S(1)} %get-tuple-element.92.shifted, ...), custom_call_target="tpu_custom_call" | custom-call | flops 4000000000 | bytes 8388608 | tf_op jit(solution)/shard_map/pallas_call | solution.py:633
  65.3 0.8 shard_map.204
  66.1 3.5 %all-to-all-start.1 = ((bf16[8,192,128]{2,1,0:T(8,128)(2,1)}), bf16[8,192,128]{2,1,0:T(8,128)(2,1)S(1)}, u32[]{:S(2)}, u32[]{:S(2)}) async-start(bf16[8,192,128]{2,1,0:T(8,128)(2,1)} %shard_map.204), calls=%async_computation.1 | async-start | bytes 786432 | tf_op jit(solution)/shard_map/all_to_all | solution.py:825
  69.7 0.9 %collective-permute-start.16 = (f32[64,128]{1,0:T(8,128)S(1)}, f32[64,128]{1,0:T(8,128)S(1)}, u32[]{:S(2)}, u32[]{:S(2)}) collective-permute-start(f32[64,128]{1,0:T(8,128)S(1)} %get-tuple-element.108), channel_id=1, source_target_pairs={{0,16},{8,24},{16,0},{24,8},{1,17},{9,25},{17,1},{25,9},{2,18},{10... | collective-permute-start | bytes 98312 | tf_op jit(solution)/shard_map/ppermute | solution.py:646
  70.5 1.0 %collective-permute-start.17 = (f32[64,128]{1,0:T(8,128)S(1)}, f32[64,128]{1,0:T(8,128)S(1)}, u32[]{:S(2)}, u32[]{:S(2)}) collective-permute-start(f32[64,128]{1,0:T(8,128)S(1)} %get-tuple-element.109), channel_id=1, source_target_pairs={{0,24},{8,16},{16,8},{24,0},{1,25},{9,17},{17,9},{25,1},{2,26},{10... | collective-permute-start | bytes 98312 | tf_op jit(solution)/shard_map/ppermute | solution.py:646
  71.5 0.1 fusion.6.refs_15_
  71.6 2.2 %collective-permute-done.16.refs_2_ = f32[64,128]{1,0:T(8,128)S(1)} collective-permute-done((f32[64,128]{1,0:T(8,128)S(1)}, f32[64,128]{1,0:T(8,128)S(1)}, u32[]{:S(2)}, u32[]{:S(2)}) %collective-permute-start.16) | collective-permute-done | bytes 32800 | tf_op jit(solution)/shard_map/ppermute | solution.py:646
  73.8 0.4 collective-permute-done.17.refs_3_
  74.1 0.8 shard_map.203
  74.9 6.3 %all-to-all-done.1.near = bf16[8,192,128]{2,1,0:T(8,128)(2,1)S(1)} async-done(((bf16[8,192,128]{2,1,0:T(8,128)(2,1)}), bf16[8,192,128]{2,1,0:T(8,128)(2,1)S(1)}, u32[]{:S(2)}, u32[]{:S(2)}) %all-to-all-start.1) | async-done | bytes 393248 | tf_op jit(solution)/shard_map/all_to_all | solution.py:825
  81.2 1.7 %collective-permute-done.20.far = bf16[8,192,128]{2,1,0:T(8,128)(2,1)S(1)} collective-permute-done((bf16[8,192,128]{2,1,0:T(8,128)(2,1)S(1)}, bf16[8,192,128]{2,1,0:T(8,128)(2,1)S(1)}, u32[]{:S(2)}, u32[]{:S(2)}) %collective-permute-start.20) | collective-permute-done | bytes 393248 | tf_op jit(solution)/shard_map/ppermute | solution.py:646
  82.9 1.3 %shard_map.205 = (f32[2,3,128,128]{3,2,1,0:T(8,128)}, f32[2,8,128,128]{3,2,1,0:T(8,128)}, f32[2,128,128]{2,1,0:T(8,128)}) custom-call(bf16[8,192,128]{2,1,0:T(8,128)(2,1)S(1)} %all-to-all-done.1.near, bf16[8,192,128]{2,1,0:T(8,128)(2,1)S(1)} %collective-permute-done.20.far), custom_call_target="tpu_custom_call" | custom-call | flops 1000000 | bytes 8388608 | tf_op jit(solution)/shard_map/pallas_call | solution.py:633
  (24 shorter events, 0.4 us)
Async XLA Ops:
  0.6 14.0 %copy-start = (f32[128,128]{1,0:T(8,128)S(1)}, f32[128,128]{1,0:T(8,128)}, u32[]{:S(2)}) copy-start(f32[128,128]{1,0:T(8,128)} %param.17) | copy-start | bytes 196612
  0.7 18.2 %copy-start.1 = (f32[2,128]{1,0:T(2,128)S(1)}, f32[2,128]{1,0:T(2,128)}, u32[]{:S(2)}) copy-start(f32[2,128]{1,0:T(2,128)} %param.21) | copy-start | bytes 3076
  2.1 16.7 %all-to-all-start = ((f32[16,24,128]{2,1,0:T(8,128)}), f32[16,24,128]{2,1,0:T(8,128)S(1)}, u32[]{:S(2)}, u32[]{:S(2)}) async-start(f32[16,24,128]{2,1,0:T(8,128)} %broadcast_in_dim.21), calls=%async_computation | async-start | bytes 393216 | tf_op jit(solution)/shard_map/all_to_all | solution.py:741
  18.8 1.4 %collective-permute-start = (f32[16,24,128]{2,1,0:T(8,128)S(1)}, f32[16,24,128]{2,1,0:T(8,128)S(1)}, u32[]{:S(2)}, u32[]{:S(2)}) collective-permute-start(f32[16,24,128]{2,1,0:T(8,128)S(1)} %all-to-all-done.near), channel_id=1, source_target_pairs={{0,8},{8,0},{16,24},{24,16},{1,9},{9,1},{17,25},{25,17},{2,10},{10... | collective-permute-start | bytes 589832 | tf_op jit(solution)/shard_map/ppermute | solution.py:646
  25.7 3.1 %collective-permute-start.3 = (f32[8,128]{1,0:T(8,128)S(1)}, f32[8,128]{1,0:T(8,128)S(1)}, u32[]{:S(2)}, u32[]{:S(2)}) collective-permute-start(f32[8,128]{1,0:T(8,128)S(1)} %get-tuple-element.71.refs_0_), channel_id=1, source_target_pairs={{0,24},{8,16},{16,8},{24,0},{1,25},{9,17},{17,9},{25,1},{2,26},{10... | collective-permute-start | bytes 12296 | tf_op jit(solution)/shard_map/ppermute | solution.py:646
  26.7 3.6 %collective-permute-start.2 = (f32[8,128]{1,0:T(8,128)S(1)}, f32[8,128]{1,0:T(8,128)S(1)}, u32[]{:S(2)}, u32[]{:S(2)}) collective-permute-start(f32[8,128]{1,0:T(8,128)S(1)} %get-tuple-element.71.refs_0_), channel_id=1, source_target_pairs={{0,16},{8,24},{16,0},{24,8},{1,17},{9,25},{17,1},{25,9},{2,18},{10... | collective-permute-start | bytes 12296 | tf_op jit(solution)/shard_map/ppermute | solution.py:646
  27.5 2.8 %collective-permute-start.1 = (f32[8,128]{1,0:T(8,128)S(1)}, f32[8,128]{1,0:T(8,128)S(1)}, u32[]{:S(2)}, u32[]{:S(2)}) collective-permute-start(f32[8,128]{1,0:T(8,128)S(1)} %get-tuple-element.71.refs_0_), channel_id=1, source_target_pairs={{0,8},{8,0},{16,24},{24,16},{1,9},{9,1},{17,25},{25,17},{2,10},{10... | collective-permute-start | bytes 12296 | tf_op jit(solution)/shard_map/ppermute | solution.py:646
  34.8 3.1 %collective-permute-start.6 = (f32[8,128]{1,0:T(8,128)S(1)}, f32[8,128]{1,0:T(8,128)S(1)}, u32[]{:S(2)}, u32[]{:S(2)}) collective-permute-start(f32[8,128]{1,0:T(8,128)S(1)} %get-tuple-element.73.refs_0_), channel_id=1, source_target_pairs={{0,24},{8,16},{16,8},{24,0},{1,25},{9,17},{17,9},{25,1},{2,26},{10... | collective-permute-start | bytes 12296 | tf_op jit(solution)/shard_map/ppermute | solution.py:646
  34.9 3.7 %collective-permute-start.5 = (f32[8,128]{1,0:T(8,128)S(1)}, f32[8,128]{1,0:T(8,128)S(1)}, u32[]{:S(2)}, u32[]{:S(2)}) collective-permute-start(f32[8,128]{1,0:T(8,128)S(1)} %get-tuple-element.73.refs_0_), channel_id=1, source_target_pairs={{0,16},{8,24},{16,0},{24,8},{1,17},{9,25},{17,1},{25,9},{2,18},{10... | collective-permute-start | bytes 12296 | tf_op jit(solution)/shard_map/ppermute | solution.py:646
  35.7 2.8 %collective-permute-start.4 = (f32[8,128]{1,0:T(8,128)S(1)}, f32[8,128]{1,0:T(8,128)S(1)}, u32[]{:S(2)}, u32[]{:S(2)}) collective-permute-start(f32[8,128]{1,0:T(8,128)S(1)} %get-tuple-element.73.refs_0_), channel_id=1, source_target_pairs={{0,8},{8,0},{16,24},{24,16},{1,9},{9,1},{17,25},{25,17},{2,10},{10... | collective-permute-start | bytes 12296 | tf_op jit(solution)/shard_map/ppermute | solution.py:646
  40.9 3.1 %collective-permute-start.9 = (f32[8,128]{1,0:T(8,128)S(1)}, f32[8,128]{1,0:T(8,128)S(1)}, u32[]{:S(2)}, u32[]{:S(2)}) collective-permute-start(f32[8,128]{1,0:T(8,128)S(1)} %get-tuple-element.77.refs_0_.refs_8_), channel_id=1, source_target_pairs={{0,24},{8,16},{16,8},{24,0},{1,25},{9,17},{17,9},{25,1},{2,26},{10... | collective-permute-start | bytes 12296 | tf_op jit(solution)/shard_map/ppermute | solution.py:646
  41.4 3.6 %collective-permute-start.8 = (f32[8,128]{1,0:T(8,128)S(1)}, f32[8,128]{1,0:T(8,128)S(1)}, u32[]{:S(2)}, u32[]{:S(2)}) collective-permute-start(f32[8,128]{1,0:T(8,128)S(1)} %get-tuple-element.77.refs_0_.refs_8_), channel_id=1, source_target_pairs={{0,16},{8,24},{16,0},{24,8},{1,17},{9,25},{17,1},{25,9},{2,18},{10... | collective-permute-start | bytes 12296 | tf_op jit(solution)/shard_map/ppermute | solution.py:646
  42.2 2.8 %collective-permute-start.7 = (f32[8,128]{1,0:T(8,128)S(1)}, f32[8,128]{1,0:T(8,128)S(1)}, u32[]{:S(2)}, u32[]{:S(2)}) collective-permute-start(f32[8,128]{1,0:T(8,128)S(1)} %get-tuple-element.77.refs_0_.refs_8_), channel_id=1, source_target_pairs={{0,8},{8,0},{16,24},{24,16},{1,9},{9,1},{17,25},{25,17},{2,10},{10... | collective-permute-start | bytes 12296 | tf_op jit(solution)/shard_map/ppermute | solution.py:646
  49.7 4.8 %collective-permute-start.12 = (f32[8,128]{1,0:T(8,128)S(1)}, f32[8,128]{1,0:T(8,128)S(1)}, u32[]{:S(2)}, u32[]{:S(2)}) collective-permute-start(f32[8,128]{1,0:T(8,128)S(1)} %get-tuple-element.84.refs_0_.refs_4_), channel_id=1, source_target_pairs={{0,24},{8,16},{16,8},{24,0},{1,25},{9,17},{17,9},{25,1},{2,26},{10... | collective-permute-start | bytes 12296 | tf_op jit(solution)/shard_map/ppermute | solution.py:646
  49.8 4.7 %collective-permute-start.11 = (f32[8,128]{1,0:T(8,128)S(1)}, f32[8,128]{1,0:T(8,128)S(1)}, u32[]{:S(2)}, u32[]{:S(2)}) collective-permute-start(f32[8,128]{1,0:T(8,128)S(1)} %get-tuple-element.84.refs_0_.refs_4_), channel_id=1, source_target_pairs={{0,16},{8,24},{16,0},{24,8},{1,17},{9,25},{17,1},{25,9},{2,18},{10... | collective-permute-start | bytes 12296 | tf_op jit(solution)/shard_map/ppermute | solution.py:646
  50.6 3.9 %collective-permute-start.10 = (f32[8,128]{1,0:T(8,128)S(1)}, f32[8,128]{1,0:T(8,128)S(1)}, u32[]{:S(2)}, u32[]{:S(2)}) collective-permute-start(f32[8,128]{1,0:T(8,128)S(1)} %get-tuple-element.84.refs_0_.refs_4_), channel_id=1, source_target_pairs={{0,8},{8,0},{16,24},{24,16},{1,9},{9,1},{17,25},{25,17},{2,10},{10... | collective-permute-start | bytes 12296 | tf_op jit(solution)/shard_map/ppermute | solution.py:646
  54.4 4.7 %collective-permute-start.14 = (f32[6,16,128]{2,1,0:T(8,128)S(1)}, f32[6,16,128]{2,1,0:T(8,128)S(1)}, u32[]{:S(2)}, u32[]{:S(2)}) collective-permute-start(f32[6,16,128]{2,1,0:T(8,128)S(1)} %get-tuple-element.105), channel_id=1, source_target_pairs={{0,8},{8,0},{16,24},{24,16},{1,9},{9,1},{17,25},{25,17},{2,10},{10... | collective-permute-start | bytes 147464 | tf_op jit(solution)/shard_map/ppermute | solution.py:646
  58.6 1.4 %collective-permute-start.13 = (f32[6,16,128]{2,1,0:T(8,128)S(1)}, f32[6,16,128]{2,1,0:T(8,128)S(1)}, u32[]{:S(2)}, u32[]{:S(2)}) collective-permute-start(f32[6,16,128]{2,1,0:T(8,128)S(1)} %get-tuple-element.99), channel_id=1, source_target_pairs={{0,8},{8,0},{16,24},{24,16},{1,9},{9,1},{17,25},{25,17},{2,10},{10... | collective-permute-start | bytes 147464 | tf_op jit(solution)/shard_map/ppermute | solution.py:646
  59.1 6.2 %collective-permute-start.19 = (f32[6,16,128]{2,1,0:T(8,128)S(1)}, f32[6,16,128]{2,1,0:T(8,128)S(1)}, u32[]{:S(2)}, u32[]{:S(2)}) collective-permute-start(f32[6,16,128]{2,1,0:T(8,128)S(1)} %add.26.ready1.second), channel_id=1, source_target_pairs={{0,16},{8,24},{16,0},{24,8},{1,17},{9,25},{17,1},{25,9},{2,18},{10... | collective-permute-start | bytes 147464 | tf_op jit(solution)/shard_map/ppermute | solution.py:646
  60.0 5.3 %collective-permute-start.18 = (f32[6,16,128]{2,1,0:T(8,128)S(1)}, f32[6,16,128]{2,1,0:T(8,128)S(1)}, u32[]{:S(2)}, u32[]{:S(2)}) collective-permute-start(f32[6,16,128]{2,1,0:T(8,128)S(1)} %add.25.ready0.first), channel_id=1, source_target_pairs={{0,16},{8,24},{16,0},{24,8},{1,17},{9,25},{17,1},{25,9},{2,18},{10... | collective-permute-start | bytes 147464 | tf_op jit(solution)/shard_map/ppermute | solution.py:646
  66.1 15.1 %all-to-all-start.1 = ((bf16[8,192,128]{2,1,0:T(8,128)(2,1)}), bf16[8,192,128]{2,1,0:T(8,128)(2,1)S(1)}, u32[]{:S(2)}, u32[]{:S(2)}) async-start(bf16[8,192,128]{2,1,0:T(8,128)(2,1)} %shard_map.204), calls=%async_computation.1 | async-start | bytes 786432 | tf_op jit(solution)/shard_map/all_to_all | solution.py:825
  69.6 2.0 %collective-permute-start.15 = (f32[64,128]{1,0:T(8,128)S(1)}, f32[64,128]{1,0:T(8,128)S(1)}, u32[]{:S(2)}, u32[]{:S(2)}) collective-permute-start(f32[64,128]{1,0:T(8,128)S(1)} %get-tuple-element.107), channel_id=1, source_target_pairs={{0,8},{8,0},{16,24},{24,16},{1,9},{9,1},{17,25},{25,17},{2,10},{10... | collective-permute-start | bytes 98312 | tf_op jit(solution)/shard_map/ppermute | solution.py:646
  69.7 4.1 %collective-permute-start.16 = (f32[64,128]{1,0:T(8,128)S(1)}, f32[64,128]{1,0:T(8,128)S(1)}, u32[]{:S(2)}, u32[]{:S(2)}) collective-permute-start(f32[64,128]{1,0:T(8,128)S(1)} %get-tuple-element.108), channel_id=1, source_target_pairs={{0,16},{8,24},{16,0},{24,8},{1,17},{9,25},{17,1},{25,9},{2,18},{10... | collective-permute-start | bytes 98312 | tf_op jit(solution)/shard_map/ppermute | solution.py:646
  70.5 3.6 %collective-permute-start.17 = (f32[64,128]{1,0:T(8,128)S(1)}, f32[64,128]{1,0:T(8,128)S(1)}, u32[]{:S(2)}, u32[]{:S(2)}) collective-permute-start(f32[64,128]{1,0:T(8,128)S(1)} %get-tuple-element.109), channel_id=1, source_target_pairs={{0,24},{8,16},{16,8},{24,0},{1,25},{9,17},{17,9},{25,1},{2,26},{10... | collective-permute-start | bytes 98312 | tf_op jit(solution)/shard_map/ppermute | solution.py:646
  81.2 1.7 %collective-permute-start.20 = (bf16[8,192,128]{2,1,0:T(8,128)(2,1)S(1)}, bf16[8,192,128]{2,1,0:T(8,128)(2,1)S(1)}, u32[]{:S(2)}, u32[]{:S(2)}) collective-permute-start(bf16[8,192,128]{2,1,0:T(8,128)(2,1)S(1)} %all-to-all-done.1.near), channel_id=1, source_target_pairs={{0,8},{8,0},{16,24},{24,16},{1,9},{9,1},{17,25},{25,17},{2,10},{10... | collective-permute-start | bytes 1179656 | tf_op jit(solution)/shard_map/ppermute | solution.py:646

commit v10 on v9

--- a/solution.py
+++ b/solution.py
@@ -261,7 +261,7 @@
                   stream, act, slope, stats, acc, per_member):
     planes, rows, lanes = stream.shape
     half = lanes // 2
-    count = planes // 4
+    count = planes // 2
     build_taps(taken(w_front, layer), taps)
     build_pair(wp[layer], pair, 0)
     fill_rims(padded, planes)
@@ -482,7 +482,7 @@
 
 
 def conv_backward(planes, padded, shifted, taps, emit):
-    count = planes // 4
+    count = planes // 2
 
     for x0 in range(0, planes, count):
         for q, total in enumerate(conv_pair(padded, shifted, taps, x0, count)):

time: 84.6 us -> 84.6 us (level)
  no operation moved by 1% of the time
where the time goes in v10:
time: 84.6 us; the launch traced here: 84.2 us
  Pallas kernels  32.3 us (38%)
  starting transfers between devices  24.2 us (29%)
  waiting for transfers between devices  22.9 us (27%)
  other arithmetic  2.22 us (3%)
  between operations  1.64 us (2%)
    pallas_call x11, Pallas kernels, call(): pl.pallas_call(kernel, out_shape=[jax.ShapeDtypeStruct(shape, dtype) for...  32.3 us
    ppermute x21, waiting for transfers between devices, swapped(): return lax.ppermute(value, axis, [(i, i ^ bit) for i in range(count)])  12.5 us
    ppermute x21, starting transfers between devices, swapped(): return lax.ppermute(value, axis, [(i, i ^ bit) for i in range(count)])  12.4 us
    all_to_all x1, starting transfers between devices, per_device_grouped(): lax.all_to_all(block, ('gz', 'gx'), 0, 0, axis_index_groups=same_core)  8.31 us
    all_to_all x1, waiting for transfers between devices, per_device_grouped(): near_grads = lax.all_to_all(spread, 'gx', 0, 0)  6.37 us
    all_to_all x1, waiting for transfers between devices, per_device_grouped(): lax.all_to_all(block, ('gz', 'gx'), 0, 0, axis_index_groups=same_core)  3.98 us
    all_to_all x1, starting transfers between devices, per_device_grouped(): near_grads = lax.all_to_all(spread, 'gx', 0, 0)  3.45 us
  transfers between devices with their start and end apart: 23, of which 12 were waited for; matrix products, arithmetic and copies ran while one was open for 2% of the time, Pallas kernels for 16%

profile of v10, /device:TPU:0, one launch (start us, length us, event | category | flops | bytes accessed | tf_op | source)
XLA Modules:
  0.0 84.2 jit_solution(16085005098666451944)
XLA Ops:
  0.7 0.7 pad_maximum_fusion
  1.4 0.7 broadcast_in_dim.21
  2.1 8.3 %all-to-all-start = ((f32[16,24,128]{2,1,0:T(8,128)}), f32[16,24,128]{2,1,0:T(8,128)S(1)}, u32[]{:S(2)}, u32[]{:S(2)}) async-start(f32[16,24,128]{2,1,0:T(8,128)} %broadcast_in_dim.21), calls=%async_computation | async-start | bytes 393216 | tf_op jit(solution)/shard_map/all_to_all | solution.py:741
  11.2 0.1 pad_maximum_fusion.1
  11.3 1.3 %convert_element_type.9.w_out_far = f32[3,128]{1,0:T(4,128)} convert(bf16[3,128]{1,0:T(4,128)(2,1)} %param.23) | non-fusion elementwise | flops 384 | bytes 2304 | tf_op jit(solution)/shard_map/convert_element_type | solution.py:763
  12.6 2.0 %shard_map.195 = (bf16[2,11,128,128]{3,2,1,0:T(8,128)(2,1)S(1)}, bf16[2,128,128]{2,1,0:T(8,128)(2,1)S(1)}, bf16[2,11,128,128]{3,2,1,0:T(8,128)(2,1)S(1)}, bf16[2...) custom-call(s32[2]{0:T(128)} %steps.1, ...), custom_call_target="tpu_custom_call" | custom-call | flops 100000000 | bytes 8388608 | tf_op jit(solution)/shard_map/pallas_call | solution.py:633
  14.6 0.2 divide_multiply_fusion
  14.8 4.0 %all-to-all-done.near = f32[16,24,128]{2,1,0:T(8,128)S(1)} async-done(((f32[16,24,128]{2,1,0:T(8,128)}), f32[16,24,128]{2,1,0:T(8,128)S(1)}, u32[]{:S(2)}, u32[]{:S(2)}) %all-to-all-start) | async-done | bytes 196640 | tf_op jit(solution)/shard_map/all_to_all | solution.py:741
  18.8 1.4 %collective-permute-done.far = f32[16,24,128]{2,1,0:T(8,128)S(1)} collective-permute-done((f32[16,24,128]{2,1,0:T(8,128)S(1)}, f32[16,24,128]{2,1,0:T(8,128)S(1)}, u32[]{:S(2)}, u32[]{:S(2)}) %collective-permute-start) | collective-permute-done | bytes 196640 | tf_op jit(solution)/shard_map/ppermute | solution.py:646
  20.3 5.4 %shard_map.196 = (f32[8,144,512]{2,1,0:T(8,128)S(1)}, bf16[10,144,512]{2,1,0:T(8,128)(2,1)S(1)}, bf16[8,144,512]{2,1,0:T(8,128)(2,1)S(1)}, bf16[8,144,512]{2,1,0...) custom-call(s32[2]{0:T(128)S(1)} %get-tuple-element.66.sc, ...), custom_call_target="tpu_custom_call" | custom-call | flops 4000000000 | bytes 8388608 | tf_op jit(solution)/shard_map/pallas_call | solution.py:633
  25.8 1.0 %collective-permute-start.3 = (f32[8,128]{1,0:T(8,128)S(1)}, f32[8,128]{1,0:T(8,128)S(1)}, u32[]{:S(2)}, u32[]{:S(2)}) collective-permute-start(f32[8,128]{1,0:T(8,128)S(1)} %get-tuple-element.71.refs_0_), channel_id=1, source_target_pairs={{0,24},{8,16},{16,8},{24,0},{1,25},{9,17},{17,9},{25,1},{2,26},{10... | collective-permute-start | bytes 12296 | tf_op jit(solution)/shard_map/ppermute | solution.py:646
  26.8 0.8 collective-permute-start.2
  27.6 0.1 collective-permute-start.1
  27.7 1.2 %collective-permute-done.3.refs_3_ = f32[8,128]{1,0:T(8,128)S(1)} collective-permute-done((f32[8,128]{1,0:T(8,128)S(1)}, f32[8,128]{1,0:T(8,128)S(1)}, u32[]{:S(2)}, u32[]{:S(2)}) %collective-permute-start.3) | collective-permute-done | bytes 4128 | tf_op jit(solution)/shard_map/ppermute | solution.py:646
  28.9 1.5 %collective-permute-done.2.refs_2_ = f32[8,128]{1,0:T(8,128)S(1)} collective-permute-done((f32[8,128]{1,0:T(8,128)S(1)}, f32[8,128]{1,0:T(8,128)S(1)}, u32[]{:S(2)}, u32[]{:S(2)}) %collective-permute-start.2) | collective-permute-done | bytes 4128 | tf_op jit(solution)/shard_map/ppermute | solution.py:646
  30.4 4.4 %shard_map.197 = (f32[8,144,512]{2,1,0:T(8,128)S(1)}, bf16[10,144,512]{2,1,0:T(8,128)(2,1)S(1)}, bf16[8,144,512]{2,1,0:T(8,128)(2,1)S(1)}, bf16[8,144,512]{2,1,0...) custom-call(s32[2]{0:T(128)S(1)} %get-tuple-element.66.sc, f32[8,128]{1,0:T(8,128)S(1)} %get-tuple-element.71.refs_0_, ...), custom_call_target="tpu_custom_call" | custom-call | flops 4000000000 | bytes 8388608 | tf_op jit(solution)/shard_map/pallas_call | solution.py:633
  34.9 0.1 collective-permute-start.6
  34.9 0.9 %collective-permute-start.5 = (f32[8,128]{1,0:T(8,128)S(1)}, f32[8,128]{1,0:T(8,128)S(1)}, u32[]{:S(2)}, u32[]{:S(2)}) collective-permute-start(f32[8,128]{1,0:T(8,128)S(1)} %get-tuple-element.73.refs_0_), channel_id=1, source_target_pairs={{0,16},{8,24},{16,0},{24,8},{1,17},{9,25},{17,1},{25,9},{2,18},{10... | collective-permute-start | bytes 12296 | tf_op jit(solution)/shard_map/ppermute | solution.py:646
  35.8 1.0 %collective-permute-start.4 = (f32[8,128]{1,0:T(8,128)S(1)}, f32[8,128]{1,0:T(8,128)S(1)}, u32[]{:S(2)}, u32[]{:S(2)}) collective-permute-start(f32[8,128]{1,0:T(8,128)S(1)} %get-tuple-element.73.refs_0_), channel_id=1, source_target_pairs={{0,8},{8,0},{16,24},{24,16},{1,9},{9,1},{17,25},{25,17},{2,10},{10... | collective-permute-start | bytes 12296 | tf_op jit(solution)/shard_map/ppermute | solution.py:646
  36.8 1.2 %collective-permute-done.6.refs_3_ = f32[8,128]{1,0:T(8,128)S(1)} collective-permute-done((f32[8,128]{1,0:T(8,128)S(1)}, f32[8,128]{1,0:T(8,128)S(1)}, u32[]{:S(2)}, u32[]{:S(2)}) %collective-permute-start.6) | collective-permute-done | bytes 4128 | tf_op jit(solution)/shard_map/ppermute | solution.py:646
  38.0 0.7 collective-permute-done.5.refs_2_
  38.6 2.3 %shard_map.198 = (f32[144,128]{1,0:T(8,128)S(1)}, bf16[8,144,128]{2,1,0:T(8,128)(2,1)S(1)}, f32[8,128]{1,0:T(8,128)S(1)}, f32[8,128]{1,0:T(8,128)S(1)}, f32[8,128]{1,0:T(8,128)S(1)}) custom-call(s32[2]{0:T(128)S(1)} %get-tuple-element.66.sc, f32[8,128]{1,0:T(8,128)S(1)} %get-tuple-element.73.refs_0_, f32[8,128]{1,0:T(8,128)S(1)} %collective-permute-done.4.refs_1_, ...), custom_call_target="tpu_custom_call" | custom-call | flops 1000000000 | bytes 8388608 | tf_op jit(solution)/shard_map/pallas_call | solution.py:633
  40.9 0.6 collective-permute-start.9
  41.5 0.8 collective-permute-start.8
  42.3 0.5 collective-permute-start.7
  42.9 1.2 %collective-permute-done.9.refs_3_.refs_11_ = f32[8,128]{1,0:T(8,128)S(1)} collective-permute-done((f32[8,128]{1,0:T(8,128)S(1)}, f32[8,128]{1,0:T(8,128)S(1)}, u32[]{:S(2)}, u32[]{:S(2)}) %collective-permute-start.9) | collective-permute-done | bytes 4128 | tf_op jit(solution)/shard_map/ppermute | solution.py:646
  44.0 1.1 %collective-permute-done.8.refs_2_.refs_10_ = f32[8,128]{1,0:T(8,128)S(1)} collective-permute-done((f32[8,128]{1,0:T(8,128)S(1)}, f32[8,128]{1,0:T(8,128)S(1)}, u32[]{:S(2)}, u32[]{:S(2)}) %collective-permute-start.8) | collective-permute-done | bytes 4128 | tf_op jit(solution)/shard_map/ppermute | solution.py:646
  45.1 4.4 %shard_map.199 = (f32[8,144,512]{2,1,0:T(8,128)S(1)}, f32[8,144,512]{2,1,0:T(8,128)S(1)}, f32[8,128]{1,0:T(8,128)S(1)}, bf16[10,144,512]{2,1,0:T(8,128)(2,1)S(1)...) custom-call(s32[2]{0:T(128)S(1)} %get-tuple-element.66.sc, ...), custom_call_target="tpu_custom_call" | custom-call | flops 6000000000 | bytes 8388608 | tf_op jit(solution)/shard_map/pallas_call | solution.py:633
  49.5 0.1 collective-permute-start.12
  49.7 0.8 %collective-permute-start.11 = (f32[8,128]{1,0:T(8,128)S(1)}, f32[8,128]{1,0:T(8,128)S(1)}, u32[]{:S(2)}, u32[]{:S(2)}) collective-permute-start(f32[8,128]{1,0:T(8,128)S(1)} %get-tuple-element.84.refs_0_.refs_4_), channel_id=1, source_target_pairs={{0,16},{8,24},{16,0},{24,8},{1,17},{9,25},{17,1},{25,9},{2,18},{10... | collective-permute-start | bytes 12296 | tf_op jit(solution)/shard_map/ppermute | solution.py:646
  50.5 0.9 %collective-permute-start.10 = (f32[8,128]{1,0:T(8,128)S(1)}, f32[8,128]{1,0:T(8,128)S(1)}, u32[]{:S(2)}, u32[]{:S(2)}) collective-permute-start(f32[8,128]{1,0:T(8,128)S(1)} %get-tuple-element.84.refs_0_.refs_4_), channel_id=1, source_target_pairs={{0,8},{8,0},{16,24},{24,16},{1,9},{9,1},{17,25},{25,17},{2,10},{10... | collective-permute-start | bytes 12296 | tf_op jit(solution)/shard_map/ppermute | solution.py:646
  51.5 2.8 %shard_map.201 = (f32[6,16,128]{2,1,0:T(8,128)S(1)}, f32[6,16,128]{2,1,0:T(8,128)S(1)}) custom-call(s32[2]{0:T(128)S(1)} %get-tuple-element.66.sc, bf16[10,144,512]{2,1,0:T(8,128)(2,1)S(1)} %get-tuple-element.100.padded, bf16[2,8,144,512]{3,2,1,0:T(8,128)(2,1)S(1)} %get-tuple-element.101.shifted, bf16[8,144,512]{2,1,0:T(8,128)(2,1)S(1)} %get-tuple-element.102.scot, ...), custom_call_target="tpu_custom_call" | custom-call | flops 2000000000 | bytes 8388608 | tf_op jit(solution)/shard_map/pallas_call | solution.py:633
  54.4 4.0 %shard_map.200 = (f32[8,144,512]{2,1,0:T(8,128)S(1)}, f32[8,128]{1,0:T(8,128)S(1)}, f32[6,16,128]{2,1,0:T(8,128)S(1)}, f32[6,16,128]{2,1,0:T(8,128)S(1)}, bf16[1...) custom-call(s32[2]{0:T(128)S(1)} %get-tuple-element.66.sc, ...), custom_call_target="tpu_custom_call" | custom-call | flops 4000000000 | bytes 8388608 | tf_op jit(solution)/shard_map/pallas_call | solution.py:633
  58.5 0.5 collective-permute-start.13
  59.0 0.8 %collective-permute-start.19 = (f32[6,16,128]{2,1,0:T(8,128)S(1)}, f32[6,16,128]{2,1,0:T(8,128)S(1)}, u32[]{:S(2)}, u32[]{:S(2)}) collective-permute-start(f32[6,16,128]{2,1,0:T(8,128)S(1)} %add.26.ready1.second), channel_id=1, source_target_pairs={{0,16},{8,24},{16,0},{24,8},{1,17},{9,25},{17,1},{25,9},{2,18},{10... | collective-permute-start | bytes 147464 | tf_op jit(solution)/shard_map/ppermute | solution.py:646
  59.9 1.3 %collective-permute-start.18 = (f32[6,16,128]{2,1,0:T(8,128)S(1)}, f32[6,16,128]{2,1,0:T(8,128)S(1)}, u32[]{:S(2)}, u32[]{:S(2)}) collective-permute-start(f32[6,16,128]{2,1,0:T(8,128)S(1)} %add.25.ready0.first), channel_id=1, source_target_pairs={{0,16},{8,24},{16,0},{24,8},{1,17},{9,25},{17,1},{25,9},{2,18},{10... | collective-permute-start | bytes 147464 | tf_op jit(solution)/shard_map/ppermute | solution.py:646
  61.2 4.0 %shard_map.202 = (f32[64,128]{1,0:T(8,128)S(1)}, f32[64,128]{1,0:T(8,128)S(1)}, f32[64,128]{1,0:T(8,128)S(1)}, f32[64,128]{1,0:T(8,128)S(1)}) custom-call(s32[2]{0:T(128)S(1)} %get-tuple-element.66.sc, bf16[10,144,512]{2,1,0:T(8,128)(2,1)S(1)} %get-tuple-element.91.padded, bf16[2,8,144,512]{3,2,1,0:T(8,128)(2,1)S(1)} %get-tuple-element.92.shifted, ...), custom_call_target="tpu_custom_call" | custom-call | flops 4000000000 | bytes 8388608 | tf_op jit(solution)/shard_map/pallas_call | solution.py:633
  65.3 0.8 shard_map.204
  66.1 3.5 %all-to-all-start.1 = ((bf16[8,192,128]{2,1,0:T(8,128)(2,1)}), bf16[8,192,128]{2,1,0:T(8,128)(2,1)S(1)}, u32[]{:S(2)}, u32[]{:S(2)}) async-start(bf16[8,192,128]{2,1,0:T(8,128)(2,1)} %shard_map.204), calls=%async_computation.1 | async-start | bytes 786432 | tf_op jit(solution)/shard_map/all_to_all | solution.py:825
  69.6 0.9 %collective-permute-start.16 = (f32[64,128]{1,0:T(8,128)S(1)}, f32[64,128]{1,0:T(8,128)S(1)}, u32[]{:S(2)}, u32[]{:S(2)}) collective-permute-start(f32[64,128]{1,0:T(8,128)S(1)} %get-tuple-element.108), channel_id=1, source_target_pairs={{0,16},{8,24},{16,0},{24,8},{1,17},{9,25},{17,1},{25,9},{2,18},{10... | collective-permute-start | bytes 98312 | tf_op jit(solution)/shard_map/ppermute | solution.py:646
  70.5 1.0 %collective-permute-start.17 = (f32[64,128]{1,0:T(8,128)S(1)}, f32[64,128]{1,0:T(8,128)S(1)}, u32[]{:S(2)}, u32[]{:S(2)}) collective-permute-start(f32[64,128]{1,0:T(8,128)S(1)} %get-tuple-element.109), channel_id=1, source_target_pairs={{0,24},{8,16},{16,8},{24,0},{1,25},{9,17},{17,9},{25,1},{2,26},{10... | collective-permute-start | bytes 98312 | tf_op jit(solution)/shard_map/ppermute | solution.py:646
  71.5 0.1 fusion.6.refs_15_
  71.5 2.1 %collective-permute-done.16.refs_2_ = f32[64,128]{1,0:T(8,128)S(1)} collective-permute-done((f32[64,128]{1,0:T(8,128)S(1)}, f32[64,128]{1,0:T(8,128)S(1)}, u32[]{:S(2)}, u32[]{:S(2)}) %collective-permute-start.16) | collective-permute-done | bytes 32800 | tf_op jit(solution)/shard_map/ppermute | solution.py:646
  73.7 0.4 collective-permute-done.17.refs_3_
  74.0 0.8 shard_map.203
  74.8 6.4 %all-to-all-done.1.near = bf16[8,192,128]{2,1,0:T(8,128)(2,1)S(1)} async-done(((bf16[8,192,128]{2,1,0:T(8,128)(2,1)}), bf16[8,192,128]{2,1,0:T(8,128)(2,1)S(1)}, u32[]{:S(2)}, u32[]{:S(2)}) %all-to-all-start.1) | async-done | bytes 393248 | tf_op jit(solution)/shard_map/all_to_all | solution.py:825
  81.2 1.7 %collective-permute-done.20.far = bf16[8,192,128]{2,1,0:T(8,128)(2,1)S(1)} collective-permute-done((bf16[8,192,128]{2,1,0:T(8,128)(2,1)S(1)}, bf16[8,192,128]{2,1,0:T(8,128)(2,1)S(1)}, u32[]{:S(2)}, u32[]{:S(2)}) %collective-permute-start.20) | collective-permute-done | bytes 393248 | tf_op jit(solution)/shard_map/ppermute | solution.py:646
  82.9 1.3 %shard_map.205 = (f32[2,3,128,128]{3,2,1,0:T(8,128)}, f32[2,8,128,128]{3,2,1,0:T(8,128)}, f32[2,128,128]{2,1,0:T(8,128)}) custom-call(bf16[8,192,128]{2,1,0:T(8,128)(2,1)S(1)} %all-to-all-done.1.near, bf16[8,192,128]{2,1,0:T(8,128)(2,1)S(1)} %collective-permute-done.20.far), custom_call_target="tpu_custom_call" | custom-call | flops 1000000 | bytes 8388608 | tf_op jit(solution)/shard_map/pallas_call | solution.py:633
  (24 shorter events, 0.3 us)
Async XLA Ops:
  0.6 14.0 %copy-start = (f32[128,128]{1,0:T(8,128)S(1)}, f32[128,128]{1,0:T(8,128)}, u32[]{:S(2)}) copy-start(f32[128,128]{1,0:T(8,128)} %param.17) | copy-start | bytes 196612
  0.7 18.2 %copy-start.1 = (f32[2,128]{1,0:T(2,128)S(1)}, f32[2,128]{1,0:T(2,128)}, u32[]{:S(2)}) copy-start(f32[2,128]{1,0:T(2,128)} %param.21) | copy-start | bytes 3076
  2.1 16.7 %all-to-all-start = ((f32[16,24,128]{2,1,0:T(8,128)}), f32[16,24,128]{2,1,0:T(8,128)S(1)}, u32[]{:S(2)}, u32[]{:S(2)}) async-start(f32[16,24,128]{2,1,0:T(8,128)} %broadcast_in_dim.21), calls=%async_computation | async-start | bytes 393216 | tf_op jit(solution)/shard_map/all_to_all | solution.py:741
  18.8 1.4 %collective-permute-start = (f32[16,24,128]{2,1,0:T(8,128)S(1)}, f32[16,24,128]{2,1,0:T(8,128)S(1)}, u32[]{:S(2)}, u32[]{:S(2)}) collective-permute-start(f32[16,24,128]{2,1,0:T(8,128)S(1)} %all-to-all-done.near), channel_id=1, source_target_pairs={{0,8},{8,0},{16,24},{24,16},{1,9},{9,1},{17,25},{25,17},{2,10},{10... | collective-permute-start | bytes 589832 | tf_op jit(solution)/shard_map/ppermute | solution.py:646
  25.8 3.1 %collective-permute-start.3 = (f32[8,128]{1,0:T(8,128)S(1)}, f32[8,128]{1,0:T(8,128)S(1)}, u32[]{:S(2)}, u32[]{:S(2)}) collective-permute-start(f32[8,128]{1,0:T(8,128)S(1)} %get-tuple-element.71.refs_0_), channel_id=1, source_target_pairs={{0,24},{8,16},{16,8},{24,0},{1,25},{9,17},{17,9},{25,1},{2,26},{10... | collective-permute-start | bytes 12296 | tf_op jit(solution)/shard_map/ppermute | solution.py:646
  26.8 3.6 %collective-permute-start.2 = (f32[8,128]{1,0:T(8,128)S(1)}, f32[8,128]{1,0:T(8,128)S(1)}, u32[]{:S(2)}, u32[]{:S(2)}) collective-permute-start(f32[8,128]{1,0:T(8,128)S(1)} %get-tuple-element.71.refs_0_), channel_id=1, source_target_pairs={{0,16},{8,24},{16,0},{24,8},{1,17},{9,25},{17,1},{25,9},{2,18},{10... | collective-permute-start | bytes 12296 | tf_op jit(solution)/shard_map/ppermute | solution.py:646
  27.6 2.8 %collective-permute-start.1 = (f32[8,128]{1,0:T(8,128)S(1)}, f32[8,128]{1,0:T(8,128)S(1)}, u32[]{:S(2)}, u32[]{:S(2)}) collective-permute-start(f32[8,128]{1,0:T(8,128)S(1)} %get-tuple-element.71.refs_0_), channel_id=1, source_target_pairs={{0,8},{8,0},{16,24},{24,16},{1,9},{9,1},{17,25},{25,17},{2,10},{10... | collective-permute-start | bytes 12296 | tf_op jit(solution)/shard_map/ppermute | solution.py:646
  34.9 3.1 %collective-permute-start.6 = (f32[8,128]{1,0:T(8,128)S(1)}, f32[8,128]{1,0:T(8,128)S(1)}, u32[]{:S(2)}, u32[]{:S(2)}) collective-permute-start(f32[8,128]{1,0:T(8,128)S(1)} %get-tuple-element.73.refs_0_), channel_id=1, source_target_pairs={{0,24},{8,16},{16,8},{24,0},{1,25},{9,17},{17,9},{25,1},{2,26},{10... | collective-permute-start | bytes 12296 | tf_op jit(solution)/shard_map/ppermute | solution.py:646
  34.9 3.7 %collective-permute-start.5 = (f32[8,128]{1,0:T(8,128)S(1)}, f32[8,128]{1,0:T(8,128)S(1)}, u32[]{:S(2)}, u32[]{:S(2)}) collective-permute-start(f32[8,128]{1,0:T(8,128)S(1)} %get-tuple-element.73.refs_0_), channel_id=1, source_target_pairs={{0,16},{8,24},{16,0},{24,8},{1,17},{9,25},{17,1},{25,9},{2,18},{10... | collective-permute-start | bytes 12296 | tf_op jit(solution)/shard_map/ppermute | solution.py:646
  35.8 2.8 %collective-permute-start.4 = (f32[8,128]{1,0:T(8,128)S(1)}, f32[8,128]{1,0:T(8,128)S(1)}, u32[]{:S(2)}, u32[]{:S(2)}) collective-permute-start(f32[8,128]{1,0:T(8,128)S(1)} %get-tuple-element.73.refs_0_), channel_id=1, source_target_pairs={{0,8},{8,0},{16,24},{24,16},{1,9},{9,1},{17,25},{25,17},{2,10},{10... | collective-permute-start | bytes 12296 | tf_op jit(solution)/shard_map/ppermute | solution.py:646
  40.9 3.1 %collective-permute-start.9 = (f32[8,128]{1,0:T(8,128)S(1)}, f32[8,128]{1,0:T(8,128)S(1)}, u32[]{:S(2)}, u32[]{:S(2)}) collective-permute-start(f32[8,128]{1,0:T(8,128)S(1)} %get-tuple-element.77.refs_0_.refs_8_), channel_id=1, source_target_pairs={{0,24},{8,16},{16,8},{24,0},{1,25},{9,17},{17,9},{25,1},{2,26},{10... | collective-permute-start | bytes 12296 | tf_op jit(solution)/shard_map/ppermute | solution.py:646
  41.5 3.6 %collective-permute-start.8 = (f32[8,128]{1,0:T(8,128)S(1)}, f32[8,128]{1,0:T(8,128)S(1)}, u32[]{:S(2)}, u32[]{:S(2)}) collective-permute-start(f32[8,128]{1,0:T(8,128)S(1)} %get-tuple-element.77.refs_0_.refs_8_), channel_id=1, source_target_pairs={{0,16},{8,24},{16,0},{24,8},{1,17},{9,25},{17,1},{25,9},{2,18},{10... | collective-permute-start | bytes 12296 | tf_op jit(solution)/shard_map/ppermute | solution.py:646
  42.3 2.8 %collective-permute-start.7 = (f32[8,128]{1,0:T(8,128)S(1)}, f32[8,128]{1,0:T(8,128)S(1)}, u32[]{:S(2)}, u32[]{:S(2)}) collective-permute-start(f32[8,128]{1,0:T(8,128)S(1)} %get-tuple-element.77.refs_0_.refs_8_), channel_id=1, source_target_pairs={{0,8},{8,0},{16,24},{24,16},{1,9},{9,1},{17,25},{25,17},{2,10},{10... | collective-permute-start | bytes 12296 | tf_op jit(solution)/shard_map/ppermute | solution.py:646
  49.5 4.8 %collective-permute-start.12 = (f32[8,128]{1,0:T(8,128)S(1)}, f32[8,128]{1,0:T(8,128)S(1)}, u32[]{:S(2)}, u32[]{:S(2)}) collective-permute-start(f32[8,128]{1,0:T(8,128)S(1)} %get-tuple-element.84.refs_0_.refs_4_), channel_id=1, source_target_pairs={{0,24},{8,16},{16,8},{24,0},{1,25},{9,17},{17,9},{25,1},{2,26},{10... | collective-permute-start | bytes 12296 | tf_op jit(solution)/shard_map/ppermute | solution.py:646
  49.7 4.7 %collective-permute-start.11 = (f32[8,128]{1,0:T(8,128)S(1)}, f32[8,128]{1,0:T(8,128)S(1)}, u32[]{:S(2)}, u32[]{:S(2)}) collective-permute-start(f32[8,128]{1,0:T(8,128)S(1)} %get-tuple-element.84.refs_0_.refs_4_), channel_id=1, source_target_pairs={{0,16},{8,24},{16,0},{24,8},{1,17},{9,25},{17,1},{25,9},{2,18},{10... | collective-permute-start | bytes 12296 | tf_op jit(solution)/shard_map/ppermute | solution.py:646
  50.5 3.9 %collective-permute-start.10 = (f32[8,128]{1,0:T(8,128)S(1)}, f32[8,128]{1,0:T(8,128)S(1)}, u32[]{:S(2)}, u32[]{:S(2)}) collective-permute-start(f32[8,128]{1,0:T(8,128)S(1)} %get-tuple-element.84.refs_0_.refs_4_), channel_id=1, source_target_pairs={{0,8},{8,0},{16,24},{24,16},{1,9},{9,1},{17,25},{25,17},{2,10},{10... | collective-permute-start | bytes 12296 | tf_op jit(solution)/shard_map/ppermute | solution.py:646
  54.3 4.7 %collective-permute-start.14 = (f32[6,16,128]{2,1,0:T(8,128)S(1)}, f32[6,16,128]{2,1,0:T(8,128)S(1)}, u32[]{:S(2)}, u32[]{:S(2)}) collective-permute-start(f32[6,16,128]{2,1,0:T(8,128)S(1)} %get-tuple-element.105), channel_id=1, source_target_pairs={{0,8},{8,0},{16,24},{24,16},{1,9},{9,1},{17,25},{25,17},{2,10},{10... | collective-permute-start | bytes 147464 | tf_op jit(solution)/shard_map/ppermute | solution.py:646
  58.5 1.4 %collective-permute-start.13 = (f32[6,16,128]{2,1,0:T(8,128)S(1)}, f32[6,16,128]{2,1,0:T(8,128)S(1)}, u32[]{:S(2)}, u32[]{:S(2)}) collective-permute-start(f32[6,16,128]{2,1,0:T(8,128)S(1)} %get-tuple-element.99), channel_id=1, source_target_pairs={{0,8},{8,0},{16,24},{24,16},{1,9},{9,1},{17,25},{25,17},{2,10},{10... | collective-permute-start | bytes 147464 | tf_op jit(solution)/shard_map/ppermute | solution.py:646
  59.0 6.2 %collective-permute-start.19 = (f32[6,16,128]{2,1,0:T(8,128)S(1)}, f32[6,16,128]{2,1,0:T(8,128)S(1)}, u32[]{:S(2)}, u32[]{:S(2)}) collective-permute-start(f32[6,16,128]{2,1,0:T(8,128)S(1)} %add.26.ready1.second), channel_id=1, source_target_pairs={{0,16},{8,24},{16,0},{24,8},{1,17},{9,25},{17,1},{25,9},{2,18},{10... | collective-permute-start | bytes 147464 | tf_op jit(solution)/shard_map/ppermute | solution.py:646
  59.9 5.4 %collective-permute-start.18 = (f32[6,16,128]{2,1,0:T(8,128)S(1)}, f32[6,16,128]{2,1,0:T(8,128)S(1)}, u32[]{:S(2)}, u32[]{:S(2)}) collective-permute-start(f32[6,16,128]{2,1,0:T(8,128)S(1)} %add.25.ready0.first), channel_id=1, source_target_pairs={{0,16},{8,24},{16,0},{24,8},{1,17},{9,25},{17,1},{25,9},{2,18},{10... | collective-permute-start | bytes 147464 | tf_op jit(solution)/shard_map/ppermute | solution.py:646
  66.1 15.1 %all-to-all-start.1 = ((bf16[8,192,128]{2,1,0:T(8,128)(2,1)}), bf16[8,192,128]{2,1,0:T(8,128)(2,1)S(1)}, u32[]{:S(2)}, u32[]{:S(2)}) async-start(bf16[8,192,128]{2,1,0:T(8,128)(2,1)} %shard_map.204), calls=%async_computation.1 | async-start | bytes 786432 | tf_op jit(solution)/shard_map/all_to_all | solution.py:825
  69.5 2.0 %collective-permute-start.15 = (f32[64,128]{1,0:T(8,128)S(1)}, f32[64,128]{1,0:T(8,128)S(1)}, u32[]{:S(2)}, u32[]{:S(2)}) collective-permute-start(f32[64,128]{1,0:T(8,128)S(1)} %get-tuple-element.107), channel_id=1, source_target_pairs={{0,8},{8,0},{16,24},{24,16},{1,9},{9,1},{17,25},{25,17},{2,10},{10... | collective-permute-start | bytes 98312 | tf_op jit(solution)/shard_map/ppermute | solution.py:646
  69.6 4.1 %collective-permute-start.16 = (f32[64,128]{1,0:T(8,128)S(1)}, f32[64,128]{1,0:T(8,128)S(1)}, u32[]{:S(2)}, u32[]{:S(2)}) collective-permute-start(f32[64,128]{1,0:T(8,128)S(1)} %get-tuple-element.108), channel_id=1, source_target_pairs={{0,16},{8,24},{16,0},{24,8},{1,17},{9,25},{17,1},{25,9},{2,18},{10... | collective-permute-start | bytes 98312 | tf_op jit(solution)/shard_map/ppermute | solution.py:646
  70.5 3.6 %collective-permute-start.17 = (f32[64,128]{1,0:T(8,128)S(1)}, f32[64,128]{1,0:T(8,128)S(1)}, u32[]{:S(2)}, u32[]{:S(2)}) collective-permute-start(f32[64,128]{1,0:T(8,128)S(1)} %get-tuple-element.109), channel_id=1, source_target_pairs={{0,24},{8,16},{16,8},{24,0},{1,25},{9,17},{17,9},{25,1},{2,26},{10... | collective-permute-start | bytes 98312 | tf_op jit(solution)/shard_map/ppermute | solution.py:646
  81.2 1.7 %collective-permute-start.20 = (bf16[8,192,128]{2,1,0:T(8,128)(2,1)S(1)}, bf16[8,192,128]{2,1,0:T(8,128)(2,1)S(1)}, u32[]{:S(2)}, u32[]{:S(2)}) collective-permute-start(bf16[8,192,128]{2,1,0:T(8,128)(2,1)S(1)} %all-to-all-done.1.near), channel_id=1, source_target_pairs={{0,8},{8,0},{16,24},{24,16},{1,9},{9,1},{17,25},{25,17},{2,10},{10... | collective-permute-start | bytes 1179656 | tf_op jit(solution)/shard_map/ppermute | solution.py:646
